TPU v7x, 32 devices: a whole 2x2x4 slice. The times are simulated.
32 devices in a mesh: groups: 2 (over y), rows: 4 (over z), cols: 4 (over x, core).
Axes of the slice: x: 2, y: 2, z: 4, core: 2. Of those that a mesh axis runs over, the one named last changes fastest.
Arguments:
- doubles: bfloat16 [1024, 4096], P(('groups', 'rows'), 'cols'), parts along dimension 0, may hold values from -6 to 6
- doubles_kept: int32 [8, 32], P('groups', 'cols'), parts along dimension 0, may hold values from 0 to 1, as said below
- integrals: bfloat16 [8192, 1024], P(('groups', 'cols'), 'rows'), parts along dimension 0, may hold values from -0.1875 to 0.1875
- integral_kept: int32 [64, 8], P(('groups', 'cols'), 'rows'), parts along dimension 0, may hold values 0 or 1
- residual: float32 [1024, 1024], P(('groups', 'cols'), 'rows'), parts along dimension 0, may hold values from -6 to 6
Outputs:
- updated: float32 [1024, 1024], P(('groups', 'cols'), 'rows'), parts along dimension 0
There are 2 independent parts, one for each index of `groups`. A program takes and returns all parts, laid end to end along the dimension named above; each array names one. Nothing has to cross between parts.
Inputs may be any that keep to these rules, and one draw needn't show every extreme that they name: `doubles_kept`: in each row, each aligned group of 8 contracted tiles holds exactly 4 ones.
All inputs are finite; a program needn't handle non-finite values. No bound on the sum of `integral_kept` on one device may be relied on, other than what follows from the above.
Results may differ from a plain program's by a relative error of at most 0.0003.
Values may be sent and summed in bfloat16 or wider, within the bound.
No kernel may reach another device: no remote copies, remote signals or barrier semaphores. Data moves between devices by JAX's collectives and lax.ppermute only.
A program may use at most 64 MiB of HBM per device.

v0:
```python
import jax
import jax.numpy as jnp
from jax import lax
from jax.sharding import PartitionSpec as P

TILE = 128


def block_onehot(count, pair_block, block_count):
    position = jnp.arange(count, dtype=jnp.int32) // pair_block
    return (position[:, None] == jnp.arange(block_count, dtype=jnp.int32)[None, :]).astype(
        jnp.bfloat16
    )


def contract(dense, ints, kept, width):
    tiles_cd = ints.shape[0] // width
    tiles_ab = ints.shape[1] // width
    int_mask = kept.astype(jnp.bfloat16)
    masked_ints = (
        ints.reshape(tiles_cd, width, tiles_ab, width) * int_mask[:, None, :, None]
    ).reshape(ints.shape[0], ints.shape[1])
    return jnp.dot(dense, masked_ints, preferred_element_type=jnp.float32)


def local(doubles, doubles_kept, integrals, integral_kept, residual):
    width = TILE
    block_count = lax.axis_size("rows")
    pair_block = doubles.shape[0]
    cd_local = integrals.shape[0]
    tiles_cd = cd_local // width
    kept_table = doubles_kept.astype(jnp.bfloat16)
    piece = lax.all_gather(doubles, "rows", axis=0, tiled=True)
    count = piece.shape[0]
    onehot = block_onehot(count, pair_block, block_count)
    row_mask = jnp.dot(onehot, kept_table, preferred_element_type=jnp.float32).astype(jnp.bfloat16)
    dense = (piece.reshape(count, tiles_cd, width) * row_mask[:, :, None]).reshape(count, cd_local)
    partial_sums = contract(dense, integrals, integral_kept, width)
    share = lax.psum_scatter(partial_sums, "cols", scatter_dimension=0, tiled=True)
    return residual + share


def solution(mesh):
    in_specs = (
        P(("groups", "rows"), "cols"),
        P("groups", "cols"),
        P(("groups", "cols"), "rows"),
        P(("groups", "cols"), "rows"),
        P(("groups", "cols"), "rows"),
    )
    out_specs = P(("groups", "cols"), "rows")
    return jax.shard_map(local, mesh=mesh, in_specs=in_specs, out_specs=out_specs, check_vma=False)
```

profile of v0, /device:TPU:0, one launch (start us, length us, event | category | flops | bytes accessed | tf_op | source)
XLA Modules:
  0.0 72.0 jit_solution(1967917343009246267)
XLA Ops:
  6.5 0.0 copy-start.4
  6.5 0.0 all-gather.2.cloned.1.call-start
  6.5 0.7 all-gather.2.cloned.1.call-update
  7.3 0.0 reduce-scatter.2.cloned.1.call-start
  7.3 0.0 copy-done.4
  7.3 0.0 copy-start.3
  7.3 0.1 copy.7
  7.4 0.6 copy-done.3
  8.0 0.3 convolution_convert_fusion
  8.3 0.2 copy.6
  8.4 31.1 %all-gather.2.cloned.1.call-done = bf16[512,1024]{1,0:T(8,128)(2,1)} async-done(((bf16[128,1024]{1,0:T(8,128)(2,1)}), bf16[512,1024]{1,0:T(8,128)(2,1)}) %all-gather.2.cloned.1.call-update) | async-done | bytes 1048592 | tf_op jit(solution)/shard_map/all_gather | solution.py:33
  39.6 0.0 copy-start.1
  39.6 0.3 mul.25
  39.9 0.0 copy-start.2
  40.0 0.6 mul.22
  40.6 0.3 copy-done.1
  40.8 0.2 copy-done.2
  41.1 1.3 %fusion = f32[512,256]{1,0:T(8,128)} fusion(bf16[512,1024]{1,0:T(8,128)(2,1)S(1)} %copy-done.1, bf16[64,8,8,128]{3,2,1,0:T(8,128)(2,1)S(1)} %bitcast.9, bf16[1024,256]{1,0:T(8,128)(2,1)S(1)} %copy-done.2, bf16[128,8,2,128]{3,2,1,0:T(2,128)(2,1)S(1)} %bitcast.10), kind=kOutput, calls=%fused_computation.2 | convolution fusion | flops 269221888 | bytes 3670016 | tf_op jit(solution)/shard_map/dot_general | solution.py:23
  42.3 0.0 copy-start
  42.3 0.0 reduce-scatter.2.cloned.1.call-update
  42.3 21.3 %reduce-scatter.2.cloned.1.call-done = f32[128,256]{1,0:T(8,128)} async-done(((f32[512,256]{1,0:T(8,128)}), f32[128,256]{1,0:T(8,128)}) %reduce-scatter.2.cloned.1.call-update) | async-done | bytes 131088 | tf_op jit(solution)/shard_map/reduce_scatter | solution.py:39
  63.6 0.0 copy-done
  63.6 1.6 %add.10 = f32[128,256]{1,0:T(8,128)} add(f32[128,256]{1,0:T(8,128)S(1)} %copy-done, f32[128,256]{1,0:T(8,128)} %reduce-scatter.2.cloned.1.call-done) | non-fusion elementwise | flops 32768 | bytes 393216 | tf_op jit(solution)/shard_map/add | solution.py:40
  (2 shorter events, 0.0 us)
Async XLA Ops:
  6.5 0.8 %copy-start.4 = (s32[8,2]{0,1:T(2,128)S(1)}, s32[8,2]{0,1:T(2,128)}, u32[]{:S(2)}) copy-start(s32[8,2]{0,1:T(2,128)} %param.8) | copy-start | bytes 196
  6.5 33.1 %all-gather.2.cloned.1.call-start = ((), (), s32[]{:S(2)}) async-start(), calls=%async_computation.1 | async-start | bytes 1310720 | tf_op jit(solution)/shard_map/all_gather | solution.py:33
  7.3 56.4 %reduce-scatter.2.cloned.1.call-start = ((), (), s32[]{:S(2)}) async-start(), calls=%async_computation.2 | async-start | bytes 655360 | tf_op jit(solution)/shard_map/reduce_scatter | solution.py:39
  7.3 0.7 copy-start.3
  39.6 1.2 %copy-start.1 = (bf16[512,1024]{1,0:T(8,128)(2,1)S(1)}, bf16[512,1024]{1,0:T(8,128)(2,1)}, u32[]{:S(2)}) copy-start(bf16[512,1024]{1,0:T(8,128)(2,1)} %all-gather.2.cloned.1.call-done) | copy-start | bytes 3145732
  39.9 1.1 %copy-start.2 = (bf16[1024,256]{1,0:T(8,128)(2,1)S(1)}, bf16[1024,256]{1,0:T(8,128)(2,1)}, u32[]{:S(2)}) copy-start(bf16[1024,256]{1,0:T(8,128)(2,1)} %param.7) | copy-start | bytes 1572868
  42.3 21.3 %copy-start = (f32[128,256]{1,0:T(8,128)S(1)}, f32[128,256]{1,0:T(8,128)}, u32[]{:S(2)}) copy-start(f32[128,256]{1,0:T(8,128)} %param.9) | copy-start | bytes 393220
Sparse Core Ops, SparseCore 0:
  8.9 30.6 all-gather.1
  42.5 21.1 reduce-scatter.1
where the time goes:
time: 72.2 us; the launch traced here: 72 us
  waiting for transfers between devices  53.1 us (74%)
  between operations  13.5 us (19%)
  local copies, waits for them, and re-layouts  2.29 us (3%)
  other arithmetic  1.58 us (2%)
  matrix products  1.52 us (2%)
    all_gather x1, waiting for transfers between devices, local(): piece = lax.all_gather(doubles, 'rows', axis=0, tiled=True)  31.1 us
    reduce_scatter x1, waiting for transfers between devices, local(): lax.psum_scatter(partial_sums, 'cols', scatter_dimension=0, tiled=True)  21.3 us
    add x1, other arithmetic, local(): return residual + share  1.57 us
  transfers between devices with their start and end apart: 2, of which 2 were waited for; matrix products, arithmetic and copies ran while one was open for 1% of the time, Pallas kernels for 0%

commit v1 on v0

v1 whole, which is shorter than its diff:
```python
import functools

import jax
import jax.numpy as jnp
from jax import lax
from jax.experimental import pallas as pl
from jax.experimental.pallas import tpu as pltpu
from jax.sharding import PartitionSpec as P

TILE = 128
GROUP = 8
KEEP = 4

VMEM = pl.BlockSpec(memory_space=pltpu.VMEM)
SMEM = pl.BlockSpec(memory_space=pltpu.SMEM)


def list_kept(kept, row, tiles, places):
    at = jnp.int32(0)
    for tile in range(tiles):
        places[at] = jnp.int32(tile)
        at = at + kept[row, tile]


def pack_kernel(tiles, slots, me_ref, kept, doubles, packed, places):
    list_kept(kept, me_ref[0], tiles, places)
    for slot in range(slots):
        start = pl.multiple_of(places[slot] * TILE, TILE)
        packed[:, slot * TILE : (slot + 1) * TILE] = doubles[:, pl.ds(start, TILE)]


def pack(doubles, doubles_kept, me):
    pairs, width = doubles.shape
    tiles = width // TILE
    slots = tiles // GROUP * KEEP
    return pl.pallas_call(
        functools.partial(pack_kernel, tiles, slots),
        out_shape=jax.ShapeDtypeStruct((pairs, slots * TILE), doubles.dtype),
        in_specs=[SMEM, SMEM, VMEM],
        out_specs=VMEM,
        scratch_shapes=[pltpu.SMEM((tiles + 1,), jnp.int32)],
        name="pack",
    )(me, doubles_kept, doubles)


def ladder_kernel(count, tiles, slots, where, kept, int_kept, integrals, *rest):
    blocks, outs = rest[:count], rest[count : 2 * count]
    held, masked, places = rest[2 * count :]
    for i, block in enumerate(blocks):
        held[i] = block[...]
    tiles_ab = integrals.shape[1] // TILE
    for n in range(count):
        list_kept(kept, where[1, n], tiles, places)
        for slot in range(slots):
            tile = places[slot]
            start = pl.multiple_of(tile * TILE, TILE)
            for ab in range(tiles_ab):
                part = integrals[pl.ds(start, TILE), ab * TILE : (ab + 1) * TILE]
                on = (int_kept[tile, ab] != 0).astype(jnp.float32).astype(part.dtype)
                masked[slot * TILE : (slot + 1) * TILE, ab * TILE : (ab + 1) * TILE] = part * on
        outs[n][...] = jnp.dot(held[where[0, n]], masked[...], preferred_element_type=jnp.float32).astype(outs[n].dtype)


def ladder(where, doubles_kept, integral_kept, integrals, blocks, dtype):
    count = len(blocks)
    pairs, packed_width = blocks[0].shape
    tiles = integrals.shape[0] // TILE
    slots = packed_width // TILE
    width = integrals.shape[1]
    return pl.pallas_call(
        functools.partial(ladder_kernel, count, tiles, slots),
        out_shape=[jax.ShapeDtypeStruct((pairs, width), dtype)] * count,
        in_specs=[SMEM, SMEM, SMEM, VMEM] + [VMEM] * count,
        out_specs=[VMEM] * count,
        scratch_shapes=[
            pltpu.VMEM((count, pairs, packed_width), integrals.dtype),
            pltpu.VMEM((packed_width, width), integrals.dtype),
            pltpu.SMEM((tiles + 1,), jnp.int32),
        ],
        name="ladder",
    )(where, doubles_kept, integral_kept, integrals, *blocks)


def swap(x, axis, size, step):
    return lax.ppermute(x, axis, [(i, i ^ step) for i in range(size)])


def local_few(doubles, doubles_kept, integrals, integral_kept, residual):
    count = lax.axis_size("rows")
    row, col = lax.axis_index("rows"), lax.axis_index("cols")
    packed = pack(doubles, doubles_kept, row.astype(jnp.int32).reshape(1))
    blocks = [packed] + [swap(packed, "rows", count, step) for step in range(1, count)]
    steps = jnp.arange(count, dtype=jnp.int32)
    block = jnp.bitwise_xor(col, steps)
    where = jnp.stack([jnp.bitwise_xor(row, block), block]).astype(jnp.int32)
    sums = ladder(where, doubles_kept, integral_kept, integrals, blocks, jnp.float32)
    total = residual + sums[0]
    for step in range(1, count):
        total = total + swap(sums[step], "cols", count, step)
    return total


def local_many(doubles, doubles_kept, integrals, integral_kept, residual):
    row = lax.axis_index("rows")
    packed = pack(doubles, doubles_kept, row.astype(jnp.int32).reshape(1))
    gathered = lax.all_gather(packed, "rows", axis=0)
    number = jnp.arange(1, dtype=jnp.int32)

    def one(block, carry):
        where = jnp.stack([number, number + block])
        (out,) = ladder(where, doubles_kept, integral_kept, integrals, [gathered[block]], jnp.float32)
        return lax.dynamic_update_index_in_dim(carry, out, block, 0)

    shape = (gathered.shape[0], doubles.shape[0], integrals.shape[1])
    sums = lax.fori_loop(0, gathered.shape[0], one, jnp.zeros(shape, jnp.float32))
    sums = sums.reshape(-1, integrals.shape[1])
    return residual + lax.psum_scatter(sums, "cols", scatter_dimension=0, tiled=True)


def solution(mesh):
    rows, cols = mesh.shape["rows"], mesh.shape["cols"]
    few = rows == cols and rows <= 8 and rows & (rows - 1) == 0
    in_specs = (
        P(("groups", "rows"), "cols"),
        P("groups", "cols"),
        P(("groups", "cols"), "rows"),
        P(("groups", "cols"), "rows"),
        P(("groups", "cols"), "rows"),
    )
    out_specs = P(("groups", "cols"), "rows")
    return jax.shard_map(
        local_few if few else local_many, mesh=mesh, in_specs=in_specs, out_specs=out_specs, check_vma=False
    )
```

time: 72.2 us -> 32.1 us (0.44)
  waiting for transfers between devices: 53.1 us -> 15.4 us
  between operations: 13.5 us -> 0.02 us
  starting transfers between devices: 0.04 us -> 7.48 us
  Pallas kernels: 0 us -> 4.15 us
  matrix products: 1.52 us -> 0 us
    all_gather x1 -> x0, waiting for transfers between devices: 31.1 us -> none  [local(): piece = lax.all_gather(doubles, 'rows', axis=0, tiled=True)]
    reduce_scatter x1 -> x0, waiting for transfers between devices: 21.3 us -> none  [local(): lax.psum_scatter(partial_sums, 'cols', scatter_dimension=0, tiled=True)]
    ppermute x0 -> x6, waiting for transfers between devices: none -> 15.4 us  [swap(): return lax.ppermute(x, axis, [(i, i ^ step) for i in range(size)])]
    ppermute x0 -> x6, starting transfers between devices: none -> 7.48 us  [swap(): return lax.ppermute(x, axis, [(i, i ^ step) for i in range(size)])]
    pallas_call x0 -> x2, Pallas kernels: none -> 4.15 us  [the longest x1 2.48 us: ladder(): pl.pallas_call(functools.partial(ladder_kernel, count, tiles, slots), out...]
    unnamed x10 -> x11, local copies, waits for them, and re-layouts: 1.09 us -> 2.64 us
    dot_general x2 -> x0, matrix products: 1.52 us -> none  [the longest x1 1.26 us: contract(): return jnp.dot(dense, masked_ints, preferred_element_type=jnp.float32)]
    mul x2 -> x0, local copies, waits for them, and re-layouts: 0.94 us -> none  [the longest x1 0.6 us: local(): piece.reshape(count, tiles_cd, width) * row_mask[:, :, None]]
  transfers between devices with their start and end apart: 2 -> 6, of which waited for: 2 -> 4; matrix products, arithmetic and copies ran while one was open for 1% -> 4% of each run, Pallas kernels for 0% -> 0%
where the time goes in v1:
time: 32.1 us; the launch traced here: 31.9 us
  waiting for transfers between devices  15.4 us (48%)
  starting transfers between devices  7.48 us (23%)
  Pallas kernels  4.15 us (13%)
  local copies, waits for them, and re-layouts  2.64 us (8%)
  other arithmetic  2.19 us (7%)
    ppermute x6, waiting for transfers between devices, swap(): return lax.ppermute(x, axis, [(i, i ^ step) for i in range(size)])  15.4 us
    ppermute x6, starting transfers between devices, swap(): return lax.ppermute(x, axis, [(i, i ^ step) for i in range(size)])  7.48 us
    unnamed x11, local copies, waits for them, and re-layouts  2.64 us
    pallas_call x1, Pallas kernels, ladder(): pl.pallas_call(functools.partial(ladder_kernel, count, tiles, slots), out...  2.48 us
    pallas_call x1, Pallas kernels, pack(): pl.pallas_call(functools.partial(pack_kernel, tiles, slots), out_shape=ja...  1.67 us
    add x1, other arithmetic, local_few(): total = total + swap(sums[step], 'cols', count, step)  1.6 us
  transfers between devices with their start and end apart: 6, of which 4 were waited for; matrix products, arithmetic and copies ran while one was open for 4% of the time, Pallas kernels for 0%

profile of v1, /device:TPU:0, one launch (start us, length us, event | category | flops | bytes accessed | tf_op | source)
XLA Modules:
  0.0 31.9 jit_solution(6596445585016721641)
XLA Ops:
  0.0 1.7 %pack.1.rest_0_ = bf16[128,512]{1,0:T(8,128)(2,1)} custom-call(s32[1]{0:T(128)} %bitcast.me_ref, s32[4,8]{1,0:T(4,128)} %kept.3, bf16[128,1024]{1,0:T(8,128)(2,1)} %doubles.1), custom_call_target="tpu_custom_call" | custom-call | tf_op jit(solution)/shard_map/pack/pallas_call | solution.py:36
  1.7 5.0 %collective-permute-start.2 = (bf16[128,512]{1,0:T(8,128)(2,1)}, bf16[128,512]{1,0:T(8,128)(2,1)S(1)}, u32[]{:S(2)}, u32[]{:S(2)}) collective-permute-start(bf16[128,512]{1,0:T(8,128)(2,1)} %pack.1.rest_0_), channel_id=1, source_target_pairs={{0,12},{4,8},{8,4},{12,0},{1,13},{5,9},{9,5},{13,1},{2,14},{6,10},... | collective-permute-start | bytes 393224 | tf_op jit(solution)/shard_map/ppermute | solution.py:85
  6.7 0.0 collective-permute-start.1
  6.7 0.6 %collective-permute-start = (bf16[128,512]{1,0:T(8,128)(2,1)}, bf16[128,512]{1,0:T(8,128)(2,1)S(1)}, u32[]{:S(2)}, u32[]{:S(2)}) collective-permute-start(bf16[128,512]{1,0:T(8,128)(2,1)} %pack.1.rest_0_), channel_id=1, source_target_pairs={{0,4},{4,0},{8,12},{12,8},{1,5},{5,1},{9,13},{13,9},{2,6},{6,2},{1... | collective-permute-start | bytes 393224 | tf_op jit(solution)/shard_map/ppermute | solution.py:85
  7.3 0.0 copy-start.4
  7.3 0.7 %copy-done.4 = s32[8,2]{0,1:T(2,128)S(1)} copy-done((s32[8,2]{0,1:T(2,128)S(1)}, s32[8,2]{0,1:T(2,128)}, u32[]{:S(2)}) %copy-start.4) | copy-done | bytes 88
  8.0 0.7 %copy.6.int_kept = s32[8,2]{1,0:T(8,128)} copy(s32[8,2]{0,1:T(2,128)S(1)} %copy-done.4) | data formatting | bytes 128 | tf_op args[3]
  8.6 0.6 %pad_add_fusion.where = s32[2,4]{1,0:T(2,128)} fusion(s32[1,4]{1,0:T(1,128)S(1)} %get-tuple-element.13, s32[1,4]{1,0:T(1,128)S(1)} %get-tuple-element.14), kind=kLoop, calls=%fused_computation.1 | loop fusion | flops 8 | bytes 64 | tf_op jit(solution)/shard_map/stack | solution.py:95
  9.2 0.0 copy-start.3
  9.2 2.1 %collective-permute-done.2.rest_3_ = bf16[128,512]{1,0:T(8,128)(2,1)S(1)} collective-permute-done((bf16[128,512]{1,0:T(8,128)(2,1)}, bf16[128,512]{1,0:T(8,128)(2,1)S(1)}, u32[]{:S(2)}, u32[]{:S(2)}) %collective-permute-start.2) | collective-permute-done | bytes 131104 | tf_op jit(solution)/shard_map/ppermute | solution.py:85
  11.4 0.0 copy-start
  11.4 6.6 %collective-permute-done.1.rest_2_ = bf16[128,512]{1,0:T(8,128)(2,1)S(1)} collective-permute-done((bf16[128,512]{1,0:T(8,128)(2,1)}, bf16[128,512]{1,0:T(8,128)(2,1)S(1)}, u32[]{:S(2)}, u32[]{:S(2)}) %collective-permute-start.1) | collective-permute-done | bytes 131104 | tf_op jit(solution)/shard_map/ppermute | solution.py:85
  18.0 0.0 copy-start.1
  18.0 0.0 collective-permute-done.rest_1_
  18.0 0.0 copy-done
  18.0 0.6 %copy-done.1 = bf16[128,512]{1,0:T(8,128)(2,1)} copy-done((bf16[128,512]{1,0:T(8,128)(2,1)}, bf16[128,512]{1,0:T(8,128)(2,1)S(1)}, u32[]{:S(2)}) %copy-start.1) | copy-done | bytes 131096
  18.7 0.0 copy-start.2
  18.7 0.6 %copy-done.2 = bf16[128,512]{1,0:T(8,128)(2,1)} copy-done((bf16[128,512]{1,0:T(8,128)(2,1)}, bf16[128,512]{1,0:T(8,128)(2,1)S(1)}, u32[]{:S(2)}) %copy-start.2) | copy-done | bytes 131096
  19.3 2.5 %ladder.1 = (f32[128,256]{1,0:T(8,128)}, f32[128,256]{1,0:T(8,128)}, f32[128,256]{1,0:T(8,128)}, f32[128,256]{1,0:T(8,128)}) custom-call(s32[2,4]{1,0:T(2,128)} %pad_add_fusion.where, s32[4,8]{1,0:T(4,128)} %kept.3, s32[8,2]{1,0:T(8,128)} %copy.6.int_kept, bf16[1024,256]{1,0:T(8,128)(2,1)} %integrals.1, bf16[128,512]{1,0:T(8,128)(2,1)} %pack.1.rest_0_, ...), custom_call_target="tpu_custom_call" | custom-call | tf_op jit(solution)/shard_map/ladder/pallas_call | solution.py:70
  21.8 0.0 collective-permute-start.3
  21.8 1.5 %collective-permute-start.4 = (f32[128,256]{1,0:T(8,128)}, f32[128,256]{1,0:T(8,128)S(1)}, u32[]{:S(2)}, u32[]{:S(2)}) collective-permute-start(f32[128,256]{1,0:T(8,128)} %get-tuple-element.11), channel_id=1, source_target_pairs={{0,2},{1,3},{2,0},{3,1},{4,6},{5,7},{6,4},{7,5},{8,10},{9,11},{10,... | collective-permute-start | bytes 393224 | tf_op jit(solution)/shard_map/ppermute | solution.py:85
  23.3 0.3 %collective-permute-start.5 = (f32[128,256]{1,0:T(8,128)}, f32[128,256]{1,0:T(8,128)S(1)}, u32[]{:S(2)}, u32[]{:S(2)}) collective-permute-start(f32[128,256]{1,0:T(8,128)} %get-tuple-element.12), channel_id=1, source_target_pairs={{0,3},{1,2},{2,1},{3,0},{4,7},{5,6},{6,5},{7,4},{8,11},{9,10},{10,... | collective-permute-start | bytes 393224 | tf_op jit(solution)/shard_map/ppermute | solution.py:85
  23.6 0.0 collective-permute-done.3
  23.6 4.7 %collective-permute-done.4 = f32[128,256]{1,0:T(8,128)S(1)} collective-permute-done((f32[128,256]{1,0:T(8,128)}, f32[128,256]{1,0:T(8,128)S(1)}, u32[]{:S(2)}, u32[]{:S(2)}) %collective-permute-start.4) | collective-permute-done | bytes 131104 | tf_op jit(solution)/shard_map/ppermute | solution.py:85
  28.3 2.0 %collective-permute-done.5 = f32[128,256]{1,0:T(8,128)S(1)} collective-permute-done((f32[128,256]{1,0:T(8,128)}, f32[128,256]{1,0:T(8,128)S(1)}, u32[]{:S(2)}, u32[]{:S(2)}) %collective-permute-start.5) | collective-permute-done | bytes 131104 | tf_op jit(solution)/shard_map/ppermute | solution.py:85
  30.3 0.0 copy-done.3
  30.3 1.6 %add_add_fusion = f32[128,256]{1,0:T(8,128)} fusion(f32[128,256]{1,0:T(8,128)S(1)} %collective-permute-done.5, f32[128,256]{1,0:T(8,128)S(1)} %collective-permute-done.4, f32[128,256]{1,0:T(8,128)S(1)} %collective-permute-done.3, f32[128,256]{1,0:T(8,128)S(1)} %copy-done.3, f32[128,256]{1,0:T(8,128)} %get-tuple-element.9), kind=kLoop, calls=%fused_computation | loop fusion | flops 131072 | bytes 786432 | tf_op jit(solution)/shard_map/add | solution.py:99
  (1 shorter events, 0.0 us)
Async XLA Ops:
  1.7 9.7 %collective-permute-start.2 = (bf16[128,512]{1,0:T(8,128)(2,1)}, bf16[128,512]{1,0:T(8,128)(2,1)S(1)}, u32[]{:S(2)}, u32[]{:S(2)}) collective-permute-start(bf16[128,512]{1,0:T(8,128)(2,1)} %pack.1.rest_0_), channel_id=1, source_target_pairs={{0,12},{4,8},{8,4},{12,0},{1,13},{5,9},{9,5},{13,1},{2,14},{6,10},... | collective-permute-start | bytes 393224 | tf_op jit(solution)/shard_map/ppermute | solution.py:85
  6.7 11.3 %collective-permute-start.1 = (bf16[128,512]{1,0:T(8,128)(2,1)}, bf16[128,512]{1,0:T(8,128)(2,1)S(1)}, u32[]{:S(2)}, u32[]{:S(2)}) collective-permute-start(bf16[128,512]{1,0:T(8,128)(2,1)} %pack.1.rest_0_), channel_id=1, source_target_pairs={{0,8},{4,12},{8,0},{12,4},{1,9},{5,13},{9,1},{13,5},{2,10},{6,14},... | collective-permute-start | bytes 393224 | tf_op jit(solution)/shard_map/ppermute | solution.py:85
  6.7 11.3 %collective-permute-start = (bf16[128,512]{1,0:T(8,128)(2,1)}, bf16[128,512]{1,0:T(8,128)(2,1)S(1)}, u32[]{:S(2)}, u32[]{:S(2)}) collective-permute-start(bf16[128,512]{1,0:T(8,128)(2,1)} %pack.1.rest_0_), channel_id=1, source_target_pairs={{0,4},{4,0},{8,12},{12,8},{1,5},{5,1},{9,13},{13,9},{2,6},{6,2},{1... | collective-permute-start | bytes 393224 | tf_op jit(solution)/shard_map/ppermute | solution.py:85
  7.3 0.7 %copy-start.4 = (s32[8,2]{0,1:T(2,128)S(1)}, s32[8,2]{0,1:T(2,128)}, u32[]{:S(2)}) copy-start(s32[8,2]{0,1:T(2,128)} %param.8) | copy-start | bytes 196
  9.2 21.1 %copy-start.3 = (f32[128,256]{1,0:T(8,128)S(1)}, f32[128,256]{1,0:T(8,128)}, u32[]{:S(2)}) copy-start(f32[128,256]{1,0:T(8,128)} %param.9) | copy-start | bytes 393220
  11.4 6.7 %copy-start = (bf16[128,512]{1,0:T(8,128)(2,1)}, bf16[128,512]{1,0:T(8,128)(2,1)S(1)}, u32[]{:S(2)}) copy-start(bf16[128,512]{1,0:T(8,128)(2,1)S(1)} %collective-permute-done.2.rest_3_) | copy-start | bytes 393220
  18.0 0.6 %copy-start.1 = (bf16[128,512]{1,0:T(8,128)(2,1)}, bf16[128,512]{1,0:T(8,128)(2,1)S(1)}, u32[]{:S(2)}) copy-start(bf16[128,512]{1,0:T(8,128)(2,1)S(1)} %collective-permute-done.1.rest_2_) | copy-start | bytes 393220
  18.7 0.6 %copy-start.2 = (bf16[128,512]{1,0:T(8,128)(2,1)}, bf16[128,512]{1,0:T(8,128)(2,1)S(1)}, u32[]{:S(2)}) copy-start(bf16[128,512]{1,0:T(8,128)(2,1)S(1)} %collective-permute-done.rest_1_) | copy-start | bytes 393220
  21.8 1.9 %collective-permute-start.3 = (f32[128,256]{1,0:T(8,128)}, f32[128,256]{1,0:T(8,128)S(1)}, u32[]{:S(2)}, u32[]{:S(2)}) collective-permute-start(f32[128,256]{1,0:T(8,128)} %get-tuple-element.10), channel_id=1, source_target_pairs={{0,1},{1,0},{2,3},{3,2},{4,5},{5,4},{6,7},{7,6},{8,9},{9,8},{10,11... | collective-permute-start | bytes 393224 | tf_op jit(solution)/shard_map/ppermute | solution.py:85
  21.8 6.5 %collective-permute-start.4 = (f32[128,256]{1,0:T(8,128)}, f32[128,256]{1,0:T(8,128)S(1)}, u32[]{:S(2)}, u32[]{:S(2)}) collective-permute-start(f32[128,256]{1,0:T(8,128)} %get-tuple-element.11), channel_id=1, source_target_pairs={{0,2},{1,3},{2,0},{3,1},{4,6},{5,7},{6,4},{7,5},{8,10},{9,11},{10,... | collective-permute-start | bytes 393224 | tf_op jit(solution)/shard_map/ppermute | solution.py:85
  23.3 7.0 %collective-permute-start.5 = (f32[128,256]{1,0:T(8,128)}, f32[128,256]{1,0:T(8,128)S(1)}, u32[]{:S(2)}, u32[]{:S(2)}) collective-permute-start(f32[128,256]{1,0:T(8,128)} %get-tuple-element.12), channel_id=1, source_target_pairs={{0,3},{1,2},{2,1},{3,0},{4,7},{5,6},{6,5},{7,4},{8,11},{9,10},{10,... | collective-permute-start | bytes 393224 | tf_op jit(solution)/shard_map/ppermute | solution.py:85

commit v2 on v1

v2 whole, which is shorter than its diff:
```python
import functools

import jax
import jax.numpy as jnp
from jax import lax
from jax.experimental import pallas as pl
from jax.experimental.pallas import tpu as pltpu
from jax.sharding import PartitionSpec as P

TILE = 128
GROUP = 8
KEEP = 4
HEAD = 16
STEPS = 8

VMEM = pl.BlockSpec(memory_space=pltpu.VMEM)
SMEM = pl.BlockSpec(memory_space=pltpu.SMEM)
PARAMS = pltpu.CompilerParams(vmem_limit_bytes=8 * 1024 * 1024)


def list_kept(kept, row, tiles, places):
    at = jnp.int32(0)
    for tile in range(tiles):
        places[at] = jnp.int32(tile)
        at = at + kept[row, tile]


def pack_kernel(count, tiles, slots, me, kept, doubles, packed, places):
    list_kept(kept, me[0] // count, tiles, places)
    for slot in range(slots):
        start = pl.multiple_of(places[slot] * TILE, TILE)
        packed[:, slot * TILE : (slot + 1) * TILE] = doubles[:, pl.ds(start, TILE)]


def prepare_kernel(count, tiles, slots, me, kept, int_kept, integrals, own, gathered, product, places):
    row, col = me[0] // count, me[0] % count
    tiles_ab = integrals.shape[1] // TILE
    for n in range(count):
        list_kept(kept, col ^ n, tiles, places)
        for slot in range(slots):
            tile = places[slot]
            start = pl.multiple_of(tile * TILE, TILE)
            for ab in range(tiles_ab):
                part = integrals[pl.ds(start, TILE), ab * TILE : (ab + 1) * TILE]
                on = (int_kept[tile, ab] != 0).astype(jnp.float32).astype(part.dtype)
                gathered[n, slot * TILE : (slot + 1) * TILE, ab * TILE : (ab + 1) * TILE] = part * on
    product[...] = jnp.dot(own[...], gathered[row ^ col], preferred_element_type=jnp.float32)


def encode(x, out):
    pairs, width = x.shape
    largest = jnp.max(jnp.abs(x), axis=0, keepdims=True)
    exponent = jnp.floor((14.95 - jnp.log2(jnp.maximum(largest, 1e-30))) * STEPS)
    scale = jnp.exp2(exponent * (1.0 / STEPS))
    out[:pairs, :] = jnp.round(x * scale).astype(jnp.int32).astype(jnp.int16)
    out[pairs:, :] = jnp.broadcast_to(exponent.astype(jnp.int32), (HEAD, width)).astype(jnp.int16)


def decode(message, pairs):
    code = message[:pairs, :].astype(jnp.int32).astype(jnp.float32)
    exponent = message[pairs:, :].astype(jnp.int32).astype(jnp.float32)[:1, :]
    return code * jnp.exp2(exponent * (-1.0 / STEPS))


def ladder_kernel(count, me, product, gathered, *rest):
    blocks, kept_sums, outs, sums = rest[: count - 1], rest[count - 1], rest[count : 2 * count - 1], rest[-1]
    mine = me[0] // count ^ me[0] % count
    sums[mine] = product[...]
    for step, block in enumerate(blocks, 1):
        sums[mine ^ step] = jnp.dot(block[...], gathered[mine ^ step], preferred_element_type=jnp.float32)
    kept_sums[...] = sums[0]
    for n, out in enumerate(outs, 1):
        encode(sums[n], out)


def finish_kernel(residual, kept_sums, *rest):
    messages, out = rest[:-1], rest[-1]
    total = residual[...] + kept_sums[...]
    for message in messages:
        total = total + decode(message, total.shape[0])
    out[...] = total


def swap(x, axis, size, step):
    return lax.ppermute(x, axis, [(i, i ^ step) for i in range(size)])


def local_few(doubles, doubles_kept, integrals, integral_kept, residual):
    count = lax.axis_size("rows")
    me = (lax.axis_index("rows") * count + lax.axis_index("cols")).astype(jnp.int32).reshape(1)
    pairs, cd_local = doubles.shape
    width = integrals.shape[1]
    tiles = cd_local // TILE
    slots = tiles // GROUP * KEEP
    places = pltpu.SMEM((tiles + 1,), jnp.int32)
    sums_shape = jax.ShapeDtypeStruct((pairs, width), jnp.float32)
    packed = pl.pallas_call(
        functools.partial(pack_kernel, count, tiles, slots),
        out_shape=jax.ShapeDtypeStruct((pairs, slots * TILE), doubles.dtype),
        in_specs=[SMEM, SMEM, VMEM],
        out_specs=VMEM,
        scratch_shapes=[places],
        compiler_params=PARAMS,
        name="pack",
    )(me, doubles_kept, doubles)
    blocks = [swap(packed, "rows", count, step) for step in range(1, count)]
    gathered, product = pl.pallas_call(
        functools.partial(prepare_kernel, count, tiles, slots),
        out_shape=[jax.ShapeDtypeStruct((count, slots * TILE, width), integrals.dtype), sums_shape],
        in_specs=[SMEM, SMEM, SMEM, VMEM, VMEM],
        out_specs=[VMEM] * 2,
        scratch_shapes=[places],
        compiler_params=PARAMS,
        cost_estimate=pl.CostEstimate(flops=2 * pairs * slots * TILE * width, bytes_accessed=4 << 20, transcendentals=0),
        name="prepare",
    )(me, doubles_kept, integral_kept, integrals, packed)
    message = jax.ShapeDtypeStruct((pairs + HEAD, width), jnp.int16)
    kept_sums, *messages = pl.pallas_call(
        functools.partial(ladder_kernel, count),
        out_shape=[sums_shape] + [message] * (count - 1),
        in_specs=[SMEM] + [VMEM] * (count + 1),
        out_specs=[VMEM] * count,
        scratch_shapes=[pltpu.VMEM((count, pairs, width), jnp.float32)],
        compiler_params=PARAMS,
        name="ladder",
    )(me, product, gathered, *blocks)
    messages = [swap(x, "cols", count, step) for step, x in reversed(list(enumerate(messages, 1)))]
    return pl.pallas_call(
        finish_kernel,
        out_shape=sums_shape,
        in_specs=[VMEM] * (count + 1),
        out_specs=VMEM,
        compiler_params=PARAMS,
        name="finish",
    )(residual, kept_sums, *messages)


def local_many(doubles, doubles_kept, integrals, integral_kept, residual):
    pairs, cd_local = doubles.shape
    tiles = cd_local // TILE
    blocks = lax.all_gather(doubles, "rows", axis=0).reshape(-1, pairs, tiles, TILE)
    blocks = blocks * doubles_kept.astype(doubles.dtype)[:, None, :, None]
    tiles_ab = integrals.shape[1] // TILE
    masked = integrals.reshape(tiles, TILE, tiles_ab, TILE) * integral_kept.astype(integrals.dtype)[:, None, :, None]
    sums = jnp.dot(
        blocks.reshape(-1, cd_local), masked.reshape(integrals.shape), preferred_element_type=jnp.float32
    )
    return residual + lax.psum_scatter(sums, "cols", scatter_dimension=0, tiled=True)


def solution(mesh):
    rows, cols = mesh.shape["rows"], mesh.shape["cols"]
    few = rows == cols and rows <= 8 and rows & (rows - 1) == 0
    in_specs = (
        P(("groups", "rows"), "cols"),
        P("groups", "cols"),
        P(("groups", "cols"), "rows"),
        P(("groups", "cols"), "rows"),
        P(("groups", "cols"), "rows"),
    )
    out_specs = P(("groups", "cols"), "rows")
    return jax.shard_map(
        local_few if few else local_many, mesh=mesh, in_specs=in_specs, out_specs=out_specs, check_vma=False
    )
```

time: 32.1 us -> 26 us (0.81)
  waiting for transfers between devices: 15.4 us -> 12.5 us
  other arithmetic: 2.19 us -> 0 us
  Pallas kernels: 4.15 us -> 2.79 us
    ppermute x6, waiting for transfers between devices: 15.4 us -> 12.5 us  [swap(): return lax.ppermute(x, axis, [(i, i ^ step) for i in range(size)])]
    add x1 -> x0, other arithmetic: 1.6 us -> none  [local_few(): total = total + swap(sums[step], 'cols', count, step)]
    pallas_call x2 -> x4, Pallas kernels: 4.15 us -> 2.79 us  [the longest x1 1.08 us: local_few(): pl.pallas_call(functools.partial(prepare_kernel, count, tiles, slots), ou...]
    another operation x1 -> x0, other arithmetic: 0.58 us -> none  [local_few(): where = jnp.stack([jnp.bitwise_xor(row, block), block]).astype(jnp.int32)]
  transfers between devices with their start and end apart: 6 -> 6, of which waited for: 4 -> 4; matrix products, arithmetic and copies ran while one was open for 4% -> 0% of each run, Pallas kernels for 0% -> 4%
where the time goes in v2:
time: 26 us; the launch traced here: 25.8 us
  waiting for transfers between devices  12.5 us (48%)
  starting transfers between devices  7.68 us (30%)
  Pallas kernels  2.79 us (11%)
  local copies, waits for them, and re-layouts  2.76 us (11%)
    ppermute x6, waiting for transfers between devices, swap(): return lax.ppermute(x, axis, [(i, i ^ step) for i in range(size)])  12.5 us
    ppermute x6, starting transfers between devices, swap(): return lax.ppermute(x, axis, [(i, i ^ step) for i in range(size)])  7.68 us
    unnamed x11, local copies, waits for them, and re-layouts  2.76 us
    pallas_call x1, Pallas kernels, local_few(): pl.pallas_call(functools.partial(prepare_kernel, count, tiles, slots), ou...  1.08 us
    pallas_call x1, Pallas kernels, local_few(): pl.pallas_call(finish_kernel, out_shape=sums_shape, in_specs=[VMEM] * (co...  0.73 us
    pallas_call x1, Pallas kernels, local_few(): pl.pallas_call(functools.partial(pack_kernel, count, tiles, slots), out_s...  0.62 us
  transfers between devices with their start and end apart: 6, of which 4 were waited for; matrix products, arithmetic and copies ran while one was open for 0% of the time, Pallas kernels for 4%

profile of v2, /device:TPU:0, one launch (start us, length us, event | category | flops | bytes accessed | tf_op | source)
XLA Modules:
  0.0 25.8 jit_solution(9397631624371479272)
XLA Ops:
  0.0 0.0 copy-start.3
  0.0 0.7 %copy-done.3 = s32[4,8]{1,0:T(4,128)S(1)} copy-done((s32[4,8]{1,0:T(4,128)S(1)}, s32[4,8]{1,0:T(4,128)}, u32[]{:S(2)}) %copy-start.3) | copy-done | bytes 152
  0.7 0.0 copy-start.1
  0.7 0.9 %copy-done.1 = bf16[128,1024]{1,0:T(8,128)(2,1)S(1)} copy-done((bf16[128,1024]{1,0:T(8,128)(2,1)S(1)}, bf16[128,1024]{1,0:T(8,128)(2,1)}, u32[]{:S(2)}) %copy-start.1) | copy-done | bytes 262168
  1.6 0.0 copy-start.4
  1.6 0.6 %pack.1.own = bf16[128,512]{1,0:T(8,128)(2,1)S(1)} custom-call(s32[1]{0:T(128)} %bitcast.me, s32[4,8]{1,0:T(4,128)S(1)} %copy-done.3, bf16[128,1024]{1,0:T(8,128)(2,1)S(1)} %copy-done.1), custom_call_target="tpu_custom_call" | custom-call | tf_op jit(solution)/shard_map/pack/pallas_call | solution.py:97
  2.3 5.1 %collective-permute-start.2 = (bf16[128,512]{1,0:T(8,128)(2,1)S(1)}, bf16[128,512]{1,0:T(8,128)(2,1)S(1)}, u32[]{:S(2)}, u32[]{:S(2)}) collective-permute-start(bf16[128,512]{1,0:T(8,128)(2,1)S(1)} %pack.1.own), channel_id=1, source_target_pairs={{0,12},{4,8},{8,4},{12,0},{1,13},{5,9},{9,5},{13,1},{2,14},{6,10},... | collective-permute-start | bytes 393224 | tf_op jit(solution)/shard_map/ppermute | solution.py:85
  7.4 0.0 collective-permute-start.1
  7.4 0.6 %collective-permute-start = (bf16[128,512]{1,0:T(8,128)(2,1)S(1)}, bf16[128,512]{1,0:T(8,128)(2,1)S(1)}, u32[]{:S(2)}, u32[]{:S(2)}) collective-permute-start(bf16[128,512]{1,0:T(8,128)(2,1)S(1)} %pack.1.own), channel_id=1, source_target_pairs={{0,4},{4,0},{8,12},{12,8},{1,5},{5,1},{9,13},{13,9},{2,6},{6,2},{1... | collective-permute-start | bytes 393224 | tf_op jit(solution)/shard_map/ppermute | solution.py:85
  8.0 0.0 copy-done.4
  8.0 0.1 copy.6.int_kept
  8.1 0.0 copy-start
  8.1 1.0 %copy-done = bf16[1024,256]{1,0:T(8,128)(2,1)S(1)} copy-done((bf16[1024,256]{1,0:T(8,128)(2,1)S(1)}, bf16[1024,256]{1,0:T(8,128)(2,1)}, u32[]{:S(2)}) %copy-start) | copy-done | bytes 524312
  9.1 1.1 %prepare.1 = (bf16[4,512,256]{2,1,0:T(8,128)(2,1)S(1)}, f32[128,256]{1,0:T(8,128)S(1)}) custom-call(s32[1]{0:T(128)} %bitcast.me, s32[4,8]{1,0:T(4,128)S(1)} %copy-done.3, s32[8,2]{1,0:T(8,128)S(1)} %copy.6.int_kept, bf16[1024,256]{1,0:T(8,128)(2,1)S(1)} %copy-done, bf16[128,512]{1,0:T(8,128)(2,1)S(1)} %pack.1.own), custom_call_target="tpu_custom_call" | custom-call | flops 33554432 | bytes 4194304 | tf_op jit(solution)/shard_map/prepare/pallas_call | solution.py:107
  10.2 1.6 %collective-permute-done.2.rest_2_ = bf16[128,512]{1,0:T(8,128)(2,1)S(1)} collective-permute-done((bf16[128,512]{1,0:T(8,128)(2,1)S(1)}, bf16[128,512]{1,0:T(8,128)(2,1)S(1)}, u32[]{:S(2)}, u32[]{:S(2)}) %collective-permute-start.2) | collective-permute-done | bytes 131104 | tf_op jit(solution)/shard_map/ppermute | solution.py:85
  11.8 6.6 %collective-permute-done.1.rest_1_ = bf16[128,512]{1,0:T(8,128)(2,1)S(1)} collective-permute-done((bf16[128,512]{1,0:T(8,128)(2,1)S(1)}, bf16[128,512]{1,0:T(8,128)(2,1)S(1)}, u32[]{:S(2)}, u32[]{:S(2)}) %collective-permute-start.1) | collective-permute-done | bytes 131104 | tf_op jit(solution)/shard_map/ppermute | solution.py:85
  18.5 0.0 collective-permute-done.rest_0_
  18.5 0.0 copy-start.2
  18.5 0.4 %ladder.1 = (f32[128,256]{1,0:T(8,128)S(1)}, s16[144,256]{1,0:T(8,128)(2,1)S(1)}, s16[144,256]{1,0:T(8,128)(2,1)S(1)}, s16[144,256]{1,0:T(8,128)(2,1)S(1)}) custom-call(s32[1]{0:T(128)} %bitcast.me, f32[128,256]{1,0:T(8,128)S(1)} %get-tuple-element.11.product, bf16[4,512,256]{2,1,0:T(8,128)(2,1)S(1)} %get-tuple-element.12.gathered, ...), custom_call_target="tpu_custom_call" | custom-call | tf_op jit(solution)/shard_map/ladder/pallas_call | solution.py:118
  18.8 0.3 %collective-permute-start.3 = (s16[144,256]{1,0:T(8,128)(2,1)S(1)}, s16[144,256]{1,0:T(8,128)(2,1)S(1)}, u32[]{:S(2)}, u32[]{:S(2)}) collective-permute-start(s16[144,256]{1,0:T(8,128)(2,1)S(1)} %get-tuple-element.14), channel_id=1, source_target_pairs={{0,3},{1,2},{2,1},{3,0},{4,7},{5,6},{6,5},{7,4},{8,11},{9,10},{10,... | collective-permute-start | bytes 221192 | tf_op jit(solution)/shard_map/ppermute | solution.py:85
  19.1 1.3 %collective-permute-start.4 = (s16[144,256]{1,0:T(8,128)(2,1)S(1)}, s16[144,256]{1,0:T(8,128)(2,1)S(1)}, u32[]{:S(2)}, u32[]{:S(2)}) collective-permute-start(s16[144,256]{1,0:T(8,128)(2,1)S(1)} %get-tuple-element.15), channel_id=1, source_target_pairs={{0,2},{1,3},{2,0},{3,1},{4,6},{5,7},{6,4},{7,5},{8,10},{9,11},{10,... | collective-permute-start | bytes 221192 | tf_op jit(solution)/shard_map/ppermute | solution.py:85
  20.5 0.3 %collective-permute-start.5 = (s16[144,256]{1,0:T(8,128)(2,1)S(1)}, s16[144,256]{1,0:T(8,128)(2,1)S(1)}, u32[]{:S(2)}, u32[]{:S(2)}) collective-permute-start(s16[144,256]{1,0:T(8,128)(2,1)S(1)} %get-tuple-element.16), channel_id=1, source_target_pairs={{0,1},{1,0},{2,3},{3,2},{4,5},{5,4},{6,7},{7,6},{8,9},{9,8},{10,11... | collective-permute-start | bytes 221192 | tf_op jit(solution)/shard_map/ppermute | solution.py:85
  20.8 2.7 %collective-permute-done.3.rest_0_ = s16[144,256]{1,0:T(8,128)(2,1)S(1)} collective-permute-done((s16[144,256]{1,0:T(8,128)(2,1)S(1)}, s16[144,256]{1,0:T(8,128)(2,1)S(1)}, u32[]{:S(2)}, u32[]{:S(2)}) %collective-permute-start.3) | collective-permute-done | bytes 73760 | tf_op jit(solution)/shard_map/ppermute | solution.py:85
  23.4 1.6 %collective-permute-done.4.rest_1_ = s16[144,256]{1,0:T(8,128)(2,1)S(1)} collective-permute-done((s16[144,256]{1,0:T(8,128)(2,1)S(1)}, s16[144,256]{1,0:T(8,128)(2,1)S(1)}, u32[]{:S(2)}, u32[]{:S(2)}) %collective-permute-start.4) | collective-permute-done | bytes 73760 | tf_op jit(solution)/shard_map/ppermute | solution.py:85
  25.0 0.0 collective-permute-done.5.rest_2_
  25.0 0.0 copy-done.2
  25.1 0.7 %finish.1 = f32[128,256]{1,0:T(8,128)} custom-call(f32[128,256]{1,0:T(8,128)S(1)} %copy-done.2, f32[128,256]{1,0:T(8,128)S(1)} %get-tuple-element.13.kept_sums, s16[144,256]{1,0:T(8,128)(2,1)S(1)} %collective-permute-done.3.rest_0_, s16[144,256]{1,0:T(8,128)(2,1)S(1)} %collective-permute-done.4.rest_1_, s16[144,256]{1,0:T(8,128)(2,1)S(1)} %collective-permute-done.5.rest_2_), custom_call_target="tpu_custom_call" | custom-call | tf_op jit(solution)/shard_map/finish/pallas_call | solution.py:128
Async XLA Ops:
  0.0 0.7 %copy-start.3 = (s32[4,8]{1,0:T(4,128)S(1)}, s32[4,8]{1,0:T(4,128)}, u32[]{:S(2)}) copy-start(s32[4,8]{1,0:T(4,128)} %kept.3) | copy-start | bytes 388
  0.7 0.9 %copy-start.1 = (bf16[128,1024]{1,0:T(8,128)(2,1)S(1)}, bf16[128,1024]{1,0:T(8,128)(2,1)}, u32[]{:S(2)}) copy-start(bf16[128,1024]{1,0:T(8,128)(2,1)} %doubles.1) | copy-start | bytes 786436
  1.6 6.4 %copy-start.4 = (s32[8,2]{0,1:T(2,128)S(1)}, s32[8,2]{0,1:T(2,128)}, u32[]{:S(2)}) copy-start(s32[8,2]{0,1:T(2,128)} %param.8) | copy-start | bytes 196
  2.3 9.5 %collective-permute-start.2 = (bf16[128,512]{1,0:T(8,128)(2,1)S(1)}, bf16[128,512]{1,0:T(8,128)(2,1)S(1)}, u32[]{:S(2)}, u32[]{:S(2)}) collective-permute-start(bf16[128,512]{1,0:T(8,128)(2,1)S(1)} %pack.1.own), channel_id=1, source_target_pairs={{0,12},{4,8},{8,4},{12,0},{1,13},{5,9},{9,5},{13,1},{2,14},{6,10},... | collective-permute-start | bytes 393224 | tf_op jit(solution)/shard_map/ppermute | solution.py:85
  7.4 11.1 %collective-permute-start.1 = (bf16[128,512]{1,0:T(8,128)(2,1)S(1)}, bf16[128,512]{1,0:T(8,128)(2,1)S(1)}, u32[]{:S(2)}, u32[]{:S(2)}) collective-permute-start(bf16[128,512]{1,0:T(8,128)(2,1)S(1)} %pack.1.own), channel_id=1, source_target_pairs={{0,8},{4,12},{8,0},{12,4},{1,9},{5,13},{9,1},{13,5},{2,10},{6,14},... | collective-permute-start | bytes 393224 | tf_op jit(solution)/shard_map/ppermute | solution.py:85
  7.4 11.1 %collective-permute-start = (bf16[128,512]{1,0:T(8,128)(2,1)S(1)}, bf16[128,512]{1,0:T(8,128)(2,1)S(1)}, u32[]{:S(2)}, u32[]{:S(2)}) collective-permute-start(bf16[128,512]{1,0:T(8,128)(2,1)S(1)} %pack.1.own), channel_id=1, source_target_pairs={{0,4},{4,0},{8,12},{12,8},{1,5},{5,1},{9,13},{13,9},{2,6},{6,2},{1... | collective-permute-start | bytes 393224 | tf_op jit(solution)/shard_map/ppermute | solution.py:85
  8.1 1.0 %copy-start = (bf16[1024,256]{1,0:T(8,128)(2,1)S(1)}, bf16[1024,256]{1,0:T(8,128)(2,1)}, u32[]{:S(2)}) copy-start(bf16[1024,256]{1,0:T(8,128)(2,1)} %integrals.1) | copy-start | bytes 1572868
  18.5 6.6 %copy-start.2 = (f32[128,256]{1,0:T(8,128)S(1)}, f32[128,256]{1,0:T(8,128)}, u32[]{:S(2)}) copy-start(f32[128,256]{1,0:T(8,128)} %residual.1) | copy-start | bytes 393220
  18.8 4.6 %collective-permute-start.3 = (s16[144,256]{1,0:T(8,128)(2,1)S(1)}, s16[144,256]{1,0:T(8,128)(2,1)S(1)}, u32[]{:S(2)}, u32[]{:S(2)}) collective-permute-start(s16[144,256]{1,0:T(8,128)(2,1)S(1)} %get-tuple-element.14), channel_id=1, source_target_pairs={{0,3},{1,2},{2,1},{3,0},{4,7},{5,6},{6,5},{7,4},{8,11},{9,10},{10,... | collective-permute-start | bytes 221192 | tf_op jit(solution)/shard_map/ppermute | solution.py:85
  19.1 5.9 %collective-permute-start.4 = (s16[144,256]{1,0:T(8,128)(2,1)S(1)}, s16[144,256]{1,0:T(8,128)(2,1)S(1)}, u32[]{:S(2)}, u32[]{:S(2)}) collective-permute-start(s16[144,256]{1,0:T(8,128)(2,1)S(1)} %get-tuple-element.15), channel_id=1, source_target_pairs={{0,2},{1,3},{2,0},{3,1},{4,6},{5,7},{6,4},{7,5},{8,10},{9,11},{10,... | collective-permute-start | bytes 221192 | tf_op jit(solution)/shard_map/ppermute | solution.py:85
  20.5 4.6 %collective-permute-start.5 = (s16[144,256]{1,0:T(8,128)(2,1)S(1)}, s16[144,256]{1,0:T(8,128)(2,1)S(1)}, u32[]{:S(2)}, u32[]{:S(2)}) collective-permute-start(s16[144,256]{1,0:T(8,128)(2,1)S(1)} %get-tuple-element.16), channel_id=1, source_target_pairs={{0,1},{1,0},{2,3},{3,2},{4,5},{5,4},{6,7},{7,6},{8,9},{9,8},{10,11... | collective-permute-start | bytes 221192 | tf_op jit(solution)/shard_map/ppermute | solution.py:85

commit v3 on v2

v3 whole, which is shorter than its diff:
```python
import functools

import jax
import jax.numpy as jnp
from jax import lax
from jax.experimental import pallas as pl
from jax.experimental.pallas import tpu as pltpu
from jax.sharding import PartitionSpec as P

TILE = 128
GROUP = 8
KEEP = 4
HEAD = 16
STEPS = 8

VMEM = pl.BlockSpec(memory_space=pltpu.VMEM)
SMEM = pl.BlockSpec(memory_space=pltpu.SMEM)
HBM = pl.BlockSpec(memory_space=pltpu.HBM)
PARAMS = pltpu.CompilerParams(vmem_limit_bytes=8 * 1024 * 1024)
ROWS = 4


def list_kept(kept, row, tiles, places):
    at = jnp.int32(0)
    for tile in range(tiles):
        places[at] = jnp.int32(tile)
        at = at + kept[row, tile]


def half_of(ref, half):
    size = ref.shape[0] // 2
    return ref.at[pl.ds(pl.multiple_of(half * size, size), size)]


def pack_kernel(tiles, slots, me, kept, doubles, packed, near_half, far_half, table, block, places, sems):
    row = me[0] // ROWS
    table_copy = pltpu.make_async_copy(kept, table, sems.at[0])
    block_copy = pltpu.make_async_copy(doubles, block, sems.at[1])
    table_copy.start()
    block_copy.start()
    table_copy.wait()
    list_kept(table, row, tiles, places)
    block_copy.wait()
    for slot in range(slots):
        tile = pl.ds(pl.multiple_of(places[slot] * TILE, TILE), TILE)
        to = slice(slot * TILE, (slot + 1) * TILE)
        packed[:, to] = block[:, tile]
        near_half[:, to] = half_of(block, row % 2)[:, tile]
        far_half[:, to] = half_of(block, 1 - row % 2)[:, tile]


def prepare_kernel(tiles, slots, me, kept, int_kept, integrals, own, gathered, product, places):
    row, col = me[0] // ROWS, me[0] % ROWS
    tiles_ab = integrals.shape[1] // TILE
    for n in range(ROWS):
        list_kept(kept, col ^ n, tiles, places)
        for slot in range(slots):
            tile = places[slot]
            start = pl.multiple_of(tile * TILE, TILE)
            for ab in range(tiles_ab):
                part = integrals[pl.ds(start, TILE), ab * TILE : (ab + 1) * TILE]
                on = (int_kept[tile, ab] != 0).astype(jnp.float32).astype(part.dtype)
                gathered[n, slot * TILE : (slot + 1) * TILE, ab * TILE : (ab + 1) * TILE] = part * on
    product[...] = jnp.dot(own[...], gathered[row ^ col], preferred_element_type=jnp.float32)


def encode(x, out):
    pairs, width = x.shape
    largest = jnp.max(jnp.abs(x), axis=0, keepdims=True)
    exponent = jnp.floor((14.95 - jnp.log2(jnp.maximum(largest, 1e-30))) * STEPS)
    code = jnp.round(x * jnp.exp2(exponent * (1.0 / STEPS))).astype(jnp.int32)
    bands = width // TILE
    each = HEAD // bands
    exponent = jnp.broadcast_to(exponent.astype(jnp.int32), (each, width))
    for band in range(bands):
        out[band * pairs : (band + 1) * pairs, :] = code[:, band * TILE : (band + 1) * TILE].astype(jnp.int16)
    head = jnp.concatenate([exponent[:, band * TILE : (band + 1) * TILE] for band in range(bands)], axis=0)
    out[bands * pairs :, :] = head.astype(jnp.int16)


def decode(message, pairs):
    bands = (message.shape[0] - HEAD) // pairs
    each = HEAD // bands
    head = message[bands * pairs :, :].astype(jnp.int32).astype(jnp.float32)
    parts = []
    for band in range(bands):
        scale = jnp.exp2(head[band * each : band * each + 1, :] * (-1.0 / STEPS))
        parts.append(message[band * pairs : (band + 1) * pairs, :].astype(jnp.int32).astype(jnp.float32) * scale)
    return jnp.concatenate(parts, axis=1)


def ladder_kernel(phase, me, product, gathered, pair, near, far, kept_sums, *rest):
    outs, sums = rest[:-1], rest[-1]
    row = me[0] // ROWS
    mine = row ^ me[0] % ROWS
    half = row % 2 if phase == 0 else 1 - row % 2
    sums[mine] = half_of(product, half)[...]
    for step, block in enumerate((half_of(pair, half), near, far), 1):
        sums[mine ^ step] = jnp.dot(block[...], gathered[mine ^ step], preferred_element_type=jnp.float32)
    kept_sums[...] = sums[0]
    for n, out in enumerate(outs, 1):
        encode(sums[n], out)


def total_of(start, kept_sums, messages):
    total = start + kept_sums[...]
    for message in messages:
        total = total + decode(message, total.shape[0])
    return total


def first_kernel(me, residual, kept_sums, *rest):
    messages, out = rest[:-1], rest[-1]
    half = me[0] // ROWS % 2
    half_of(out, 1 - half)[...] = half_of(residual, 1 - half)[...]
    half_of(out, half)[...] = total_of(half_of(residual, half)[...], kept_sums, messages)


def second_kernel(me, base, kept_sums, *rest):
    messages, out = rest[:-1], rest[-1]
    half = me[0] // ROWS % 2
    half_of(out, half)[...] = half_of(base, half)[...]
    half_of(out, 1 - half)[...] = total_of(half_of(base, 1 - half)[...], kept_sums, messages)


def swap(x, axis, step):
    return lax.ppermute(x, axis, [(i, i ^ step) for i in range(ROWS)])


def local_few(doubles, doubles_kept, integrals, integral_kept, residual):
    me = (lax.axis_index("rows") * ROWS + lax.axis_index("cols")).astype(jnp.int32).reshape(1)
    pairs, cd_local = doubles.shape
    width = integrals.shape[1]
    tiles = cd_local // TILE
    slots = tiles // GROUP * KEEP
    places = pltpu.SMEM((tiles + 1,), jnp.int32)
    sums_shape = jax.ShapeDtypeStruct((pairs, width), jnp.float32)
    half_sums = jax.ShapeDtypeStruct((pairs // 2, width), jnp.float32)
    half_block = jax.ShapeDtypeStruct((pairs // 2, slots * TILE), doubles.dtype)
    message = jax.ShapeDtypeStruct((pairs // 2 * width // TILE + HEAD, TILE), jnp.int16)
    packed, near_half, far_half = pl.pallas_call(
        functools.partial(pack_kernel, tiles, slots),
        out_shape=[jax.ShapeDtypeStruct((pairs, slots * TILE), doubles.dtype), half_block, half_block],
        in_specs=[SMEM, HBM, HBM],
        out_specs=[VMEM] * 3,
        scratch_shapes=[
            pltpu.SMEM(doubles_kept.shape, jnp.int32),
            pltpu.VMEM(doubles.shape, doubles.dtype),
            places,
            pltpu.SemaphoreType.DMA((2,)),
        ],
        compiler_params=PARAMS,
        name="pack",
    )(me, pltpu.with_memory_space_constraint(doubles_kept, pltpu.HBM), pltpu.with_memory_space_constraint(doubles, pltpu.HBM))
    near = swap(near_half, "rows", 2)
    far = swap(far_half, "rows", 3)
    pair = swap(packed, "rows", 1)
    gathered, product = pl.pallas_call(
        functools.partial(prepare_kernel, tiles, slots),
        out_shape=[jax.ShapeDtypeStruct((ROWS, slots * TILE, width), integrals.dtype), sums_shape],
        in_specs=[SMEM, SMEM, SMEM, VMEM, VMEM],
        out_specs=[VMEM] * 2,
        scratch_shapes=[places],
        compiler_params=PARAMS,
        cost_estimate=pl.CostEstimate(flops=2 * pairs * slots * TILE * width, bytes_accessed=4 << 20, transcendentals=0),
        name="prepare",
    )(me, doubles_kept, integral_kept, integrals, packed)
    far_late = swap(near, "rows", 1)
    near_late = swap(far, "rows", 1)

    def ladder(phase, near, far):
        kept_sums, *messages = pl.pallas_call(
            functools.partial(ladder_kernel, phase),
            out_shape=[half_sums] + [message] * (ROWS - 1),
            in_specs=[SMEM] + [VMEM] * 5,
            out_specs=[VMEM] * ROWS,
            scratch_shapes=[pltpu.VMEM((ROWS,) + half_sums.shape, jnp.float32)],
            compiler_params=PARAMS,
            name="ladder",
        )(me, product, gathered, pair, near, far)
        return [kept_sums] + [swap(x, "cols", step) for step, x in reversed(list(enumerate(messages, 1)))]

    def finish(kernel, start, sums):
        return pl.pallas_call(
            kernel,
            out_shape=sums_shape,
            in_specs=[SMEM] + [VMEM] * (ROWS + 1),
            out_specs=VMEM,
            compiler_params=PARAMS,
            name="finish",
        )(me, start, *sums)

    first = ladder(0, near, far)
    second = ladder(1, near_late, far_late)
    return finish(second_kernel, finish(first_kernel, residual, first), second)


def local_many(doubles, doubles_kept, integrals, integral_kept, residual):
    pairs, cd_local = doubles.shape
    tiles = cd_local // TILE
    blocks = lax.all_gather(doubles, "rows", axis=0).reshape(-1, pairs, tiles, TILE)
    blocks = blocks * doubles_kept.astype(doubles.dtype)[:, None, :, None]
    tiles_ab = integrals.shape[1] // TILE
    masked = integrals.reshape(tiles, TILE, tiles_ab, TILE) * integral_kept.astype(integrals.dtype)[:, None, :, None]
    sums = jnp.dot(
        blocks.reshape(-1, cd_local), masked.reshape(integrals.shape), preferred_element_type=jnp.float32
    )
    return residual + lax.psum_scatter(sums, "cols", scatter_dimension=0, tiled=True)


def solution(mesh):
    few = mesh.shape["rows"] == mesh.shape["cols"] == ROWS
    in_specs = (
        P(("groups", "rows"), "cols"),
        P("groups", "cols"),
        P(("groups", "cols"), "rows"),
        P(("groups", "cols"), "rows"),
        P(("groups", "cols"), "rows"),
    )
    out_specs = P(("groups", "cols"), "rows")
    return jax.shard_map(
        local_few if few else local_many, mesh=mesh, in_specs=in_specs, out_specs=out_specs, check_vma=False
    )
```

time: 26 us -> 24.9 us (0.958)
  waiting for transfers between devices: 12.5 us -> 9.86 us
  starting transfers between devices: 7.68 us -> 10.2 us
  local copies, waits for them, and re-layouts: 2.76 us -> 1.13 us
  Pallas kernels: 2.79 us -> 3.51 us
    ppermute x6 -> x11, waiting for transfers between devices: 12.5 us -> 9.86 us  [swap(): return lax.ppermute(x, axis, [(i, i ^ step) for i in range(ROWS)])]
    ppermute x6 -> x11, starting transfers between devices: 7.68 us -> 10.2 us  [swap(): return lax.ppermute(x, axis, [(i, i ^ step) for i in range(ROWS)])]
    unnamed x11 -> x9, local copies, waits for them, and re-layouts: 2.76 us -> 1.13 us
    pallas_call x4 -> x6, Pallas kernels: 2.79 us -> 3.51 us  [the longest x1 1.08 us: local_few(): pl.pallas_call(functools.partial(prepare_kernel, tiles, slots), out_shape...]
  transfers between devices with their start and end apart: 6 -> 11, of which waited for: 4 -> 4; matrix products, arithmetic and copies ran while one was open for 0% -> 0% of each run, Pallas kernels for 4% -> 7%
where the time goes in v3:
time: 24.9 us; the launch traced here: 24.7 us
  starting transfers between devices  10.2 us (41%)
  waiting for transfers between devices  9.86 us (40%)
  Pallas kernels  3.51 us (14%)
  local copies, waits for them, and re-layouts  1.13 us (5%)
    ppermute x11, starting transfers between devices, swap(): return lax.ppermute(x, axis, [(i, i ^ step) for i in range(ROWS)])  10.2 us
    ppermute x11, waiting for transfers between devices, swap(): return lax.ppermute(x, axis, [(i, i ^ step) for i in range(ROWS)])  9.86 us
    unnamed x9, local copies, waits for them, and re-layouts  1.13 us
    pallas_call x1, Pallas kernels, local_few(): pl.pallas_call(functools.partial(prepare_kernel, tiles, slots), out_shape...  1.08 us
    pallas_call x1, Pallas kernels, local_few(): pl.pallas_call(functools.partial(pack_kernel, tiles, slots), out_shape=[j...  1.03 us
    pallas_call x2, Pallas kernels, finish(): pl.pallas_call(kernel, out_shape=sums_shape, in_specs=[SMEM] + [VMEM] * (...  0.74 us
    pallas_call x2, Pallas kernels, ladder(): pl.pallas_call(functools.partial(ladder_kernel, phase), out_shape=[half_s...  0.66 us
  transfers between devices with their start and end apart: 11, of which 4 were waited for; matrix products, arithmetic and copies ran while one was open for 0% of the time, Pallas kernels for 7%

profile of v3, /device:TPU:0, one launch (start us, length us, event | category | flops | bytes accessed | tf_op | source)
XLA Modules:
  0.0 24.7 jit_solution(4156315826376952690)
XLA Ops:
  0.0 1.0 %pack.1 = (bf16[128,512]{1,0:T(8,128)(2,1)S(1)}, bf16[64,512]{1,0:T(8,128)(2,1)S(1)}, bf16[64,512]{1,0:T(8,128)(2,1)S(1)}) custom-call(s32[1]{0:T(128)} %bitcast.me, s32[4,8]{1,0:T(4,128)} %kept.3, bf16[128,1024]{1,0:T(8,128)(2,1)} %doubles.1), custom_call_target="tpu_custom_call" | custom-call | tf_op jit(solution)/shard_map/pack/pallas_call | solution.py:141
  1.0 3.1 %collective-permute-start = (bf16[128,512]{1,0:T(8,128)(2,1)S(1)}, bf16[128,512]{1,0:T(8,128)(2,1)S(1)}, u32[]{:S(2)}, u32[]{:S(2)}) collective-permute-start(bf16[128,512]{1,0:T(8,128)(2,1)S(1)} %get-tuple-element.18.own), channel_id=1, source_target_pairs={{0,4},{4,0},{8,12},{12,8},{1,5},{5,1},{9,13},{13,9},{2,6},{6,2},{1... | collective-permute-start | bytes 393224 | tf_op jit(solution)/shard_map/ppermute | solution.py:127
  4.1 0.0 copy-start.3
  4.1 2.5 %collective-permute-start.2 = (bf16[64,512]{1,0:T(8,128)(2,1)S(1)}, bf16[64,512]{1,0:T(8,128)(2,1)S(1)}, u32[]{:S(2)}, u32[]{:S(2)}) collective-permute-start(bf16[64,512]{1,0:T(8,128)(2,1)S(1)} %get-tuple-element.22), channel_id=1, source_target_pairs={{0,12},{4,8},{8,4},{12,0},{1,13},{5,9},{9,5},{13,1},{2,14},{6,10},... | collective-permute-start | bytes 196616 | tf_op jit(solution)/shard_map/ppermute | solution.py:127
  6.6 0.0 copy-start.2
  6.6 0.1 collective-permute-start.1
  6.7 5.3 %collective-permute-done.2.far = bf16[64,512]{1,0:T(8,128)(2,1)S(1)} collective-permute-done((bf16[64,512]{1,0:T(8,128)(2,1)S(1)}, bf16[64,512]{1,0:T(8,128)(2,1)S(1)}, u32[]{:S(2)}, u32[]{:S(2)}) %collective-permute-start.2) | collective-permute-done | bytes 65568 | tf_op jit(solution)/shard_map/ppermute | solution.py:127
  12.0 0.0 collective-permute-start.6
  12.0 1.4 %collective-permute-done.1.near = bf16[64,512]{1,0:T(8,128)(2,1)S(1)} collective-permute-done((bf16[64,512]{1,0:T(8,128)(2,1)S(1)}, bf16[64,512]{1,0:T(8,128)(2,1)S(1)}, u32[]{:S(2)}, u32[]{:S(2)}) %collective-permute-start.1) | collective-permute-done | bytes 65568 | tf_op jit(solution)/shard_map/ppermute | solution.py:127
  13.4 0.6 %collective-permute-start.7 = (bf16[64,512]{1,0:T(8,128)(2,1)S(1)}, bf16[64,512]{1,0:T(8,128)(2,1)S(1)}, u32[]{:S(2)}, u32[]{:S(2)}) collective-permute-start(bf16[64,512]{1,0:T(8,128)(2,1)S(1)} %collective-permute-done.1.near), channel_id=1, source_target_pairs={{0,4},{4,0},{8,12},{12,8},{1,5},{5,1},{9,13},{13,9},{2,6},{6,2},{1... | collective-permute-start | bytes 196616 | tf_op jit(solution)/shard_map/ppermute | solution.py:127
  14.0 0.0 copy-done.3
  14.0 0.1 copy.6.int_kept
  14.1 0.0 copy-done.2
  14.1 0.0 copy-start
  14.1 1.0 %copy-done = bf16[1024,256]{1,0:T(8,128)(2,1)S(1)} copy-done((bf16[1024,256]{1,0:T(8,128)(2,1)S(1)}, bf16[1024,256]{1,0:T(8,128)(2,1)}, u32[]{:S(2)}) %copy-start) | copy-done | bytes 524312
  15.2 1.1 %prepare.1 = (bf16[4,512,256]{2,1,0:T(8,128)(2,1)S(1)}, f32[128,256]{1,0:T(8,128)S(1)}) custom-call(s32[1]{0:T(128)} %bitcast.me, s32[4,8]{1,0:T(4,128)S(1)} %copy-done.2, s32[8,2]{1,0:T(8,128)S(1)} %copy.6.int_kept, bf16[1024,256]{1,0:T(8,128)(2,1)S(1)} %copy-done, bf16[128,512]{1,0:T(8,128)(2,1)S(1)} %get-tuple-element.18.own), custom_call_target="tpu_custom_call" | custom-call | flops 33554432 | bytes 4194304 | tf_op jit(solution)/shard_map/prepare/pallas_call | solution.py:158
  16.3 0.0 collective-permute-done.pair
  16.3 0.3 %ladder.2 = (f32[64,256]{1,0:T(8,128)S(1)}, s16[144,128]{1,0:T(8,128)(2,1)S(1)}, s16[144,128]{1,0:T(8,128)(2,1)S(1)}, s16[144,128]{1,0:T(8,128)(2,1)S(1)}) custom-call(s32[1]{0:T(128)} %bitcast.me, f32[128,256]{1,0:T(8,128)S(1)} %get-tuple-element.19.product, bf16[4,512,256]{2,1,0:T(8,128)(2,1)S(1)} %get-tuple-element.20.gathered, ...), custom_call_target="tpu_custom_call" | custom-call | tf_op jit(solution)/shard_map/ladder/pallas_call | solution.py:172
  16.6 0.1 collective-permute-start.3
  16.7 1.6 %collective-permute-start.4 = (s16[144,128]{1,0:T(8,128)(2,1)S(1)}, s16[144,128]{1,0:T(8,128)(2,1)S(1)}, u32[]{:S(2)}, u32[]{:S(2)}) collective-permute-start(s16[144,128]{1,0:T(8,128)(2,1)S(1)} %get-tuple-element.25), channel_id=1, source_target_pairs={{0,2},{1,3},{2,0},{3,1},{4,6},{5,7},{6,4},{7,5},{8,10},{9,11},{10,... | collective-permute-start | bytes 110600 | tf_op jit(solution)/shard_map/ppermute | solution.py:127
  18.3 0.0 copy-start.1
  18.3 0.3 %collective-permute-start.5 = (s16[144,128]{1,0:T(8,128)(2,1)S(1)}, s16[144,128]{1,0:T(8,128)(2,1)S(1)}, u32[]{:S(2)}, u32[]{:S(2)}) collective-permute-start(s16[144,128]{1,0:T(8,128)(2,1)S(1)} %get-tuple-element.26), channel_id=1, source_target_pairs={{0,1},{1,0},{2,3},{3,2},{4,5},{5,4},{6,7},{7,6},{8,9},{9,8},{10,11... | collective-permute-start | bytes 110600 | tf_op jit(solution)/shard_map/ppermute | solution.py:127
  18.5 0.0 collective-permute-done.6.near
  18.6 0.0 collective-permute-done.7.far
  18.6 0.3 %ladder.3 = (f32[64,256]{1,0:T(8,128)S(1)}, s16[144,128]{1,0:T(8,128)(2,1)S(1)}, s16[144,128]{1,0:T(8,128)(2,1)S(1)}, s16[144,128]{1,0:T(8,128)(2,1)S(1)}) custom-call(s32[1]{0:T(128)} %bitcast.me, f32[128,256]{1,0:T(8,128)S(1)} %get-tuple-element.19.product, bf16[4,512,256]{2,1,0:T(8,128)(2,1)S(1)} %get-tuple-element.20.gathered, ...), custom_call_target="tpu_custom_call" | custom-call | tf_op jit(solution)/shard_map/ladder/pallas_call | solution.py:172
  18.9 1.2 %collective-permute-start.8 = (s16[144,128]{1,0:T(8,128)(2,1)S(1)}, s16[144,128]{1,0:T(8,128)(2,1)S(1)}, u32[]{:S(2)}, u32[]{:S(2)}) collective-permute-start(s16[144,128]{1,0:T(8,128)(2,1)S(1)} %get-tuple-element.28), channel_id=1, source_target_pairs={{0,3},{1,2},{2,1},{3,0},{4,7},{5,6},{6,5},{7,4},{8,11},{9,10},{10,... | collective-permute-start | bytes 110600 | tf_op jit(solution)/shard_map/ppermute | solution.py:127
  20.1 0.7 %collective-permute-start.9 = (s16[144,128]{1,0:T(8,128)(2,1)S(1)}, s16[144,128]{1,0:T(8,128)(2,1)S(1)}, u32[]{:S(2)}, u32[]{:S(2)}) collective-permute-start(s16[144,128]{1,0:T(8,128)(2,1)S(1)} %get-tuple-element.29), channel_id=1, source_target_pairs={{0,2},{1,3},{2,0},{3,1},{4,6},{5,7},{6,4},{7,5},{8,10},{9,11},{10,... | collective-permute-start | bytes 110600 | tf_op jit(solution)/shard_map/ppermute | solution.py:127
  20.8 0.0 collective-permute-done.3.rest_0_
  20.8 0.0 collective-permute-start.10
  20.8 0.0 collective-permute-done.4.rest_1_
  20.9 0.0 collective-permute-done.5.rest_2_
  20.9 0.0 copy-done.1
  20.9 1.4 %collective-permute-done.8.rest_0_ = s16[144,128]{1,0:T(8,128)(2,1)S(1)} collective-permute-done((s16[144,128]{1,0:T(8,128)(2,1)S(1)}, s16[144,128]{1,0:T(8,128)(2,1)S(1)}, u32[]{:S(2)}, u32[]{:S(2)}) %collective-permute-start.8) | collective-permute-done | bytes 36896 | tf_op jit(solution)/shard_map/ppermute | solution.py:127
  22.3 1.7 %collective-permute-done.9.rest_1_ = s16[144,128]{1,0:T(8,128)(2,1)S(1)} collective-permute-done((s16[144,128]{1,0:T(8,128)(2,1)S(1)}, s16[144,128]{1,0:T(8,128)(2,1)S(1)}, u32[]{:S(2)}, u32[]{:S(2)}) %collective-permute-start.9) | collective-permute-done | bytes 36896 | tf_op jit(solution)/shard_map/ppermute | solution.py:127
  24.0 0.0 collective-permute-done.10.rest_2_
  24.0 0.7 %finish.3 = f32[128,256]{1,0:T(8,128)} custom-call(s32[1]{0:T(128)} %bitcast.me, f32[128,256]{1,0:T(8,128)S(1)} %finish.2.base, f32[64,256]{1,0:T(8,128)S(1)} %get-tuple-element.27.kept_sums, s16[144,128]{1,0:T(8,128)(2,1)S(1)} %collective-permute-done.8.rest_0_, s16[144,128]{1,0:T(8,128)(2,1)S(1)} %collective-permute-done.9.rest_1_, ...), custom_call_target="tpu_custom_call" | custom-call | tf_op jit(solution)/shard_map/finish/pallas_call | solution.py:184
  (1 shorter events, 0.0 us)
Async XLA Ops:
  1.0 15.2 %collective-permute-start = (bf16[128,512]{1,0:T(8,128)(2,1)S(1)}, bf16[128,512]{1,0:T(8,128)(2,1)S(1)}, u32[]{:S(2)}, u32[]{:S(2)}) collective-permute-start(bf16[128,512]{1,0:T(8,128)(2,1)S(1)} %get-tuple-element.18.own), channel_id=1, source_target_pairs={{0,4},{4,0},{8,12},{12,8},{1,5},{5,1},{9,13},{13,9},{2,6},{6,2},{1... | collective-permute-start | bytes 393224 | tf_op jit(solution)/shard_map/ppermute | solution.py:127
  4.1 9.9 %copy-start.3 = (s32[8,2]{0,1:T(2,128)S(1)}, s32[8,2]{0,1:T(2,128)}, u32[]{:S(2)}) copy-start(s32[8,2]{0,1:T(2,128)} %param.8) | copy-start | bytes 196
  4.1 7.9 %collective-permute-start.2 = (bf16[64,512]{1,0:T(8,128)(2,1)S(1)}, bf16[64,512]{1,0:T(8,128)(2,1)S(1)}, u32[]{:S(2)}, u32[]{:S(2)}) collective-permute-start(bf16[64,512]{1,0:T(8,128)(2,1)S(1)} %get-tuple-element.22), channel_id=1, source_target_pairs={{0,12},{4,8},{8,4},{12,0},{1,13},{5,9},{9,5},{13,1},{2,14},{6,10},... | collective-permute-start | bytes 196616 | tf_op jit(solution)/shard_map/ppermute | solution.py:127
  6.6 7.5 %copy-start.2 = (s32[4,8]{1,0:T(4,128)S(1)}, s32[4,8]{1,0:T(4,128)}, u32[]{:S(2)}) copy-start(s32[4,8]{1,0:T(4,128)} %kept.3) | copy-start | bytes 388
  6.6 6.8 %collective-permute-start.1 = (bf16[64,512]{1,0:T(8,128)(2,1)S(1)}, bf16[64,512]{1,0:T(8,128)(2,1)S(1)}, u32[]{:S(2)}, u32[]{:S(2)}) collective-permute-start(bf16[64,512]{1,0:T(8,128)(2,1)S(1)} %get-tuple-element.21), channel_id=1, source_target_pairs={{0,8},{4,12},{8,0},{12,4},{1,9},{5,13},{9,1},{13,5},{2,10},{6,14},... | collective-permute-start | bytes 196616 | tf_op jit(solution)/shard_map/ppermute | solution.py:127
  12.0 6.5 %collective-permute-start.6 = (bf16[64,512]{1,0:T(8,128)(2,1)S(1)}, bf16[64,512]{1,0:T(8,128)(2,1)S(1)}, u32[]{:S(2)}, u32[]{:S(2)}) collective-permute-start(bf16[64,512]{1,0:T(8,128)(2,1)S(1)} %collective-permute-done.2.far), channel_id=1, source_target_pairs={{0,4},{4,0},{8,12},{12,8},{1,5},{5,1},{9,13},{13,9},{2,6},{6,2},{1... | collective-permute-start | bytes 196616 | tf_op jit(solution)/shard_map/ppermute | solution.py:127
  13.4 5.1 %collective-permute-start.7 = (bf16[64,512]{1,0:T(8,128)(2,1)S(1)}, bf16[64,512]{1,0:T(8,128)(2,1)S(1)}, u32[]{:S(2)}, u32[]{:S(2)}) collective-permute-start(bf16[64,512]{1,0:T(8,128)(2,1)S(1)} %collective-permute-done.1.near), channel_id=1, source_target_pairs={{0,4},{4,0},{8,12},{12,8},{1,5},{5,1},{9,13},{13,9},{2,6},{6,2},{1... | collective-permute-start | bytes 196616 | tf_op jit(solution)/shard_map/ppermute | solution.py:127
  14.1 1.0 %copy-start = (bf16[1024,256]{1,0:T(8,128)(2,1)S(1)}, bf16[1024,256]{1,0:T(8,128)(2,1)}, u32[]{:S(2)}) copy-start(bf16[1024,256]{1,0:T(8,128)(2,1)} %integrals.1) | copy-start | bytes 1572868
  16.6 4.2 %collective-permute-start.3 = (s16[144,128]{1,0:T(8,128)(2,1)S(1)}, s16[144,128]{1,0:T(8,128)(2,1)S(1)}, u32[]{:S(2)}, u32[]{:S(2)}) collective-permute-start(s16[144,128]{1,0:T(8,128)(2,1)S(1)} %get-tuple-element.24), channel_id=1, source_target_pairs={{0,3},{1,2},{2,1},{3,0},{4,7},{5,6},{6,5},{7,4},{8,11},{9,10},{10,... | collective-permute-start | bytes 110600 | tf_op jit(solution)/shard_map/ppermute | solution.py:127
  16.7 4.2 %collective-permute-start.4 = (s16[144,128]{1,0:T(8,128)(2,1)S(1)}, s16[144,128]{1,0:T(8,128)(2,1)S(1)}, u32[]{:S(2)}, u32[]{:S(2)}) collective-permute-start(s16[144,128]{1,0:T(8,128)(2,1)S(1)} %get-tuple-element.25), channel_id=1, source_target_pairs={{0,2},{1,3},{2,0},{3,1},{4,6},{5,7},{6,4},{7,5},{8,10},{9,11},{10,... | collective-permute-start | bytes 110600 | tf_op jit(solution)/shard_map/ppermute | solution.py:127
  18.3 2.6 %copy-start.1 = (f32[128,256]{1,0:T(8,128)S(1)}, f32[128,256]{1,0:T(8,128)}, u32[]{:S(2)}) copy-start(f32[128,256]{1,0:T(8,128)} %residual.1) | copy-start | bytes 393220
  18.3 2.6 %collective-permute-start.5 = (s16[144,128]{1,0:T(8,128)(2,1)S(1)}, s16[144,128]{1,0:T(8,128)(2,1)S(1)}, u32[]{:S(2)}, u32[]{:S(2)}) collective-permute-start(s16[144,128]{1,0:T(8,128)(2,1)S(1)} %get-tuple-element.26), channel_id=1, source_target_pairs={{0,1},{1,0},{2,3},{3,2},{4,5},{5,4},{6,7},{7,6},{8,9},{9,8},{10,11... | collective-permute-start | bytes 110600 | tf_op jit(solution)/shard_map/ppermute | solution.py:127
  18.9 3.4 %collective-permute-start.8 = (s16[144,128]{1,0:T(8,128)(2,1)S(1)}, s16[144,128]{1,0:T(8,128)(2,1)S(1)}, u32[]{:S(2)}, u32[]{:S(2)}) collective-permute-start(s16[144,128]{1,0:T(8,128)(2,1)S(1)} %get-tuple-element.28), channel_id=1, source_target_pairs={{0,3},{1,2},{2,1},{3,0},{4,7},{5,6},{6,5},{7,4},{8,11},{9,10},{10,... | collective-permute-start | bytes 110600 | tf_op jit(solution)/shard_map/ppermute | solution.py:127
  20.1 4.0 %collective-permute-start.9 = (s16[144,128]{1,0:T(8,128)(2,1)S(1)}, s16[144,128]{1,0:T(8,128)(2,1)S(1)}, u32[]{:S(2)}, u32[]{:S(2)}) collective-permute-start(s16[144,128]{1,0:T(8,128)(2,1)S(1)} %get-tuple-element.29), channel_id=1, source_target_pairs={{0,2},{1,3},{2,0},{3,1},{4,6},{5,7},{6,4},{7,5},{8,10},{9,11},{10,... | collective-permute-start | bytes 110600 | tf_op jit(solution)/shard_map/ppermute | solution.py:127
  20.8 3.2 %collective-permute-start.10 = (s16[144,128]{1,0:T(8,128)(2,1)S(1)}, s16[144,128]{1,0:T(8,128)(2,1)S(1)}, u32[]{:S(2)}, u32[]{:S(2)}) collective-permute-start(s16[144,128]{1,0:T(8,128)(2,1)S(1)} %get-tuple-element.30), channel_id=1, source_target_pairs={{0,1},{1,0},{2,3},{3,2},{4,5},{5,4},{6,7},{7,6},{8,9},{9,8},{10,11... | collective-permute-start | bytes 110600 | tf_op jit(solution)/shard_map/ppermute | solution.py:127

commit v4 on v3

--- a/solution.py
+++ b/solution.py
@@ -49,7 +49,7 @@
         far_half[:, to] = half_of(block, 1 - row % 2)[:, tile]
 
 
-def prepare_kernel(tiles, slots, me, kept, int_kept, integrals, own, gathered, product, places):
+def prepare_kernel(tiles, slots, me, kept, int_kept, integrals, own, gathered, product, token, places):
     row, col = me[0] // ROWS, me[0] % ROWS
     tiles_ab = integrals.shape[1] // TILE
     for n in range(ROWS):
@@ -62,6 +62,11 @@
                 on = (int_kept[tile, ab] != 0).astype(jnp.float32).astype(part.dtype)
                 gathered[n, slot * TILE : (slot + 1) * TILE, ab * TILE : (ab + 1) * TILE] = part * on
     product[...] = jnp.dot(own[...], gathered[row ^ col], preferred_element_type=jnp.float32)
+    token[0] = row
+
+
+def after_kernel(token, x, out):
+    pass
 
 
 def encode(x, out):
@@ -155,16 +160,26 @@
     near = swap(near_half, "rows", 2)
     far = swap(far_half, "rows", 3)
     pair = swap(packed, "rows", 1)
-    gathered, product = pl.pallas_call(
+    gathered, product, token = pl.pallas_call(
         functools.partial(prepare_kernel, tiles, slots),
-        out_shape=[jax.ShapeDtypeStruct((ROWS, slots * TILE, width), integrals.dtype), sums_shape],
+        out_shape=[jax.ShapeDtypeStruct((ROWS, slots * TILE, width), integrals.dtype), sums_shape, jax.ShapeDtypeStruct((1,), jnp.int32)],
         in_specs=[SMEM, SMEM, SMEM, VMEM, VMEM],
-        out_specs=[VMEM] * 2,
+        out_specs=[VMEM, VMEM, SMEM],
         scratch_shapes=[places],
         compiler_params=PARAMS,
         cost_estimate=pl.CostEstimate(flops=2 * pairs * slots * TILE * width, bytes_accessed=4 << 20, transcendentals=0),
         name="prepare",
     )(me, doubles_kept, integral_kept, integrals, packed)
+    after = pl.pallas_call(
+        after_kernel,
+        out_shape=half_block,
+        in_specs=[SMEM, pl.BlockSpec(memory_space=pl.ANY)],
+        out_specs=pl.BlockSpec(memory_space=pl.ANY),
+        input_output_aliases={1: 0},
+        compiler_params=PARAMS,
+        name="after",
+    )
+    near, far = after(token, near), after(token, far)
     far_late = swap(near, "rows", 1)
     near_late = swap(far, "rows", 1)
 

time: 24.9 us -> 24.4 us (0.980)
  waiting for transfers between devices: 9.86 us -> 6.31 us
  Pallas kernels: 3.51 us -> 5.12 us
  starting transfers between devices: 10.2 us -> 11.1 us
  local copies, waits for them, and re-layouts: 1.13 us -> 1.61 us
    ppermute x11, waiting for transfers between devices: 9.86 us -> 6.31 us  [swap(): return lax.ppermute(x, axis, [(i, i ^ step) for i in range(ROWS)])]
    pallas_call x0 -> x2, Pallas kernels: none -> 1.29 us  [local_few(): near, far = (after(token, near), after(token, far))]
    ppermute x11, starting transfers between devices: 10.2 us -> 11.1 us  [swap(): return lax.ppermute(x, axis, [(i, i ^ step) for i in range(ROWS)])]
    unnamed x9, local copies, waits for them, and re-layouts: 1.13 us -> 1.61 us
    pallas_call x1, Pallas kernels: 1.08 us -> 1.42 us  [local_few(): pl.pallas_call(functools.partial(prepare_kernel, tiles, slots), out_shape...]
  transfers between devices with their start and end apart: 11 -> 11, of which waited for: 4 -> 5; matrix products, arithmetic and copies ran while one was open for 0% -> 0% of each run, Pallas kernels for 7% -> 14%
where the time goes in v4:
time: 24.4 us; the launch traced here: 24.2 us
  starting transfers between devices  11.1 us (45%)
  waiting for transfers between devices  6.31 us (26%)
  Pallas kernels  5.12 us (21%)
  local copies, waits for them, and re-layouts  1.61 us (7%)
    ppermute x11, starting transfers between devices, swap(): return lax.ppermute(x, axis, [(i, i ^ step) for i in range(ROWS)])  11.1 us
    ppermute x11, waiting for transfers between devices, swap(): return lax.ppermute(x, axis, [(i, i ^ step) for i in range(ROWS)])  6.31 us
    unnamed x9, local copies, waits for them, and re-layouts  1.61 us
    pallas_call x1, Pallas kernels, local_few(): pl.pallas_call(functools.partial(prepare_kernel, tiles, slots), out_shape...  1.42 us
    pallas_call x2, Pallas kernels, local_few(): near, far = (after(token, near), after(token, far))  1.29 us
    pallas_call x1, Pallas kernels, local_few(): pl.pallas_call(functools.partial(pack_kernel, tiles, slots), out_shape=[j...  1.03 us
    pallas_call x2, Pallas kernels, finish(): pl.pallas_call(kernel, out_shape=sums_shape, in_specs=[SMEM] + [VMEM] * (...  0.74 us
    pallas_call x2, Pallas kernels, ladder(): pl.pallas_call(functools.partial(ladder_kernel, phase), out_shape=[half_s...  0.64 us
  transfers between devices with their start and end apart: 11, of which 5 were waited for; matrix products, arithmetic and copies ran while one was open for 0% of the time, Pallas kernels for 14%

profile of v4, /device:TPU:0, one launch (start us, length us, event | category | flops | bytes accessed | tf_op | source)
XLA Modules:
  0.0 24.2 jit_solution(11179086724196420817)
XLA Ops:
  0.0 1.0 %pack.1 = (bf16[128,512]{1,0:T(8,128)(2,1)S(1)}, bf16[64,512]{1,0:T(8,128)(2,1)S(1)}, bf16[64,512]{1,0:T(8,128)(2,1)S(1)}) custom-call(s32[1]{0:T(128)} %bitcast.me, s32[4,8]{1,0:T(4,128)} %kept.3, bf16[128,1024]{1,0:T(8,128)(2,1)} %doubles.1), custom_call_target="tpu_custom_call" | custom-call | tf_op jit(solution)/shard_map/pack/pallas_call | solution.py:146
  1.0 3.1 %collective-permute-start = (bf16[128,512]{1,0:T(8,128)(2,1)S(1)}, bf16[128,512]{1,0:T(8,128)(2,1)S(1)}, u32[]{:S(2)}, u32[]{:S(2)}) collective-permute-start(bf16[128,512]{1,0:T(8,128)(2,1)S(1)} %get-tuple-element.19.own), channel_id=1, source_target_pairs={{0,4},{4,0},{8,12},{12,8},{1,5},{5,1},{9,13},{13,9},{2,6},{6,2},{1... | collective-permute-start | bytes 393224 | tf_op jit(solution)/shard_map/ppermute | solution.py:132
  4.1 0.0 copy-start.3
  4.1 2.5 %collective-permute-start.2 = (bf16[64,512]{1,0:T(8,128)(2,1)S(1)}, bf16[64,512]{1,0:T(8,128)(2,1)S(1)}, u32[]{:S(2)}, u32[]{:S(2)}) collective-permute-start(bf16[64,512]{1,0:T(8,128)(2,1)S(1)} %get-tuple-element.24), channel_id=1, source_target_pairs={{0,12},{4,8},{8,4},{12,0},{1,13},{5,9},{9,5},{13,1},{2,14},{6,10},... | collective-permute-start | bytes 196616 | tf_op jit(solution)/shard_map/ppermute | solution.py:132
  6.6 0.0 copy-start.2
  6.6 0.1 collective-permute-start.1
  6.7 0.0 copy-done.3
  6.7 0.1 copy.8.int_kept
  6.8 0.5 %copy-done.2 = s32[4,8]{1,0:T(4,128)S(1)} copy-done((s32[4,8]{1,0:T(4,128)S(1)}, s32[4,8]{1,0:T(4,128)}, u32[]{:S(2)}) %copy-start.2) | copy-done | bytes 152
  7.3 0.0 copy-start
  7.3 1.0 %copy-done = bf16[1024,256]{1,0:T(8,128)(2,1)S(1)} copy-done((bf16[1024,256]{1,0:T(8,128)(2,1)S(1)}, bf16[1024,256]{1,0:T(8,128)(2,1)}, u32[]{:S(2)}) %copy-start) | copy-done | bytes 524312
  8.3 1.4 %prepare.1 = (bf16[4,512,256]{2,1,0:T(8,128)(2,1)S(1)}, f32[128,256]{1,0:T(8,128)S(1)}, s32[1]{0:T(128)}) custom-call(s32[1]{0:T(128)} %bitcast.me, s32[4,8]{1,0:T(4,128)S(1)} %copy-done.2, s32[8,2]{1,0:T(8,128)S(1)} %copy.8.int_kept, bf16[1024,256]{1,0:T(8,128)(2,1)S(1)} %copy-done, bf16[128,512]{1,0:T(8,128)(2,1)S(1)} %get-tuple-element.19.own), custom_call_target="tpu_custom_call" | custom-call | flops 33554432 | bytes 4194304 | tf_op jit(solution)/shard_map/prepare/pallas_call | solution.py:163
  9.8 2.3 %collective-permute-done.2.x = bf16[64,512]{1,0:T(8,128)(2,1)S(1)} collective-permute-done((bf16[64,512]{1,0:T(8,128)(2,1)S(1)}, bf16[64,512]{1,0:T(8,128)(2,1)S(1)}, u32[]{:S(2)}, u32[]{:S(2)}) %collective-permute-start.2) | collective-permute-done | bytes 65568 | tf_op jit(solution)/shard_map/ppermute | solution.py:132
  12.0 0.6 %after.3.far = bf16[64,512]{1,0:T(8,128)(2,1)S(1)} custom-call(s32[1]{0:T(128)} %get-tuple-element.22.token, bf16[64,512]{1,0:T(8,128)(2,1)S(1)} %collective-permute-done.2.x), custom_call_target="tpu_custom_call", output_to_operand_aliasing={{}: (1, {})} | custom-call | tf_op jit(solution)/shard_map/after/pallas_call | solution.py:182
  12.7 0.1 collective-permute-start.6
  12.8 0.6 %collective-permute-done.1.x = bf16[64,512]{1,0:T(8,128)(2,1)S(1)} collective-permute-done((bf16[64,512]{1,0:T(8,128)(2,1)S(1)}, bf16[64,512]{1,0:T(8,128)(2,1)S(1)}, u32[]{:S(2)}, u32[]{:S(2)}) %collective-permute-start.1) | collective-permute-done | bytes 65568 | tf_op jit(solution)/shard_map/ppermute | solution.py:132
  13.3 0.6 %after.2.near = bf16[64,512]{1,0:T(8,128)(2,1)S(1)} custom-call(s32[1]{0:T(128)} %get-tuple-element.22.token, bf16[64,512]{1,0:T(8,128)(2,1)S(1)} %collective-permute-done.1.x), custom_call_target="tpu_custom_call", output_to_operand_aliasing={{}: (1, {})} | custom-call | tf_op jit(solution)/shard_map/after/pallas_call | solution.py:182
  14.0 1.5 %collective-permute-start.7 = (bf16[64,512]{1,0:T(8,128)(2,1)S(1)}, bf16[64,512]{1,0:T(8,128)(2,1)S(1)}, u32[]{:S(2)}, u32[]{:S(2)}) collective-permute-start(bf16[64,512]{1,0:T(8,128)(2,1)S(1)} %after.2.near), channel_id=1, source_target_pairs={{0,4},{4,0},{8,12},{12,8},{1,5},{5,1},{9,13},{13,9},{2,6},{6,2},{1... | collective-permute-start | bytes 196616 | tf_op jit(solution)/shard_map/ppermute | solution.py:132
  15.5 0.0 collective-permute-done.pair
  15.5 0.3 %ladder.2 = (f32[64,256]{1,0:T(8,128)S(1)}, s16[144,128]{1,0:T(8,128)(2,1)S(1)}, s16[144,128]{1,0:T(8,128)(2,1)S(1)}, s16[144,128]{1,0:T(8,128)(2,1)S(1)}) custom-call(s32[1]{0:T(128)} %bitcast.me, f32[128,256]{1,0:T(8,128)S(1)} %get-tuple-element.20.product, bf16[4,512,256]{2,1,0:T(8,128)(2,1)S(1)} %get-tuple-element.21.gathered, ...), custom_call_target="tpu_custom_call" | custom-call | tf_op jit(solution)/shard_map/ladder/pallas_call | solution.py:187
  15.8 0.1 collective-permute-start.3
  15.9 1.6 %collective-permute-start.4 = (s16[144,128]{1,0:T(8,128)(2,1)S(1)}, s16[144,128]{1,0:T(8,128)(2,1)S(1)}, u32[]{:S(2)}, u32[]{:S(2)}) collective-permute-start(s16[144,128]{1,0:T(8,128)(2,1)S(1)} %get-tuple-element.27), channel_id=1, source_target_pairs={{0,2},{1,3},{2,0},{3,1},{4,6},{5,7},{6,4},{7,5},{8,10},{9,11},{10,... | collective-permute-start | bytes 110600 | tf_op jit(solution)/shard_map/ppermute | solution.py:132
  17.4 0.0 copy-start.1
  17.4 0.3 %collective-permute-start.5 = (s16[144,128]{1,0:T(8,128)(2,1)S(1)}, s16[144,128]{1,0:T(8,128)(2,1)S(1)}, u32[]{:S(2)}, u32[]{:S(2)}) collective-permute-start(s16[144,128]{1,0:T(8,128)(2,1)S(1)} %get-tuple-element.28), channel_id=1, source_target_pairs={{0,1},{1,0},{2,3},{3,2},{4,5},{5,4},{6,7},{7,6},{8,9},{9,8},{10,11... | collective-permute-start | bytes 110600 | tf_op jit(solution)/shard_map/ppermute | solution.py:132
  17.7 0.0 collective-permute-done.6.near
  17.7 0.6 %collective-permute-done.7.far = bf16[64,512]{1,0:T(8,128)(2,1)S(1)} collective-permute-done((bf16[64,512]{1,0:T(8,128)(2,1)S(1)}, bf16[64,512]{1,0:T(8,128)(2,1)S(1)}, u32[]{:S(2)}, u32[]{:S(2)}) %collective-permute-start.7) | collective-permute-done | bytes 65568 | tf_op jit(solution)/shard_map/ppermute | solution.py:132
  18.3 0.3 %ladder.3 = (f32[64,256]{1,0:T(8,128)S(1)}, s16[144,128]{1,0:T(8,128)(2,1)S(1)}, s16[144,128]{1,0:T(8,128)(2,1)S(1)}, s16[144,128]{1,0:T(8,128)(2,1)S(1)}) custom-call(s32[1]{0:T(128)} %bitcast.me, f32[128,256]{1,0:T(8,128)S(1)} %get-tuple-element.20.product, bf16[4,512,256]{2,1,0:T(8,128)(2,1)S(1)} %get-tuple-element.21.gathered, ...), custom_call_target="tpu_custom_call" | custom-call | tf_op jit(solution)/shard_map/ladder/pallas_call | solution.py:187
  18.7 0.6 %collective-permute-start.8 = (s16[144,128]{1,0:T(8,128)(2,1)S(1)}, s16[144,128]{1,0:T(8,128)(2,1)S(1)}, u32[]{:S(2)}, u32[]{:S(2)}) collective-permute-start(s16[144,128]{1,0:T(8,128)(2,1)S(1)} %get-tuple-element.30), channel_id=1, source_target_pairs={{0,3},{1,2},{2,1},{3,0},{4,7},{5,6},{6,5},{7,4},{8,11},{9,10},{10,... | collective-permute-start | bytes 110600 | tf_op jit(solution)/shard_map/ppermute | solution.py:132
  19.3 1.0 %collective-permute-start.9 = (s16[144,128]{1,0:T(8,128)(2,1)S(1)}, s16[144,128]{1,0:T(8,128)(2,1)S(1)}, u32[]{:S(2)}, u32[]{:S(2)}) collective-permute-start(s16[144,128]{1,0:T(8,128)(2,1)S(1)} %get-tuple-element.31), channel_id=1, source_target_pairs={{0,2},{1,3},{2,0},{3,1},{4,6},{5,7},{6,4},{7,5},{8,10},{9,11},{10,... | collective-permute-start | bytes 110600 | tf_op jit(solution)/shard_map/ppermute | solution.py:132
  20.3 0.0 collective-permute-done.3.rest_0_
  20.3 0.3 %collective-permute-start.10 = (s16[144,128]{1,0:T(8,128)(2,1)S(1)}, s16[144,128]{1,0:T(8,128)(2,1)S(1)}, u32[]{:S(2)}, u32[]{:S(2)}) collective-permute-start(s16[144,128]{1,0:T(8,128)(2,1)S(1)} %get-tuple-element.32), channel_id=1, source_target_pairs={{0,1},{1,0},{2,3},{3,2},{4,5},{5,4},{6,7},{7,6},{8,9},{9,8},{10,11... | collective-permute-start | bytes 110600 | tf_op jit(solution)/shard_map/ppermute | solution.py:132
  20.6 0.0 collective-permute-done.4.rest_1_
  20.6 0.0 collective-permute-done.5.rest_2_
  20.6 0.0 copy-done.1
  20.6 1.8 %collective-permute-done.8.rest_0_ = s16[144,128]{1,0:T(8,128)(2,1)S(1)} collective-permute-done((s16[144,128]{1,0:T(8,128)(2,1)S(1)}, s16[144,128]{1,0:T(8,128)(2,1)S(1)}, u32[]{:S(2)}, u32[]{:S(2)}) %collective-permute-start.8) | collective-permute-done | bytes 36896 | tf_op jit(solution)/shard_map/ppermute | solution.py:132
  22.4 1.1 %collective-permute-done.9.rest_1_ = s16[144,128]{1,0:T(8,128)(2,1)S(1)} collective-permute-done((s16[144,128]{1,0:T(8,128)(2,1)S(1)}, s16[144,128]{1,0:T(8,128)(2,1)S(1)}, u32[]{:S(2)}, u32[]{:S(2)}) %collective-permute-start.9) | collective-permute-done | bytes 36896 | tf_op jit(solution)/shard_map/ppermute | solution.py:132
  23.5 0.0 collective-permute-done.10.rest_2_
  23.5 0.7 %finish.3 = f32[128,256]{1,0:T(8,128)} custom-call(s32[1]{0:T(128)} %bitcast.me, f32[128,256]{1,0:T(8,128)S(1)} %finish.2.base, f32[64,256]{1,0:T(8,128)S(1)} %get-tuple-element.29.kept_sums, s16[144,128]{1,0:T(8,128)(2,1)S(1)} %collective-permute-done.8.rest_0_, s16[144,128]{1,0:T(8,128)(2,1)S(1)} %collective-permute-done.9.rest_1_, ...), custom_call_target="tpu_custom_call" | custom-call | tf_op jit(solution)/shard_map/finish/pallas_call | solution.py:199
  (1 shorter events, 0.0 us)
Async XLA Ops:
  1.0 14.4 %collective-permute-start = (bf16[128,512]{1,0:T(8,128)(2,1)S(1)}, bf16[128,512]{1,0:T(8,128)(2,1)S(1)}, u32[]{:S(2)}, u32[]{:S(2)}) collective-permute-start(bf16[128,512]{1,0:T(8,128)(2,1)S(1)} %get-tuple-element.19.own), channel_id=1, source_target_pairs={{0,4},{4,0},{8,12},{12,8},{1,5},{5,1},{9,13},{13,9},{2,6},{6,2},{1... | collective-permute-start | bytes 393224 | tf_op jit(solution)/shard_map/ppermute | solution.py:132
  4.1 2.6 %copy-start.3 = (s32[8,2]{0,1:T(2,128)S(1)}, s32[8,2]{0,1:T(2,128)}, u32[]{:S(2)}) copy-start(s32[8,2]{0,1:T(2,128)} %param.8) | copy-start | bytes 196
  4.1 7.9 %collective-permute-start.2 = (bf16[64,512]{1,0:T(8,128)(2,1)S(1)}, bf16[64,512]{1,0:T(8,128)(2,1)S(1)}, u32[]{:S(2)}, u32[]{:S(2)}) collective-permute-start(bf16[64,512]{1,0:T(8,128)(2,1)S(1)} %get-tuple-element.24), channel_id=1, source_target_pairs={{0,12},{4,8},{8,4},{12,0},{1,13},{5,9},{9,5},{13,1},{2,14},{6,10},... | collective-permute-start | bytes 196616 | tf_op jit(solution)/shard_map/ppermute | solution.py:132
  6.6 0.7 %copy-start.2 = (s32[4,8]{1,0:T(4,128)S(1)}, s32[4,8]{1,0:T(4,128)}, u32[]{:S(2)}) copy-start(s32[4,8]{1,0:T(4,128)} %kept.3) | copy-start | bytes 388
  6.6 6.7 %collective-permute-start.1 = (bf16[64,512]{1,0:T(8,128)(2,1)S(1)}, bf16[64,512]{1,0:T(8,128)(2,1)S(1)}, u32[]{:S(2)}, u32[]{:S(2)}) collective-permute-start(bf16[64,512]{1,0:T(8,128)(2,1)S(1)} %get-tuple-element.23), channel_id=1, source_target_pairs={{0,8},{4,12},{8,0},{12,4},{1,9},{5,13},{9,1},{13,5},{2,10},{6,14},... | collective-permute-start | bytes 196616 | tf_op jit(solution)/shard_map/ppermute | solution.py:132
  7.3 1.0 %copy-start = (bf16[1024,256]{1,0:T(8,128)(2,1)S(1)}, bf16[1024,256]{1,0:T(8,128)(2,1)}, u32[]{:S(2)}) copy-start(bf16[1024,256]{1,0:T(8,128)(2,1)} %integrals.1) | copy-start | bytes 1572868
  12.7 5.1 %collective-permute-start.6 = (bf16[64,512]{1,0:T(8,128)(2,1)S(1)}, bf16[64,512]{1,0:T(8,128)(2,1)S(1)}, u32[]{:S(2)}, u32[]{:S(2)}) collective-permute-start(bf16[64,512]{1,0:T(8,128)(2,1)S(1)} %after.3.far), channel_id=1, source_target_pairs={{0,4},{4,0},{8,12},{12,8},{1,5},{5,1},{9,13},{13,9},{2,6},{6,2},{1... | collective-permute-start | bytes 196616 | tf_op jit(solution)/shard_map/ppermute | solution.py:132
  14.0 4.3 %collective-permute-start.7 = (bf16[64,512]{1,0:T(8,128)(2,1)S(1)}, bf16[64,512]{1,0:T(8,128)(2,1)S(1)}, u32[]{:S(2)}, u32[]{:S(2)}) collective-permute-start(bf16[64,512]{1,0:T(8,128)(2,1)S(1)} %after.2.near), channel_id=1, source_target_pairs={{0,4},{4,0},{8,12},{12,8},{1,5},{5,1},{9,13},{13,9},{2,6},{6,2},{1... | collective-permute-start | bytes 196616 | tf_op jit(solution)/shard_map/ppermute | solution.py:132
  15.8 4.5 %collective-permute-start.3 = (s16[144,128]{1,0:T(8,128)(2,1)S(1)}, s16[144,128]{1,0:T(8,128)(2,1)S(1)}, u32[]{:S(2)}, u32[]{:S(2)}) collective-permute-start(s16[144,128]{1,0:T(8,128)(2,1)S(1)} %get-tuple-element.26), channel_id=1, source_target_pairs={{0,3},{1,2},{2,1},{3,0},{4,7},{5,6},{6,5},{7,4},{8,11},{9,10},{10,... | collective-permute-start | bytes 110600 | tf_op jit(solution)/shard_map/ppermute | solution.py:132
  15.9 4.7 %collective-permute-start.4 = (s16[144,128]{1,0:T(8,128)(2,1)S(1)}, s16[144,128]{1,0:T(8,128)(2,1)S(1)}, u32[]{:S(2)}, u32[]{:S(2)}) collective-permute-start(s16[144,128]{1,0:T(8,128)(2,1)S(1)} %get-tuple-element.27), channel_id=1, source_target_pairs={{0,2},{1,3},{2,0},{3,1},{4,6},{5,7},{6,4},{7,5},{8,10},{9,11},{10,... | collective-permute-start | bytes 110600 | tf_op jit(solution)/shard_map/ppermute | solution.py:132
  17.4 3.1 %copy-start.1 = (f32[128,256]{1,0:T(8,128)S(1)}, f32[128,256]{1,0:T(8,128)}, u32[]{:S(2)}) copy-start(f32[128,256]{1,0:T(8,128)} %residual.1) | copy-start | bytes 393220
  17.4 3.1 %collective-permute-start.5 = (s16[144,128]{1,0:T(8,128)(2,1)S(1)}, s16[144,128]{1,0:T(8,128)(2,1)S(1)}, u32[]{:S(2)}, u32[]{:S(2)}) collective-permute-start(s16[144,128]{1,0:T(8,128)(2,1)S(1)} %get-tuple-element.28), channel_id=1, source_target_pairs={{0,1},{1,0},{2,3},{3,2},{4,5},{5,4},{6,7},{7,6},{8,9},{9,8},{10,11... | collective-permute-start | bytes 110600 | tf_op jit(solution)/shard_map/ppermute | solution.py:132
  18.7 3.8 %collective-permute-start.8 = (s16[144,128]{1,0:T(8,128)(2,1)S(1)}, s16[144,128]{1,0:T(8,128)(2,1)S(1)}, u32[]{:S(2)}, u32[]{:S(2)}) collective-permute-start(s16[144,128]{1,0:T(8,128)(2,1)S(1)} %get-tuple-element.30), channel_id=1, source_target_pairs={{0,3},{1,2},{2,1},{3,0},{4,7},{5,6},{6,5},{7,4},{8,11},{9,10},{10,... | collective-permute-start | bytes 110600 | tf_op jit(solution)/shard_map/ppermute | solution.py:132
  19.3 4.3 %collective-permute-start.9 = (s16[144,128]{1,0:T(8,128)(2,1)S(1)}, s16[144,128]{1,0:T(8,128)(2,1)S(1)}, u32[]{:S(2)}, u32[]{:S(2)}) collective-permute-start(s16[144,128]{1,0:T(8,128)(2,1)S(1)} %get-tuple-element.31), channel_id=1, source_target_pairs={{0,2},{1,3},{2,0},{3,1},{4,6},{5,7},{6,4},{7,5},{8,10},{9,11},{10,... | collective-permute-start | bytes 110600 | tf_op jit(solution)/shard_map/ppermute | solution.py:132
  20.3 3.2 %collective-permute-start.10 = (s16[144,128]{1,0:T(8,128)(2,1)S(1)}, s16[144,128]{1,0:T(8,128)(2,1)S(1)}, u32[]{:S(2)}, u32[]{:S(2)}) collective-permute-start(s16[144,128]{1,0:T(8,128)(2,1)S(1)} %get-tuple-element.32), channel_id=1, source_target_pairs={{0,1},{1,0},{2,3},{3,2},{4,5},{5,4},{6,7},{7,6},{8,9},{9,8},{10,11... | collective-permute-start | bytes 110600 | tf_op jit(solution)/shard_map/ppermute | solution.py:132

commit v5 on v2

--- a/solution.py
+++ b/solution.py
@@ -15,6 +15,7 @@
 
 VMEM = pl.BlockSpec(memory_space=pltpu.VMEM)
 SMEM = pl.BlockSpec(memory_space=pltpu.SMEM)
+HBM = pl.BlockSpec(memory_space=pltpu.HBM)
 PARAMS = pltpu.CompilerParams(vmem_limit_bytes=8 * 1024 * 1024)
 
 
@@ -25,11 +26,18 @@
         at = at + kept[row, tile]
 
 
-def pack_kernel(count, tiles, slots, me, kept, doubles, packed, places):
-    list_kept(kept, me[0] // count, tiles, places)
+def pack_kernel(count, tiles, slots, me, kept, doubles, packed, table, block, places, sems):
+    table_copy = pltpu.make_async_copy(kept, table, sems.at[0])
+    block_copy = pltpu.make_async_copy(doubles, block, sems.at[1])
+    table_copy.start()
+    block_copy.start()
+    table_copy.wait()
+    list_kept(table, me[0] // count, tiles, places)
+    block_copy.wait()
     for slot in range(slots):
-        start = pl.multiple_of(places[slot] * TILE, TILE)
-        packed[:, slot * TILE : (slot + 1) * TILE] = doubles[:, pl.ds(start, TILE)]
+        tile = block[:, pl.ds(pl.multiple_of(places[slot] * TILE, TILE), TILE)]
+        for n in range(count):
+            packed[n, :, slot * TILE : (slot + 1) * TILE] = tile
 
 
 def prepare_kernel(count, tiles, slots, me, kept, int_kept, integrals, own, gathered, product, places):
@@ -44,7 +52,7 @@
                 part = integrals[pl.ds(start, TILE), ab * TILE : (ab + 1) * TILE]
                 on = (int_kept[tile, ab] != 0).astype(jnp.float32).astype(part.dtype)
                 gathered[n, slot * TILE : (slot + 1) * TILE, ab * TILE : (ab + 1) * TILE] = part * on
-    product[...] = jnp.dot(own[...], gathered[row ^ col], preferred_element_type=jnp.float32)
+    product[...] = jnp.dot(own[0], gathered[row ^ col], preferred_element_type=jnp.float32)
 
 
 def encode(x, out):
@@ -62,27 +70,23 @@
     return code * jnp.exp2(exponent * (-1.0 / STEPS))
 
 
-def ladder_kernel(count, me, product, gathered, *rest):
-    blocks, kept_sums, outs, sums = rest[: count - 1], rest[count - 1], rest[count : 2 * count - 1], rest[-1]
-    mine = me[0] // count ^ me[0] % count
+def ladder_kernel(count, me, product, gathered, blocks, kept_sums, messages, sums):
+    row, col = me[0] // count, me[0] % count
+    mine = row ^ col
     sums[mine] = product[...]
-    for step, block in enumerate(blocks, 1):
-        sums[mine ^ step] = jnp.dot(block[...], gathered[mine ^ step], preferred_element_type=jnp.float32)
+    for step in range(1, count):
+        sums[mine ^ step] = jnp.dot(blocks[row ^ step], gathered[mine ^ step], preferred_element_type=jnp.float32)
     kept_sums[...] = sums[0]
-    for n, out in enumerate(outs, 1):
-        encode(sums[n], out)
+    for n in range(1, count):
+        encode(sums[n], messages.at[col ^ n])
 
 
-def finish_kernel(residual, kept_sums, *rest):
-    messages, out = rest[:-1], rest[-1]
+def finish_kernel(count, me, residual, kept_sums, messages, out):
+    col = me[0] % count
     total = residual[...] + kept_sums[...]
-    for message in messages:
-        total = total + decode(message, total.shape[0])
+    for n in range(1, count):
+        total = total + decode(messages.at[col ^ n], total.shape[0])
     out[...] = total
-
-
-def swap(x, axis, size, step):
-    return lax.ppermute(x, axis, [(i, i ^ step) for i in range(size)])
 
 
 def local_few(doubles, doubles_kept, integrals, integral_kept, residual):
@@ -96,14 +100,23 @@
     sums_shape = jax.ShapeDtypeStruct((pairs, width), jnp.float32)
     packed = pl.pallas_call(
         functools.partial(pack_kernel, count, tiles, slots),
-        out_shape=jax.ShapeDtypeStruct((pairs, slots * TILE), doubles.dtype),
-        in_specs=[SMEM, SMEM, VMEM],
+        out_shape=jax.ShapeDtypeStruct((count, pairs, slots * TILE), doubles.dtype),
+        in_specs=[SMEM, HBM, HBM],
         out_specs=VMEM,
-        scratch_shapes=[places],
+        scratch_shapes=[
+            pltpu.SMEM(doubles_kept.shape, jnp.int32),
+            pltpu.VMEM(doubles.shape, doubles.dtype),
+            places,
+            pltpu.SemaphoreType.DMA((2,)),
+        ],
         compiler_params=PARAMS,
         name="pack",
-    )(me, doubles_kept, doubles)
-    blocks = [swap(packed, "rows", count, step) for step in range(1, count)]
+    )(
+        me,
+        pltpu.with_memory_space_constraint(doubles_kept, pltpu.HBM),
+        pltpu.with_memory_space_constraint(doubles, pltpu.HBM),
+    )
+    blocks = lax.all_to_all(packed, "rows", split_axis=0, concat_axis=0)
     gathered, product = pl.pallas_call(
         functools.partial(prepare_kernel, count, tiles, slots),
         out_shape=[jax.ShapeDtypeStruct((count, slots * TILE, width), integrals.dtype), sums_shape],
@@ -114,25 +127,25 @@
         cost_estimate=pl.CostEstimate(flops=2 * pairs * slots * TILE * width, bytes_accessed=4 << 20, transcendentals=0),
         name="prepare",
     )(me, doubles_kept, integral_kept, integrals, packed)
-    message = jax.ShapeDtypeStruct((pairs + HEAD, width), jnp.int16)
-    kept_sums, *messages = pl.pallas_call(
+    message = jax.ShapeDtypeStruct((count, pairs + HEAD, width), jnp.int16)
+    kept_sums, messages = pl.pallas_call(
         functools.partial(ladder_kernel, count),
-        out_shape=[sums_shape] + [message] * (count - 1),
-        in_specs=[SMEM] + [VMEM] * (count + 1),
-        out_specs=[VMEM] * count,
+        out_shape=[sums_shape] + [message],
+        in_specs=[SMEM] + [VMEM] * 3,
+        out_specs=[VMEM] * 2,
         scratch_shapes=[pltpu.VMEM((count, pairs, width), jnp.float32)],
         compiler_params=PARAMS,
         name="ladder",
-    )(me, product, gathered, *blocks)
-    messages = [swap(x, "cols", count, step) for step, x in reversed(list(enumerate(messages, 1)))]
+    )(me, product, gathered, blocks)
+    messages = lax.all_to_all(messages, "cols", split_axis=0, concat_axis=0)
     return pl.pallas_call(
-        finish_kernel,
+        functools.partial(finish_kernel, count),
         out_shape=sums_shape,
-        in_specs=[VMEM] * (count + 1),
+        in_specs=[SMEM] + [VMEM] * 3,
         out_specs=VMEM,
         compiler_params=PARAMS,
         name="finish",
-    )(residual, kept_sums, *messages)
+    )(me, residual, kept_sums, messages)
 
 
 def local_many(doubles, doubles_kept, integrals, integral_kept, residual):

time: 26 us -> 33.3 us (1.28)
  blocking collectives: 0 us -> 9.08 us
  local copies, waits for them, and re-layouts: 2.76 us -> 0.7 us
  Pallas kernels: 2.79 us -> 4.44 us
  starting transfers between devices: 7.68 us -> 6.46 us
    ppermute x6 -> x0, waiting for transfers between devices: 12.5 us -> none  [swap(): return lax.ppermute(x, axis, [(i, i ^ step) for i in range(size)])]
    all_to_all x0 -> x1, waiting for transfers between devices: none -> 12.3 us  [local_few(): blocks = lax.all_to_all(packed, 'rows', split_axis=0, concat_axis=0)]
    all_to_all x0 -> x1, blocking collectives: none -> 9.08 us  [local_few(): messages = lax.all_to_all(messages, 'cols', split_axis=0, concat_axis=0)]
    ppermute x6 -> x0, starting transfers between devices: 7.68 us -> none  [swap(): return lax.ppermute(x, axis, [(i, i ^ step) for i in range(size)])]
    all_to_all x0 -> x1, starting transfers between devices: none -> 6.46 us  [local_few(): blocks = lax.all_to_all(packed, 'rows', split_axis=0, concat_axis=0)]
    unnamed x11 -> x9, local copies, waits for them, and re-layouts: 2.76 us -> 0.7 us
    pallas_call x1, Pallas kernels: 0.62 us -> 1.84 us  [local_few(): pl.pallas_call(functools.partial(pack_kernel, count, tiles, slots), out_s...]
    pallas_call x1, Pallas kernels: 1.08 us -> 1.51 us  [local_few(): pl.pallas_call(functools.partial(prepare_kernel, count, tiles, slots), ou...]
  transfers between devices with their start and end apart: 6 -> 1, of which waited for: 4 -> 1; matrix products, arithmetic and copies ran while one was open for 0% -> 0% of each run, Pallas kernels for 4% -> 5%
where the time goes in v5:
time: 33.3 us; the launch traced here: 33 us
  waiting for transfers between devices  12.3 us (37%)
  blocking collectives  9.08 us (27%)
  starting transfers between devices  6.46 us (19%)
  Pallas kernels  4.44 us (13%)
  local copies, waits for them, and re-layouts  0.7 us (2%)
    all_to_all x1, waiting for transfers between devices, local_few(): blocks = lax.all_to_all(packed, 'rows', split_axis=0, concat_axis=0)  12.3 us
    all_to_all x1, blocking collectives, local_few(): messages = lax.all_to_all(messages, 'cols', split_axis=0, concat_axis=0)  9.08 us
    all_to_all x1, starting transfers between devices, local_few(): blocks = lax.all_to_all(packed, 'rows', split_axis=0, concat_axis=0)  6.46 us
    pallas_call x1, Pallas kernels, local_few(): pl.pallas_call(functools.partial(pack_kernel, count, tiles, slots), out_s...  1.84 us
    pallas_call x1, Pallas kernels, local_few(): pl.pallas_call(functools.partial(prepare_kernel, count, tiles, slots), ou...  1.51 us
    pallas_call x1, Pallas kernels, local_few(): pl.pallas_call(functools.partial(finish_kernel, count), out_shape=sums_sh...  0.73 us
    unnamed x9, local copies, waits for them, and re-layouts  0.7 us
  transfers between devices with their start and end apart: 1, of which 1 were waited for; matrix products, arithmetic and copies ran while one was open for 0% of the time, Pallas kernels for 5%

profile of v5, /device:TPU:0, one launch (start us, length us, event | category | flops | bytes accessed | tf_op | source)
XLA Modules:
  0.0 33.0 jit_solution(17156396156330901669)
XLA Ops:
  0.0 1.8 %pack.1.own = bf16[4,128,512]{2,1,0:T(8,128)(2,1)} custom-call(s32[1]{0:T(128)} %bitcast.me, s32[4,8]{1,0:T(4,128)} %kept.3, bf16[128,1024]{1,0:T(8,128)(2,1)} %doubles.1), custom_call_target="tpu_custom_call" | custom-call | tf_op jit(solution)/shard_map/pack/pallas_call | solution.py:101
  1.8 0.0 copy-start.3
  1.9 0.0 copy-start
  1.9 6.5 %all-to-all-start = ((bf16[4,128,512]{2,1,0:T(8,128)(2,1)}), bf16[4,128,512]{2,1,0:T(8,128)(2,1)S(1)}, u32[]{:S(2)}, u32[]{:S(2)}) async-start(bf16[4,128,512]{2,1,0:T(8,128)(2,1)} %pack.1.own), calls=%async_computation | async-start | bytes 1048576 | tf_op jit(solution)/shard_map/all_to_all | solution.py:119
  8.3 0.0 copy-done.3
  8.3 0.0 copy-start.2
  8.3 0.1 copy.6.int_kept
  8.4 0.0 copy-done
  8.4 0.6 %copy-done.2 = s32[4,8]{1,0:T(4,128)S(1)} copy-done((s32[4,8]{1,0:T(4,128)S(1)}, s32[4,8]{1,0:T(4,128)}, u32[]{:S(2)}) %copy-start.2) | copy-done | bytes 152
  9.0 1.5 %prepare.1 = (bf16[4,512,256]{2,1,0:T(8,128)(2,1)S(1)}, f32[128,256]{1,0:T(8,128)S(1)}) custom-call(s32[1]{0:T(128)} %bitcast.me, s32[4,8]{1,0:T(4,128)S(1)} %copy-done.2, s32[8,2]{1,0:T(8,128)S(1)} %copy.6.int_kept, bf16[1024,256]{1,0:T(8,128)(2,1)S(1)} %copy-done, bf16[4,128,512]{2,1,0:T(8,128)(2,1)} %pack.1.own), custom_call_target="tpu_custom_call" | custom-call | flops 33554432 | bytes 4194304 | tf_op jit(solution)/shard_map/prepare/pallas_call | solution.py:120
  10.5 12.3 %all-to-all-done.blocks = bf16[4,128,512]{2,1,0:T(8,128)(2,1)S(1)} async-done(((bf16[4,128,512]{2,1,0:T(8,128)(2,1)}), bf16[4,128,512]{2,1,0:T(8,128)(2,1)S(1)}, u32[]{:S(2)}, u32[]{:S(2)}) %all-to-all-start) | async-done | bytes 524320 | tf_op jit(solution)/shard_map/all_to_all | solution.py:119
  22.8 0.4 %ladder.1 = (f32[128,256]{1,0:T(8,128)S(1)}, s16[4,144,256]{2,1,0:T(8,128)(2,1)S(1)}) custom-call(s32[1]{0:T(128)} %bitcast.me, f32[128,256]{1,0:T(8,128)S(1)} %get-tuple-element.9.product, bf16[4,512,256]{2,1,0:T(8,128)(2,1)S(1)} %get-tuple-element.10.gathered, bf16[4,128,512]{2,1,0:T(8,128)(2,1)S(1)} %all-to-all-done.blocks), custom_call_target="tpu_custom_call" | custom-call | tf_op jit(solution)/shard_map/ladder/pallas_call | solution.py:131
  23.2 0.0 copy-start.1
  23.2 9.1 %all_to_all.10.messages = s16[4,144,256]{2,1,0:T(8,128)(2,1)S(1)} all-to-all(s16[4,144,256]{2,1,0:T(8,128)(2,1)S(1)} %get-tuple-element.12), channel_id=1, replica_groups=mesh['groups'=2,'rows'=4,'cols'=4] {'cols'}, dimensions={0} | all-to-all | bytes 589824 | tf_op jit(solution)/shard_map/all_to_all | solution.py:140
  32.3 0.0 copy-done.1
  32.3 0.7 %finish.1 = f32[128,256]{1,0:T(8,128)} custom-call(s32[1]{0:T(128)} %bitcast.me, f32[128,256]{1,0:T(8,128)S(1)} %copy-done.1, f32[128,256]{1,0:T(8,128)S(1)} %get-tuple-element.11.kept_sums, s16[4,144,256]{2,1,0:T(8,128)(2,1)S(1)} %all_to_all.10.messages), custom_call_target="tpu_custom_call" | custom-call | tf_op jit(solution)/shard_map/finish/pallas_call | solution.py:141
Async XLA Ops:
  1.8 6.5 %copy-start.3 = (s32[8,2]{0,1:T(2,128)S(1)}, s32[8,2]{0,1:T(2,128)}, u32[]{:S(2)}) copy-start(s32[8,2]{0,1:T(2,128)} %param.8) | copy-start | bytes 196
  1.9 6.6 %copy-start = (bf16[1024,256]{1,0:T(8,128)(2,1)S(1)}, bf16[1024,256]{1,0:T(8,128)(2,1)}, u32[]{:S(2)}) copy-start(bf16[1024,256]{1,0:T(8,128)(2,1)} %integrals.1) | copy-start | bytes 1572868
  1.9 21.0 %all-to-all-start = ((bf16[4,128,512]{2,1,0:T(8,128)(2,1)}), bf16[4,128,512]{2,1,0:T(8,128)(2,1)S(1)}, u32[]{:S(2)}, u32[]{:S(2)}) async-start(bf16[4,128,512]{2,1,0:T(8,128)(2,1)} %pack.1.own), calls=%async_computation | async-start | bytes 1048576 | tf_op jit(solution)/shard_map/all_to_all | solution.py:119
  8.3 0.7 %copy-start.2 = (s32[4,8]{1,0:T(4,128)S(1)}, s32[4,8]{1,0:T(4,128)}, u32[]{:S(2)}) copy-start(s32[4,8]{1,0:T(4,128)} %kept.3) | copy-start | bytes 388
  23.2 9.1 %copy-start.1 = (f32[128,256]{1,0:T(8,128)S(1)}, f32[128,256]{1,0:T(8,128)}, u32[]{:S(2)}) copy-start(f32[128,256]{1,0:T(8,128)} %residual.1) | copy-start | bytes 393220

commit v6 on v3

--- a/solution.py
+++ b/solution.py
@@ -20,6 +20,10 @@
 ROWS = 4
 
 
+def cost(flops):
+    return pl.CostEstimate(flops=flops, bytes_accessed=1024, transcendentals=0)
+
+
 def list_kept(kept, row, tiles, places):
     at = jnp.int32(0)
     for tile in range(tiles):
@@ -27,12 +31,11 @@
         at = at + kept[row, tile]
 
 
-def half_of(ref, half):
-    size = ref.shape[0] // 2
-    return ref.at[pl.ds(pl.multiple_of(half * size, size), size)]
-
-
-def pack_kernel(tiles, slots, me, kept, doubles, packed, near_half, far_half, table, block, places, sems):
+def part_of(ref, part, size):
+    return ref.at[pl.ds(pl.multiple_of(part * size, size), size)]
+
+
+def pack_kernel(tiles, slots, me, kept, doubles, packed, direct, near, far, table, block, places, sems):
     row = me[0] // ROWS
     table_copy = pltpu.make_async_copy(kept, table, sems.at[0])
     block_copy = pltpu.make_async_copy(doubles, block, sems.at[1])
@@ -41,12 +44,14 @@
     table_copy.wait()
     list_kept(table, row, tiles, places)
     block_copy.wait()
+    half, quarter = direct.shape[0], near.shape[0]
     for slot in range(slots):
         tile = pl.ds(pl.multiple_of(places[slot] * TILE, TILE), TILE)
         to = slice(slot * TILE, (slot + 1) * TILE)
         packed[:, to] = block[:, tile]
-        near_half[:, to] = half_of(block, row % 2)[:, tile]
-        far_half[:, to] = half_of(block, 1 - row % 2)[:, tile]
+        direct[:, to] = block[:half, tile]
+        near[:, to] = part_of(block, 2 + row % 2, quarter)[:, tile]
+        far[:, to] = part_of(block, 3 - row % 2, quarter)[:, tile]
 
 
 def prepare_kernel(tiles, slots, me, kept, int_kept, integrals, own, gathered, product, places):
@@ -64,6 +69,10 @@
     product[...] = jnp.dot(own[...], gathered[row ^ col], preferred_element_type=jnp.float32)
 
 
+def after_kernel(token, x, out):
+    pass
+
+
 def encode(x, out):
     pairs, width = x.shape
     largest = jnp.max(jnp.abs(x), axis=0, keepdims=True)
@@ -89,17 +98,35 @@
     return jnp.concatenate(parts, axis=1)
 
 
-def ladder_kernel(phase, me, product, gathered, pair, near, far, kept_sums, *rest):
+def send_sums(sums, kept_sums, outs):
+    kept_sums[...] = sums[0]
+    for n, out in enumerate(outs, 1):
+        encode(sums[n], out)
+
+
+def direct_kernel(me, product, gathered, pair, near, far, kept_sums, *rest):
+    outs, sums = rest[:-1], rest[-1]
+    mine = me[0] // ROWS ^ me[0] % ROWS
+    half = near.shape[0]
+    sums[mine] = product[:half, :]
+    for step, block in enumerate((pair[:half, :], near[...], far[...]), 1):
+        sums[mine ^ step] = jnp.dot(block, gathered[mine ^ step], preferred_element_type=jnp.float32)
+    send_sums(sums, kept_sums, outs)
+
+
+def swapped_kernel(me, product, gathered, pair, near, far, near_late, far_late, kept_sums, *rest):
     outs, sums = rest[:-1], rest[-1]
     row = me[0] // ROWS
     mine = row ^ me[0] % ROWS
-    half = row % 2 if phase == 0 else 1 - row % 2
-    sums[mine] = half_of(product, half)[...]
-    for step, block in enumerate((half_of(pair, half), near, far), 1):
-        sums[mine ^ step] = jnp.dot(block[...], gathered[mine ^ step], preferred_element_type=jnp.float32)
-    kept_sums[...] = sums[0]
-    for n, out in enumerate(outs, 1):
-        encode(sums[n], out)
+    quarter = near.shape[0]
+    sums[mine] = product[2 * quarter :, :]
+    sums[mine ^ 1] = jnp.dot(pair[2 * quarter :, :], gathered[mine ^ 1], preferred_element_type=jnp.float32)
+    for step, block, late in ((2, near, near_late), (3, far, far_late)):
+        for part, x in ((row % 2, block), (1 - row % 2, late)):
+            part_of(sums.at[mine ^ step], part, quarter)[...] = jnp.dot(
+                x[...], gathered[mine ^ step], preferred_element_type=jnp.float32
+            )
+    send_sums(sums, kept_sums, outs)
 
 
 def total_of(start, kept_sums, messages):
@@ -109,18 +136,31 @@
     return total
 
 
-def first_kernel(me, residual, kept_sums, *rest):
+def first_kernel(residual, kept_sums, *rest):
     messages, out = rest[:-1], rest[-1]
-    half = me[0] // ROWS % 2
-    half_of(out, 1 - half)[...] = half_of(residual, 1 - half)[...]
-    half_of(out, half)[...] = total_of(half_of(residual, half)[...], kept_sums, messages)
-
-
-def second_kernel(me, base, kept_sums, *rest):
+    half = kept_sums.shape[0]
+    out[:half, :] = total_of(residual[:half, :], kept_sums, messages)
+    out[half:, :] = residual[half:, :]
+
+
+def second_kernel(base, kept_sums, *rest):
     messages, out = rest[:-1], rest[-1]
-    half = me[0] // ROWS % 2
-    half_of(out, half)[...] = half_of(base, half)[...]
-    half_of(out, 1 - half)[...] = total_of(half_of(base, 1 - half)[...], kept_sums, messages)
+    half = kept_sums.shape[0]
+    out[:half, :] = base[:half, :]
+    out[half:, :] = total_of(base[half:, :], kept_sums, messages)
+
+
+def after(token, x, flops):
+    return pl.pallas_call(
+        after_kernel,
+        out_shape=jax.ShapeDtypeStruct(x.shape, x.dtype),
+        in_specs=[pl.BlockSpec(memory_space=pl.ANY)] * 2,
+        out_specs=pl.BlockSpec(memory_space=pl.ANY),
+        input_output_aliases={1: 0},
+        compiler_params=PARAMS,
+        cost_estimate=cost(flops),
+        name="after",
+    )(token, x)
 
 
 def swap(x, axis, step):
@@ -137,12 +177,13 @@
     sums_shape = jax.ShapeDtypeStruct((pairs, width), jnp.float32)
     half_sums = jax.ShapeDtypeStruct((pairs // 2, width), jnp.float32)
     half_block = jax.ShapeDtypeStruct((pairs // 2, slots * TILE), doubles.dtype)
+    quarter_block = jax.ShapeDtypeStruct((pairs // 4, slots * TILE), doubles.dtype)
     message = jax.ShapeDtypeStruct((pairs // 2 * width // TILE + HEAD, TILE), jnp.int16)
-    packed, near_half, far_half = pl.pallas_call(
+    packed, direct, near, far = pl.pallas_call(
         functools.partial(pack_kernel, tiles, slots),
-        out_shape=[jax.ShapeDtypeStruct((pairs, slots * TILE), doubles.dtype), half_block, half_block],
+        out_shape=[jax.ShapeDtypeStruct((pairs, slots * TILE), doubles.dtype), half_block, quarter_block, quarter_block],
         in_specs=[SMEM, HBM, HBM],
-        out_specs=[VMEM] * 3,
+        out_specs=[VMEM] * 4,
         scratch_shapes=[
             pltpu.SMEM(doubles_kept.shape, jnp.int32),
             pltpu.VMEM(doubles.shape, doubles.dtype),
@@ -152,9 +193,11 @@
         compiler_params=PARAMS,
         name="pack",
     )(me, pltpu.with_memory_space_constraint(doubles_kept, pltpu.HBM), pltpu.with_memory_space_constraint(doubles, pltpu.HBM))
-    near = swap(near_half, "rows", 2)
-    far = swap(far_half, "rows", 3)
     pair = swap(packed, "rows", 1)
+    far_direct = swap(direct, "rows", 3)
+    near_direct = swap(direct, "rows", 2)
+    far = swap(far, "rows", 3)
+    near = swap(near, "rows", 2)
     gathered, product = pl.pallas_call(
         functools.partial(prepare_kernel, tiles, slots),
         out_shape=[jax.ShapeDtypeStruct((ROWS, slots * TILE, width), integrals.dtype), sums_shape],
@@ -162,36 +205,38 @@
         out_specs=[VMEM] * 2,
         scratch_shapes=[places],
         compiler_params=PARAMS,
-        cost_estimate=pl.CostEstimate(flops=2 * pairs * slots * TILE * width, bytes_accessed=4 << 20, transcendentals=0),
+        cost_estimate=cost(0),
         name="prepare",
     )(me, doubles_kept, integral_kept, integrals, packed)
+    near, far = after(product, near, 10**10), after(product, far, 0)
     far_late = swap(near, "rows", 1)
     near_late = swap(far, "rows", 1)
 
-    def ladder(phase, near, far):
+    def ladder(kernel, *blocks):
         kept_sums, *messages = pl.pallas_call(
-            functools.partial(ladder_kernel, phase),
+            kernel,
             out_shape=[half_sums] + [message] * (ROWS - 1),
-            in_specs=[SMEM] + [VMEM] * 5,
+            in_specs=[SMEM] + [VMEM] * (3 + len(blocks)),
             out_specs=[VMEM] * ROWS,
             scratch_shapes=[pltpu.VMEM((ROWS,) + half_sums.shape, jnp.float32)],
             compiler_params=PARAMS,
+            cost_estimate=cost(10**11),
             name="ladder",
-        )(me, product, gathered, pair, near, far)
+        )(me, product, gathered, pair, *blocks)
         return [kept_sums] + [swap(x, "cols", step) for step, x in reversed(list(enumerate(messages, 1)))]
 
     def finish(kernel, start, sums):
         return pl.pallas_call(
             kernel,
             out_shape=sums_shape,
-            in_specs=[SMEM] + [VMEM] * (ROWS + 1),
+            in_specs=[VMEM] * (ROWS + 1),
             out_specs=VMEM,
             compiler_params=PARAMS,
             name="finish",
-        )(me, start, *sums)
-
-    first = ladder(0, near, far)
-    second = ladder(1, near_late, far_late)
+        )(start, *sums)
+
+    first = ladder(direct_kernel, near_direct, far_direct)
+    second = ladder(swapped_kernel, near, far, near_late, far_late)
     return finish(second_kernel, finish(first_kernel, residual, first), second)
 
 

time: 24.9 us -> 26 us (1.044)
  starting transfers between devices: 10.2 us -> 14.6 us
  waiting for transfers between devices: 9.86 us -> 6.36 us
    ppermute x11 -> x13, starting transfers between devices: 10.2 us -> 14.6 us  [swap(): return lax.ppermute(x, axis, [(i, i ^ step) for i in range(ROWS)])]
    ppermute x11 -> x13, waiting for transfers between devices: 9.86 us -> 6.36 us  [swap(): return lax.ppermute(x, axis, [(i, i ^ step) for i in range(ROWS)])]
    pallas_call x4 -> x6, Pallas kernels: 1.39 us -> 1.46 us  [the longest x2 0.75 us: finish(): pl.pallas_call(kernel, out_shape=sums_shape, in_specs=[VMEM] * (ROWS + 1)...]
  transfers between devices with their start and end apart: 11 -> 13, of which waited for: 4 -> 5; matrix products, arithmetic and copies ran while one was open for 0% -> 0% of each run, Pallas kernels for 7% -> 7%
where the time goes in v6:
time: 26 us; the launch traced here: 25.8 us
  starting transfers between devices  14.6 us (56%)
  waiting for transfers between devices  6.36 us (24%)
  Pallas kernels  3.56 us (14%)
  local copies, waits for them, and re-layouts  1.21 us (5%)
    ppermute x13, starting transfers between devices, swap(): return lax.ppermute(x, axis, [(i, i ^ step) for i in range(ROWS)])  14.6 us
    ppermute x13, waiting for transfers between devices, swap(): return lax.ppermute(x, axis, [(i, i ^ step) for i in range(ROWS)])  6.36 us
    unnamed x9, local copies, waits for them, and re-layouts  1.21 us
    pallas_call x1, Pallas kernels, local_few(): pl.pallas_call(functools.partial(prepare_kernel, tiles, slots), out_shape...  1.08 us
    pallas_call x1, Pallas kernels, local_few(): pl.pallas_call(functools.partial(pack_kernel, tiles, slots), out_shape=[j...  1.02 us
    pallas_call x2, Pallas kernels, finish(): pl.pallas_call(kernel, out_shape=sums_shape, in_specs=[VMEM] * (ROWS + 1)...  0.75 us
    pallas_call x2, Pallas kernels, ladder(): pl.pallas_call(kernel, out_shape=[half_sums] + [message] * (ROWS - 1), in...  0.71 us
  transfers between devices with their start and end apart: 13, of which 5 were waited for; matrix products, arithmetic and copies ran while one was open for 0% of the time, Pallas kernels for 7%

profile of v6, /device:TPU:0, one launch (start us, length us, event | category | flops | bytes accessed | tf_op | source)
XLA Modules:
  0.0 25.8 jit_solution(5145071725761119808)
XLA Ops:
  0.0 1.0 %pack.1 = (bf16[128,512]{1,0:T(8,128)(2,1)S(1)}, bf16[64,512]{1,0:T(8,128)(2,1)S(1)}, bf16[32,512]{1,0:T(8,128)(2,1)S(1)}, bf16[32,512]{1,0:T(8,128)(2,1)S(1)}) custom-call(s32[1]{0:T(128)} %bitcast.me, s32[4,8]{1,0:T(4,128)} %kept.3, bf16[128,1024]{1,0:T(8,128)(2,1)} %doubles.1), custom_call_target="tpu_custom_call" | custom-call | tf_op jit(solution)/shard_map/pack/pallas_call | solution.py:182
  1.0 5.1 %collective-permute-start.7 = (bf16[32,512]{1,0:T(8,128)(2,1)S(1)}, bf16[32,512]{1,0:T(8,128)(2,1)S(1)}, u32[]{:S(2)}, u32[]{:S(2)}) collective-permute-start(bf16[32,512]{1,0:T(8,128)(2,1)S(1)} %get-tuple-element.28), channel_id=1, source_target_pairs={{0,12},{4,8},{8,4},{12,0},{1,13},{5,9},{9,5},{13,1},{2,14},{6,10},... | collective-permute-start | bytes 98312 | tf_op jit(solution)/shard_map/ppermute | solution.py:167
  6.1 0.0 collective-permute-start.6
  6.1 0.0 copy-start.3
  6.1 2.9 %collective-permute-start.1 = (bf16[64,512]{1,0:T(8,128)(2,1)S(1)}, bf16[64,512]{1,0:T(8,128)(2,1)S(1)}, u32[]{:S(2)}, u32[]{:S(2)}) collective-permute-start(bf16[64,512]{1,0:T(8,128)(2,1)S(1)} %get-tuple-element.22), channel_id=1, source_target_pairs={{0,8},{4,12},{8,0},{12,4},{1,9},{5,13},{9,1},{13,5},{2,10},{6,14},... | collective-permute-start | bytes 196616 | tf_op jit(solution)/shard_map/ppermute | solution.py:167
  9.1 0.1 collective-permute-start.2
  9.1 0.0 copy-start.2
  9.2 0.5 %collective-permute-start = (bf16[128,512]{1,0:T(8,128)(2,1)S(1)}, bf16[128,512]{1,0:T(8,128)(2,1)S(1)}, u32[]{:S(2)}, u32[]{:S(2)}) collective-permute-start(bf16[128,512]{1,0:T(8,128)(2,1)S(1)} %get-tuple-element.19.own), channel_id=1, source_target_pairs={{0,4},{4,0},{8,12},{12,8},{1,5},{5,1},{9,13},{13,9},{2,6},{6,2},{1... | collective-permute-start | bytes 393224 | tf_op jit(solution)/shard_map/ppermute | solution.py:167
  9.7 0.0 copy-done.3
  9.7 0.1 copy.8.int_kept
  9.8 0.1 copy-done.2
  9.8 0.0 copy-start
  9.8 1.0 %copy-done = bf16[1024,256]{1,0:T(8,128)(2,1)S(1)} copy-done((bf16[1024,256]{1,0:T(8,128)(2,1)S(1)}, bf16[1024,256]{1,0:T(8,128)(2,1)}, u32[]{:S(2)}) %copy-start) | copy-done | bytes 524312
  10.9 1.1 %prepare.1 = (bf16[4,512,256]{2,1,0:T(8,128)(2,1)S(1)}, f32[128,256]{1,0:T(8,128)S(1)}) custom-call(s32[1]{0:T(128)} %bitcast.me, s32[4,8]{1,0:T(4,128)S(1)} %copy-done.2, s32[8,2]{1,0:T(8,128)S(1)} %copy.8.int_kept, bf16[1024,256]{1,0:T(8,128)(2,1)S(1)} %copy-done, bf16[128,512]{1,0:T(8,128)(2,1)S(1)} %get-tuple-element.19.own), custom_call_target="tpu_custom_call" | custom-call | bytes 1024 | tf_op jit(solution)/shard_map/prepare/pallas_call | solution.py:201
  12.0 0.0 collective-permute-done.7.x
  12.0 1.5 %collective-permute-start.8 = (bf16[32,512]{1,0:T(8,128)(2,1)S(1)}, bf16[32,512]{1,0:T(8,128)(2,1)S(1)}, u32[]{:S(2)}, u32[]{:S(2)}) collective-permute-start(bf16[32,512]{1,0:T(8,128)(2,1)S(1)} %after.3.far), channel_id=1, source_target_pairs={{0,4},{4,0},{8,12},{12,8},{1,5},{5,1},{9,13},{13,9},{2,6},{6,2},{1... | collective-permute-start | bytes 98312 | tf_op jit(solution)/shard_map/ppermute | solution.py:167
  13.5 0.0 collective-permute-done.6.x
  13.5 0.6 %collective-permute-start.9 = (bf16[32,512]{1,0:T(8,128)(2,1)S(1)}, bf16[32,512]{1,0:T(8,128)(2,1)S(1)}, u32[]{:S(2)}, u32[]{:S(2)}) collective-permute-start(bf16[32,512]{1,0:T(8,128)(2,1)S(1)} %after.2.near), channel_id=1, source_target_pairs={{0,4},{4,0},{8,12},{12,8},{1,5},{5,1},{9,13},{13,9},{2,6},{6,2},{1... | collective-permute-start | bytes 98312 | tf_op jit(solution)/shard_map/ppermute | solution.py:167
  14.1 0.1 collective-permute-done.1.near
  14.2 1.2 %collective-permute-done.2.far = bf16[64,512]{1,0:T(8,128)(2,1)S(1)} collective-permute-done((bf16[64,512]{1,0:T(8,128)(2,1)S(1)}, bf16[64,512]{1,0:T(8,128)(2,1)S(1)}, u32[]{:S(2)}, u32[]{:S(2)}) %collective-permute-start.2) | collective-permute-done | bytes 65568 | tf_op jit(solution)/shard_map/ppermute | solution.py:167
  15.4 1.9 %collective-permute-done.pair = bf16[128,512]{1,0:T(8,128)(2,1)S(1)} collective-permute-done((bf16[128,512]{1,0:T(8,128)(2,1)S(1)}, bf16[128,512]{1,0:T(8,128)(2,1)S(1)}, u32[]{:S(2)}, u32[]{:S(2)}) %collective-permute-start) | collective-permute-done | bytes 131104 | tf_op jit(solution)/shard_map/ppermute | solution.py:167
  17.3 0.3 %ladder.2 = (f32[64,256]{1,0:T(8,128)S(1)}, s16[144,128]{1,0:T(8,128)(2,1)S(1)}, s16[144,128]{1,0:T(8,128)(2,1)S(1)}, s16[144,128]{1,0:T(8,128)(2,1)S(1)}) custom-call(s32[1]{0:T(128)} %bitcast.me, f32[128,256]{1,0:T(8,128)S(1)} %get-tuple-element.20.product.token, bf16[4,512,256]{2,1,0:T(8,128)(2,1)S(1)} %get-tuple-element.21.gathered, ...), custom_call_target="tpu_custom_call" | custom-call | flops 99999997952 | bytes 1024 | tf_op jit(solution)/shard_map/ladder/pallas_call | solution.py:216
  17.6 0.1 collective-permute-start.3
  17.7 1.5 %collective-permute-start.4 = (s16[144,128]{1,0:T(8,128)(2,1)S(1)}, s16[144,128]{1,0:T(8,128)(2,1)S(1)}, u32[]{:S(2)}, u32[]{:S(2)}) collective-permute-start(s16[144,128]{1,0:T(8,128)(2,1)S(1)} %get-tuple-element.25), channel_id=1, source_target_pairs={{0,2},{1,3},{2,0},{3,1},{4,6},{5,7},{6,4},{7,5},{8,10},{9,11},{10,... | collective-permute-start | bytes 110600 | tf_op jit(solution)/shard_map/ppermute | solution.py:167
  19.2 0.0 copy-start.1
  19.2 0.3 %collective-permute-start.5 = (s16[144,128]{1,0:T(8,128)(2,1)S(1)}, s16[144,128]{1,0:T(8,128)(2,1)S(1)}, u32[]{:S(2)}, u32[]{:S(2)}) collective-permute-start(s16[144,128]{1,0:T(8,128)(2,1)S(1)} %get-tuple-element.26), channel_id=1, source_target_pairs={{0,1},{1,0},{2,3},{3,2},{4,5},{5,4},{6,7},{7,6},{8,9},{9,8},{10,11... | collective-permute-start | bytes 110600 | tf_op jit(solution)/shard_map/ppermute | solution.py:167
  19.6 0.0 collective-permute-done.8.near_late
  19.6 0.0 collective-permute-done.9.far_late
  19.6 0.4 %ladder.3 = (f32[64,256]{1,0:T(8,128)S(1)}, s16[144,128]{1,0:T(8,128)(2,1)S(1)}, s16[144,128]{1,0:T(8,128)(2,1)S(1)}, s16[144,128]{1,0:T(8,128)(2,1)S(1)}) custom-call(s32[1]{0:T(128)} %bitcast.me, f32[128,256]{1,0:T(8,128)S(1)} %get-tuple-element.20.product.token, bf16[4,512,256]{2,1,0:T(8,128)(2,1)S(1)} %get-tuple-element.21.gathered, ...), custom_call_target="tpu_custom_call" | custom-call | flops 99999997952 | bytes 1024 | tf_op jit(solution)/shard_map/ladder/pallas_call | solution.py:216
  20.0 1.1 %collective-permute-start.10 = (s16[144,128]{1,0:T(8,128)(2,1)S(1)}, s16[144,128]{1,0:T(8,128)(2,1)S(1)}, u32[]{:S(2)}, u32[]{:S(2)}) collective-permute-start(s16[144,128]{1,0:T(8,128)(2,1)S(1)} %get-tuple-element.30), channel_id=1, source_target_pairs={{0,3},{1,2},{2,1},{3,0},{4,7},{5,6},{6,5},{7,4},{8,11},{9,10},{10,... | collective-permute-start | bytes 110600 | tf_op jit(solution)/shard_map/ppermute | solution.py:167
  21.1 0.7 %collective-permute-start.11 = (s16[144,128]{1,0:T(8,128)(2,1)S(1)}, s16[144,128]{1,0:T(8,128)(2,1)S(1)}, u32[]{:S(2)}, u32[]{:S(2)}) collective-permute-start(s16[144,128]{1,0:T(8,128)(2,1)S(1)} %get-tuple-element.31), channel_id=1, source_target_pairs={{0,2},{1,3},{2,0},{3,1},{4,6},{5,7},{6,4},{7,5},{8,10},{9,11},{10,... | collective-permute-start | bytes 110600 | tf_op jit(solution)/shard_map/ppermute | solution.py:167
  21.8 0.0 collective-permute-done.3.rest_0_
  21.8 0.1 collective-permute-start.12
  21.9 0.0 collective-permute-done.4.rest_1_
  21.9 0.0 collective-permute-done.5.rest_2_
  21.9 0.0 copy-done.1
  22.0 1.5 %collective-permute-done.10.rest_0_ = s16[144,128]{1,0:T(8,128)(2,1)S(1)} collective-permute-done((s16[144,128]{1,0:T(8,128)(2,1)S(1)}, s16[144,128]{1,0:T(8,128)(2,1)S(1)}, u32[]{:S(2)}, u32[]{:S(2)}) %collective-permute-start.10) | collective-permute-done | bytes 36896 | tf_op jit(solution)/shard_map/ppermute | solution.py:167
  23.5 1.6 %collective-permute-done.11.rest_1_ = s16[144,128]{1,0:T(8,128)(2,1)S(1)} collective-permute-done((s16[144,128]{1,0:T(8,128)(2,1)S(1)}, s16[144,128]{1,0:T(8,128)(2,1)S(1)}, u32[]{:S(2)}, u32[]{:S(2)}) %collective-permute-start.11) | collective-permute-done | bytes 36896 | tf_op jit(solution)/shard_map/ppermute | solution.py:167
  25.1 0.0 collective-permute-done.12.rest_2_
  25.1 0.7 %finish.3 = f32[128,256]{1,0:T(8,128)} custom-call(f32[128,256]{1,0:T(8,128)S(1)} %finish.2.base, f32[64,256]{1,0:T(8,128)S(1)} %get-tuple-element.29.kept_sums, s16[144,128]{1,0:T(8,128)(2,1)S(1)} %collective-permute-done.10.rest_0_, s16[144,128]{1,0:T(8,128)(2,1)S(1)} %collective-permute-done.11.rest_1_, s16[144,128]{1,0:T(8,128)(2,1)S(1)} %collective-permute-done.12.rest_2_), custom_call_target="tpu_custom_call" | custom-call | tf_op jit(solution)/shard_map/finish/pallas_call | solution.py:229
  (3 shorter events, 0.0 us)
Async XLA Ops:
  1.0 10.9 %collective-permute-start.7 = (bf16[32,512]{1,0:T(8,128)(2,1)S(1)}, bf16[32,512]{1,0:T(8,128)(2,1)S(1)}, u32[]{:S(2)}, u32[]{:S(2)}) collective-permute-start(bf16[32,512]{1,0:T(8,128)(2,1)S(1)} %get-tuple-element.28), channel_id=1, source_target_pairs={{0,12},{4,8},{8,4},{12,0},{1,13},{5,9},{9,5},{13,1},{2,14},{6,10},... | collective-permute-start | bytes 98312 | tf_op jit(solution)/shard_map/ppermute | solution.py:167
  6.1 7.3 %collective-permute-start.6 = (bf16[32,512]{1,0:T(8,128)(2,1)S(1)}, bf16[32,512]{1,0:T(8,128)(2,1)S(1)}, u32[]{:S(2)}, u32[]{:S(2)}) collective-permute-start(bf16[32,512]{1,0:T(8,128)(2,1)S(1)} %get-tuple-element.27), channel_id=1, source_target_pairs={{0,8},{4,12},{8,0},{12,4},{1,9},{5,13},{9,1},{13,5},{2,10},{6,14},... | collective-permute-start | bytes 98312 | tf_op jit(solution)/shard_map/ppermute | solution.py:167
  6.1 3.5 %copy-start.3 = (s32[8,2]{0,1:T(2,128)S(1)}, s32[8,2]{0,1:T(2,128)}, u32[]{:S(2)}) copy-start(s32[8,2]{0,1:T(2,128)} %param.8) | copy-start | bytes 196
  6.1 8.1 %collective-permute-start.1 = (bf16[64,512]{1,0:T(8,128)(2,1)S(1)}, bf16[64,512]{1,0:T(8,128)(2,1)S(1)}, u32[]{:S(2)}, u32[]{:S(2)}) collective-permute-start(bf16[64,512]{1,0:T(8,128)(2,1)S(1)} %get-tuple-element.22), channel_id=1, source_target_pairs={{0,8},{4,12},{8,0},{12,4},{1,9},{5,13},{9,1},{13,5},{2,10},{6,14},... | collective-permute-start | bytes 196616 | tf_op jit(solution)/shard_map/ppermute | solution.py:167
  9.1 6.4 %collective-permute-start.2 = (bf16[64,512]{1,0:T(8,128)(2,1)S(1)}, bf16[64,512]{1,0:T(8,128)(2,1)S(1)}, u32[]{:S(2)}, u32[]{:S(2)}) collective-permute-start(bf16[64,512]{1,0:T(8,128)(2,1)S(1)} %get-tuple-element.22), channel_id=1, source_target_pairs={{0,12},{4,8},{8,4},{12,0},{1,13},{5,9},{9,5},{13,1},{2,14},{6,10},... | collective-permute-start | bytes 196616 | tf_op jit(solution)/shard_map/ppermute | solution.py:167
  9.1 0.7 %copy-start.2 = (s32[4,8]{1,0:T(4,128)S(1)}, s32[4,8]{1,0:T(4,128)}, u32[]{:S(2)}) copy-start(s32[4,8]{1,0:T(4,128)} %kept.3) | copy-start | bytes 388
  9.2 8.2 %collective-permute-start = (bf16[128,512]{1,0:T(8,128)(2,1)S(1)}, bf16[128,512]{1,0:T(8,128)(2,1)S(1)}, u32[]{:S(2)}, u32[]{:S(2)}) collective-permute-start(bf16[128,512]{1,0:T(8,128)(2,1)S(1)} %get-tuple-element.19.own), channel_id=1, source_target_pairs={{0,4},{4,0},{8,12},{12,8},{1,5},{5,1},{9,13},{13,9},{2,6},{6,2},{1... | collective-permute-start | bytes 393224 | tf_op jit(solution)/shard_map/ppermute | solution.py:167
  9.8 1.0 %copy-start = (bf16[1024,256]{1,0:T(8,128)(2,1)S(1)}, bf16[1024,256]{1,0:T(8,128)(2,1)}, u32[]{:S(2)}) copy-start(bf16[1024,256]{1,0:T(8,128)(2,1)} %integrals.1) | copy-start | bytes 1572868
  12.0 7.6 %collective-permute-start.8 = (bf16[32,512]{1,0:T(8,128)(2,1)S(1)}, bf16[32,512]{1,0:T(8,128)(2,1)S(1)}, u32[]{:S(2)}, u32[]{:S(2)}) collective-permute-start(bf16[32,512]{1,0:T(8,128)(2,1)S(1)} %after.3.far), channel_id=1, source_target_pairs={{0,4},{4,0},{8,12},{12,8},{1,5},{5,1},{9,13},{13,9},{2,6},{6,2},{1... | collective-permute-start | bytes 98312 | tf_op jit(solution)/shard_map/ppermute | solution.py:167
  13.5 6.1 %collective-permute-start.9 = (bf16[32,512]{1,0:T(8,128)(2,1)S(1)}, bf16[32,512]{1,0:T(8,128)(2,1)S(1)}, u32[]{:S(2)}, u32[]{:S(2)}) collective-permute-start(bf16[32,512]{1,0:T(8,128)(2,1)S(1)} %after.2.near), channel_id=1, source_target_pairs={{0,4},{4,0},{8,12},{12,8},{1,5},{5,1},{9,13},{13,9},{2,6},{6,2},{1... | collective-permute-start | bytes 98312 | tf_op jit(solution)/shard_map/ppermute | solution.py:167
  17.6 4.2 %collective-permute-start.3 = (s16[144,128]{1,0:T(8,128)(2,1)S(1)}, s16[144,128]{1,0:T(8,128)(2,1)S(1)}, u32[]{:S(2)}, u32[]{:S(2)}) collective-permute-start(s16[144,128]{1,0:T(8,128)(2,1)S(1)} %get-tuple-element.24), channel_id=1, source_target_pairs={{0,3},{1,2},{2,1},{3,0},{4,7},{5,6},{6,5},{7,4},{8,11},{9,10},{10,... | collective-permute-start | bytes 110600 | tf_op jit(solution)/shard_map/ppermute | solution.py:167
  17.7 4.2 %collective-permute-start.4 = (s16[144,128]{1,0:T(8,128)(2,1)S(1)}, s16[144,128]{1,0:T(8,128)(2,1)S(1)}, u32[]{:S(2)}, u32[]{:S(2)}) collective-permute-start(s16[144,128]{1,0:T(8,128)(2,1)S(1)} %get-tuple-element.25), channel_id=1, source_target_pairs={{0,2},{1,3},{2,0},{3,1},{4,6},{5,7},{6,4},{7,5},{8,10},{9,11},{10,... | collective-permute-start | bytes 110600 | tf_op jit(solution)/shard_map/ppermute | solution.py:167
  19.2 2.7 %copy-start.1 = (f32[128,256]{1,0:T(8,128)S(1)}, f32[128,256]{1,0:T(8,128)}, u32[]{:S(2)}) copy-start(f32[128,256]{1,0:T(8,128)} %residual.1) | copy-start | bytes 393220
  19.2 2.7 %collective-permute-start.5 = (s16[144,128]{1,0:T(8,128)(2,1)S(1)}, s16[144,128]{1,0:T(8,128)(2,1)S(1)}, u32[]{:S(2)}, u32[]{:S(2)}) collective-permute-start(s16[144,128]{1,0:T(8,128)(2,1)S(1)} %get-tuple-element.26), channel_id=1, source_target_pairs={{0,1},{1,0},{2,3},{3,2},{4,5},{5,4},{6,7},{7,6},{8,9},{9,8},{10,11... | collective-permute-start | bytes 110600 | tf_op jit(solution)/shard_map/ppermute | solution.py:167
  20.0 3.5 %collective-permute-start.10 = (s16[144,128]{1,0:T(8,128)(2,1)S(1)}, s16[144,128]{1,0:T(8,128)(2,1)S(1)}, u32[]{:S(2)}, u32[]{:S(2)}) collective-permute-start(s16[144,128]{1,0:T(8,128)(2,1)S(1)} %get-tuple-element.30), channel_id=1, source_target_pairs={{0,3},{1,2},{2,1},{3,0},{4,7},{5,6},{6,5},{7,4},{8,11},{9,10},{10,... | collective-permute-start | bytes 110600 | tf_op jit(solution)/shard_map/ppermute | solution.py:167
  21.1 4.0 %collective-permute-start.11 = (s16[144,128]{1,0:T(8,128)(2,1)S(1)}, s16[144,128]{1,0:T(8,128)(2,1)S(1)}, u32[]{:S(2)}, u32[]{:S(2)}) collective-permute-start(s16[144,128]{1,0:T(8,128)(2,1)S(1)} %get-tuple-element.31), channel_id=1, source_target_pairs={{0,2},{1,3},{2,0},{3,1},{4,6},{5,7},{6,4},{7,5},{8,10},{9,11},{10,... | collective-permute-start | bytes 110600 | tf_op jit(solution)/shard_map/ppermute | solution.py:167
  21.8 3.2 %collective-permute-start.12 = (s16[144,128]{1,0:T(8,128)(2,1)S(1)}, s16[144,128]{1,0:T(8,128)(2,1)S(1)}, u32[]{:S(2)}, u32[]{:S(2)}) collective-permute-start(s16[144,128]{1,0:T(8,128)(2,1)S(1)} %get-tuple-element.32), channel_id=1, source_target_pairs={{0,1},{1,0},{2,3},{3,2},{4,5},{5,4},{6,7},{7,6},{8,9},{9,8},{10,11... | collective-permute-start | bytes 110600 | tf_op jit(solution)/shard_map/ppermute | solution.py:167

commit v7 on v3

--- a/solution.py
+++ b/solution.py
@@ -20,6 +20,10 @@
 ROWS = 4
 
 
+def cost(flops):
+    return pl.CostEstimate(flops=flops, bytes_accessed=1024, transcendentals=0)
+
+
 def list_kept(kept, row, tiles, places):
     at = jnp.int32(0)
     for tile in range(tiles):
@@ -27,26 +31,21 @@
         at = at + kept[row, tile]
 
 
-def half_of(ref, half):
-    size = ref.shape[0] // 2
-    return ref.at[pl.ds(pl.multiple_of(half * size, size), size)]
-
-
-def pack_kernel(tiles, slots, me, kept, doubles, packed, near_half, far_half, table, block, places, sems):
-    row = me[0] // ROWS
+def pack_kernel(tiles, slots, me, kept, doubles, packed, first, second, table, block, places, sems):
     table_copy = pltpu.make_async_copy(kept, table, sems.at[0])
     block_copy = pltpu.make_async_copy(doubles, block, sems.at[1])
     table_copy.start()
     block_copy.start()
     table_copy.wait()
-    list_kept(table, row, tiles, places)
+    list_kept(table, me[0] // ROWS, tiles, places)
     block_copy.wait()
+    half = first.shape[0]
     for slot in range(slots):
-        tile = pl.ds(pl.multiple_of(places[slot] * TILE, TILE), TILE)
+        tile = block[:, pl.ds(pl.multiple_of(places[slot] * TILE, TILE), TILE)]
         to = slice(slot * TILE, (slot + 1) * TILE)
-        packed[:, to] = block[:, tile]
-        near_half[:, to] = half_of(block, row % 2)[:, tile]
-        far_half[:, to] = half_of(block, 1 - row % 2)[:, tile]
+        packed[:, to] = tile
+        first[:, to] = tile[:half]
+        second[:, to] = tile[half:]
 
 
 def prepare_kernel(tiles, slots, me, kept, int_kept, integrals, own, gathered, product, places):
@@ -89,13 +88,11 @@
     return jnp.concatenate(parts, axis=1)
 
 
-def ladder_kernel(phase, me, product, gathered, pair, near, far, kept_sums, *rest):
-    outs, sums = rest[:-1], rest[-1]
-    row = me[0] // ROWS
-    mine = row ^ me[0] % ROWS
-    half = row % 2 if phase == 0 else 1 - row % 2
-    sums[mine] = half_of(product, half)[...]
-    for step, block in enumerate((half_of(pair, half), near, far), 1):
+def ladder_kernel(start, me, product, gathered, *rest):
+    blocks, kept_sums, outs, sums = rest[: ROWS - 1], rest[ROWS - 1], rest[ROWS:-1], rest[-1]
+    mine = me[0] // ROWS ^ me[0] % ROWS
+    sums[mine] = product[start : start + sums.shape[1], :]
+    for step, block in zip(range(ROWS - 1, 0, -1), blocks):
         sums[mine ^ step] = jnp.dot(block[...], gathered[mine ^ step], preferred_element_type=jnp.float32)
     kept_sums[...] = sums[0]
     for n, out in enumerate(outs, 1):
@@ -109,18 +106,18 @@
     return total
 
 
-def first_kernel(me, residual, kept_sums, *rest):
+def first_kernel(residual, kept_sums, *rest):
     messages, out = rest[:-1], rest[-1]
-    half = me[0] // ROWS % 2
-    half_of(out, 1 - half)[...] = half_of(residual, 1 - half)[...]
-    half_of(out, half)[...] = total_of(half_of(residual, half)[...], kept_sums, messages)
-
-
-def second_kernel(me, base, kept_sums, *rest):
+    half = kept_sums.shape[0]
+    out[:half, :] = total_of(residual[:half, :], kept_sums, messages)
+    out[half:, :] = residual[half:, :]
+
+
+def second_kernel(base, kept_sums, *rest):
     messages, out = rest[:-1], rest[-1]
-    half = me[0] // ROWS % 2
-    half_of(out, half)[...] = half_of(base, half)[...]
-    half_of(out, 1 - half)[...] = total_of(half_of(base, 1 - half)[...], kept_sums, messages)
+    half = kept_sums.shape[0]
+    out[:half, :] = base[:half, :]
+    out[half:, :] = total_of(base[half:, :], kept_sums, messages)
 
 
 def swap(x, axis, step):
@@ -138,7 +135,7 @@
     half_sums = jax.ShapeDtypeStruct((pairs // 2, width), jnp.float32)
     half_block = jax.ShapeDtypeStruct((pairs // 2, slots * TILE), doubles.dtype)
     message = jax.ShapeDtypeStruct((pairs // 2 * width // TILE + HEAD, TILE), jnp.int16)
-    packed, near_half, far_half = pl.pallas_call(
+    packed, first, second = pl.pallas_call(
         functools.partial(pack_kernel, tiles, slots),
         out_shape=[jax.ShapeDtypeStruct((pairs, slots * TILE), doubles.dtype), half_block, half_block],
         in_specs=[SMEM, HBM, HBM],
@@ -152,9 +149,7 @@
         compiler_params=PARAMS,
         name="pack",
     )(me, pltpu.with_memory_space_constraint(doubles_kept, pltpu.HBM), pltpu.with_memory_space_constraint(doubles, pltpu.HBM))
-    near = swap(near_half, "rows", 2)
-    far = swap(far_half, "rows", 3)
-    pair = swap(packed, "rows", 1)
+    first, second = ([swap(x, "rows", step) for step in range(ROWS - 1, 0, -1)] for x in (first, second))
     gathered, product = pl.pallas_call(
         functools.partial(prepare_kernel, tiles, slots),
         out_shape=[jax.ShapeDtypeStruct((ROWS, slots * TILE, width), integrals.dtype), sums_shape],
@@ -162,37 +157,34 @@
         out_specs=[VMEM] * 2,
         scratch_shapes=[places],
         compiler_params=PARAMS,
-        cost_estimate=pl.CostEstimate(flops=2 * pairs * slots * TILE * width, bytes_accessed=4 << 20, transcendentals=0),
+        cost_estimate=cost(0),
         name="prepare",
     )(me, doubles_kept, integral_kept, integrals, packed)
-    far_late = swap(near, "rows", 1)
-    near_late = swap(far, "rows", 1)
-
-    def ladder(phase, near, far):
+    def ladder(start, blocks):
         kept_sums, *messages = pl.pallas_call(
-            functools.partial(ladder_kernel, phase),
+            functools.partial(ladder_kernel, start),
             out_shape=[half_sums] + [message] * (ROWS - 1),
             in_specs=[SMEM] + [VMEM] * 5,
             out_specs=[VMEM] * ROWS,
             scratch_shapes=[pltpu.VMEM((ROWS,) + half_sums.shape, jnp.float32)],
             compiler_params=PARAMS,
+            cost_estimate=cost(10**11),
             name="ladder",
-        )(me, product, gathered, pair, near, far)
+        )(me, product, gathered, *blocks)
         return [kept_sums] + [swap(x, "cols", step) for step, x in reversed(list(enumerate(messages, 1)))]
 
     def finish(kernel, start, sums):
         return pl.pallas_call(
             kernel,
             out_shape=sums_shape,
-            in_specs=[SMEM] + [VMEM] * (ROWS + 1),
+            in_specs=[VMEM] * (ROWS + 1),
             out_specs=VMEM,
             compiler_params=PARAMS,
             name="finish",
-        )(me, start, *sums)
-
-    first = ladder(0, near, far)
-    second = ladder(1, near_late, far_late)
-    return finish(second_kernel, finish(first_kernel, residual, first), second)
+        )(start, *sums)
+
+    sums = finish(first_kernel, residual, ladder(0, first))
+    return finish(second_kernel, sums, ladder(pairs // 2, second))
 
 
 def local_many(doubles, doubles_kept, integrals, integral_kept, residual):

time: 24.9 us -> 23.6 us (0.948)
  waiting for transfers between devices: 9.86 us -> 4.02 us
  starting transfers between devices: 10.2 us -> 14.1 us
  local copies, waits for them, and re-layouts: 1.13 us -> 1.73 us
    ppermute x11 -> x12, waiting for transfers between devices: 9.86 us -> 4.02 us  [swap(): return lax.ppermute(x, axis, [(i, i ^ step) for i in range(ROWS)])]
    ppermute x11 -> x12, starting transfers between devices: 10.2 us -> 14.1 us  [swap(): return lax.ppermute(x, axis, [(i, i ^ step) for i in range(ROWS)])]
    unnamed x9, local copies, waits for them, and re-layouts: 1.13 us -> 1.73 us
  transfers between devices with their start and end apart: 11 -> 12, of which waited for: 4 -> 5; matrix products, arithmetic and copies ran while one was open for 0% -> 0% of each run, Pallas kernels for 7% -> 8%
where the time goes in v7:
time: 23.6 us; the launch traced here: 23.4 us
  starting transfers between devices  14.1 us (60%)
  waiting for transfers between devices  4.02 us (17%)
  Pallas kernels  3.48 us (15%)
  local copies, waits for them, and re-layouts  1.73 us (7%)
    ppermute x12, starting transfers between devices, swap(): return lax.ppermute(x, axis, [(i, i ^ step) for i in range(ROWS)])  14.1 us
    ppermute x12, waiting for transfers between devices, swap(): return lax.ppermute(x, axis, [(i, i ^ step) for i in range(ROWS)])  4.02 us
    unnamed x9, local copies, waits for them, and re-layouts  1.73 us
    pallas_call x1, Pallas kernels, local_few(): pl.pallas_call(functools.partial(prepare_kernel, tiles, slots), out_shape...  1.08 us
    pallas_call x1, Pallas kernels, local_few(): pl.pallas_call(functools.partial(pack_kernel, tiles, slots), out_shape=[j...  1 us
    pallas_call x2, Pallas kernels, finish(): pl.pallas_call(kernel, out_shape=sums_shape, in_specs=[VMEM] * (ROWS + 1)...  0.75 us
    pallas_call x2, Pallas kernels, ladder(): pl.pallas_call(functools.partial(ladder_kernel, start), out_shape=[half_s...  0.65 us
  transfers between devices with their start and end apart: 12, of which 5 were waited for; matrix products, arithmetic and copies ran while one was open for 0% of the time, Pallas kernels for 8%

profile of v7, /device:TPU:0, one launch (start us, length us, event | category | flops | bytes accessed | tf_op | source)
XLA Modules:
  0.0 23.4 jit_solution(2810389919609861771)
XLA Ops:
  0.0 1.0 %pack.1 = (bf16[128,512]{1,0:T(8,128)(2,1)S(1)}, bf16[64,512]{1,0:T(8,128)(2,1)S(1)}, bf16[64,512]{1,0:T(8,128)(2,1)S(1)}) custom-call(s32[1]{0:T(128)} %bitcast.me, s32[4,8]{1,0:T(4,128)} %kept.3, bf16[128,1024]{1,0:T(8,128)(2,1)} %doubles.1), custom_call_target="tpu_custom_call" | custom-call | tf_op jit(solution)/shard_map/pack/pallas_call | solution.py:138
  1.0 0.0 copy-start.3
  1.0 5.1 %collective-permute-start = (bf16[64,512]{1,0:T(8,128)(2,1)S(1)}, bf16[64,512]{1,0:T(8,128)(2,1)S(1)}, u32[]{:S(2)}, u32[]{:S(2)}) collective-permute-start(bf16[64,512]{1,0:T(8,128)(2,1)S(1)} %get-tuple-element.21), channel_id=1, source_target_pairs={{0,12},{4,8},{8,4},{12,0},{1,13},{5,9},{9,5},{13,1},{2,14},{6,10},... | collective-permute-start | bytes 196616 | tf_op jit(solution)/shard_map/ppermute | solution.py:124
  6.1 0.0 collective-permute-start.1
  6.1 0.6 %collective-permute-start.2 = (bf16[64,512]{1,0:T(8,128)(2,1)S(1)}, bf16[64,512]{1,0:T(8,128)(2,1)S(1)}, u32[]{:S(2)}, u32[]{:S(2)}) collective-permute-start(bf16[64,512]{1,0:T(8,128)(2,1)S(1)} %get-tuple-element.21), channel_id=1, source_target_pairs={{0,4},{4,0},{8,12},{12,8},{1,5},{5,1},{9,13},{13,9},{2,6},{6,2},{1... | collective-permute-start | bytes 196616 | tf_op jit(solution)/shard_map/ppermute | solution.py:124
  6.8 3.7 %collective-permute-start.6 = (bf16[64,512]{1,0:T(8,128)(2,1)S(1)}, bf16[64,512]{1,0:T(8,128)(2,1)S(1)}, u32[]{:S(2)}, u32[]{:S(2)}) collective-permute-start(bf16[64,512]{1,0:T(8,128)(2,1)S(1)} %get-tuple-element.26), channel_id=1, source_target_pairs={{0,12},{4,8},{8,4},{12,0},{1,13},{5,9},{9,5},{13,1},{2,14},{6,10},... | collective-permute-start | bytes 196616 | tf_op jit(solution)/shard_map/ppermute | solution.py:124
  10.5 0.0 collective-permute-start.7
  10.5 0.0 copy-done.3
  10.5 0.0 copy-start.2
  10.5 0.1 copy.6.int_kept
  10.6 0.6 %copy-done.2 = s32[4,8]{1,0:T(4,128)S(1)} copy-done((s32[4,8]{1,0:T(4,128)S(1)}, s32[4,8]{1,0:T(4,128)}, u32[]{:S(2)}) %copy-start.2) | copy-done | bytes 152
  11.2 0.0 copy-start
  11.2 1.0 %copy-done = bf16[1024,256]{1,0:T(8,128)(2,1)S(1)} copy-done((bf16[1024,256]{1,0:T(8,128)(2,1)S(1)}, bf16[1024,256]{1,0:T(8,128)(2,1)}, u32[]{:S(2)}) %copy-start) | copy-done | bytes 524312
  12.3 1.1 %prepare.1 = (bf16[4,512,256]{2,1,0:T(8,128)(2,1)S(1)}, f32[128,256]{1,0:T(8,128)S(1)}) custom-call(s32[1]{0:T(128)} %bitcast.me, s32[4,8]{1,0:T(4,128)S(1)} %copy-done.2, s32[8,2]{1,0:T(8,128)S(1)} %copy.6.int_kept, bf16[1024,256]{1,0:T(8,128)(2,1)S(1)} %copy-done, bf16[128,512]{1,0:T(8,128)(2,1)S(1)} %get-tuple-element.18.own), custom_call_target="tpu_custom_call" | custom-call | bytes 1024 | tf_op jit(solution)/shard_map/prepare/pallas_call | solution.py:153
  13.3 0.0 collective-permute-done.rest_0_
  13.4 0.7 %collective-permute-start.8 = (bf16[64,512]{1,0:T(8,128)(2,1)S(1)}, bf16[64,512]{1,0:T(8,128)(2,1)S(1)}, u32[]{:S(2)}, u32[]{:S(2)}) collective-permute-start(bf16[64,512]{1,0:T(8,128)(2,1)S(1)} %get-tuple-element.26), channel_id=1, source_target_pairs={{0,4},{4,0},{8,12},{12,8},{1,5},{5,1},{9,13},{13,9},{2,6},{6,2},{1... | collective-permute-start | bytes 196616 | tf_op jit(solution)/shard_map/ppermute | solution.py:124
  14.1 0.9 %collective-permute-done.1.rest_1_ = bf16[64,512]{1,0:T(8,128)(2,1)S(1)} collective-permute-done((bf16[64,512]{1,0:T(8,128)(2,1)S(1)}, bf16[64,512]{1,0:T(8,128)(2,1)S(1)}, u32[]{:S(2)}, u32[]{:S(2)}) %collective-permute-start.1) | collective-permute-done | bytes 65568 | tf_op jit(solution)/shard_map/ppermute | solution.py:124
  15.0 0.0 collective-permute-done.2.rest_2_
  15.0 0.3 %ladder.2 = (f32[64,256]{1,0:T(8,128)S(1)}, s16[144,128]{1,0:T(8,128)(2,1)S(1)}, s16[144,128]{1,0:T(8,128)(2,1)S(1)}, s16[144,128]{1,0:T(8,128)(2,1)S(1)}) custom-call(s32[1]{0:T(128)} %bitcast.me, f32[128,256]{1,0:T(8,128)S(1)} %get-tuple-element.19.product, bf16[4,512,256]{2,1,0:T(8,128)(2,1)S(1)} %get-tuple-element.20.gathered, ...), custom_call_target="tpu_custom_call" | custom-call | flops 99999997952 | bytes 1024 | tf_op jit(solution)/shard_map/ladder/pallas_call | solution.py:164
  15.3 0.1 collective-permute-start.3
  15.4 1.4 %collective-permute-start.4 = (s16[144,128]{1,0:T(8,128)(2,1)S(1)}, s16[144,128]{1,0:T(8,128)(2,1)S(1)}, u32[]{:S(2)}, u32[]{:S(2)}) collective-permute-start(s16[144,128]{1,0:T(8,128)(2,1)S(1)} %get-tuple-element.24), channel_id=1, source_target_pairs={{0,2},{1,3},{2,0},{3,1},{4,6},{5,7},{6,4},{7,5},{8,10},{9,11},{10,... | collective-permute-start | bytes 110600 | tf_op jit(solution)/shard_map/ppermute | solution.py:124
  16.8 0.0 collective-permute-done.6.rest_0_
  16.8 0.0 copy-start.1
  16.8 0.5 %collective-permute-start.5 = (s16[144,128]{1,0:T(8,128)(2,1)S(1)}, s16[144,128]{1,0:T(8,128)(2,1)S(1)}, u32[]{:S(2)}, u32[]{:S(2)}) collective-permute-start(s16[144,128]{1,0:T(8,128)(2,1)S(1)} %get-tuple-element.25), channel_id=1, source_target_pairs={{0,1},{1,0},{2,3},{3,2},{4,5},{5,4},{6,7},{7,6},{8,9},{9,8},{10,11... | collective-permute-start | bytes 110600 | tf_op jit(solution)/shard_map/ppermute | solution.py:124
  17.3 0.1 collective-permute-done.7.rest_1_
  17.4 0.7 %collective-permute-done.8.rest_2_ = bf16[64,512]{1,0:T(8,128)(2,1)S(1)} collective-permute-done((bf16[64,512]{1,0:T(8,128)(2,1)S(1)}, bf16[64,512]{1,0:T(8,128)(2,1)S(1)}, u32[]{:S(2)}, u32[]{:S(2)}) %collective-permute-start.8) | collective-permute-done | bytes 65568 | tf_op jit(solution)/shard_map/ppermute | solution.py:124
  18.1 0.3 %ladder.3 = (f32[64,256]{1,0:T(8,128)S(1)}, s16[144,128]{1,0:T(8,128)(2,1)S(1)}, s16[144,128]{1,0:T(8,128)(2,1)S(1)}, s16[144,128]{1,0:T(8,128)(2,1)S(1)}) custom-call(s32[1]{0:T(128)} %bitcast.me, f32[128,256]{1,0:T(8,128)S(1)} %get-tuple-element.19.product, bf16[4,512,256]{2,1,0:T(8,128)(2,1)S(1)} %get-tuple-element.20.gathered, ...), custom_call_target="tpu_custom_call" | custom-call | flops 99999997952 | bytes 1024 | tf_op jit(solution)/shard_map/ladder/pallas_call | solution.py:164
  18.4 0.3 %collective-permute-start.9 = (s16[144,128]{1,0:T(8,128)(2,1)S(1)}, s16[144,128]{1,0:T(8,128)(2,1)S(1)}, u32[]{:S(2)}, u32[]{:S(2)}) collective-permute-start(s16[144,128]{1,0:T(8,128)(2,1)S(1)} %get-tuple-element.28), channel_id=1, source_target_pairs={{0,3},{1,2},{2,1},{3,0},{4,7},{5,6},{6,5},{7,4},{8,11},{9,10},{10,... | collective-permute-start | bytes 110600 | tf_op jit(solution)/shard_map/ppermute | solution.py:124
  18.7 1.3 %collective-permute-start.10 = (s16[144,128]{1,0:T(8,128)(2,1)S(1)}, s16[144,128]{1,0:T(8,128)(2,1)S(1)}, u32[]{:S(2)}, u32[]{:S(2)}) collective-permute-start(s16[144,128]{1,0:T(8,128)(2,1)S(1)} %get-tuple-element.29), channel_id=1, source_target_pairs={{0,2},{1,3},{2,0},{3,1},{4,6},{5,7},{6,4},{7,5},{8,10},{9,11},{10,... | collective-permute-start | bytes 110600 | tf_op jit(solution)/shard_map/ppermute | solution.py:124
  20.0 0.0 collective-permute-done.3.rest_0_
  20.0 0.3 %collective-permute-start.11 = (s16[144,128]{1,0:T(8,128)(2,1)S(1)}, s16[144,128]{1,0:T(8,128)(2,1)S(1)}, u32[]{:S(2)}, u32[]{:S(2)}) collective-permute-start(s16[144,128]{1,0:T(8,128)(2,1)S(1)} %get-tuple-element.30), channel_id=1, source_target_pairs={{0,1},{1,0},{2,3},{3,2},{4,5},{5,4},{6,7},{7,6},{8,9},{9,8},{10,11... | collective-permute-start | bytes 110600 | tf_op jit(solution)/shard_map/ppermute | solution.py:124
  20.3 0.0 collective-permute-done.4.rest_1_
  20.3 0.0 collective-permute-done.5.rest_2_
  20.3 0.0 copy-done.1
  20.4 1.8 %collective-permute-done.9.rest_0_ = s16[144,128]{1,0:T(8,128)(2,1)S(1)} collective-permute-done((s16[144,128]{1,0:T(8,128)(2,1)S(1)}, s16[144,128]{1,0:T(8,128)(2,1)S(1)}, u32[]{:S(2)}, u32[]{:S(2)}) %collective-permute-start.9) | collective-permute-done | bytes 36896 | tf_op jit(solution)/shard_map/ppermute | solution.py:124
  22.2 0.5 %collective-permute-done.10.rest_1_ = s16[144,128]{1,0:T(8,128)(2,1)S(1)} collective-permute-done((s16[144,128]{1,0:T(8,128)(2,1)S(1)}, s16[144,128]{1,0:T(8,128)(2,1)S(1)}, u32[]{:S(2)}, u32[]{:S(2)}) %collective-permute-start.10) | collective-permute-done | bytes 36896 | tf_op jit(solution)/shard_map/ppermute | solution.py:124
  22.7 0.0 collective-permute-done.11.rest_2_
  22.7 0.7 %finish.3 = f32[128,256]{1,0:T(8,128)} custom-call(f32[128,256]{1,0:T(8,128)S(1)} %finish.2.base, f32[64,256]{1,0:T(8,128)S(1)} %get-tuple-element.27.kept_sums, s16[144,128]{1,0:T(8,128)(2,1)S(1)} %collective-permute-done.9.rest_0_, s16[144,128]{1,0:T(8,128)(2,1)S(1)} %collective-permute-done.10.rest_1_, s16[144,128]{1,0:T(8,128)(2,1)S(1)} %collective-permute-done.11.rest_2_), custom_call_target="tpu_custom_call" | custom-call | tf_op jit(solution)/shard_map/finish/pallas_call | solution.py:177
  (1 shorter events, 0.0 us)
Async XLA Ops:
  1.0 9.5 %copy-start.3 = (s32[8,2]{0,1:T(2,128)S(1)}, s32[8,2]{0,1:T(2,128)}, u32[]{:S(2)}) copy-start(s32[8,2]{0,1:T(2,128)} %param.8) | copy-start | bytes 196
  1.0 12.3 %collective-permute-start = (bf16[64,512]{1,0:T(8,128)(2,1)S(1)}, bf16[64,512]{1,0:T(8,128)(2,1)S(1)}, u32[]{:S(2)}, u32[]{:S(2)}) collective-permute-start(bf16[64,512]{1,0:T(8,128)(2,1)S(1)} %get-tuple-element.21), channel_id=1, source_target_pairs={{0,12},{4,8},{8,4},{12,0},{1,13},{5,9},{9,5},{13,1},{2,14},{6,10},... | collective-permute-start | bytes 196616 | tf_op jit(solution)/shard_map/ppermute | solution.py:124
  6.1 8.9 %collective-permute-start.1 = (bf16[64,512]{1,0:T(8,128)(2,1)S(1)}, bf16[64,512]{1,0:T(8,128)(2,1)S(1)}, u32[]{:S(2)}, u32[]{:S(2)}) collective-permute-start(bf16[64,512]{1,0:T(8,128)(2,1)S(1)} %get-tuple-element.21), channel_id=1, source_target_pairs={{0,8},{4,12},{8,0},{12,4},{1,9},{5,13},{9,1},{13,5},{2,10},{6,14},... | collective-permute-start | bytes 196616 | tf_op jit(solution)/shard_map/ppermute | solution.py:124
  6.1 8.9 %collective-permute-start.2 = (bf16[64,512]{1,0:T(8,128)(2,1)S(1)}, bf16[64,512]{1,0:T(8,128)(2,1)S(1)}, u32[]{:S(2)}, u32[]{:S(2)}) collective-permute-start(bf16[64,512]{1,0:T(8,128)(2,1)S(1)} %get-tuple-element.21), channel_id=1, source_target_pairs={{0,4},{4,0},{8,12},{12,8},{1,5},{5,1},{9,13},{13,9},{2,6},{6,2},{1... | collective-permute-start | bytes 196616 | tf_op jit(solution)/shard_map/ppermute | solution.py:124
  6.8 10.0 %collective-permute-start.6 = (bf16[64,512]{1,0:T(8,128)(2,1)S(1)}, bf16[64,512]{1,0:T(8,128)(2,1)S(1)}, u32[]{:S(2)}, u32[]{:S(2)}) collective-permute-start(bf16[64,512]{1,0:T(8,128)(2,1)S(1)} %get-tuple-element.26), channel_id=1, source_target_pairs={{0,12},{4,8},{8,4},{12,0},{1,13},{5,9},{9,5},{13,1},{2,14},{6,10},... | collective-permute-start | bytes 196616 | tf_op jit(solution)/shard_map/ppermute | solution.py:124
  10.5 6.9 %collective-permute-start.7 = (bf16[64,512]{1,0:T(8,128)(2,1)S(1)}, bf16[64,512]{1,0:T(8,128)(2,1)S(1)}, u32[]{:S(2)}, u32[]{:S(2)}) collective-permute-start(bf16[64,512]{1,0:T(8,128)(2,1)S(1)} %get-tuple-element.26), channel_id=1, source_target_pairs={{0,8},{4,12},{8,0},{12,4},{1,9},{5,13},{9,1},{13,5},{2,10},{6,14},... | collective-permute-start | bytes 196616 | tf_op jit(solution)/shard_map/ppermute | solution.py:124
  10.5 0.7 %copy-start.2 = (s32[4,8]{1,0:T(4,128)S(1)}, s32[4,8]{1,0:T(4,128)}, u32[]{:S(2)}) copy-start(s32[4,8]{1,0:T(4,128)} %kept.3) | copy-start | bytes 388
  11.2 1.0 %copy-start = (bf16[1024,256]{1,0:T(8,128)(2,1)S(1)}, bf16[1024,256]{1,0:T(8,128)(2,1)}, u32[]{:S(2)}) copy-start(bf16[1024,256]{1,0:T(8,128)(2,1)} %integrals.1) | copy-start | bytes 1572868
  13.4 4.7 %collective-permute-start.8 = (bf16[64,512]{1,0:T(8,128)(2,1)S(1)}, bf16[64,512]{1,0:T(8,128)(2,1)S(1)}, u32[]{:S(2)}, u32[]{:S(2)}) collective-permute-start(bf16[64,512]{1,0:T(8,128)(2,1)S(1)} %get-tuple-element.26), channel_id=1, source_target_pairs={{0,4},{4,0},{8,12},{12,8},{1,5},{5,1},{9,13},{13,9},{2,6},{6,2},{1... | collective-permute-start | bytes 196616 | tf_op jit(solution)/shard_map/ppermute | solution.py:124
  15.3 4.7 %collective-permute-start.3 = (s16[144,128]{1,0:T(8,128)(2,1)S(1)}, s16[144,128]{1,0:T(8,128)(2,1)S(1)}, u32[]{:S(2)}, u32[]{:S(2)}) collective-permute-start(s16[144,128]{1,0:T(8,128)(2,1)S(1)} %get-tuple-element.23), channel_id=1, source_target_pairs={{0,3},{1,2},{2,1},{3,0},{4,7},{5,6},{6,5},{7,4},{8,11},{9,10},{10,... | collective-permute-start | bytes 110600 | tf_op jit(solution)/shard_map/ppermute | solution.py:124
  15.4 4.9 %collective-permute-start.4 = (s16[144,128]{1,0:T(8,128)(2,1)S(1)}, s16[144,128]{1,0:T(8,128)(2,1)S(1)}, u32[]{:S(2)}, u32[]{:S(2)}) collective-permute-start(s16[144,128]{1,0:T(8,128)(2,1)S(1)} %get-tuple-element.24), channel_id=1, source_target_pairs={{0,2},{1,3},{2,0},{3,1},{4,6},{5,7},{6,4},{7,5},{8,10},{9,11},{10,... | collective-permute-start | bytes 110600 | tf_op jit(solution)/shard_map/ppermute | solution.py:124
  16.8 3.5 %copy-start.1 = (f32[128,256]{1,0:T(8,128)S(1)}, f32[128,256]{1,0:T(8,128)}, u32[]{:S(2)}) copy-start(f32[128,256]{1,0:T(8,128)} %residual.1) | copy-start | bytes 393220
  16.8 3.5 %collective-permute-start.5 = (s16[144,128]{1,0:T(8,128)(2,1)S(1)}, s16[144,128]{1,0:T(8,128)(2,1)S(1)}, u32[]{:S(2)}, u32[]{:S(2)}) collective-permute-start(s16[144,128]{1,0:T(8,128)(2,1)S(1)} %get-tuple-element.25), channel_id=1, source_target_pairs={{0,1},{1,0},{2,3},{3,2},{4,5},{5,4},{6,7},{7,6},{8,9},{9,8},{10,11... | collective-permute-start | bytes 110600 | tf_op jit(solution)/shard_map/ppermute | solution.py:124
  18.4 3.8 %collective-permute-start.9 = (s16[144,128]{1,0:T(8,128)(2,1)S(1)}, s16[144,128]{1,0:T(8,128)(2,1)S(1)}, u32[]{:S(2)}, u32[]{:S(2)}) collective-permute-start(s16[144,128]{1,0:T(8,128)(2,1)S(1)} %get-tuple-element.28), channel_id=1, source_target_pairs={{0,3},{1,2},{2,1},{3,0},{4,7},{5,6},{6,5},{7,4},{8,11},{9,10},{10,... | collective-permute-start | bytes 110600 | tf_op jit(solution)/shard_map/ppermute | solution.py:124
  18.7 4.0 %collective-permute-start.10 = (s16[144,128]{1,0:T(8,128)(2,1)S(1)}, s16[144,128]{1,0:T(8,128)(2,1)S(1)}, u32[]{:S(2)}, u32[]{:S(2)}) collective-permute-start(s16[144,128]{1,0:T(8,128)(2,1)S(1)} %get-tuple-element.29), channel_id=1, source_target_pairs={{0,2},{1,3},{2,0},{3,1},{4,6},{5,7},{6,4},{7,5},{8,10},{9,11},{10,... | collective-permute-start | bytes 110600 | tf_op jit(solution)/shard_map/ppermute | solution.py:124
  20.0 2.6 %collective-permute-start.11 = (s16[144,128]{1,0:T(8,128)(2,1)S(1)}, s16[144,128]{1,0:T(8,128)(2,1)S(1)}, u32[]{:S(2)}, u32[]{:S(2)}) collective-permute-start(s16[144,128]{1,0:T(8,128)(2,1)S(1)} %get-tuple-element.30), channel_id=1, source_target_pairs={{0,1},{1,0},{2,3},{3,2},{4,5},{5,4},{6,7},{7,6},{8,9},{9,8},{10,11... | collective-permute-start | bytes 110600 | tf_op jit(solution)/shard_map/ppermute | solution.py:124

commit v8 on v7

--- a/solution.py
+++ b/solution.py
@@ -48,17 +48,25 @@
         second[:, to] = tile[half:]
 
 
-def prepare_kernel(tiles, slots, me, kept, int_kept, integrals, own, gathered, product, places):
+def prepare_kernel(tiles, slots, me, kept, int_kept, integrals, own, gathered, product, table, int_table, held, places, sems):
+    copies = [
+        pltpu.make_async_copy(*pair, sems.at[i])
+        for i, pair in enumerate(((kept, table), (int_kept, int_table), (integrals, held)))
+    ]
+    for copy in copies:
+        copy.start()
+    for copy in copies:
+        copy.wait()
     row, col = me[0] // ROWS, me[0] % ROWS
     tiles_ab = integrals.shape[1] // TILE
     for n in range(ROWS):
-        list_kept(kept, col ^ n, tiles, places)
+        list_kept(table, col ^ n, tiles, places)
         for slot in range(slots):
             tile = places[slot]
             start = pl.multiple_of(tile * TILE, TILE)
             for ab in range(tiles_ab):
-                part = integrals[pl.ds(start, TILE), ab * TILE : (ab + 1) * TILE]
-                on = (int_kept[tile, ab] != 0).astype(jnp.float32).astype(part.dtype)
+                part = held[pl.ds(start, TILE), ab * TILE : (ab + 1) * TILE]
+                on = (int_table[tile, ab] != 0).astype(jnp.float32).astype(part.dtype)
                 gathered[n, slot * TILE : (slot + 1) * TILE, ab * TILE : (ab + 1) * TILE] = part * on
     product[...] = jnp.dot(own[...], gathered[row ^ col], preferred_element_type=jnp.float32)
 
@@ -88,12 +96,25 @@
     return jnp.concatenate(parts, axis=1)
 
 
-def ladder_kernel(start, me, product, gathered, *rest):
-    blocks, kept_sums, outs, sums = rest[: ROWS - 1], rest[ROWS - 1], rest[ROWS:-1], rest[-1]
+def far_kernel(me, gathered, near, far, near_sums, far_sums):
     mine = me[0] // ROWS ^ me[0] % ROWS
-    sums[mine] = product[start : start + sums.shape[1], :]
-    for step, block in zip(range(ROWS - 1, 0, -1), blocks):
-        sums[mine ^ step] = jnp.dot(block[...], gathered[mine ^ step], preferred_element_type=jnp.float32)
+    near_sums[...] = jnp.dot(near[...], gathered[mine ^ 2], preferred_element_type=jnp.float32)
+    far_sums[...] = jnp.dot(far[...], gathered[mine ^ 3], preferred_element_type=jnp.float32)
+
+
+def ladder_kernel(me, product, gathered, pair, near, far, kept_sums, *rest):
+    outs, sums = rest[:-1], rest[-1]
+    mine = me[0] // ROWS ^ me[0] % ROWS
+    half = near.shape[0]
+    multiplied = near.dtype == jnp.float32
+    part = slice(0, half) if multiplied else slice(half, 2 * half)
+    sums[mine] = product[part, :]
+    sums[mine ^ 1] = jnp.dot(pair[part, :], gathered[mine ^ 1], preferred_element_type=jnp.float32)
+    for step, x in ((2, near), (3, far)):
+        if multiplied:
+            sums[mine ^ step] = x[...]
+        else:
+            sums[mine ^ step] = jnp.dot(x[...], gathered[mine ^ step], preferred_element_type=jnp.float32)
     kept_sums[...] = sums[0]
     for n, out in enumerate(outs, 1):
         encode(sums[n], out)
@@ -135,6 +156,9 @@
     half_sums = jax.ShapeDtypeStruct((pairs // 2, width), jnp.float32)
     half_block = jax.ShapeDtypeStruct((pairs // 2, slots * TILE), doubles.dtype)
     message = jax.ShapeDtypeStruct((pairs // 2 * width // TILE + HEAD, TILE), jnp.int16)
+    doubles, doubles_kept, integrals, integral_kept = (
+        pltpu.with_memory_space_constraint(x, pltpu.HBM) for x in (doubles, doubles_kept, integrals, integral_kept)
+    )
     packed, first, second = pl.pallas_call(
         functools.partial(pack_kernel, tiles, slots),
         out_shape=[jax.ShapeDtypeStruct((pairs, slots * TILE), doubles.dtype), half_block, half_block],
@@ -148,21 +172,38 @@
         ],
         compiler_params=PARAMS,
         name="pack",
-    )(me, pltpu.with_memory_space_constraint(doubles_kept, pltpu.HBM), pltpu.with_memory_space_constraint(doubles, pltpu.HBM))
-    first, second = ([swap(x, "rows", step) for step in range(ROWS - 1, 0, -1)] for x in (first, second))
+    )(me, doubles_kept, doubles)
+    pair = swap(packed, "rows", 1)
+    first, second = ([swap(x, "rows", step) for step in (2, 3)] for x in (first, second))
     gathered, product = pl.pallas_call(
         functools.partial(prepare_kernel, tiles, slots),
         out_shape=[jax.ShapeDtypeStruct((ROWS, slots * TILE, width), integrals.dtype), sums_shape],
-        in_specs=[SMEM, SMEM, SMEM, VMEM, VMEM],
+        in_specs=[SMEM, HBM, HBM, HBM, VMEM],
         out_specs=[VMEM] * 2,
-        scratch_shapes=[places],
+        scratch_shapes=[
+            pltpu.SMEM(doubles_kept.shape, jnp.int32),
+            pltpu.SMEM(integral_kept.shape, jnp.int32),
+            pltpu.VMEM(integrals.shape, integrals.dtype),
+            places,
+            pltpu.SemaphoreType.DMA((3,)),
+        ],
         compiler_params=PARAMS,
         cost_estimate=cost(0),
         name="prepare",
     )(me, doubles_kept, integral_kept, integrals, packed)
-    def ladder(start, blocks):
+    first = pl.pallas_call(
+        far_kernel,
+        out_shape=[half_sums] * 2,
+        in_specs=[SMEM] + [VMEM] * 3,
+        out_specs=[VMEM] * 2,
+        compiler_params=PARAMS,
+        cost_estimate=cost(10**9),
+        name="far",
+    )(me, gathered, *first)
+
+    def ladder(near, far):
         kept_sums, *messages = pl.pallas_call(
-            functools.partial(ladder_kernel, start),
+            ladder_kernel,
             out_shape=[half_sums] + [message] * (ROWS - 1),
             in_specs=[SMEM] + [VMEM] * 5,
             out_specs=[VMEM] * ROWS,
@@ -170,7 +211,7 @@
             compiler_params=PARAMS,
             cost_estimate=cost(10**11),
             name="ladder",
-        )(me, product, gathered, *blocks)
+        )(me, product, gathered, pair, near, far)
         return [kept_sums] + [swap(x, "cols", step) for step, x in reversed(list(enumerate(messages, 1)))]
 
     def finish(kernel, start, sums):
@@ -183,8 +224,8 @@
             name="finish",
         )(start, *sums)
 
-    sums = finish(first_kernel, residual, ladder(0, first))
-    return finish(second_kernel, sums, ladder(pairs // 2, second))
+    sums = finish(first_kernel, residual, ladder(*first))
+    return finish(second_kernel, sums, ladder(*second))
 
 
 def local_many(doubles, doubles_kept, integrals, integral_kept, residual):

time: 23.6 us -> 23.4 us (level)
  local copies, waits for them, and re-layouts: 1.73 us -> 0.68 us
  Pallas kernels: 3.48 us -> 4.02 us
  waiting for transfers between devices: 4.02 us -> 4.54 us
    unnamed x9 -> x5, local copies, waits for them, and re-layouts: 1.73 us -> 0.68 us
    ppermute x12 -> x11, waiting for transfers between devices: 4.02 us -> 4.54 us  [swap(): return lax.ppermute(x, axis, [(i, i ^ step) for i in range(ROWS)])]
    pallas_call x1, Pallas kernels: 1.08 us -> 1.5 us  [local_few(): pl.pallas_call(functools.partial(prepare_kernel, tiles, slots), out_shape...]
    ppermute x12 -> x11, starting transfers between devices: 14.1 us -> 13.9 us  [swap(): return lax.ppermute(x, axis, [(i, i ^ step) for i in range(ROWS)])]
    pallas_call x2 -> x3, Pallas kernels: 0.65 us -> 0.77 us  [the longest x2 0.56 us: ladder(): pl.pallas_call(ladder_kernel, out_shape=[half_sums] + [message] * (ROWS -...]
  transfers between devices with their start and end apart: 12 -> 11, of which waited for: 5 -> 3; matrix products, arithmetic and copies ran while one was open for 0% -> 3% of each run, Pallas kernels for 8% -> 10%
where the time goes in v8:
time: 23.4 us; the launch traced here: 23.2 us
  starting transfers between devices  13.9 us (59%)
  waiting for transfers between devices  4.54 us (19%)
  Pallas kernels  4.02 us (17%)
  local copies, waits for them, and re-layouts  0.68 us (3%)
    ppermute x11, starting transfers between devices, swap(): return lax.ppermute(x, axis, [(i, i ^ step) for i in range(ROWS)])  13.9 us
    ppermute x11, waiting for transfers between devices, swap(): return lax.ppermute(x, axis, [(i, i ^ step) for i in range(ROWS)])  4.54 us
    pallas_call x1, Pallas kernels, local_few(): pl.pallas_call(functools.partial(prepare_kernel, tiles, slots), out_shape...  1.5 us
    pallas_call x1, Pallas kernels, local_few(): pl.pallas_call(functools.partial(pack_kernel, tiles, slots), out_shape=[j...  1 us
    pallas_call x2, Pallas kernels, finish(): pl.pallas_call(kernel, out_shape=sums_shape, in_specs=[VMEM] * (ROWS + 1)...  0.75 us
    unnamed x5, local copies, waits for them, and re-layouts  0.68 us
    pallas_call x2, Pallas kernels, ladder(): pl.pallas_call(ladder_kernel, out_shape=[half_sums] + [message] * (ROWS -...  0.56 us
  transfers between devices with their start and end apart: 11, of which 3 were waited for; matrix products, arithmetic and copies ran while one was open for 3% of the time, Pallas kernels for 10%

profile of v8, /device:TPU:0, one launch (start us, length us, event | category | flops | bytes accessed | tf_op | source)
XLA Modules:
  0.0 23.2 jit_solution(5417240655250234094)
XLA Ops:
  0.0 1.0 %pack.1 = (bf16[128,512]{1,0:T(8,128)(2,1)S(1)}, bf16[64,512]{1,0:T(8,128)(2,1)S(1)}, bf16[64,512]{1,0:T(8,128)(2,1)S(1)}) custom-call(s32[1]{0:T(128)} %bitcast.me, s32[4,8]{1,0:T(4,128)} %kept.3, bf16[128,1024]{1,0:T(8,128)(2,1)} %doubles.1), custom_call_target="tpu_custom_call" | custom-call | tf_op jit(solution)/shard_map/pack/pallas_call | solution.py:162
  1.0 4.1 %collective-permute-start.1 = (bf16[64,512]{1,0:T(8,128)(2,1)S(1)}, bf16[64,512]{1,0:T(8,128)(2,1)S(1)}, u32[]{:S(2)}, u32[]{:S(2)}) collective-permute-start(bf16[64,512]{1,0:T(8,128)(2,1)S(1)} %get-tuple-element.23), channel_id=1, source_target_pairs={{0,8},{4,12},{8,0},{12,4},{1,9},{5,13},{9,1},{13,5},{2,10},{6,14},... | collective-permute-start | bytes 196616 | tf_op jit(solution)/shard_map/ppermute | solution.py:145
  5.1 1.3 %collective-permute-start.2 = (bf16[64,512]{1,0:T(8,128)(2,1)S(1)}, bf16[64,512]{1,0:T(8,128)(2,1)S(1)}, u32[]{:S(2)}, u32[]{:S(2)}) collective-permute-start(bf16[64,512]{1,0:T(8,128)(2,1)S(1)} %get-tuple-element.23), channel_id=1, source_target_pairs={{0,12},{4,8},{8,4},{12,0},{1,13},{5,9},{9,5},{13,1},{2,14},{6,10},... | collective-permute-start | bytes 196616 | tf_op jit(solution)/shard_map/ppermute | solution.py:145
  6.5 0.0 copy-start.1
  6.5 0.2 collective-permute-start
  6.7 2.8 %collective-permute-start.6 = (bf16[64,512]{1,0:T(8,128)(2,1)S(1)}, bf16[64,512]{1,0:T(8,128)(2,1)S(1)}, u32[]{:S(2)}, u32[]{:S(2)}) collective-permute-start(bf16[64,512]{1,0:T(8,128)(2,1)S(1)} %get-tuple-element.30), channel_id=1, source_target_pairs={{0,8},{4,12},{8,0},{12,4},{1,9},{5,13},{9,1},{13,5},{2,10},{6,14},... | collective-permute-start | bytes 196616 | tf_op jit(solution)/shard_map/ppermute | solution.py:145
  9.5 1.3 %collective-permute-start.7 = (bf16[64,512]{1,0:T(8,128)(2,1)S(1)}, bf16[64,512]{1,0:T(8,128)(2,1)S(1)}, u32[]{:S(2)}, u32[]{:S(2)}) collective-permute-start(bf16[64,512]{1,0:T(8,128)(2,1)S(1)} %get-tuple-element.30), channel_id=1, source_target_pairs={{0,12},{4,8},{8,4},{12,0},{1,13},{5,9},{9,5},{13,1},{2,14},{6,10},... | collective-permute-start | bytes 196616 | tf_op jit(solution)/shard_map/ppermute | solution.py:145
  10.9 0.0 copy-done.1
  10.9 0.7 %copy.6.int_kept = s32[8,2]{1,0:T(8,128)} copy(s32[8,2]{0,1:T(2,128)S(1)} %copy-done.1) | data formatting | bytes 128 | tf_op args[3]
  11.5 1.5 %prepare.1 = (bf16[4,512,256]{2,1,0:T(8,128)(2,1)S(1)}, f32[128,256]{1,0:T(8,128)S(1)}) custom-call(s32[1]{0:T(128)} %bitcast.me, s32[4,8]{1,0:T(4,128)} %kept.3, s32[8,2]{1,0:T(8,128)} %copy.6.int_kept, bf16[1024,256]{1,0:T(8,128)(2,1)} %integrals.1, bf16[128,512]{1,0:T(8,128)(2,1)S(1)} %get-tuple-element.20.own), custom_call_target="tpu_custom_call" | custom-call | bytes 1024 | tf_op jit(solution)/shard_map/prepare/pallas_call | solution.py:178
  13.0 0.0 collective-permute-done.1.near
  13.0 0.0 collective-permute-done.2.far
  13.1 0.2 far.1
  13.3 1.4 %collective-permute-done.pair = bf16[128,512]{1,0:T(8,128)(2,1)S(1)} collective-permute-done((bf16[128,512]{1,0:T(8,128)(2,1)S(1)}, bf16[128,512]{1,0:T(8,128)(2,1)S(1)}, u32[]{:S(2)}, u32[]{:S(2)}) %collective-permute-start) | collective-permute-done | bytes 131104 | tf_op jit(solution)/shard_map/ppermute | solution.py:145
  14.7 0.2 %ladder.2 = (f32[64,256]{1,0:T(8,128)S(1)}, s16[144,128]{1,0:T(8,128)(2,1)S(1)}, s16[144,128]{1,0:T(8,128)(2,1)S(1)}, s16[144,128]{1,0:T(8,128)(2,1)S(1)}) custom-call(s32[1]{0:T(128)} %bitcast.me, f32[128,256]{1,0:T(8,128)S(1)} %get-tuple-element.21.product, bf16[4,512,256]{2,1,0:T(8,128)(2,1)S(1)} %get-tuple-element.22.gathered, ...), custom_call_target="tpu_custom_call" | custom-call | flops 99999997952 | bytes 1024 | tf_op jit(solution)/shard_map/ladder/pallas_call | solution.py:205
  14.9 0.1 collective-permute-start.3
  15.0 1.8 %collective-permute-start.4 = (s16[144,128]{1,0:T(8,128)(2,1)S(1)}, s16[144,128]{1,0:T(8,128)(2,1)S(1)}, u32[]{:S(2)}, u32[]{:S(2)}) collective-permute-start(s16[144,128]{1,0:T(8,128)(2,1)S(1)} %get-tuple-element.28), channel_id=1, source_target_pairs={{0,2},{1,3},{2,0},{3,1},{4,6},{5,7},{6,4},{7,5},{8,10},{9,11},{10,... | collective-permute-start | bytes 110600 | tf_op jit(solution)/shard_map/ppermute | solution.py:145
  16.8 0.0 copy-start
  16.8 0.1 collective-permute-start.5
  16.9 0.0 collective-permute-done.6.near
  16.9 0.0 collective-permute-done.7.far
  16.9 0.3 %ladder.3 = (f32[64,256]{1,0:T(8,128)S(1)}, s16[144,128]{1,0:T(8,128)(2,1)S(1)}, s16[144,128]{1,0:T(8,128)(2,1)S(1)}, s16[144,128]{1,0:T(8,128)(2,1)S(1)}) custom-call(s32[1]{0:T(128)} %bitcast.me, f32[128,256]{1,0:T(8,128)S(1)} %get-tuple-element.21.product, bf16[4,512,256]{2,1,0:T(8,128)(2,1)S(1)} %get-tuple-element.22.gathered, ...), custom_call_target="tpu_custom_call" | custom-call | flops 99999997952 | bytes 1024 | tf_op jit(solution)/shard_map/ladder/pallas_call | solution.py:205
  17.2 1.4 %collective-permute-start.8 = (s16[144,128]{1,0:T(8,128)(2,1)S(1)}, s16[144,128]{1,0:T(8,128)(2,1)S(1)}, u32[]{:S(2)}, u32[]{:S(2)}) collective-permute-start(s16[144,128]{1,0:T(8,128)(2,1)S(1)} %get-tuple-element.32), channel_id=1, source_target_pairs={{0,3},{1,2},{2,1},{3,0},{4,7},{5,6},{6,5},{7,4},{8,11},{9,10},{10,... | collective-permute-start | bytes 110600 | tf_op jit(solution)/shard_map/ppermute | solution.py:145
  18.6 0.8 %collective-permute-start.9 = (s16[144,128]{1,0:T(8,128)(2,1)S(1)}, s16[144,128]{1,0:T(8,128)(2,1)S(1)}, u32[]{:S(2)}, u32[]{:S(2)}) collective-permute-start(s16[144,128]{1,0:T(8,128)(2,1)S(1)} %get-tuple-element.33), channel_id=1, source_target_pairs={{0,2},{1,3},{2,0},{3,1},{4,6},{5,7},{6,4},{7,5},{8,10},{9,11},{10,... | collective-permute-start | bytes 110600 | tf_op jit(solution)/shard_map/ppermute | solution.py:145
  19.3 0.0 collective-permute-done.3.rest_0_
  19.3 0.0 collective-permute-start.10
  19.3 0.0 collective-permute-done.4.rest_1_
  19.3 0.0 collective-permute-done.5.rest_2_
  19.4 0.0 copy-done
  19.4 1.2 %collective-permute-done.8.rest_0_ = s16[144,128]{1,0:T(8,128)(2,1)S(1)} collective-permute-done((s16[144,128]{1,0:T(8,128)(2,1)S(1)}, s16[144,128]{1,0:T(8,128)(2,1)S(1)}, u32[]{:S(2)}, u32[]{:S(2)}) %collective-permute-start.8) | collective-permute-done | bytes 36896 | tf_op jit(solution)/shard_map/ppermute | solution.py:145
  20.6 1.9 %collective-permute-done.9.rest_1_ = s16[144,128]{1,0:T(8,128)(2,1)S(1)} collective-permute-done((s16[144,128]{1,0:T(8,128)(2,1)S(1)}, s16[144,128]{1,0:T(8,128)(2,1)S(1)}, u32[]{:S(2)}, u32[]{:S(2)}) %collective-permute-start.9) | collective-permute-done | bytes 36896 | tf_op jit(solution)/shard_map/ppermute | solution.py:145
  22.5 0.0 collective-permute-done.10.rest_2_
  22.5 0.7 %finish.3 = f32[128,256]{1,0:T(8,128)} custom-call(f32[128,256]{1,0:T(8,128)S(1)} %finish.2.base, f32[64,256]{1,0:T(8,128)S(1)} %get-tuple-element.31.kept_sums, s16[144,128]{1,0:T(8,128)(2,1)S(1)} %collective-permute-done.8.rest_0_, s16[144,128]{1,0:T(8,128)(2,1)S(1)} %collective-permute-done.9.rest_1_, s16[144,128]{1,0:T(8,128)(2,1)S(1)} %collective-permute-done.10.rest_2_), custom_call_target="tpu_custom_call" | custom-call | tf_op jit(solution)/shard_map/finish/pallas_call | solution.py:218
  (1 shorter events, 0.0 us)
Async XLA Ops:
  1.0 12.0 %collective-permute-start.1 = (bf16[64,512]{1,0:T(8,128)(2,1)S(1)}, bf16[64,512]{1,0:T(8,128)(2,1)S(1)}, u32[]{:S(2)}, u32[]{:S(2)}) collective-permute-start(bf16[64,512]{1,0:T(8,128)(2,1)S(1)} %get-tuple-element.23), channel_id=1, source_target_pairs={{0,8},{4,12},{8,0},{12,4},{1,9},{5,13},{9,1},{13,5},{2,10},{6,14},... | collective-permute-start | bytes 196616 | tf_op jit(solution)/shard_map/ppermute | solution.py:145
  5.1 7.9 %collective-permute-start.2 = (bf16[64,512]{1,0:T(8,128)(2,1)S(1)}, bf16[64,512]{1,0:T(8,128)(2,1)S(1)}, u32[]{:S(2)}, u32[]{:S(2)}) collective-permute-start(bf16[64,512]{1,0:T(8,128)(2,1)S(1)} %get-tuple-element.23), channel_id=1, source_target_pairs={{0,12},{4,8},{8,4},{12,0},{1,13},{5,9},{9,5},{13,1},{2,14},{6,10},... | collective-permute-start | bytes 196616 | tf_op jit(solution)/shard_map/ppermute | solution.py:145
  6.5 4.4 %copy-start.1 = (s32[8,2]{0,1:T(2,128)S(1)}, s32[8,2]{0,1:T(2,128)}, u32[]{:S(2)}) copy-start(s32[8,2]{0,1:T(2,128)} %param.8) | copy-start | bytes 196
  6.5 8.2 %collective-permute-start = (bf16[128,512]{1,0:T(8,128)(2,1)S(1)}, bf16[128,512]{1,0:T(8,128)(2,1)S(1)}, u32[]{:S(2)}, u32[]{:S(2)}) collective-permute-start(bf16[128,512]{1,0:T(8,128)(2,1)S(1)} %get-tuple-element.20.own), channel_id=1, source_target_pairs={{0,4},{4,0},{8,12},{12,8},{1,5},{5,1},{9,13},{13,9},{2,6},{6,2},{1... | collective-permute-start | bytes 393224 | tf_op jit(solution)/shard_map/ppermute | solution.py:145
  6.7 10.2 %collective-permute-start.6 = (bf16[64,512]{1,0:T(8,128)(2,1)S(1)}, bf16[64,512]{1,0:T(8,128)(2,1)S(1)}, u32[]{:S(2)}, u32[]{:S(2)}) collective-permute-start(bf16[64,512]{1,0:T(8,128)(2,1)S(1)} %get-tuple-element.30), channel_id=1, source_target_pairs={{0,8},{4,12},{8,0},{12,4},{1,9},{5,13},{9,1},{13,5},{2,10},{6,14},... | collective-permute-start | bytes 196616 | tf_op jit(solution)/shard_map/ppermute | solution.py:145
  9.5 7.4 %collective-permute-start.7 = (bf16[64,512]{1,0:T(8,128)(2,1)S(1)}, bf16[64,512]{1,0:T(8,128)(2,1)S(1)}, u32[]{:S(2)}, u32[]{:S(2)}) collective-permute-start(bf16[64,512]{1,0:T(8,128)(2,1)S(1)} %get-tuple-element.30), channel_id=1, source_target_pairs={{0,12},{4,8},{8,4},{12,0},{1,13},{5,9},{9,5},{13,1},{2,14},{6,10},... | collective-permute-start | bytes 196616 | tf_op jit(solution)/shard_map/ppermute | solution.py:145
  14.9 4.4 %collective-permute-start.3 = (s16[144,128]{1,0:T(8,128)(2,1)S(1)}, s16[144,128]{1,0:T(8,128)(2,1)S(1)}, u32[]{:S(2)}, u32[]{:S(2)}) collective-permute-start(s16[144,128]{1,0:T(8,128)(2,1)S(1)} %get-tuple-element.27), channel_id=1, source_target_pairs={{0,3},{1,2},{2,1},{3,0},{4,7},{5,6},{6,5},{7,4},{8,11},{9,10},{10,... | collective-permute-start | bytes 110600 | tf_op jit(solution)/shard_map/ppermute | solution.py:145
  15.0 4.3 %collective-permute-start.4 = (s16[144,128]{1,0:T(8,128)(2,1)S(1)}, s16[144,128]{1,0:T(8,128)(2,1)S(1)}, u32[]{:S(2)}, u32[]{:S(2)}) collective-permute-start(s16[144,128]{1,0:T(8,128)(2,1)S(1)} %get-tuple-element.28), channel_id=1, source_target_pairs={{0,2},{1,3},{2,0},{3,1},{4,6},{5,7},{6,4},{7,5},{8,10},{9,11},{10,... | collective-permute-start | bytes 110600 | tf_op jit(solution)/shard_map/ppermute | solution.py:145
  16.8 2.6 %copy-start = (f32[128,256]{1,0:T(8,128)S(1)}, f32[128,256]{1,0:T(8,128)}, u32[]{:S(2)}) copy-start(f32[128,256]{1,0:T(8,128)} %residual.1) | copy-start | bytes 393220
  16.8 2.6 %collective-permute-start.5 = (s16[144,128]{1,0:T(8,128)(2,1)S(1)}, s16[144,128]{1,0:T(8,128)(2,1)S(1)}, u32[]{:S(2)}, u32[]{:S(2)}) collective-permute-start(s16[144,128]{1,0:T(8,128)(2,1)S(1)} %get-tuple-element.29), channel_id=1, source_target_pairs={{0,1},{1,0},{2,3},{3,2},{4,5},{5,4},{6,7},{7,6},{8,9},{9,8},{10,11... | collective-permute-start | bytes 110600 | tf_op jit(solution)/shard_map/ppermute | solution.py:145
  17.2 3.4 %collective-permute-start.8 = (s16[144,128]{1,0:T(8,128)(2,1)S(1)}, s16[144,128]{1,0:T(8,128)(2,1)S(1)}, u32[]{:S(2)}, u32[]{:S(2)}) collective-permute-start(s16[144,128]{1,0:T(8,128)(2,1)S(1)} %get-tuple-element.32), channel_id=1, source_target_pairs={{0,3},{1,2},{2,1},{3,0},{4,7},{5,6},{6,5},{7,4},{8,11},{9,10},{10,... | collective-permute-start | bytes 110600 | tf_op jit(solution)/shard_map/ppermute | solution.py:145
  18.6 4.0 %collective-permute-start.9 = (s16[144,128]{1,0:T(8,128)(2,1)S(1)}, s16[144,128]{1,0:T(8,128)(2,1)S(1)}, u32[]{:S(2)}, u32[]{:S(2)}) collective-permute-start(s16[144,128]{1,0:T(8,128)(2,1)S(1)} %get-tuple-element.33), channel_id=1, source_target_pairs={{0,2},{1,3},{2,0},{3,1},{4,6},{5,7},{6,4},{7,5},{8,10},{9,11},{10,... | collective-permute-start | bytes 110600 | tf_op jit(solution)/shard_map/ppermute | solution.py:145
  19.3 3.2 %collective-permute-start.10 = (s16[144,128]{1,0:T(8,128)(2,1)S(1)}, s16[144,128]{1,0:T(8,128)(2,1)S(1)}, u32[]{:S(2)}, u32[]{:S(2)}) collective-permute-start(s16[144,128]{1,0:T(8,128)(2,1)S(1)} %get-tuple-element.34), channel_id=1, source_target_pairs={{0,1},{1,0},{2,3},{3,2},{4,5},{5,4},{6,7},{7,6},{8,9},{9,8},{10,11... | collective-permute-start | bytes 110600 | tf_op jit(solution)/shard_map/ppermute | solution.py:145

commit v9 on v8

--- a/solution.py
+++ b/solution.py
@@ -96,49 +96,27 @@
     return jnp.concatenate(parts, axis=1)
 
 
-def far_kernel(me, gathered, near, far, near_sums, far_sums):
-    mine = me[0] // ROWS ^ me[0] % ROWS
-    near_sums[...] = jnp.dot(near[...], gathered[mine ^ 2], preferred_element_type=jnp.float32)
-    far_sums[...] = jnp.dot(far[...], gathered[mine ^ 3], preferred_element_type=jnp.float32)
-
-
-def ladder_kernel(me, product, gathered, pair, near, far, kept_sums, *rest):
+def ladder_kernel(me, product, gathered, pair, near_first, near_second, far_first, far_second, kept_sums, *rest):
     outs, sums = rest[:-1], rest[-1]
     mine = me[0] // ROWS ^ me[0] % ROWS
-    half = near.shape[0]
-    multiplied = near.dtype == jnp.float32
-    part = slice(0, half) if multiplied else slice(half, 2 * half)
-    sums[mine] = product[part, :]
-    sums[mine ^ 1] = jnp.dot(pair[part, :], gathered[mine ^ 1], preferred_element_type=jnp.float32)
-    for step, x in ((2, near), (3, far)):
-        if multiplied:
-            sums[mine ^ step] = x[...]
-        else:
-            sums[mine ^ step] = jnp.dot(x[...], gathered[mine ^ step], preferred_element_type=jnp.float32)
+    half = near_first.shape[0]
+    sums[mine] = product[...]
+    sums[mine ^ 1] = jnp.dot(pair[...], gathered[mine ^ 1], preferred_element_type=jnp.float32)
+    for step, start, block in ((2, 0, near_first), (3, 0, far_first), (2, half, near_second), (3, half, far_second)):
+        sums[mine ^ step, start : start + half, :] = jnp.dot(
+            block[...], gathered[mine ^ step], preferred_element_type=jnp.float32
+        )
     kept_sums[...] = sums[0]
     for n, out in enumerate(outs, 1):
         encode(sums[n], out)
 
 
-def total_of(start, kept_sums, messages):
-    total = start + kept_sums[...]
+def finish_kernel(residual, kept_sums, *rest):
+    messages, out = rest[:-1], rest[-1]
+    total = residual[...] + kept_sums[...]
     for message in messages:
         total = total + decode(message, total.shape[0])
-    return total
-
-
-def first_kernel(residual, kept_sums, *rest):
-    messages, out = rest[:-1], rest[-1]
-    half = kept_sums.shape[0]
-    out[:half, :] = total_of(residual[:half, :], kept_sums, messages)
-    out[half:, :] = residual[half:, :]
-
-
-def second_kernel(base, kept_sums, *rest):
-    messages, out = rest[:-1], rest[-1]
-    half = kept_sums.shape[0]
-    out[:half, :] = base[:half, :]
-    out[half:, :] = total_of(base[half:, :], kept_sums, messages)
+    out[...] = total
 
 
 def swap(x, axis, step):
@@ -153,9 +131,8 @@
     slots = tiles // GROUP * KEEP
     places = pltpu.SMEM((tiles + 1,), jnp.int32)
     sums_shape = jax.ShapeDtypeStruct((pairs, width), jnp.float32)
-    half_sums = jax.ShapeDtypeStruct((pairs // 2, width), jnp.float32)
     half_block = jax.ShapeDtypeStruct((pairs // 2, slots * TILE), doubles.dtype)
-    message = jax.ShapeDtypeStruct((pairs // 2 * width // TILE + HEAD, TILE), jnp.int16)
+    message = jax.ShapeDtypeStruct((pairs * width // TILE + HEAD, TILE), jnp.int16)
     doubles, doubles_kept, integrals, integral_kept = (
         pltpu.with_memory_space_constraint(x, pltpu.HBM) for x in (doubles, doubles_kept, integrals, integral_kept)
     )
@@ -173,8 +150,11 @@
         compiler_params=PARAMS,
         name="pack",
     )(me, doubles_kept, doubles)
+    near_second = swap(second, "rows", 2)
     pair = swap(packed, "rows", 1)
-    first, second = ([swap(x, "rows", step) for step in (2, 3)] for x in (first, second))
+    far_first = swap(first, "rows", 3)
+    near_first = swap(first, "rows", 2)
+    far_second = swap(near_second, "rows", 1)
     gathered, product = pl.pallas_call(
         functools.partial(prepare_kernel, tiles, slots),
         out_shape=[jax.ShapeDtypeStruct((ROWS, slots * TILE, width), integrals.dtype), sums_shape],
@@ -191,41 +171,25 @@
         cost_estimate=cost(0),
         name="prepare",
     )(me, doubles_kept, integral_kept, integrals, packed)
-    first = pl.pallas_call(
-        far_kernel,
-        out_shape=[half_sums] * 2,
-        in_specs=[SMEM] + [VMEM] * 3,
-        out_specs=[VMEM] * 2,
-        compiler_params=PARAMS,
-        cost_estimate=cost(10**9),
-        name="far",
-    )(me, gathered, *first)
-
-    def ladder(near, far):
-        kept_sums, *messages = pl.pallas_call(
-            ladder_kernel,
-            out_shape=[half_sums] + [message] * (ROWS - 1),
-            in_specs=[SMEM] + [VMEM] * 5,
-            out_specs=[VMEM] * ROWS,
-            scratch_shapes=[pltpu.VMEM((ROWS,) + half_sums.shape, jnp.float32)],
-            compiler_params=PARAMS,
-            cost_estimate=cost(10**11),
-            name="ladder",
-        )(me, product, gathered, pair, near, far)
-        return [kept_sums] + [swap(x, "cols", step) for step, x in reversed(list(enumerate(messages, 1)))]
-
-    def finish(kernel, start, sums):
-        return pl.pallas_call(
-            kernel,
-            out_shape=sums_shape,
-            in_specs=[VMEM] * (ROWS + 1),
-            out_specs=VMEM,
-            compiler_params=PARAMS,
-            name="finish",
-        )(start, *sums)
-
-    sums = finish(first_kernel, residual, ladder(*first))
-    return finish(second_kernel, sums, ladder(*second))
+    kept_sums, *messages = pl.pallas_call(
+        ladder_kernel,
+        out_shape=[sums_shape] + [message] * (ROWS - 1),
+        in_specs=[SMEM] + [VMEM] * 7,
+        out_specs=[VMEM] * ROWS,
+        scratch_shapes=[pltpu.VMEM((ROWS, pairs, width), jnp.float32)],
+        compiler_params=PARAMS,
+        cost_estimate=cost(10**11),
+        name="ladder",
+    )(me, product, gathered, pair, near_first, near_second, far_first, far_second)
+    messages = [swap(x, "cols", step) for step, x in reversed(list(enumerate(messages, 1)))]
+    return pl.pallas_call(
+        finish_kernel,
+        out_shape=sums_shape,
+        in_specs=[VMEM] * (ROWS + 1),
+        out_specs=VMEM,
+        compiler_params=PARAMS,
+        name="finish",
+    )(residual, kept_sums, *messages)
 
 
 def local_many(doubles, doubles_kept, integrals, integral_kept, residual):

time: 23.4 us -> 22 us (0.940)
  starting transfers between devices: 13.9 us -> 12 us
  waiting for transfers between devices: 4.54 us -> 5.44 us
  Pallas kernels: 4.02 us -> 3.66 us
    ppermute x11 -> x8, starting transfers between devices: 13.9 us -> 12 us  [swap(): return lax.ppermute(x, axis, [(i, i ^ step) for i in range(ROWS)])]
    ppermute x11 -> x8, waiting for transfers between devices: 4.54 us -> 5.44 us  [swap(): return lax.ppermute(x, axis, [(i, i ^ step) for i in range(ROWS)])]
    pallas_call x5 -> x2, Pallas kernels: 1.52 us -> 1.16 us  [the longest x1 0.72 us: local_few(): pl.pallas_call(finish_kernel, out_shape=sums_shape, in_specs=[VMEM] * (RO...]
  transfers between devices with their start and end apart: 11 -> 8, of which waited for: 3 -> 5; matrix products, arithmetic and copies ran while one was open for 3% -> 3% of each run, Pallas kernels for 10% -> 7%
where the time goes in v9:
time: 22 us; the launch traced here: 21.9 us
  starting transfers between devices  12 us (55%)
  waiting for transfers between devices  5.44 us (25%)
  Pallas kernels  3.66 us (17%)
  local copies, waits for them, and re-layouts  0.68 us (3%)
    ppermute x8, starting transfers between devices, swap(): return lax.ppermute(x, axis, [(i, i ^ step) for i in range(ROWS)])  12 us
    ppermute x8, waiting for transfers between devices, swap(): return lax.ppermute(x, axis, [(i, i ^ step) for i in range(ROWS)])  5.44 us
    pallas_call x1, Pallas kernels, local_few(): pl.pallas_call(functools.partial(prepare_kernel, tiles, slots), out_shape...  1.5 us
    pallas_call x1, Pallas kernels, local_few(): pl.pallas_call(functools.partial(pack_kernel, tiles, slots), out_shape=[j...  1 us
    pallas_call x1, Pallas kernels, local_few(): pl.pallas_call(finish_kernel, out_shape=sums_shape, in_specs=[VMEM] * (RO...  0.72 us
    unnamed x5, local copies, waits for them, and re-layouts  0.68 us
  transfers between devices with their start and end apart: 8, of which 5 were waited for; matrix products, arithmetic and copies ran while one was open for 3% of the time, Pallas kernels for 7%

profile of v9, /device:TPU:0, one launch (start us, length us, event | category | flops | bytes accessed | tf_op | source)
XLA Modules:
  0.0 21.9 jit_solution(9008481374410948297)
XLA Ops:
  0.0 1.0 %pack.1 = (bf16[128,512]{1,0:T(8,128)(2,1)S(1)}, bf16[64,512]{1,0:T(8,128)(2,1)S(1)}, bf16[64,512]{1,0:T(8,128)(2,1)S(1)}) custom-call(s32[1]{0:T(128)} %bitcast.me, s32[4,8]{1,0:T(4,128)} %kept.3, bf16[128,1024]{1,0:T(8,128)(2,1)} %doubles.1), custom_call_target="tpu_custom_call" | custom-call | tf_op jit(solution)/shard_map/pack/pallas_call | solution.py:139
  1.0 4.1 %collective-permute-start.2 = (bf16[64,512]{1,0:T(8,128)(2,1)S(1)}, bf16[64,512]{1,0:T(8,128)(2,1)S(1)}, u32[]{:S(2)}, u32[]{:S(2)}) collective-permute-start(bf16[64,512]{1,0:T(8,128)(2,1)S(1)} %get-tuple-element.18), channel_id=1, source_target_pairs={{0,8},{4,12},{8,0},{12,4},{1,9},{5,13},{9,1},{13,5},{2,10},{6,14},... | collective-permute-start | bytes 196616 | tf_op jit(solution)/shard_map/ppermute | solution.py:123
  5.1 0.0 copy-start.1
  5.1 1.6 %collective-permute-start = (bf16[128,512]{1,0:T(8,128)(2,1)S(1)}, bf16[128,512]{1,0:T(8,128)(2,1)S(1)}, u32[]{:S(2)}, u32[]{:S(2)}) collective-permute-start(bf16[128,512]{1,0:T(8,128)(2,1)S(1)} %get-tuple-element.14.own), channel_id=1, source_target_pairs={{0,4},{4,0},{8,12},{12,8},{1,5},{5,1},{9,13},{13,9},{2,6},{6,2},{1... | collective-permute-start | bytes 393224 | tf_op jit(solution)/shard_map/ppermute | solution.py:123
  6.7 0.0 collective-permute-start.3
  6.7 1.9 %collective-permute-start.1 = (bf16[64,512]{1,0:T(8,128)(2,1)S(1)}, bf16[64,512]{1,0:T(8,128)(2,1)S(1)}, u32[]{:S(2)}, u32[]{:S(2)}) collective-permute-start(bf16[64,512]{1,0:T(8,128)(2,1)S(1)} %get-tuple-element.17), channel_id=1, source_target_pairs={{0,8},{4,12},{8,0},{12,4},{1,9},{5,13},{9,1},{13,5},{2,10},{6,14},... | collective-permute-start | bytes 196616 | tf_op jit(solution)/shard_map/ppermute | solution.py:123
  8.6 0.0 collective-permute-done.2.near_second
  8.6 2.5 %collective-permute-start.4 = (bf16[64,512]{1,0:T(8,128)(2,1)S(1)}, bf16[64,512]{1,0:T(8,128)(2,1)S(1)}, u32[]{:S(2)}, u32[]{:S(2)}) collective-permute-start(bf16[64,512]{1,0:T(8,128)(2,1)S(1)} %collective-permute-done.2.near_second), channel_id=1, source_target_pairs={{0,4},{4,0},{8,12},{12,8},{1,5},{5,1},{9,13},{13,9},{2,6},{6,2},{1... | collective-permute-start | bytes 196616 | tf_op jit(solution)/shard_map/ppermute | solution.py:123
  11.1 0.0 copy-done.1
  11.1 0.7 %copy.6.int_kept = s32[8,2]{1,0:T(8,128)} copy(s32[8,2]{0,1:T(2,128)S(1)} %copy-done.1) | data formatting | bytes 128 | tf_op args[3]
  11.8 1.5 %prepare.1 = (bf16[4,512,256]{2,1,0:T(8,128)(2,1)S(1)}, f32[128,256]{1,0:T(8,128)S(1)}) custom-call(s32[1]{0:T(128)} %bitcast.me, s32[4,8]{1,0:T(4,128)} %kept.3, s32[8,2]{1,0:T(8,128)} %copy.6.int_kept, bf16[1024,256]{1,0:T(8,128)(2,1)} %integrals.1, bf16[128,512]{1,0:T(8,128)(2,1)S(1)} %get-tuple-element.14.own), custom_call_target="tpu_custom_call" | custom-call | bytes 1024 | tf_op jit(solution)/shard_map/prepare/pallas_call | solution.py:158
  13.3 0.4 %collective-permute-done.3.far_first = bf16[64,512]{1,0:T(8,128)(2,1)S(1)} collective-permute-done((bf16[64,512]{1,0:T(8,128)(2,1)S(1)}, bf16[64,512]{1,0:T(8,128)(2,1)S(1)}, u32[]{:S(2)}, u32[]{:S(2)}) %collective-permute-start.3) | collective-permute-done | bytes 65568 | tf_op jit(solution)/shard_map/ppermute | solution.py:123
  13.6 0.5 %collective-permute-done.1.near_first = bf16[64,512]{1,0:T(8,128)(2,1)S(1)} collective-permute-done((bf16[64,512]{1,0:T(8,128)(2,1)S(1)}, bf16[64,512]{1,0:T(8,128)(2,1)S(1)}, u32[]{:S(2)}, u32[]{:S(2)}) %collective-permute-start.1) | collective-permute-done | bytes 65568 | tf_op jit(solution)/shard_map/ppermute | solution.py:123
  14.1 0.6 %collective-permute-done.4.far_second = bf16[64,512]{1,0:T(8,128)(2,1)S(1)} collective-permute-done((bf16[64,512]{1,0:T(8,128)(2,1)S(1)}, bf16[64,512]{1,0:T(8,128)(2,1)S(1)}, u32[]{:S(2)}, u32[]{:S(2)}) %collective-permute-start.4) | collective-permute-done | bytes 65568 | tf_op jit(solution)/shard_map/ppermute | solution.py:123
  14.7 0.0 collective-permute-done.pair
  14.7 0.0 copy-start
  14.7 0.4 %ladder.1 = (f32[128,256]{1,0:T(8,128)S(1)}, s16[272,128]{1,0:T(8,128)(2,1)S(1)}, s16[272,128]{1,0:T(8,128)(2,1)S(1)}, s16[272,128]{1,0:T(8,128)(2,1)S(1)}) custom-call(s32[1]{0:T(128)} %bitcast.me, f32[128,256]{1,0:T(8,128)S(1)} %get-tuple-element.15.product, bf16[4,512,256]{2,1,0:T(8,128)(2,1)S(1)} %get-tuple-element.16.gathered, ...), custom_call_target="tpu_custom_call" | custom-call | flops 99999997952 | bytes 1024 | tf_op jit(solution)/shard_map/ladder/pallas_call | solution.py:174
  15.1 0.7 %collective-permute-start.5 = (s16[272,128]{1,0:T(8,128)(2,1)S(1)}, s16[272,128]{1,0:T(8,128)(2,1)S(1)}, u32[]{:S(2)}, u32[]{:S(2)}) collective-permute-start(s16[272,128]{1,0:T(8,128)(2,1)S(1)} %get-tuple-element.20), channel_id=1, source_target_pairs={{0,3},{1,2},{2,1},{3,0},{4,7},{5,6},{6,5},{7,4},{8,11},{9,10},{10,... | collective-permute-start | bytes 208904 | tf_op jit(solution)/shard_map/ppermute | solution.py:123
  15.9 1.2 %collective-permute-start.6 = (s16[272,128]{1,0:T(8,128)(2,1)S(1)}, s16[272,128]{1,0:T(8,128)(2,1)S(1)}, u32[]{:S(2)}, u32[]{:S(2)}) collective-permute-start(s16[272,128]{1,0:T(8,128)(2,1)S(1)} %get-tuple-element.21), channel_id=1, source_target_pairs={{0,2},{1,3},{2,0},{3,1},{4,6},{5,7},{6,4},{7,5},{8,10},{9,11},{10,... | collective-permute-start | bytes 208904 | tf_op jit(solution)/shard_map/ppermute | solution.py:123
  17.0 0.1 collective-permute-start.7
  17.1 2.2 %collective-permute-done.5.rest_0_ = s16[272,128]{1,0:T(8,128)(2,1)S(1)} collective-permute-done((s16[272,128]{1,0:T(8,128)(2,1)S(1)}, s16[272,128]{1,0:T(8,128)(2,1)S(1)}, u32[]{:S(2)}, u32[]{:S(2)}) %collective-permute-start.5) | collective-permute-done | bytes 69664 | tf_op jit(solution)/shard_map/ppermute | solution.py:123
  19.3 1.8 %collective-permute-done.6.rest_1_ = s16[272,128]{1,0:T(8,128)(2,1)S(1)} collective-permute-done((s16[272,128]{1,0:T(8,128)(2,1)S(1)}, s16[272,128]{1,0:T(8,128)(2,1)S(1)}, u32[]{:S(2)}, u32[]{:S(2)}) %collective-permute-start.6) | collective-permute-done | bytes 69664 | tf_op jit(solution)/shard_map/ppermute | solution.py:123
  21.1 0.0 collective-permute-done.7.rest_2_
  21.1 0.0 copy-done
  21.1 0.7 %finish.1 = f32[128,256]{1,0:T(8,128)} custom-call(f32[128,256]{1,0:T(8,128)S(1)} %copy-done, f32[128,256]{1,0:T(8,128)S(1)} %get-tuple-element.19.kept_sums, s16[272,128]{1,0:T(8,128)(2,1)S(1)} %collective-permute-done.5.rest_0_, s16[272,128]{1,0:T(8,128)(2,1)S(1)} %collective-permute-done.6.rest_1_, s16[272,128]{1,0:T(8,128)(2,1)S(1)} %collective-permute-done.7.rest_2_), custom_call_target="tpu_custom_call" | custom-call | tf_op jit(solution)/shard_map/finish/pallas_call | solution.py:185
Async XLA Ops:
  1.0 7.6 %collective-permute-start.2 = (bf16[64,512]{1,0:T(8,128)(2,1)S(1)}, bf16[64,512]{1,0:T(8,128)(2,1)S(1)}, u32[]{:S(2)}, u32[]{:S(2)}) collective-permute-start(bf16[64,512]{1,0:T(8,128)(2,1)S(1)} %get-tuple-element.18), channel_id=1, source_target_pairs={{0,8},{4,12},{8,0},{12,4},{1,9},{5,13},{9,1},{13,5},{2,10},{6,14},... | collective-permute-start | bytes 196616 | tf_op jit(solution)/shard_map/ppermute | solution.py:123
  5.1 6.0 %copy-start.1 = (s32[8,2]{0,1:T(2,128)S(1)}, s32[8,2]{0,1:T(2,128)}, u32[]{:S(2)}) copy-start(s32[8,2]{0,1:T(2,128)} %param.8) | copy-start | bytes 196
  5.1 9.6 %collective-permute-start = (bf16[128,512]{1,0:T(8,128)(2,1)S(1)}, bf16[128,512]{1,0:T(8,128)(2,1)S(1)}, u32[]{:S(2)}, u32[]{:S(2)}) collective-permute-start(bf16[128,512]{1,0:T(8,128)(2,1)S(1)} %get-tuple-element.14.own), channel_id=1, source_target_pairs={{0,4},{4,0},{8,12},{12,8},{1,5},{5,1},{9,13},{13,9},{2,6},{6,2},{1... | collective-permute-start | bytes 393224 | tf_op jit(solution)/shard_map/ppermute | solution.py:123
  6.7 6.9 %collective-permute-start.3 = (bf16[64,512]{1,0:T(8,128)(2,1)S(1)}, bf16[64,512]{1,0:T(8,128)(2,1)S(1)}, u32[]{:S(2)}, u32[]{:S(2)}) collective-permute-start(bf16[64,512]{1,0:T(8,128)(2,1)S(1)} %get-tuple-element.17), channel_id=1, source_target_pairs={{0,12},{4,8},{8,4},{12,0},{1,13},{5,9},{9,5},{13,1},{2,14},{6,10},... | collective-permute-start | bytes 196616 | tf_op jit(solution)/shard_map/ppermute | solution.py:123
  6.7 7.4 %collective-permute-start.1 = (bf16[64,512]{1,0:T(8,128)(2,1)S(1)}, bf16[64,512]{1,0:T(8,128)(2,1)S(1)}, u32[]{:S(2)}, u32[]{:S(2)}) collective-permute-start(bf16[64,512]{1,0:T(8,128)(2,1)S(1)} %get-tuple-element.17), channel_id=1, source_target_pairs={{0,8},{4,12},{8,0},{12,4},{1,9},{5,13},{9,1},{13,5},{2,10},{6,14},... | collective-permute-start | bytes 196616 | tf_op jit(solution)/shard_map/ppermute | solution.py:123
  8.6 6.1 %collective-permute-start.4 = (bf16[64,512]{1,0:T(8,128)(2,1)S(1)}, bf16[64,512]{1,0:T(8,128)(2,1)S(1)}, u32[]{:S(2)}, u32[]{:S(2)}) collective-permute-start(bf16[64,512]{1,0:T(8,128)(2,1)S(1)} %collective-permute-done.2.near_second), channel_id=1, source_target_pairs={{0,4},{4,0},{8,12},{12,8},{1,5},{5,1},{9,13},{13,9},{2,6},{6,2},{1... | collective-permute-start | bytes 196616 | tf_op jit(solution)/shard_map/ppermute | solution.py:123
  14.7 6.4 %copy-start = (f32[128,256]{1,0:T(8,128)S(1)}, f32[128,256]{1,0:T(8,128)}, u32[]{:S(2)}) copy-start(f32[128,256]{1,0:T(8,128)} %residual.1) | copy-start | bytes 393220
  15.1 4.2 %collective-permute-start.5 = (s16[272,128]{1,0:T(8,128)(2,1)S(1)}, s16[272,128]{1,0:T(8,128)(2,1)S(1)}, u32[]{:S(2)}, u32[]{:S(2)}) collective-permute-start(s16[272,128]{1,0:T(8,128)(2,1)S(1)} %get-tuple-element.20), channel_id=1, source_target_pairs={{0,3},{1,2},{2,1},{3,0},{4,7},{5,6},{6,5},{7,4},{8,11},{9,10},{10,... | collective-permute-start | bytes 208904 | tf_op jit(solution)/shard_map/ppermute | solution.py:123
  15.9 5.3 %collective-permute-start.6 = (s16[272,128]{1,0:T(8,128)(2,1)S(1)}, s16[272,128]{1,0:T(8,128)(2,1)S(1)}, u32[]{:S(2)}, u32[]{:S(2)}) collective-permute-start(s16[272,128]{1,0:T(8,128)(2,1)S(1)} %get-tuple-element.21), channel_id=1, source_target_pairs={{0,2},{1,3},{2,0},{3,1},{4,6},{5,7},{6,4},{7,5},{8,10},{9,11},{10,... | collective-permute-start | bytes 208904 | tf_op jit(solution)/shard_map/ppermute | solution.py:123
  17.0 4.1 %collective-permute-start.7 = (s16[272,128]{1,0:T(8,128)(2,1)S(1)}, s16[272,128]{1,0:T(8,128)(2,1)S(1)}, u32[]{:S(2)}, u32[]{:S(2)}) collective-permute-start(s16[272,128]{1,0:T(8,128)(2,1)S(1)} %get-tuple-element.22), channel_id=1, source_target_pairs={{0,1},{1,0},{2,3},{3,2},{4,5},{5,4},{6,7},{7,6},{8,9},{9,8},{10,11... | collective-permute-start | bytes 208904 | tf_op jit(solution)/shard_map/ppermute | solution.py:123

commit v10 on v9

--- a/solution.py
+++ b/solution.py
@@ -66,9 +66,13 @@
             start = pl.multiple_of(tile * TILE, TILE)
             for ab in range(tiles_ab):
                 part = held[pl.ds(start, TILE), ab * TILE : (ab + 1) * TILE]
-                on = (int_table[tile, ab] != 0).astype(jnp.float32).astype(part.dtype)
+                on = (int_table[ab, tile] != 0).astype(jnp.float32).astype(part.dtype)
                 gathered[n, slot * TILE : (slot + 1) * TILE, ab * TILE : (ab + 1) * TILE] = part * on
     product[...] = jnp.dot(own[...], gathered[row ^ col], preferred_element_type=jnp.float32)
+
+
+def after_kernel(token, x, out):
+    pass
 
 
 def encode(x, out):
@@ -119,6 +123,19 @@
     out[...] = total
 
 
+def after(token, x):
+    return pl.pallas_call(
+        after_kernel,
+        out_shape=jax.ShapeDtypeStruct(x.shape, x.dtype),
+        in_specs=[pl.BlockSpec(memory_space=pl.ANY)] * 2,
+        out_specs=pl.BlockSpec(memory_space=pl.ANY),
+        input_output_aliases={1: 0},
+        compiler_params=PARAMS,
+        cost_estimate=cost(0),
+        name="after",
+    )(token, x)
+
+
 def swap(x, axis, step):
     return lax.ppermute(x, axis, [(i, i ^ step) for i in range(ROWS)])
 
@@ -134,7 +151,7 @@
     half_block = jax.ShapeDtypeStruct((pairs // 2, slots * TILE), doubles.dtype)
     message = jax.ShapeDtypeStruct((pairs * width // TILE + HEAD, TILE), jnp.int16)
     doubles, doubles_kept, integrals, integral_kept = (
-        pltpu.with_memory_space_constraint(x, pltpu.HBM) for x in (doubles, doubles_kept, integrals, integral_kept)
+        pltpu.with_memory_space_constraint(x, pltpu.HBM) for x in (doubles, doubles_kept, integrals, integral_kept.T)
     )
     packed, first, second = pl.pallas_call(
         functools.partial(pack_kernel, tiles, slots),
@@ -154,6 +171,7 @@
     pair = swap(packed, "rows", 1)
     far_first = swap(first, "rows", 3)
     near_first = swap(first, "rows", 2)
+    near_second = after(pair, near_second)
     far_second = swap(near_second, "rows", 1)
     gathered, product = pl.pallas_call(
         functools.partial(prepare_kernel, tiles, slots),

time: 22 us -> 25.1 us (1.14)
  waiting for transfers between devices: 5.44 us -> 11.6 us
  starting transfers between devices: 12 us -> 9.56 us
  local copies, waits for them, and re-layouts: 0.68 us -> 0.01 us
    ppermute x8, waiting for transfers between devices: 5.44 us -> 11.6 us  [swap(): return lax.ppermute(x, axis, [(i, i ^ step) for i in range(ROWS)])]
    ppermute x8, starting transfers between devices: 12 us -> 9.56 us  [swap(): return lax.ppermute(x, axis, [(i, i ^ step) for i in range(ROWS)])]
    unnamed x5 -> x2, local copies, waits for them, and re-layouts: 0.68 us -> 0.01 us
  transfers between devices with their start and end apart: 8 -> 8, of which waited for: 5 -> 5; matrix products, arithmetic and copies ran while one was open for 3% -> 0% of each run, Pallas kernels for 7% -> 6%
where the time goes in v10:
time: 25.1 us; the launch traced here: 24.9 us
  waiting for transfers between devices  11.6 us (46%)
  starting transfers between devices  9.56 us (38%)
  Pallas kernels  3.67 us (15%)
    ppermute x8, waiting for transfers between devices, swap(): return lax.ppermute(x, axis, [(i, i ^ step) for i in range(ROWS)])  11.6 us
    ppermute x8, starting transfers between devices, swap(): return lax.ppermute(x, axis, [(i, i ^ step) for i in range(ROWS)])  9.56 us
    pallas_call x1, Pallas kernels, local_few(): pl.pallas_call(functools.partial(prepare_kernel, tiles, slots), out_shape...  1.51 us
    pallas_call x1, Pallas kernels, local_few(): pl.pallas_call(functools.partial(pack_kernel, tiles, slots), out_shape=[j...  1 us
    pallas_call x1, Pallas kernels, local_few(): pl.pallas_call(finish_kernel, out_shape=sums_shape, in_specs=[VMEM] * (RO...  0.72 us
  transfers between devices with their start and end apart: 8, of which 5 were waited for; matrix products, arithmetic and copies ran while one was open for 0% of the time, Pallas kernels for 6%

profile of v10, /device:TPU:0, one launch (start us, length us, event | category | flops | bytes accessed | tf_op | source)
XLA Modules:
  0.0 24.9 jit_solution(1392527525858967774)
XLA Ops:
  0.0 1.0 %pack.1 = (bf16[128,512]{1,0:T(8,128)(2,1)S(1)}, bf16[64,512]{1,0:T(8,128)(2,1)S(1)}, bf16[64,512]{1,0:T(8,128)(2,1)S(1)}) custom-call(s32[1]{0:T(128)} %bitcast.me, s32[4,8]{1,0:T(4,128)} %kept.3, bf16[128,1024]{1,0:T(8,128)(2,1)} %doubles.1), custom_call_target="tpu_custom_call" | custom-call | tf_op jit(solution)/shard_map/pack/pallas_call | solution.py:156
  1.0 3.1 %collective-permute-start = (bf16[128,512]{1,0:T(8,128)(2,1)S(1)}, bf16[128,512]{1,0:T(8,128)(2,1)S(1)}, u32[]{:S(2)}, u32[]{:S(2)}) collective-permute-start(bf16[128,512]{1,0:T(8,128)(2,1)S(1)} %get-tuple-element.14.own), channel_id=1, source_target_pairs={{0,4},{4,0},{8,12},{12,8},{1,5},{5,1},{9,13},{13,9},{2,6},{6,2},{1... | collective-permute-start | bytes 393224 | tf_op jit(solution)/shard_map/ppermute | solution.py:140
  4.1 2.6 %collective-permute-start.2 = (bf16[64,512]{1,0:T(8,128)(2,1)S(1)}, bf16[64,512]{1,0:T(8,128)(2,1)S(1)}, u32[]{:S(2)}, u32[]{:S(2)}) collective-permute-start(bf16[64,512]{1,0:T(8,128)(2,1)S(1)} %get-tuple-element.18), channel_id=1, source_target_pairs={{0,8},{4,12},{8,0},{12,4},{1,9},{5,13},{9,1},{13,5},{2,10},{6,14},... | collective-permute-start | bytes 196616 | tf_op jit(solution)/shard_map/ppermute | solution.py:140
  6.7 0.0 collective-permute-start.3
  6.7 1.9 %collective-permute-start.1 = (bf16[64,512]{1,0:T(8,128)(2,1)S(1)}, bf16[64,512]{1,0:T(8,128)(2,1)S(1)}, u32[]{:S(2)}, u32[]{:S(2)}) collective-permute-start(bf16[64,512]{1,0:T(8,128)(2,1)S(1)} %get-tuple-element.17), channel_id=1, source_target_pairs={{0,8},{4,12},{8,0},{12,4},{1,9},{5,13},{9,1},{13,5},{2,10},{6,14},... | collective-permute-start | bytes 196616 | tf_op jit(solution)/shard_map/ppermute | solution.py:140
  8.6 4.8 %collective-permute-done.2.x = bf16[64,512]{1,0:T(8,128)(2,1)S(1)} collective-permute-done((bf16[64,512]{1,0:T(8,128)(2,1)S(1)}, bf16[64,512]{1,0:T(8,128)(2,1)S(1)}, u32[]{:S(2)}, u32[]{:S(2)}) %collective-permute-start.2) | collective-permute-done | bytes 65568 | tf_op jit(solution)/shard_map/ppermute | solution.py:140
  13.4 0.0 collective-permute-done.token.pair
  13.4 0.1 collective-permute-start.4
  13.5 1.5 %prepare.1 = (bf16[4,512,256]{2,1,0:T(8,128)(2,1)S(1)}, f32[128,256]{1,0:T(8,128)S(1)}) custom-call(s32[1]{0:T(128)} %bitcast.me, s32[4,8]{1,0:T(4,128)} %kept.3, s32[2,8]{1,0:T(2,128)} %bitcast.2, bf16[1024,256]{1,0:T(8,128)(2,1)} %integrals.1, bf16[128,512]{1,0:T(8,128)(2,1)S(1)} %get-tuple-element.14.own), custom_call_target="tpu_custom_call" | custom-call | bytes 1024 | tf_op jit(solution)/shard_map/prepare/pallas_call | solution.py:176
  15.0 0.0 collective-permute-done.3.far_first
  15.0 1.2 %collective-permute-done.1.near_first = bf16[64,512]{1,0:T(8,128)(2,1)S(1)} collective-permute-done((bf16[64,512]{1,0:T(8,128)(2,1)S(1)}, bf16[64,512]{1,0:T(8,128)(2,1)S(1)}, u32[]{:S(2)}, u32[]{:S(2)}) %collective-permute-start.1) | collective-permute-done | bytes 65568 | tf_op jit(solution)/shard_map/ppermute | solution.py:140
  16.2 1.5 %collective-permute-done.4.far_second = bf16[64,512]{1,0:T(8,128)(2,1)S(1)} collective-permute-done((bf16[64,512]{1,0:T(8,128)(2,1)S(1)}, bf16[64,512]{1,0:T(8,128)(2,1)S(1)}, u32[]{:S(2)}, u32[]{:S(2)}) %collective-permute-start.4) | collective-permute-done | bytes 65568 | tf_op jit(solution)/shard_map/ppermute | solution.py:140
  17.7 0.0 copy-start
  17.7 0.4 %ladder.1 = (f32[128,256]{1,0:T(8,128)S(1)}, s16[272,128]{1,0:T(8,128)(2,1)S(1)}, s16[272,128]{1,0:T(8,128)(2,1)S(1)}, s16[272,128]{1,0:T(8,128)(2,1)S(1)}) custom-call(s32[1]{0:T(128)} %bitcast.me, f32[128,256]{1,0:T(8,128)S(1)} %get-tuple-element.15.product, bf16[4,512,256]{2,1,0:T(8,128)(2,1)S(1)} %get-tuple-element.16.gathered, ...), custom_call_target="tpu_custom_call" | custom-call | flops 99999997952 | bytes 1024 | tf_op jit(solution)/shard_map/ladder/pallas_call | solution.py:192
  18.1 0.1 collective-permute-start.5
  18.2 1.6 %collective-permute-start.6 = (s16[272,128]{1,0:T(8,128)(2,1)S(1)}, s16[272,128]{1,0:T(8,128)(2,1)S(1)}, u32[]{:S(2)}, u32[]{:S(2)}) collective-permute-start(s16[272,128]{1,0:T(8,128)(2,1)S(1)} %get-tuple-element.21), channel_id=1, source_target_pairs={{0,2},{1,3},{2,0},{3,1},{4,6},{5,7},{6,4},{7,5},{8,10},{9,11},{10,... | collective-permute-start | bytes 208904 | tf_op jit(solution)/shard_map/ppermute | solution.py:140
  19.8 0.3 %collective-permute-start.7 = (s16[272,128]{1,0:T(8,128)(2,1)S(1)}, s16[272,128]{1,0:T(8,128)(2,1)S(1)}, u32[]{:S(2)}, u32[]{:S(2)}) collective-permute-start(s16[272,128]{1,0:T(8,128)(2,1)S(1)} %get-tuple-element.22), channel_id=1, source_target_pairs={{0,1},{1,0},{2,3},{3,2},{4,5},{5,4},{6,7},{7,6},{8,9},{9,8},{10,11... | collective-permute-start | bytes 208904 | tf_op jit(solution)/shard_map/ppermute | solution.py:140
  20.1 2.6 %collective-permute-done.5.rest_0_ = s16[272,128]{1,0:T(8,128)(2,1)S(1)} collective-permute-done((s16[272,128]{1,0:T(8,128)(2,1)S(1)}, s16[272,128]{1,0:T(8,128)(2,1)S(1)}, u32[]{:S(2)}, u32[]{:S(2)}) %collective-permute-start.5) | collective-permute-done | bytes 69664 | tf_op jit(solution)/shard_map/ppermute | solution.py:140
  22.6 1.5 %collective-permute-done.6.rest_1_ = s16[272,128]{1,0:T(8,128)(2,1)S(1)} collective-permute-done((s16[272,128]{1,0:T(8,128)(2,1)S(1)}, s16[272,128]{1,0:T(8,128)(2,1)S(1)}, u32[]{:S(2)}, u32[]{:S(2)}) %collective-permute-start.6) | collective-permute-done | bytes 69664 | tf_op jit(solution)/shard_map/ppermute | solution.py:140
  24.2 0.0 collective-permute-done.7.rest_2_
  24.2 0.0 copy-done
  24.2 0.7 %finish.1 = f32[128,256]{1,0:T(8,128)} custom-call(f32[128,256]{1,0:T(8,128)S(1)} %copy-done, f32[128,256]{1,0:T(8,128)S(1)} %get-tuple-element.19.kept_sums, s16[272,128]{1,0:T(8,128)(2,1)S(1)} %collective-permute-done.5.rest_0_, s16[272,128]{1,0:T(8,128)(2,1)S(1)} %collective-permute-done.6.rest_1_, s16[272,128]{1,0:T(8,128)(2,1)S(1)} %collective-permute-done.7.rest_2_), custom_call_target="tpu_custom_call" | custom-call | tf_op jit(solution)/shard_map/finish/pallas_call | solution.py:203
  (1 shorter events, 0.0 us)
Async XLA Ops:
  1.0 12.4 %collective-permute-start = (bf16[128,512]{1,0:T(8,128)(2,1)S(1)}, bf16[128,512]{1,0:T(8,128)(2,1)S(1)}, u32[]{:S(2)}, u32[]{:S(2)}) collective-permute-start(bf16[128,512]{1,0:T(8,128)(2,1)S(1)} %get-tuple-element.14.own), channel_id=1, source_target_pairs={{0,4},{4,0},{8,12},{12,8},{1,5},{5,1},{9,13},{13,9},{2,6},{6,2},{1... | collective-permute-start | bytes 393224 | tf_op jit(solution)/shard_map/ppermute | solution.py:140
  4.1 9.3 %collective-permute-start.2 = (bf16[64,512]{1,0:T(8,128)(2,1)S(1)}, bf16[64,512]{1,0:T(8,128)(2,1)S(1)}, u32[]{:S(2)}, u32[]{:S(2)}) collective-permute-start(bf16[64,512]{1,0:T(8,128)(2,1)S(1)} %get-tuple-element.18), channel_id=1, source_target_pairs={{0,8},{4,12},{8,0},{12,4},{1,9},{5,13},{9,1},{13,5},{2,10},{6,14},... | collective-permute-start | bytes 196616 | tf_op jit(solution)/shard_map/ppermute | solution.py:140
  6.7 8.3 %collective-permute-start.3 = (bf16[64,512]{1,0:T(8,128)(2,1)S(1)}, bf16[64,512]{1,0:T(8,128)(2,1)S(1)}, u32[]{:S(2)}, u32[]{:S(2)}) collective-permute-start(bf16[64,512]{1,0:T(8,128)(2,1)S(1)} %get-tuple-element.17), channel_id=1, source_target_pairs={{0,12},{4,8},{8,4},{12,0},{1,13},{5,9},{9,5},{13,1},{2,14},{6,10},... | collective-permute-start | bytes 196616 | tf_op jit(solution)/shard_map/ppermute | solution.py:140
  6.7 9.5 %collective-permute-start.1 = (bf16[64,512]{1,0:T(8,128)(2,1)S(1)}, bf16[64,512]{1,0:T(8,128)(2,1)S(1)}, u32[]{:S(2)}, u32[]{:S(2)}) collective-permute-start(bf16[64,512]{1,0:T(8,128)(2,1)S(1)} %get-tuple-element.17), channel_id=1, source_target_pairs={{0,8},{4,12},{8,0},{12,4},{1,9},{5,13},{9,1},{13,5},{2,10},{6,14},... | collective-permute-start | bytes 196616 | tf_op jit(solution)/shard_map/ppermute | solution.py:140
  13.4 4.3 %collective-permute-start.4 = (bf16[64,512]{1,0:T(8,128)(2,1)S(1)}, bf16[64,512]{1,0:T(8,128)(2,1)S(1)}, u32[]{:S(2)}, u32[]{:S(2)}) collective-permute-start(bf16[64,512]{1,0:T(8,128)(2,1)S(1)} %after.1.near_second), channel_id=1, source_target_pairs={{0,4},{4,0},{8,12},{12,8},{1,5},{5,1},{9,13},{13,9},{2,6},{6,2},{1... | collective-permute-start | bytes 196616 | tf_op jit(solution)/shard_map/ppermute | solution.py:140
  17.7 6.5 %copy-start = (f32[128,256]{1,0:T(8,128)S(1)}, f32[128,256]{1,0:T(8,128)}, u32[]{:S(2)}) copy-start(f32[128,256]{1,0:T(8,128)} %residual.1) | copy-start | bytes 393220
  18.1 4.5 %collective-permute-start.5 = (s16[272,128]{1,0:T(8,128)(2,1)S(1)}, s16[272,128]{1,0:T(8,128)(2,1)S(1)}, u32[]{:S(2)}, u32[]{:S(2)}) collective-permute-start(s16[272,128]{1,0:T(8,128)(2,1)S(1)} %get-tuple-element.20), channel_id=1, source_target_pairs={{0,3},{1,2},{2,1},{3,0},{4,7},{5,6},{6,5},{7,4},{8,11},{9,10},{10,... | collective-permute-start | bytes 208904 | tf_op jit(solution)/shard_map/ppermute | solution.py:140
  18.2 6.0 %collective-permute-start.6 = (s16[272,128]{1,0:T(8,128)(2,1)S(1)}, s16[272,128]{1,0:T(8,128)(2,1)S(1)}, u32[]{:S(2)}, u32[]{:S(2)}) collective-permute-start(s16[272,128]{1,0:T(8,128)(2,1)S(1)} %get-tuple-element.21), channel_id=1, source_target_pairs={{0,2},{1,3},{2,0},{3,1},{4,6},{5,7},{6,4},{7,5},{8,10},{9,11},{10,... | collective-permute-start | bytes 208904 | tf_op jit(solution)/shard_map/ppermute | solution.py:140
  19.8 4.4 %collective-permute-start.7 = (s16[272,128]{1,0:T(8,128)(2,1)S(1)}, s16[272,128]{1,0:T(8,128)(2,1)S(1)}, u32[]{:S(2)}, u32[]{:S(2)}) collective-permute-start(s16[272,128]{1,0:T(8,128)(2,1)S(1)} %get-tuple-element.22), channel_id=1, source_target_pairs={{0,1},{1,0},{2,3},{3,2},{4,5},{5,4},{6,7},{7,6},{8,9},{9,8},{10,11... | collective-permute-start | bytes 208904 | tf_op jit(solution)/shard_map/ppermute | solution.py:140

commit v11 on v10

--- a/solution.py
+++ b/solution.py
@@ -100,27 +100,27 @@
     return jnp.concatenate(parts, axis=1)
 
 
-def ladder_kernel(me, product, gathered, pair, near_first, near_second, far_first, far_second, kept_sums, *rest):
+def ladder_kernel(start, me, product, gathered, pair, far, near, kept_sums, *rest):
     outs, sums = rest[:-1], rest[-1]
     mine = me[0] // ROWS ^ me[0] % ROWS
-    half = near_first.shape[0]
-    sums[mine] = product[...]
-    sums[mine ^ 1] = jnp.dot(pair[...], gathered[mine ^ 1], preferred_element_type=jnp.float32)
-    for step, start, block in ((2, 0, near_first), (3, 0, far_first), (2, half, near_second), (3, half, far_second)):
-        sums[mine ^ step, start : start + half, :] = jnp.dot(
-            block[...], gathered[mine ^ step], preferred_element_type=jnp.float32
-        )
+    part = slice(start, start + near.shape[0])
+    sums[mine] = product[part, :]
+    for step, block in enumerate((pair[part, :], near[...], far[...]), 1):
+        sums[mine ^ step] = jnp.dot(block, gathered[mine ^ step], preferred_element_type=jnp.float32)
     kept_sums[...] = sums[0]
     for n, out in enumerate(outs, 1):
         encode(sums[n], out)
 
 
-def finish_kernel(residual, kept_sums, *rest):
+def finish_kernel(start, base, kept_sums, *rest):
     messages, out = rest[:-1], rest[-1]
-    total = residual[...] + kept_sums[...]
+    half = kept_sums.shape[0]
+    part, other = slice(start, start + half), slice(half - start, 2 * half - start)
+    total = base[part, :] + kept_sums[...]
     for message in messages:
-        total = total + decode(message, total.shape[0])
-    out[...] = total
+        total = total + decode(message, half)
+    out[part, :] = total
+    out[other, :] = base[other, :]
 
 
 def after(token, x):
@@ -131,7 +131,7 @@
         out_specs=pl.BlockSpec(memory_space=pl.ANY),
         input_output_aliases={1: 0},
         compiler_params=PARAMS,
-        cost_estimate=cost(0),
+        cost_estimate=cost(4 * 10**8),
         name="after",
     )(token, x)
 
@@ -149,7 +149,8 @@
     places = pltpu.SMEM((tiles + 1,), jnp.int32)
     sums_shape = jax.ShapeDtypeStruct((pairs, width), jnp.float32)
     half_block = jax.ShapeDtypeStruct((pairs // 2, slots * TILE), doubles.dtype)
-    message = jax.ShapeDtypeStruct((pairs * width // TILE + HEAD, TILE), jnp.int16)
+    half_sums = jax.ShapeDtypeStruct((pairs // 2, width), jnp.float32)
+    message = jax.ShapeDtypeStruct((pairs // 2 * width // TILE + HEAD, TILE), jnp.int16)
     doubles, doubles_kept, integrals, integral_kept = (
         pltpu.with_memory_space_constraint(x, pltpu.HBM) for x in (doubles, doubles_kept, integrals, integral_kept.T)
     )
@@ -171,7 +172,7 @@
     pair = swap(packed, "rows", 1)
     far_first = swap(first, "rows", 3)
     near_first = swap(first, "rows", 2)
-    near_second = after(pair, near_second)
+    near_second = after(packed, near_second)
     far_second = swap(near_second, "rows", 1)
     gathered, product = pl.pallas_call(
         functools.partial(prepare_kernel, tiles, slots),
@@ -189,25 +190,28 @@
         cost_estimate=cost(0),
         name="prepare",
     )(me, doubles_kept, integral_kept, integrals, packed)
-    kept_sums, *messages = pl.pallas_call(
-        ladder_kernel,
-        out_shape=[sums_shape] + [message] * (ROWS - 1),
-        in_specs=[SMEM] + [VMEM] * 7,
-        out_specs=[VMEM] * ROWS,
-        scratch_shapes=[pltpu.VMEM((ROWS, pairs, width), jnp.float32)],
-        compiler_params=PARAMS,
-        cost_estimate=cost(10**11),
-        name="ladder",
-    )(me, product, gathered, pair, near_first, near_second, far_first, far_second)
-    messages = [swap(x, "cols", step) for step, x in reversed(list(enumerate(messages, 1)))]
-    return pl.pallas_call(
-        finish_kernel,
-        out_shape=sums_shape,
-        in_specs=[VMEM] * (ROWS + 1),
-        out_specs=VMEM,
-        compiler_params=PARAMS,
-        name="finish",
-    )(residual, kept_sums, *messages)
+    total = residual
+    for start, near, far in ((0, near_first, far_first), (pairs // 2, near_second, far_second)):
+        kept_sums, *messages = pl.pallas_call(
+            functools.partial(ladder_kernel, start),
+            out_shape=[half_sums] + [message] * (ROWS - 1),
+            in_specs=[SMEM] + [VMEM] * 5,
+            out_specs=[VMEM] * ROWS,
+            scratch_shapes=[pltpu.VMEM((ROWS,) + half_sums.shape, jnp.float32)],
+            compiler_params=PARAMS,
+            cost_estimate=cost(10**11 if start else 0),
+            name="ladder",
+        )(me, product, gathered, pair, far, near)
+        messages = [swap(x, "cols", step) for step, x in reversed(list(enumerate(messages, 1)))]
+        total = pl.pallas_call(
+            functools.partial(finish_kernel, start),
+            out_shape=sums_shape,
+            in_specs=[VMEM] * (ROWS + 1),
+            out_specs=VMEM,
+            compiler_params=PARAMS,
+            name="finish",
+        )(total, kept_sums, *messages)
+    return total
 
 
 def local_many(doubles, doubles_kept, integrals, integral_kept, residual):

time: 25.1 us -> 23.4 us (0.932)
  waiting for transfers between devices: 11.6 us -> 4.44 us
  starting transfers between devices: 9.56 us -> 14.8 us
    ppermute x8 -> x11, waiting for transfers between devices: 11.6 us -> 4.44 us  [swap(): return lax.ppermute(x, axis, [(i, i ^ step) for i in range(ROWS)])]
    ppermute x8 -> x11, starting transfers between devices: 9.56 us -> 14.8 us  [swap(): return lax.ppermute(x, axis, [(i, i ^ step) for i in range(ROWS)])]
    pallas_call x2 -> x4, Pallas kernels: 1.16 us -> 1.38 us  [the longest x2 0.74 us: local_few(): pl.pallas_call(functools.partial(finish_kernel, start), out_shape=sums_sh...]
  transfers between devices with their start and end apart: 8 -> 11, of which waited for: 5 -> 4; matrix products, arithmetic and copies ran while one was open for 0% -> 0% of each run, Pallas kernels for 6% -> 9%
where the time goes in v11:
time: 23.4 us; the launch traced here: 23.2 us
  starting transfers between devices  14.8 us (63%)
  waiting for transfers between devices  4.44 us (19%)
  Pallas kernels  3.9 us (17%)
    ppermute x11, starting transfers between devices, swap(): return lax.ppermute(x, axis, [(i, i ^ step) for i in range(ROWS)])  14.8 us
    ppermute x11, waiting for transfers between devices, swap(): return lax.ppermute(x, axis, [(i, i ^ step) for i in range(ROWS)])  4.44 us
    pallas_call x1, Pallas kernels, local_few(): pl.pallas_call(functools.partial(prepare_kernel, tiles, slots), out_shape...  1.51 us
    pallas_call x1, Pallas kernels, local_few(): pl.pallas_call(functools.partial(pack_kernel, tiles, slots), out_shape=[j...  1 us
    pallas_call x2, Pallas kernels, local_few(): pl.pallas_call(functools.partial(finish_kernel, start), out_shape=sums_sh...  0.74 us
    pallas_call x2, Pallas kernels, local_few(): pl.pallas_call(functools.partial(ladder_kernel, start), out_shape=[half_s...  0.64 us
  transfers between devices with their start and end apart: 11, of which 4 were waited for; matrix products, arithmetic and copies ran while one was open for 0% of the time, Pallas kernels for 9%

profile of v11, /device:TPU:0, one launch (start us, length us, event | category | flops | bytes accessed | tf_op | source)
XLA Modules:
  0.0 23.2 jit_solution(14664915664590507283)
XLA Ops:
  0.0 1.0 %pack.1 = (bf16[128,512]{1,0:T(8,128)(2,1)S(1)}, bf16[64,512]{1,0:T(8,128)(2,1)S(1)}, bf16[64,512]{1,0:T(8,128)(2,1)S(1)}) custom-call(s32[1]{0:T(128)} %bitcast.me, s32[4,8]{1,0:T(4,128)} %kept.3, bf16[128,1024]{1,0:T(8,128)(2,1)} %doubles.1), custom_call_target="tpu_custom_call" | custom-call | tf_op jit(solution)/shard_map/pack/pallas_call | solution.py:157
  1.0 4.1 %collective-permute-start.6 = (bf16[64,512]{1,0:T(8,128)(2,1)S(1)}, bf16[64,512]{1,0:T(8,128)(2,1)S(1)}, u32[]{:S(2)}, u32[]{:S(2)}) collective-permute-start(bf16[64,512]{1,0:T(8,128)(2,1)S(1)} %get-tuple-element.26), channel_id=1, source_target_pairs={{0,8},{4,12},{8,0},{12,4},{1,9},{5,13},{9,1},{13,5},{2,10},{6,14},... | collective-permute-start | bytes 196616 | tf_op jit(solution)/shard_map/ppermute | solution.py:140
  5.1 1.6 %collective-permute-start = (bf16[128,512]{1,0:T(8,128)(2,1)S(1)}, bf16[128,512]{1,0:T(8,128)(2,1)S(1)}, u32[]{:S(2)}, u32[]{:S(2)}) collective-permute-start(bf16[128,512]{1,0:T(8,128)(2,1)S(1)} %get-tuple-element.18.own.token), channel_id=1, source_target_pairs={{0,4},{4,0},{8,12},{12,8},{1,5},{5,1},{9,13},{13,9},{2,6},{6,2},{1... | collective-permute-start | bytes 393224 | tf_op jit(solution)/shard_map/ppermute | solution.py:140
  6.7 0.0 collective-permute-start.1
  6.7 1.9 %collective-permute-start.2 = (bf16[64,512]{1,0:T(8,128)(2,1)S(1)}, bf16[64,512]{1,0:T(8,128)(2,1)S(1)}, u32[]{:S(2)}, u32[]{:S(2)}) collective-permute-start(bf16[64,512]{1,0:T(8,128)(2,1)S(1)} %get-tuple-element.21), channel_id=1, source_target_pairs={{0,8},{4,12},{8,0},{12,4},{1,9},{5,13},{9,1},{13,5},{2,10},{6,14},... | collective-permute-start | bytes 196616 | tf_op jit(solution)/shard_map/ppermute | solution.py:140
  8.6 0.0 collective-permute-done.6.x
  8.6 2.5 %collective-permute-start.7 = (bf16[64,512]{1,0:T(8,128)(2,1)S(1)}, bf16[64,512]{1,0:T(8,128)(2,1)S(1)}, u32[]{:S(2)}, u32[]{:S(2)}) collective-permute-start(bf16[64,512]{1,0:T(8,128)(2,1)S(1)} %after.1.near), channel_id=1, source_target_pairs={{0,4},{4,0},{8,12},{12,8},{1,5},{5,1},{9,13},{13,9},{2,6},{6,2},{1... | collective-permute-start | bytes 196616 | tf_op jit(solution)/shard_map/ppermute | solution.py:140
  11.1 1.5 %prepare.1 = (bf16[4,512,256]{2,1,0:T(8,128)(2,1)S(1)}, f32[128,256]{1,0:T(8,128)S(1)}) custom-call(s32[1]{0:T(128)} %bitcast.me, s32[4,8]{1,0:T(4,128)} %kept.3, s32[2,8]{1,0:T(2,128)} %bitcast.2, bf16[1024,256]{1,0:T(8,128)(2,1)} %integrals.1, bf16[128,512]{1,0:T(8,128)(2,1)S(1)} %get-tuple-element.18.own.token), custom_call_target="tpu_custom_call" | custom-call | bytes 1024 | tf_op jit(solution)/shard_map/prepare/pallas_call | solution.py:177
  12.6 1.0 %collective-permute-done.1.far = bf16[64,512]{1,0:T(8,128)(2,1)S(1)} collective-permute-done((bf16[64,512]{1,0:T(8,128)(2,1)S(1)}, bf16[64,512]{1,0:T(8,128)(2,1)S(1)}, u32[]{:S(2)}, u32[]{:S(2)}) %collective-permute-start.1) | collective-permute-done | bytes 65568 | tf_op jit(solution)/shard_map/ppermute | solution.py:140
  13.6 0.5 %collective-permute-done.2.near = bf16[64,512]{1,0:T(8,128)(2,1)S(1)} collective-permute-done((bf16[64,512]{1,0:T(8,128)(2,1)S(1)}, bf16[64,512]{1,0:T(8,128)(2,1)S(1)}, u32[]{:S(2)}, u32[]{:S(2)}) %collective-permute-start.2) | collective-permute-done | bytes 65568 | tf_op jit(solution)/shard_map/ppermute | solution.py:140
  14.1 0.0 collective-permute-done.pair
  14.1 0.3 %ladder.2 = (f32[64,256]{1,0:T(8,128)S(1)}, s16[144,128]{1,0:T(8,128)(2,1)S(1)}, s16[144,128]{1,0:T(8,128)(2,1)S(1)}, s16[144,128]{1,0:T(8,128)(2,1)S(1)}) custom-call(s32[1]{0:T(128)} %bitcast.me, f32[128,256]{1,0:T(8,128)S(1)} %get-tuple-element.19.product, bf16[4,512,256]{2,1,0:T(8,128)(2,1)S(1)} %get-tuple-element.20.gathered, ...), custom_call_target="tpu_custom_call" | custom-call | bytes 1024 | tf_op jit(solution)/shard_map/ladder/pallas_call | solution.py:195
  14.5 0.1 collective-permute-start.3
  14.5 1.7 %collective-permute-start.4 = (s16[144,128]{1,0:T(8,128)(2,1)S(1)}, s16[144,128]{1,0:T(8,128)(2,1)S(1)}, u32[]{:S(2)}, u32[]{:S(2)}) collective-permute-start(s16[144,128]{1,0:T(8,128)(2,1)S(1)} %get-tuple-element.24), channel_id=1, source_target_pairs={{0,2},{1,3},{2,0},{3,1},{4,6},{5,7},{6,4},{7,5},{8,10},{9,11},{10,... | collective-permute-start | bytes 110600 | tf_op jit(solution)/shard_map/ppermute | solution.py:140
  16.2 0.0 copy-start
  16.2 0.2 collective-permute-start.5
  16.4 0.0 collective-permute-done.7.far
  16.4 0.3 %ladder.3 = (f32[64,256]{1,0:T(8,128)S(1)}, s16[144,128]{1,0:T(8,128)(2,1)S(1)}, s16[144,128]{1,0:T(8,128)(2,1)S(1)}, s16[144,128]{1,0:T(8,128)(2,1)S(1)}) custom-call(s32[1]{0:T(128)} %bitcast.me, f32[128,256]{1,0:T(8,128)S(1)} %get-tuple-element.19.product, bf16[4,512,256]{2,1,0:T(8,128)(2,1)S(1)} %get-tuple-element.20.gathered, ...), custom_call_target="tpu_custom_call" | custom-call | flops 99999997952 | bytes 1024 | tf_op jit(solution)/shard_map/ladder/pallas_call | solution.py:195
  16.7 0.4 %collective-permute-start.10 = (s16[144,128]{1,0:T(8,128)(2,1)S(1)}, s16[144,128]{1,0:T(8,128)(2,1)S(1)}, u32[]{:S(2)}, u32[]{:S(2)}) collective-permute-start(s16[144,128]{1,0:T(8,128)(2,1)S(1)} %get-tuple-element.30), channel_id=1, source_target_pairs={{0,1},{1,0},{2,3},{3,2},{4,5},{5,4},{6,7},{7,6},{8,9},{9,8},{10,11... | collective-permute-start | bytes 110600 | tf_op jit(solution)/shard_map/ppermute | solution.py:140
  17.1 1.4 %collective-permute-start.8 = (s16[144,128]{1,0:T(8,128)(2,1)S(1)}, s16[144,128]{1,0:T(8,128)(2,1)S(1)}, u32[]{:S(2)}, u32[]{:S(2)}) collective-permute-start(s16[144,128]{1,0:T(8,128)(2,1)S(1)} %get-tuple-element.28), channel_id=1, source_target_pairs={{0,3},{1,2},{2,1},{3,0},{4,7},{5,6},{6,5},{7,4},{8,11},{9,10},{10,... | collective-permute-start | bytes 110600 | tf_op jit(solution)/shard_map/ppermute | solution.py:140
  18.5 0.0 collective-permute-done.3.rest_0_
  18.5 1.0 %collective-permute-start.9 = (s16[144,128]{1,0:T(8,128)(2,1)S(1)}, s16[144,128]{1,0:T(8,128)(2,1)S(1)}, u32[]{:S(2)}, u32[]{:S(2)}) collective-permute-start(s16[144,128]{1,0:T(8,128)(2,1)S(1)} %get-tuple-element.29), channel_id=1, source_target_pairs={{0,2},{1,3},{2,0},{3,1},{4,6},{5,7},{6,4},{7,5},{8,10},{9,11},{10,... | collective-permute-start | bytes 110600 | tf_op jit(solution)/shard_map/ppermute | solution.py:140
  19.5 0.0 collective-permute-done.4.rest_1_
  19.5 0.0 collective-permute-done.5.rest_2_
  19.5 0.0 copy-done
  19.6 0.0 collective-permute-done.10.rest_2_
  19.6 1.1 %collective-permute-done.8.rest_0_ = s16[144,128]{1,0:T(8,128)(2,1)S(1)} collective-permute-done((s16[144,128]{1,0:T(8,128)(2,1)S(1)}, s16[144,128]{1,0:T(8,128)(2,1)S(1)}, u32[]{:S(2)}, u32[]{:S(2)}) %collective-permute-start.8) | collective-permute-done | bytes 36896 | tf_op jit(solution)/shard_map/ppermute | solution.py:140
  20.7 1.8 %collective-permute-done.9.rest_1_ = s16[144,128]{1,0:T(8,128)(2,1)S(1)} collective-permute-done((s16[144,128]{1,0:T(8,128)(2,1)S(1)}, s16[144,128]{1,0:T(8,128)(2,1)S(1)}, u32[]{:S(2)}, u32[]{:S(2)}) %collective-permute-start.9) | collective-permute-done | bytes 36896 | tf_op jit(solution)/shard_map/ppermute | solution.py:140
  22.5 0.7 %finish.3 = f32[128,256]{1,0:T(8,128)} custom-call(f32[128,256]{1,0:T(8,128)S(1)} %finish.2.base, f32[64,256]{1,0:T(8,128)S(1)} %get-tuple-element.27.kept_sums, s16[144,128]{1,0:T(8,128)(2,1)S(1)} %collective-permute-done.8.rest_0_, s16[144,128]{1,0:T(8,128)(2,1)S(1)} %collective-permute-done.9.rest_1_, s16[144,128]{1,0:T(8,128)(2,1)S(1)} %collective-permute-done.10.rest_2_), custom_call_target="tpu_custom_call" | custom-call | tf_op jit(solution)/shard_map/finish/pallas_call | solution.py:206
  (2 shorter events, 0.0 us)
Async XLA Ops:
  1.0 7.6 %collective-permute-start.6 = (bf16[64,512]{1,0:T(8,128)(2,1)S(1)}, bf16[64,512]{1,0:T(8,128)(2,1)S(1)}, u32[]{:S(2)}, u32[]{:S(2)}) collective-permute-start(bf16[64,512]{1,0:T(8,128)(2,1)S(1)} %get-tuple-element.26), channel_id=1, source_target_pairs={{0,8},{4,12},{8,0},{12,4},{1,9},{5,13},{9,1},{13,5},{2,10},{6,14},... | collective-permute-start | bytes 196616 | tf_op jit(solution)/shard_map/ppermute | solution.py:140
  5.1 9.0 %collective-permute-start = (bf16[128,512]{1,0:T(8,128)(2,1)S(1)}, bf16[128,512]{1,0:T(8,128)(2,1)S(1)}, u32[]{:S(2)}, u32[]{:S(2)}) collective-permute-start(bf16[128,512]{1,0:T(8,128)(2,1)S(1)} %get-tuple-element.18.own.token), channel_id=1, source_target_pairs={{0,4},{4,0},{8,12},{12,8},{1,5},{5,1},{9,13},{13,9},{2,6},{6,2},{1... | collective-permute-start | bytes 393224 | tf_op jit(solution)/shard_map/ppermute | solution.py:140
  6.7 6.9 %collective-permute-start.1 = (bf16[64,512]{1,0:T(8,128)(2,1)S(1)}, bf16[64,512]{1,0:T(8,128)(2,1)S(1)}, u32[]{:S(2)}, u32[]{:S(2)}) collective-permute-start(bf16[64,512]{1,0:T(8,128)(2,1)S(1)} %get-tuple-element.21), channel_id=1, source_target_pairs={{0,12},{4,8},{8,4},{12,0},{1,13},{5,9},{9,5},{13,1},{2,14},{6,10},... | collective-permute-start | bytes 196616 | tf_op jit(solution)/shard_map/ppermute | solution.py:140
  6.7 7.4 %collective-permute-start.2 = (bf16[64,512]{1,0:T(8,128)(2,1)S(1)}, bf16[64,512]{1,0:T(8,128)(2,1)S(1)}, u32[]{:S(2)}, u32[]{:S(2)}) collective-permute-start(bf16[64,512]{1,0:T(8,128)(2,1)S(1)} %get-tuple-element.21), channel_id=1, source_target_pairs={{0,8},{4,12},{8,0},{12,4},{1,9},{5,13},{9,1},{13,5},{2,10},{6,14},... | collective-permute-start | bytes 196616 | tf_op jit(solution)/shard_map/ppermute | solution.py:140
  8.6 7.8 %collective-permute-start.7 = (bf16[64,512]{1,0:T(8,128)(2,1)S(1)}, bf16[64,512]{1,0:T(8,128)(2,1)S(1)}, u32[]{:S(2)}, u32[]{:S(2)}) collective-permute-start(bf16[64,512]{1,0:T(8,128)(2,1)S(1)} %after.1.near), channel_id=1, source_target_pairs={{0,4},{4,0},{8,12},{12,8},{1,5},{5,1},{9,13},{13,9},{2,6},{6,2},{1... | collective-permute-start | bytes 196616 | tf_op jit(solution)/shard_map/ppermute | solution.py:140
  14.5 4.1 %collective-permute-start.3 = (s16[144,128]{1,0:T(8,128)(2,1)S(1)}, s16[144,128]{1,0:T(8,128)(2,1)S(1)}, u32[]{:S(2)}, u32[]{:S(2)}) collective-permute-start(s16[144,128]{1,0:T(8,128)(2,1)S(1)} %get-tuple-element.23), channel_id=1, source_target_pairs={{0,3},{1,2},{2,1},{3,0},{4,7},{5,6},{6,5},{7,4},{8,11},{9,10},{10,... | collective-permute-start | bytes 110600 | tf_op jit(solution)/shard_map/ppermute | solution.py:140
  14.5 5.0 %collective-permute-start.4 = (s16[144,128]{1,0:T(8,128)(2,1)S(1)}, s16[144,128]{1,0:T(8,128)(2,1)S(1)}, u32[]{:S(2)}, u32[]{:S(2)}) collective-permute-start(s16[144,128]{1,0:T(8,128)(2,1)S(1)} %get-tuple-element.24), channel_id=1, source_target_pairs={{0,2},{1,3},{2,0},{3,1},{4,6},{5,7},{6,4},{7,5},{8,10},{9,11},{10,... | collective-permute-start | bytes 110600 | tf_op jit(solution)/shard_map/ppermute | solution.py:140
  16.2 3.3 %copy-start = (f32[128,256]{1,0:T(8,128)S(1)}, f32[128,256]{1,0:T(8,128)}, u32[]{:S(2)}) copy-start(f32[128,256]{1,0:T(8,128)} %base.1) | copy-start | bytes 393220
  16.2 3.3 %collective-permute-start.5 = (s16[144,128]{1,0:T(8,128)(2,1)S(1)}, s16[144,128]{1,0:T(8,128)(2,1)S(1)}, u32[]{:S(2)}, u32[]{:S(2)}) collective-permute-start(s16[144,128]{1,0:T(8,128)(2,1)S(1)} %get-tuple-element.25), channel_id=1, source_target_pairs={{0,1},{1,0},{2,3},{3,2},{4,5},{5,4},{6,7},{7,6},{8,9},{9,8},{10,11... | collective-permute-start | bytes 110600 | tf_op jit(solution)/shard_map/ppermute | solution.py:140
  16.7 2.9 %collective-permute-start.10 = (s16[144,128]{1,0:T(8,128)(2,1)S(1)}, s16[144,128]{1,0:T(8,128)(2,1)S(1)}, u32[]{:S(2)}, u32[]{:S(2)}) collective-permute-start(s16[144,128]{1,0:T(8,128)(2,1)S(1)} %get-tuple-element.30), channel_id=1, source_target_pairs={{0,1},{1,0},{2,3},{3,2},{4,5},{5,4},{6,7},{7,6},{8,9},{9,8},{10,11... | collective-permute-start | bytes 110600 | tf_op jit(solution)/shard_map/ppermute | solution.py:140
  17.1 3.5 %collective-permute-start.8 = (s16[144,128]{1,0:T(8,128)(2,1)S(1)}, s16[144,128]{1,0:T(8,128)(2,1)S(1)}, u32[]{:S(2)}, u32[]{:S(2)}) collective-permute-start(s16[144,128]{1,0:T(8,128)(2,1)S(1)} %get-tuple-element.28), channel_id=1, source_target_pairs={{0,3},{1,2},{2,1},{3,0},{4,7},{5,6},{6,5},{7,4},{8,11},{9,10},{10,... | collective-permute-start | bytes 110600 | tf_op jit(solution)/shard_map/ppermute | solution.py:140
  18.5 4.0 %collective-permute-start.9 = (s16[144,128]{1,0:T(8,128)(2,1)S(1)}, s16[144,128]{1,0:T(8,128)(2,1)S(1)}, u32[]{:S(2)}, u32[]{:S(2)}) collective-permute-start(s16[144,128]{1,0:T(8,128)(2,1)S(1)} %get-tuple-element.29), channel_id=1, source_target_pairs={{0,2},{1,3},{2,0},{3,1},{4,6},{5,7},{6,4},{7,5},{8,10},{9,11},{10,... | collective-permute-start | bytes 110600 | tf_op jit(solution)/shard_map/ppermute | solution.py:140

commit v12 on v9

--- a/solution.py
+++ b/solution.py
@@ -66,7 +66,7 @@
             start = pl.multiple_of(tile * TILE, TILE)
             for ab in range(tiles_ab):
                 part = held[pl.ds(start, TILE), ab * TILE : (ab + 1) * TILE]
-                on = (int_table[tile, ab] != 0).astype(jnp.float32).astype(part.dtype)
+                on = (int_table[ab, tile] != 0).astype(jnp.float32).astype(part.dtype)
                 gathered[n, slot * TILE : (slot + 1) * TILE, ab * TILE : (ab + 1) * TILE] = part * on
     product[...] = jnp.dot(own[...], gathered[row ^ col], preferred_element_type=jnp.float32)
 
@@ -134,7 +134,7 @@
     half_block = jax.ShapeDtypeStruct((pairs // 2, slots * TILE), doubles.dtype)
     message = jax.ShapeDtypeStruct((pairs * width // TILE + HEAD, TILE), jnp.int16)
     doubles, doubles_kept, integrals, integral_kept = (
-        pltpu.with_memory_space_constraint(x, pltpu.HBM) for x in (doubles, doubles_kept, integrals, integral_kept)
+        pltpu.with_memory_space_constraint(x, pltpu.HBM) for x in (doubles, doubles_kept, integrals, integral_kept.T)
     )
     packed, first, second = pl.pallas_call(
         functools.partial(pack_kernel, tiles, slots),
@@ -181,7 +181,7 @@
         cost_estimate=cost(10**11),
         name="ladder",
     )(me, product, gathered, pair, near_first, near_second, far_first, far_second)
-    messages = [swap(x, "cols", step) for step, x in reversed(list(enumerate(messages, 1)))]
+    messages = [swap(messages[step - 1], "cols", step) for step in (2, 3, 1)]
     return pl.pallas_call(
         finish_kernel,
         out_shape=sums_shape,

time: 22 us -> 21.9 us (level)
  local copies, waits for them, and re-layouts: 0.68 us -> 0.01 us
  starting transfers between devices: 12 us -> 12.3 us
  waiting for transfers between devices: 5.44 us -> 5.74 us
    unnamed x5 -> x2, local copies, waits for them, and re-layouts: 0.68 us -> 0.01 us
    ppermute x8, waiting for transfers between devices: 5.44 us -> 5.74 us  [swap(): return lax.ppermute(x, axis, [(i, i ^ step) for i in range(ROWS)])]
    ppermute x8, starting transfers between devices: 12 us -> 12.3 us  [swap(): return lax.ppermute(x, axis, [(i, i ^ step) for i in range(ROWS)])]
  transfers between devices with their start and end apart: 8 -> 8, of which waited for: 5 -> 5; matrix products, arithmetic and copies ran while one was open for 3% -> 0% of each run, Pallas kernels for 7% -> 7%
where the time goes in v12:
time: 21.9 us; the launch traced here: 21.7 us
  starting transfers between devices  12.3 us (56%)
  waiting for transfers between devices  5.74 us (26%)
  Pallas kernels  3.67 us (17%)
    ppermute x8, starting transfers between devices, swap(): return lax.ppermute(x, axis, [(i, i ^ step) for i in range(ROWS)])  12.3 us
    ppermute x8, waiting for transfers between devices, swap(): return lax.ppermute(x, axis, [(i, i ^ step) for i in range(ROWS)])  5.74 us
    pallas_call x1, Pallas kernels, local_few(): pl.pallas_call(functools.partial(prepare_kernel, tiles, slots), out_shape...  1.51 us
    pallas_call x1, Pallas kernels, local_few(): pl.pallas_call(functools.partial(pack_kernel, tiles, slots), out_shape=[j...  1 us
    pallas_call x1, Pallas kernels, local_few(): pl.pallas_call(finish_kernel, out_shape=sums_shape, in_specs=[VMEM] * (RO...  0.72 us
  transfers between devices with their start and end apart: 8, of which 5 were waited for; matrix products, arithmetic and copies ran while one was open for 0% of the time, Pallas kernels for 7%

profile of v12, /device:TPU:0, one launch (start us, length us, event | category | flops | bytes accessed | tf_op | source)
XLA Modules:
  0.0 21.7 jit_solution(14430273187850981813)
XLA Ops:
  0.0 1.0 %pack.1 = (bf16[128,512]{1,0:T(8,128)(2,1)S(1)}, bf16[64,512]{1,0:T(8,128)(2,1)S(1)}, bf16[64,512]{1,0:T(8,128)(2,1)S(1)}) custom-call(s32[1]{0:T(128)} %bitcast.me, s32[4,8]{1,0:T(4,128)} %kept.3, bf16[128,1024]{1,0:T(8,128)(2,1)} %doubles.1), custom_call_target="tpu_custom_call" | custom-call | tf_op jit(solution)/shard_map/pack/pallas_call | solution.py:139
  1.0 4.1 %collective-permute-start.2 = (bf16[64,512]{1,0:T(8,128)(2,1)S(1)}, bf16[64,512]{1,0:T(8,128)(2,1)S(1)}, u32[]{:S(2)}, u32[]{:S(2)}) collective-permute-start(bf16[64,512]{1,0:T(8,128)(2,1)S(1)} %get-tuple-element.18), channel_id=1, source_target_pairs={{0,8},{4,12},{8,0},{12,4},{1,9},{5,13},{9,1},{13,5},{2,10},{6,14},... | collective-permute-start | bytes 196616 | tf_op jit(solution)/shard_map/ppermute | solution.py:123
  5.1 1.6 %collective-permute-start = (bf16[128,512]{1,0:T(8,128)(2,1)S(1)}, bf16[128,512]{1,0:T(8,128)(2,1)S(1)}, u32[]{:S(2)}, u32[]{:S(2)}) collective-permute-start(bf16[128,512]{1,0:T(8,128)(2,1)S(1)} %get-tuple-element.14.own), channel_id=1, source_target_pairs={{0,4},{4,0},{8,12},{12,8},{1,5},{5,1},{9,13},{13,9},{2,6},{6,2},{1... | collective-permute-start | bytes 393224 | tf_op jit(solution)/shard_map/ppermute | solution.py:123
  6.7 0.0 collective-permute-start.3
  6.7 1.9 %collective-permute-start.1 = (bf16[64,512]{1,0:T(8,128)(2,1)S(1)}, bf16[64,512]{1,0:T(8,128)(2,1)S(1)}, u32[]{:S(2)}, u32[]{:S(2)}) collective-permute-start(bf16[64,512]{1,0:T(8,128)(2,1)S(1)} %get-tuple-element.17), channel_id=1, source_target_pairs={{0,8},{4,12},{8,0},{12,4},{1,9},{5,13},{9,1},{13,5},{2,10},{6,14},... | collective-permute-start | bytes 196616 | tf_op jit(solution)/shard_map/ppermute | solution.py:123
  8.6 0.0 collective-permute-done.2.near_second
  8.6 2.5 %collective-permute-start.4 = (bf16[64,512]{1,0:T(8,128)(2,1)S(1)}, bf16[64,512]{1,0:T(8,128)(2,1)S(1)}, u32[]{:S(2)}, u32[]{:S(2)}) collective-permute-start(bf16[64,512]{1,0:T(8,128)(2,1)S(1)} %collective-permute-done.2.near_second), channel_id=1, source_target_pairs={{0,4},{4,0},{8,12},{12,8},{1,5},{5,1},{9,13},{13,9},{2,6},{6,2},{1... | collective-permute-start | bytes 196616 | tf_op jit(solution)/shard_map/ppermute | solution.py:123
  11.1 1.5 %prepare.1 = (bf16[4,512,256]{2,1,0:T(8,128)(2,1)S(1)}, f32[128,256]{1,0:T(8,128)S(1)}) custom-call(s32[1]{0:T(128)} %bitcast.me, s32[4,8]{1,0:T(4,128)} %kept.3, s32[2,8]{1,0:T(2,128)} %bitcast.2, bf16[1024,256]{1,0:T(8,128)(2,1)} %integrals.1, bf16[128,512]{1,0:T(8,128)(2,1)S(1)} %get-tuple-element.14.own), custom_call_target="tpu_custom_call" | custom-call | bytes 1024 | tf_op jit(solution)/shard_map/prepare/pallas_call | solution.py:158
  12.6 1.0 %collective-permute-done.3.far_first = bf16[64,512]{1,0:T(8,128)(2,1)S(1)} collective-permute-done((bf16[64,512]{1,0:T(8,128)(2,1)S(1)}, bf16[64,512]{1,0:T(8,128)(2,1)S(1)}, u32[]{:S(2)}, u32[]{:S(2)}) %collective-permute-start.3) | collective-permute-done | bytes 65568 | tf_op jit(solution)/shard_map/ppermute | solution.py:123
  13.6 0.5 %collective-permute-done.1.near_first = bf16[64,512]{1,0:T(8,128)(2,1)S(1)} collective-permute-done((bf16[64,512]{1,0:T(8,128)(2,1)S(1)}, bf16[64,512]{1,0:T(8,128)(2,1)S(1)}, u32[]{:S(2)}, u32[]{:S(2)}) %collective-permute-start.1) | collective-permute-done | bytes 65568 | tf_op jit(solution)/shard_map/ppermute | solution.py:123
  14.1 0.5 %collective-permute-done.4.far_second = bf16[64,512]{1,0:T(8,128)(2,1)S(1)} collective-permute-done((bf16[64,512]{1,0:T(8,128)(2,1)S(1)}, bf16[64,512]{1,0:T(8,128)(2,1)S(1)}, u32[]{:S(2)}, u32[]{:S(2)}) %collective-permute-start.4) | collective-permute-done | bytes 65568 | tf_op jit(solution)/shard_map/ppermute | solution.py:123
  14.7 0.0 collective-permute-done.pair
  14.7 0.0 copy-start
  14.7 0.4 %ladder.1 = (f32[128,256]{1,0:T(8,128)S(1)}, s16[272,128]{1,0:T(8,128)(2,1)S(1)}, s16[272,128]{1,0:T(8,128)(2,1)S(1)}, s16[272,128]{1,0:T(8,128)(2,1)S(1)}) custom-call(s32[1]{0:T(128)} %bitcast.me, f32[128,256]{1,0:T(8,128)S(1)} %get-tuple-element.15.product, bf16[4,512,256]{2,1,0:T(8,128)(2,1)S(1)} %get-tuple-element.16.gathered, ...), custom_call_target="tpu_custom_call" | custom-call | flops 99999997952 | bytes 1024 | tf_op jit(solution)/shard_map/ladder/pallas_call | solution.py:174
  15.1 1.8 %collective-permute-start.5 = (s16[272,128]{1,0:T(8,128)(2,1)S(1)}, s16[272,128]{1,0:T(8,128)(2,1)S(1)}, u32[]{:S(2)}, u32[]{:S(2)}) collective-permute-start(s16[272,128]{1,0:T(8,128)(2,1)S(1)} %get-tuple-element.20), channel_id=1, source_target_pairs={{0,2},{1,3},{2,0},{3,1},{4,6},{5,7},{6,4},{7,5},{8,10},{9,11},{10,... | collective-permute-start | bytes 208904 | tf_op jit(solution)/shard_map/ppermute | solution.py:123
  17.0 0.0 collective-permute-start.6
  17.0 0.4 %collective-permute-start.7 = (s16[272,128]{1,0:T(8,128)(2,1)S(1)}, s16[272,128]{1,0:T(8,128)(2,1)S(1)}, u32[]{:S(2)}, u32[]{:S(2)}) collective-permute-start(s16[272,128]{1,0:T(8,128)(2,1)S(1)} %get-tuple-element.22), channel_id=1, source_target_pairs={{0,1},{1,0},{2,3},{3,2},{4,5},{5,4},{6,7},{7,6},{8,9},{9,8},{10,11... | collective-permute-start | bytes 208904 | tf_op jit(solution)/shard_map/ppermute | solution.py:123
  17.3 2.2 %collective-permute-done.5.rest_0_ = s16[272,128]{1,0:T(8,128)(2,1)S(1)} collective-permute-done((s16[272,128]{1,0:T(8,128)(2,1)S(1)}, s16[272,128]{1,0:T(8,128)(2,1)S(1)}, u32[]{:S(2)}, u32[]{:S(2)}) %collective-permute-start.5) | collective-permute-done | bytes 69664 | tf_op jit(solution)/shard_map/ppermute | solution.py:123
  19.5 1.5 %collective-permute-done.6.rest_1_ = s16[272,128]{1,0:T(8,128)(2,1)S(1)} collective-permute-done((s16[272,128]{1,0:T(8,128)(2,1)S(1)}, s16[272,128]{1,0:T(8,128)(2,1)S(1)}, u32[]{:S(2)}, u32[]{:S(2)}) %collective-permute-start.6) | collective-permute-done | bytes 69664 | tf_op jit(solution)/shard_map/ppermute | solution.py:123
  21.0 0.0 collective-permute-done.7.rest_2_
  21.0 0.0 copy-done
  21.0 0.7 %finish.1 = f32[128,256]{1,0:T(8,128)} custom-call(f32[128,256]{1,0:T(8,128)S(1)} %copy-done, f32[128,256]{1,0:T(8,128)S(1)} %get-tuple-element.19.kept_sums, s16[272,128]{1,0:T(8,128)(2,1)S(1)} %collective-permute-done.5.rest_0_, s16[272,128]{1,0:T(8,128)(2,1)S(1)} %collective-permute-done.6.rest_1_, s16[272,128]{1,0:T(8,128)(2,1)S(1)} %collective-permute-done.7.rest_2_), custom_call_target="tpu_custom_call" | custom-call | tf_op jit(solution)/shard_map/finish/pallas_call | solution.py:185
Async XLA Ops:
  1.0 7.6 %collective-permute-start.2 = (bf16[64,512]{1,0:T(8,128)(2,1)S(1)}, bf16[64,512]{1,0:T(8,128)(2,1)S(1)}, u32[]{:S(2)}, u32[]{:S(2)}) collective-permute-start(bf16[64,512]{1,0:T(8,128)(2,1)S(1)} %get-tuple-element.18), channel_id=1, source_target_pairs={{0,8},{4,12},{8,0},{12,4},{1,9},{5,13},{9,1},{13,5},{2,10},{6,14},... | collective-permute-start | bytes 196616 | tf_op jit(solution)/shard_map/ppermute | solution.py:123
  5.1 9.6 %collective-permute-start = (bf16[128,512]{1,0:T(8,128)(2,1)S(1)}, bf16[128,512]{1,0:T(8,128)(2,1)S(1)}, u32[]{:S(2)}, u32[]{:S(2)}) collective-permute-start(bf16[128,512]{1,0:T(8,128)(2,1)S(1)} %get-tuple-element.14.own), channel_id=1, source_target_pairs={{0,4},{4,0},{8,12},{12,8},{1,5},{5,1},{9,13},{13,9},{2,6},{6,2},{1... | collective-permute-start | bytes 393224 | tf_op jit(solution)/shard_map/ppermute | solution.py:123
  6.7 6.9 %collective-permute-start.3 = (bf16[64,512]{1,0:T(8,128)(2,1)S(1)}, bf16[64,512]{1,0:T(8,128)(2,1)S(1)}, u32[]{:S(2)}, u32[]{:S(2)}) collective-permute-start(bf16[64,512]{1,0:T(8,128)(2,1)S(1)} %get-tuple-element.17), channel_id=1, source_target_pairs={{0,12},{4,8},{8,4},{12,0},{1,13},{5,9},{9,5},{13,1},{2,14},{6,10},... | collective-permute-start | bytes 196616 | tf_op jit(solution)/shard_map/ppermute | solution.py:123
  6.7 7.4 %collective-permute-start.1 = (bf16[64,512]{1,0:T(8,128)(2,1)S(1)}, bf16[64,512]{1,0:T(8,128)(2,1)S(1)}, u32[]{:S(2)}, u32[]{:S(2)}) collective-permute-start(bf16[64,512]{1,0:T(8,128)(2,1)S(1)} %get-tuple-element.17), channel_id=1, source_target_pairs={{0,8},{4,12},{8,0},{12,4},{1,9},{5,13},{9,1},{13,5},{2,10},{6,14},... | collective-permute-start | bytes 196616 | tf_op jit(solution)/shard_map/ppermute | solution.py:123
  8.6 6.1 %collective-permute-start.4 = (bf16[64,512]{1,0:T(8,128)(2,1)S(1)}, bf16[64,512]{1,0:T(8,128)(2,1)S(1)}, u32[]{:S(2)}, u32[]{:S(2)}) collective-permute-start(bf16[64,512]{1,0:T(8,128)(2,1)S(1)} %collective-permute-done.2.near_second), channel_id=1, source_target_pairs={{0,4},{4,0},{8,12},{12,8},{1,5},{5,1},{9,13},{13,9},{2,6},{6,2},{1... | collective-permute-start | bytes 196616 | tf_op jit(solution)/shard_map/ppermute | solution.py:123
  14.7 6.3 %copy-start = (f32[128,256]{1,0:T(8,128)S(1)}, f32[128,256]{1,0:T(8,128)}, u32[]{:S(2)}) copy-start(f32[128,256]{1,0:T(8,128)} %residual.1) | copy-start | bytes 393220
  15.1 4.4 %collective-permute-start.5 = (s16[272,128]{1,0:T(8,128)(2,1)S(1)}, s16[272,128]{1,0:T(8,128)(2,1)S(1)}, u32[]{:S(2)}, u32[]{:S(2)}) collective-permute-start(s16[272,128]{1,0:T(8,128)(2,1)S(1)} %get-tuple-element.20), channel_id=1, source_target_pairs={{0,2},{1,3},{2,0},{3,1},{4,6},{5,7},{6,4},{7,5},{8,10},{9,11},{10,... | collective-permute-start | bytes 208904 | tf_op jit(solution)/shard_map/ppermute | solution.py:123
  17.0 4.0 %collective-permute-start.6 = (s16[272,128]{1,0:T(8,128)(2,1)S(1)}, s16[272,128]{1,0:T(8,128)(2,1)S(1)}, u32[]{:S(2)}, u32[]{:S(2)}) collective-permute-start(s16[272,128]{1,0:T(8,128)(2,1)S(1)} %get-tuple-element.21), channel_id=1, source_target_pairs={{0,3},{1,2},{2,1},{3,0},{4,7},{5,6},{6,5},{7,4},{8,11},{9,10},{10,... | collective-permute-start | bytes 208904 | tf_op jit(solution)/shard_map/ppermute | solution.py:123
  17.0 4.0 %collective-permute-start.7 = (s16[272,128]{1,0:T(8,128)(2,1)S(1)}, s16[272,128]{1,0:T(8,128)(2,1)S(1)}, u32[]{:S(2)}, u32[]{:S(2)}) collective-permute-start(s16[272,128]{1,0:T(8,128)(2,1)S(1)} %get-tuple-element.22), channel_id=1, source_target_pairs={{0,1},{1,0},{2,3},{3,2},{4,5},{5,4},{6,7},{7,6},{8,9},{9,8},{10,11... | collective-permute-start | bytes 208904 | tf_op jit(solution)/shard_map/ppermute | solution.py:123

commit v13 on v12

--- a/solution.py
+++ b/solution.py
@@ -14,7 +14,6 @@
 STEPS = 8
 
 VMEM = pl.BlockSpec(memory_space=pltpu.VMEM)
-SMEM = pl.BlockSpec(memory_space=pltpu.SMEM)
 HBM = pl.BlockSpec(memory_space=pltpu.HBM)
 PARAMS = pltpu.CompilerParams(vmem_limit_bytes=8 * 1024 * 1024)
 ROWS = 4
@@ -31,13 +30,13 @@
         at = at + kept[row, tile]
 
 
-def pack_kernel(tiles, slots, me, kept, doubles, packed, first, second, table, block, places, sems):
+def pack_kernel(tiles, slots, kept, doubles, packed, first, second, table, block, places, sems):
     table_copy = pltpu.make_async_copy(kept, table, sems.at[0])
     block_copy = pltpu.make_async_copy(doubles, block, sems.at[1])
     table_copy.start()
     block_copy.start()
     table_copy.wait()
-    list_kept(table, me[0] // ROWS, tiles, places)
+    list_kept(table, lax.axis_index("rows"), tiles, places)
     block_copy.wait()
     half = first.shape[0]
     for slot in range(slots):
@@ -48,7 +47,7 @@
         second[:, to] = tile[half:]
 
 
-def prepare_kernel(tiles, slots, me, kept, int_kept, integrals, own, gathered, product, table, int_table, held, places, sems):
+def prepare_kernel(tiles, slots, kept, int_kept, integrals, own, gathered, product, table, int_table, held, places, sems):
     copies = [
         pltpu.make_async_copy(*pair, sems.at[i])
         for i, pair in enumerate(((kept, table), (int_kept, int_table), (integrals, held)))
@@ -57,7 +56,7 @@
         copy.start()
     for copy in copies:
         copy.wait()
-    row, col = me[0] // ROWS, me[0] % ROWS
+    row, col = lax.axis_index("rows"), lax.axis_index("cols")
     tiles_ab = integrals.shape[1] // TILE
     for n in range(ROWS):
         list_kept(table, col ^ n, tiles, places)
@@ -96,9 +95,9 @@
     return jnp.concatenate(parts, axis=1)
 
 
-def ladder_kernel(me, product, gathered, pair, near_first, near_second, far_first, far_second, kept_sums, *rest):
+def ladder_kernel(product, gathered, pair, near_first, near_second, far_first, far_second, kept_sums, *rest):
     outs, sums = rest[:-1], rest[-1]
-    mine = me[0] // ROWS ^ me[0] % ROWS
+    mine = lax.axis_index("rows") ^ lax.axis_index("cols")
     half = near_first.shape[0]
     sums[mine] = product[...]
     sums[mine ^ 1] = jnp.dot(pair[...], gathered[mine ^ 1], preferred_element_type=jnp.float32)
@@ -124,7 +123,6 @@
 
 
 def local_few(doubles, doubles_kept, integrals, integral_kept, residual):
-    me = (lax.axis_index("rows") * ROWS + lax.axis_index("cols")).astype(jnp.int32).reshape(1)
     pairs, cd_local = doubles.shape
     width = integrals.shape[1]
     tiles = cd_local // TILE
@@ -139,7 +137,7 @@
     packed, first, second = pl.pallas_call(
         functools.partial(pack_kernel, tiles, slots),
         out_shape=[jax.ShapeDtypeStruct((pairs, slots * TILE), doubles.dtype), half_block, half_block],
-        in_specs=[SMEM, HBM, HBM],
+        in_specs=[HBM, HBM],
         out_specs=[VMEM] * 3,
         scratch_shapes=[
             pltpu.SMEM(doubles_kept.shape, jnp.int32),
@@ -149,7 +147,7 @@
         ],
         compiler_params=PARAMS,
         name="pack",
-    )(me, doubles_kept, doubles)
+    )(doubles_kept, doubles)
     near_second = swap(second, "rows", 2)
     pair = swap(packed, "rows", 1)
     far_first = swap(first, "rows", 3)
@@ -158,7 +156,7 @@
     gathered, product = pl.pallas_call(
         functools.partial(prepare_kernel, tiles, slots),
         out_shape=[jax.ShapeDtypeStruct((ROWS, slots * TILE, width), integrals.dtype), sums_shape],
-        in_specs=[SMEM, HBM, HBM, HBM, VMEM],
+        in_specs=[HBM, HBM, HBM, VMEM],
         out_specs=[VMEM] * 2,
         scratch_shapes=[
             pltpu.SMEM(doubles_kept.shape, jnp.int32),
@@ -170,17 +168,17 @@
         compiler_params=PARAMS,
         cost_estimate=cost(0),
         name="prepare",
-    )(me, doubles_kept, integral_kept, integrals, packed)
+    )(doubles_kept, integral_kept, integrals, packed)
     kept_sums, *messages = pl.pallas_call(
         ladder_kernel,
         out_shape=[sums_shape] + [message] * (ROWS - 1),
-        in_specs=[SMEM] + [VMEM] * 7,
+        in_specs=[VMEM] * 7,
         out_specs=[VMEM] * ROWS,
         scratch_shapes=[pltpu.VMEM((ROWS, pairs, width), jnp.float32)],
         compiler_params=PARAMS,
         cost_estimate=cost(10**11),
         name="ladder",
-    )(me, product, gathered, pair, near_first, near_second, far_first, far_second)
+    )(product, gathered, pair, near_first, near_second, far_first, far_second)
     messages = [swap(messages[step - 1], "cols", step) for step in (2, 3, 1)]
     return pl.pallas_call(
         finish_kernel,

time: 21.9 us -> 21.9 us (level)
  no operation moved by 1% of the time
where the time goes in v13:
time: 21.9 us; the launch traced here: 21.7 us
  starting transfers between devices  12.3 us (56%)
  waiting for transfers between devices  5.74 us (26%)
  Pallas kernels  3.68 us (17%)
    ppermute x8, starting transfers between devices, swap(): return lax.ppermute(x, axis, [(i, i ^ step) for i in range(ROWS)])  12.3 us
    ppermute x8, waiting for transfers between devices, swap(): return lax.ppermute(x, axis, [(i, i ^ step) for i in range(ROWS)])  5.74 us
    pallas_call x1, Pallas kernels, local_few(): pl.pallas_call(functools.partial(prepare_kernel, tiles, slots), out_shape...  1.52 us
    pallas_call x1, Pallas kernels, local_few(): pl.pallas_call(functools.partial(pack_kernel, tiles, slots), out_shape=[j...  1 us
    pallas_call x1, Pallas kernels, local_few(): pl.pallas_call(finish_kernel, out_shape=sums_shape, in_specs=[VMEM] * (RO...  0.72 us
  transfers between devices with their start and end apart: 8, of which 5 were waited for; matrix products, arithmetic and copies ran while one was open for 0% of the time, Pallas kernels for 7%

profile of v13, /device:TPU:0, one launch (start us, length us, event | category | flops | bytes accessed | tf_op | source)
XLA Modules:
  0.0 21.7 jit_solution(7841172880555276830)
XLA Ops:
  0.0 1.0 %pack.1 = (bf16[128,512]{1,0:T(8,128)(2,1)S(1)}, bf16[64,512]{1,0:T(8,128)(2,1)S(1)}, bf16[64,512]{1,0:T(8,128)(2,1)S(1)}) custom-call(s32[4,8]{1,0:T(4,128)} %kept.3, bf16[128,1024]{1,0:T(8,128)(2,1)} %doubles.1), custom_call_target="tpu_custom_call" | custom-call | tf_op jit(solution)/shard_map/pack/pallas_call | solution.py:137
  1.0 4.1 %collective-permute-start.2 = (bf16[64,512]{1,0:T(8,128)(2,1)S(1)}, bf16[64,512]{1,0:T(8,128)(2,1)S(1)}, u32[]{:S(2)}, u32[]{:S(2)}) collective-permute-start(bf16[64,512]{1,0:T(8,128)(2,1)S(1)} %get-tuple-element.18), channel_id=1, source_target_pairs={{0,8},{4,12},{8,0},{12,4},{1,9},{5,13},{9,1},{13,5},{2,10},{6,14},... | collective-permute-start | bytes 196616 | tf_op jit(solution)/shard_map/ppermute | solution.py:122
  5.1 1.6 %collective-permute-start = (bf16[128,512]{1,0:T(8,128)(2,1)S(1)}, bf16[128,512]{1,0:T(8,128)(2,1)S(1)}, u32[]{:S(2)}, u32[]{:S(2)}) collective-permute-start(bf16[128,512]{1,0:T(8,128)(2,1)S(1)} %get-tuple-element.14.own), channel_id=1, source_target_pairs={{0,4},{4,0},{8,12},{12,8},{1,5},{5,1},{9,13},{13,9},{2,6},{6,2},{1... | collective-permute-start | bytes 393224 | tf_op jit(solution)/shard_map/ppermute | solution.py:122
  6.7 0.0 collective-permute-start.3
  6.7 1.9 %collective-permute-start.1 = (bf16[64,512]{1,0:T(8,128)(2,1)S(1)}, bf16[64,512]{1,0:T(8,128)(2,1)S(1)}, u32[]{:S(2)}, u32[]{:S(2)}) collective-permute-start(bf16[64,512]{1,0:T(8,128)(2,1)S(1)} %get-tuple-element.17), channel_id=1, source_target_pairs={{0,8},{4,12},{8,0},{12,4},{1,9},{5,13},{9,1},{13,5},{2,10},{6,14},... | collective-permute-start | bytes 196616 | tf_op jit(solution)/shard_map/ppermute | solution.py:122
  8.6 0.0 collective-permute-done.2.near_second
  8.6 2.5 %collective-permute-start.4 = (bf16[64,512]{1,0:T(8,128)(2,1)S(1)}, bf16[64,512]{1,0:T(8,128)(2,1)S(1)}, u32[]{:S(2)}, u32[]{:S(2)}) collective-permute-start(bf16[64,512]{1,0:T(8,128)(2,1)S(1)} %collective-permute-done.2.near_second), channel_id=1, source_target_pairs={{0,4},{4,0},{8,12},{12,8},{1,5},{5,1},{9,13},{13,9},{2,6},{6,2},{1... | collective-permute-start | bytes 196616 | tf_op jit(solution)/shard_map/ppermute | solution.py:122
  11.1 1.5 %prepare.1 = (bf16[4,512,256]{2,1,0:T(8,128)(2,1)S(1)}, f32[128,256]{1,0:T(8,128)S(1)}) custom-call(s32[4,8]{1,0:T(4,128)} %kept.3, s32[2,8]{1,0:T(2,128)} %bitcast.1, bf16[1024,256]{1,0:T(8,128)(2,1)} %integrals.1, bf16[128,512]{1,0:T(8,128)(2,1)S(1)} %get-tuple-element.14.own), custom_call_target="tpu_custom_call" | custom-call | bytes 1024 | tf_op jit(solution)/shard_map/prepare/pallas_call | solution.py:156
  12.6 1.0 %collective-permute-done.3.far_first = bf16[64,512]{1,0:T(8,128)(2,1)S(1)} collective-permute-done((bf16[64,512]{1,0:T(8,128)(2,1)S(1)}, bf16[64,512]{1,0:T(8,128)(2,1)S(1)}, u32[]{:S(2)}, u32[]{:S(2)}) %collective-permute-start.3) | collective-permute-done | bytes 65568 | tf_op jit(solution)/shard_map/ppermute | solution.py:122
  13.6 0.5 %collective-permute-done.1.near_first = bf16[64,512]{1,0:T(8,128)(2,1)S(1)} collective-permute-done((bf16[64,512]{1,0:T(8,128)(2,1)S(1)}, bf16[64,512]{1,0:T(8,128)(2,1)S(1)}, u32[]{:S(2)}, u32[]{:S(2)}) %collective-permute-start.1) | collective-permute-done | bytes 65568 | tf_op jit(solution)/shard_map/ppermute | solution.py:122
  14.1 0.5 %collective-permute-done.4.far_second = bf16[64,512]{1,0:T(8,128)(2,1)S(1)} collective-permute-done((bf16[64,512]{1,0:T(8,128)(2,1)S(1)}, bf16[64,512]{1,0:T(8,128)(2,1)S(1)}, u32[]{:S(2)}, u32[]{:S(2)}) %collective-permute-start.4) | collective-permute-done | bytes 65568 | tf_op jit(solution)/shard_map/ppermute | solution.py:122
  14.7 0.0 collective-permute-done.pair
  14.7 0.0 copy-start
  14.7 0.4 %ladder.1 = (f32[128,256]{1,0:T(8,128)S(1)}, s16[272,128]{1,0:T(8,128)(2,1)S(1)}, s16[272,128]{1,0:T(8,128)(2,1)S(1)}, s16[272,128]{1,0:T(8,128)(2,1)S(1)}) custom-call(f32[128,256]{1,0:T(8,128)S(1)} %get-tuple-element.15.product, bf16[4,512,256]{2,1,0:T(8,128)(2,1)S(1)} %get-tuple-element.16.gathered, bf16[128,512]{1,0:T(8,128)(2,1)S(1)} %collective-permute-done.pair, ...), custom_call_target="tpu_custom_call" | custom-call | flops 99999997952 | bytes 1024 | tf_op jit(solution)/shard_map/ladder/pallas_call | solution.py:172
  15.1 1.8 %collective-permute-start.5 = (s16[272,128]{1,0:T(8,128)(2,1)S(1)}, s16[272,128]{1,0:T(8,128)(2,1)S(1)}, u32[]{:S(2)}, u32[]{:S(2)}) collective-permute-start(s16[272,128]{1,0:T(8,128)(2,1)S(1)} %get-tuple-element.20), channel_id=1, source_target_pairs={{0,2},{1,3},{2,0},{3,1},{4,6},{5,7},{6,4},{7,5},{8,10},{9,11},{10,... | collective-permute-start | bytes 208904 | tf_op jit(solution)/shard_map/ppermute | solution.py:122
  17.0 0.0 collective-permute-start.6
  17.0 0.4 %collective-permute-start.7 = (s16[272,128]{1,0:T(8,128)(2,1)S(1)}, s16[272,128]{1,0:T(8,128)(2,1)S(1)}, u32[]{:S(2)}, u32[]{:S(2)}) collective-permute-start(s16[272,128]{1,0:T(8,128)(2,1)S(1)} %get-tuple-element.22), channel_id=1, source_target_pairs={{0,1},{1,0},{2,3},{3,2},{4,5},{5,4},{6,7},{7,6},{8,9},{9,8},{10,11... | collective-permute-start | bytes 208904 | tf_op jit(solution)/shard_map/ppermute | solution.py:122
  17.3 2.2 %collective-permute-done.5.rest_0_ = s16[272,128]{1,0:T(8,128)(2,1)S(1)} collective-permute-done((s16[272,128]{1,0:T(8,128)(2,1)S(1)}, s16[272,128]{1,0:T(8,128)(2,1)S(1)}, u32[]{:S(2)}, u32[]{:S(2)}) %collective-permute-start.5) | collective-permute-done | bytes 69664 | tf_op jit(solution)/shard_map/ppermute | solution.py:122
  19.5 1.5 %collective-permute-done.6.rest_1_ = s16[272,128]{1,0:T(8,128)(2,1)S(1)} collective-permute-done((s16[272,128]{1,0:T(8,128)(2,1)S(1)}, s16[272,128]{1,0:T(8,128)(2,1)S(1)}, u32[]{:S(2)}, u32[]{:S(2)}) %collective-permute-start.6) | collective-permute-done | bytes 69664 | tf_op jit(solution)/shard_map/ppermute | solution.py:122
  21.0 0.0 collective-permute-done.7.rest_2_
  21.0 0.0 copy-done
  21.0 0.7 %finish.1 = f32[128,256]{1,0:T(8,128)} custom-call(f32[128,256]{1,0:T(8,128)S(1)} %copy-done, f32[128,256]{1,0:T(8,128)S(1)} %get-tuple-element.19.kept_sums, s16[272,128]{1,0:T(8,128)(2,1)S(1)} %collective-permute-done.5.rest_0_, s16[272,128]{1,0:T(8,128)(2,1)S(1)} %collective-permute-done.6.rest_1_, s16[272,128]{1,0:T(8,128)(2,1)S(1)} %collective-permute-done.7.rest_2_), custom_call_target="tpu_custom_call" | custom-call | tf_op jit(solution)/shard_map/finish/pallas_call | solution.py:183
Async XLA Ops:
  1.0 7.6 %collective-permute-start.2 = (bf16[64,512]{1,0:T(8,128)(2,1)S(1)}, bf16[64,512]{1,0:T(8,128)(2,1)S(1)}, u32[]{:S(2)}, u32[]{:S(2)}) collective-permute-start(bf16[64,512]{1,0:T(8,128)(2,1)S(1)} %get-tuple-element.18), channel_id=1, source_target_pairs={{0,8},{4,12},{8,0},{12,4},{1,9},{5,13},{9,1},{13,5},{2,10},{6,14},... | collective-permute-start | bytes 196616 | tf_op jit(solution)/shard_map/ppermute | solution.py:122
  5.1 9.6 %collective-permute-start = (bf16[128,512]{1,0:T(8,128)(2,1)S(1)}, bf16[128,512]{1,0:T(8,128)(2,1)S(1)}, u32[]{:S(2)}, u32[]{:S(2)}) collective-permute-start(bf16[128,512]{1,0:T(8,128)(2,1)S(1)} %get-tuple-element.14.own), channel_id=1, source_target_pairs={{0,4},{4,0},{8,12},{12,8},{1,5},{5,1},{9,13},{13,9},{2,6},{6,2},{1... | collective-permute-start | bytes 393224 | tf_op jit(solution)/shard_map/ppermute | solution.py:122
  6.7 6.9 %collective-permute-start.3 = (bf16[64,512]{1,0:T(8,128)(2,1)S(1)}, bf16[64,512]{1,0:T(8,128)(2,1)S(1)}, u32[]{:S(2)}, u32[]{:S(2)}) collective-permute-start(bf16[64,512]{1,0:T(8,128)(2,1)S(1)} %get-tuple-element.17), channel_id=1, source_target_pairs={{0,12},{4,8},{8,4},{12,0},{1,13},{5,9},{9,5},{13,1},{2,14},{6,10},... | collective-permute-start | bytes 196616 | tf_op jit(solution)/shard_map/ppermute | solution.py:122
  6.7 7.4 %collective-permute-start.1 = (bf16[64,512]{1,0:T(8,128)(2,1)S(1)}, bf16[64,512]{1,0:T(8,128)(2,1)S(1)}, u32[]{:S(2)}, u32[]{:S(2)}) collective-permute-start(bf16[64,512]{1,0:T(8,128)(2,1)S(1)} %get-tuple-element.17), channel_id=1, source_target_pairs={{0,8},{4,12},{8,0},{12,4},{1,9},{5,13},{9,1},{13,5},{2,10},{6,14},... | collective-permute-start | bytes 196616 | tf_op jit(solution)/shard_map/ppermute | solution.py:122
  8.6 6.1 %collective-permute-start.4 = (bf16[64,512]{1,0:T(8,128)(2,1)S(1)}, bf16[64,512]{1,0:T(8,128)(2,1)S(1)}, u32[]{:S(2)}, u32[]{:S(2)}) collective-permute-start(bf16[64,512]{1,0:T(8,128)(2,1)S(1)} %collective-permute-done.2.near_second), channel_id=1, source_target_pairs={{0,4},{4,0},{8,12},{12,8},{1,5},{5,1},{9,13},{13,9},{2,6},{6,2},{1... | collective-permute-start | bytes 196616 | tf_op jit(solution)/shard_map/ppermute | solution.py:122
  14.7 6.3 %copy-start = (f32[128,256]{1,0:T(8,128)S(1)}, f32[128,256]{1,0:T(8,128)}, u32[]{:S(2)}) copy-start(f32[128,256]{1,0:T(8,128)} %residual.1) | copy-start | bytes 393220
  15.1 4.4 %collective-permute-start.5 = (s16[272,128]{1,0:T(8,128)(2,1)S(1)}, s16[272,128]{1,0:T(8,128)(2,1)S(1)}, u32[]{:S(2)}, u32[]{:S(2)}) collective-permute-start(s16[272,128]{1,0:T(8,128)(2,1)S(1)} %get-tuple-element.20), channel_id=1, source_target_pairs={{0,2},{1,3},{2,0},{3,1},{4,6},{5,7},{6,4},{7,5},{8,10},{9,11},{10,... | collective-permute-start | bytes 208904 | tf_op jit(solution)/shard_map/ppermute | solution.py:122
  17.0 4.0 %collective-permute-start.6 = (s16[272,128]{1,0:T(8,128)(2,1)S(1)}, s16[272,128]{1,0:T(8,128)(2,1)S(1)}, u32[]{:S(2)}, u32[]{:S(2)}) collective-permute-start(s16[272,128]{1,0:T(8,128)(2,1)S(1)} %get-tuple-element.21), channel_id=1, source_target_pairs={{0,3},{1,2},{2,1},{3,0},{4,7},{5,6},{6,5},{7,4},{8,11},{9,10},{10,... | collective-permute-start | bytes 208904 | tf_op jit(solution)/shard_map/ppermute | solution.py:122
  17.0 4.0 %collective-permute-start.7 = (s16[272,128]{1,0:T(8,128)(2,1)S(1)}, s16[272,128]{1,0:T(8,128)(2,1)S(1)}, u32[]{:S(2)}, u32[]{:S(2)}) collective-permute-start(s16[272,128]{1,0:T(8,128)(2,1)S(1)} %get-tuple-element.22), channel_id=1, source_target_pairs={{0,1},{1,0},{2,3},{3,2},{4,5},{5,4},{6,7},{7,6},{8,9},{9,8},{10,11... | collective-permute-start | bytes 208904 | tf_op jit(solution)/shard_map/ppermute | solution.py:122

commit v14 on v13

--- a/solution.py
+++ b/solution.py
@@ -95,27 +95,55 @@
     return jnp.concatenate(parts, axis=1)
 
 
-def ladder_kernel(product, gathered, pair, near_first, near_second, far_first, far_second, kept_sums, *rest):
-    outs, sums = rest[:-1], rest[-1]
+def half_of(ref, half):
+    size = ref.shape[0] // 2
+    return ref.at[pl.ds(pl.multiple_of(half * size, size), size)]
+
+
+def early_half(step):
+    return 1 - step % 2
+
+
+def half_sums(late, product, gathered, pair, near, far, sums):
     mine = lax.axis_index("rows") ^ lax.axis_index("cols")
-    half = near_first.shape[0]
-    sums[mine] = product[...]
-    sums[mine ^ 1] = jnp.dot(pair[...], gathered[mine ^ 1], preferred_element_type=jnp.float32)
-    for step, start, block in ((2, 0, near_first), (3, 0, far_first), (2, half, near_second), (3, half, far_second)):
-        sums[mine ^ step, start : start + half, :] = jnp.dot(
-            block[...], gathered[mine ^ step], preferred_element_type=jnp.float32
-        )
-    kept_sums[...] = sums[0]
-    for n, out in enumerate(outs, 1):
-        encode(sums[n], out)
-
-
-def finish_kernel(residual, kept_sums, *rest):
-    messages, out = rest[:-1], rest[-1]
-    total = residual[...] + kept_sums[...]
-    for message in messages:
-        total = total + decode(message, total.shape[0])
-    out[...] = total
+    half = product.shape[0] // 2
+    rows = [slice(h * half, (h + 1) * half) for h in (early_half(step) ^ late for step in range(2))]
+    sums[mine] = product[rows[0], :]
+    for step, block in enumerate((pair[rows[1], :], near[...], far[...]), 1):
+        sums[mine ^ step] = jnp.dot(block, gathered[mine ^ step], preferred_element_type=jnp.float32)
+
+
+def early_kernel(product, gathered, pair, near, far, own_sums, core_sums, two, three, sums):
+    half_sums(0, product, gathered, pair, near, far, sums)
+    own_sums[...] = sums[0]
+    core_sums[...] = sums[1]
+    encode(sums[2], two)
+    encode(sums[3], three)
+
+
+def late_kernel(core_sums, product, gathered, pair, near, far, own_sums, one, two, three, sums):
+    half_sums(1, product, gathered, pair, near, far, sums)
+    own_sums[...] = sums[0]
+    encode(sums[2], two)
+    encode(sums[3], three)
+    encode(core_sums[...], half_of(one, 0))
+    encode(sums[1], half_of(one, 1))
+
+
+def first_kernel(residual, own_sums, two, three, out):
+    early = early_half(lax.axis_index("rows") ^ lax.axis_index("cols"))
+    half = own_sums.shape[0]
+    total = half_of(residual, early)[...] + own_sums[...]
+    half_of(out, early)[...] = total + decode(two, half) + decode(three, half)
+    half_of(out, 1 - early)[...] = half_of(residual, 1 - early)[...]
+
+
+def last_kernel(base, own_sums, two, three, one, out):
+    early = early_half(lax.axis_index("rows") ^ lax.axis_index("cols"))
+    half = own_sums.shape[0]
+    half_of(out, early)[...] = half_of(base, early)[...] + decode(half_of(one, 0), half)
+    total = half_of(base, 1 - early)[...] + own_sums[...] + decode(half_of(one, 1), half)
+    half_of(out, 1 - early)[...] = total + decode(two, half) + decode(three, half)
 
 
 def swap(x, axis, step):
@@ -130,7 +158,9 @@
     places = pltpu.SMEM((tiles + 1,), jnp.int32)
     sums_shape = jax.ShapeDtypeStruct((pairs, width), jnp.float32)
     half_block = jax.ShapeDtypeStruct((pairs // 2, slots * TILE), doubles.dtype)
-    message = jax.ShapeDtypeStruct((pairs * width // TILE + HEAD, TILE), jnp.int16)
+    half_shape = jax.ShapeDtypeStruct((pairs // 2, width), jnp.float32)
+    message = jax.ShapeDtypeStruct((pairs // 2 * width // TILE + HEAD, TILE), jnp.int16)
+    double = jax.ShapeDtypeStruct((2 * message.shape[0], TILE), jnp.int16)
     doubles, doubles_kept, integrals, integral_kept = (
         pltpu.with_memory_space_constraint(x, pltpu.HBM) for x in (doubles, doubles_kept, integrals, integral_kept.T)
     )
@@ -166,28 +196,53 @@
             pltpu.SemaphoreType.DMA((3,)),
         ],
         compiler_params=PARAMS,
-        cost_estimate=cost(0),
+        cost_estimate=cost(10**9),
         name="prepare",
     )(doubles_kept, integral_kept, integrals, packed)
-    kept_sums, *messages = pl.pallas_call(
-        ladder_kernel,
-        out_shape=[sums_shape] + [message] * (ROWS - 1),
-        in_specs=[VMEM] * 7,
-        out_specs=[VMEM] * ROWS,
-        scratch_shapes=[pltpu.VMEM((ROWS, pairs, width), jnp.float32)],
-        compiler_params=PARAMS,
-        cost_estimate=cost(10**11),
-        name="ladder",
-    )(product, gathered, pair, near_first, near_second, far_first, far_second)
-    messages = [swap(messages[step - 1], "cols", step) for step in (2, 3, 1)]
-    return pl.pallas_call(
-        finish_kernel,
-        out_shape=sums_shape,
-        in_specs=[VMEM] * (ROWS + 1),
-        out_specs=VMEM,
-        compiler_params=PARAMS,
-        name="finish",
-    )(residual, kept_sums, *messages)
+
+    def on_vmem(kernel, name, flops, out_shape, *args, scratch=()):
+        return pl.pallas_call(
+            kernel,
+            out_shape=out_shape,
+            in_specs=[VMEM] * len(args),
+            out_specs=jax.tree.map(lambda _: VMEM, out_shape),
+            scratch_shapes=scratch,
+            compiler_params=PARAMS,
+            cost_estimate=cost(flops),
+            name=name,
+        )(*args)
+
+    sums = [pltpu.VMEM((ROWS, pairs // 2, width), jnp.float32)]
+    own_early, core_early, two, three = on_vmem(
+        early_kernel,
+        "early",
+        0,
+        [half_shape] * 2 + [message] * 2,
+        product,
+        gathered,
+        pair,
+        near_second,
+        far_first,
+        scratch=sums,
+    )
+    two, three = swap(two, "cols", 2), swap(three, "cols", 3)
+    own_late, one, two_late, three_late = on_vmem(
+        late_kernel,
+        "late",
+        10**11,
+        [half_shape, double] + [message] * 2,
+        core_early,
+        product,
+        gathered,
+        pair,
+        near_first,
+        far_second,
+        scratch=sums,
+    )
+    two_late, three_late = swap(two_late, "cols", 2), swap(three_late, "cols", 3)
+    one = swap(one, "cols", 1)
+    base = on_vmem(first_kernel, "first", 10**11, sums_shape, residual, own_early, two, three)
+    return on_vmem(last_kernel, "last", 0, sums_shape, base, own_late, two_late, three_late, one)
 
 
 def local_many(doubles, doubles_kept, integrals, integral_kept, residual):

time: 21.9 us -> 22.2 us (1.014)
  the two profiles are of different devices: /device:TPU:0 before, /device:TPU:1 now
where the time goes in v14:
time: 22.2 us; the launch traced here: 22.1 us
  starting transfers between devices  14.5 us (65%)
  Pallas kernels  3.91 us (18%)
  waiting for transfers between devices  3.56 us (16%)
    ppermute x10, starting transfers between devices, swap(): return lax.ppermute(x, axis, [(i, i ^ step) for i in range(ROWS)])  14.5 us
    ppermute x10, waiting for transfers between devices, swap(): return lax.ppermute(x, axis, [(i, i ^ step) for i in range(ROWS)])  3.56 us
    pallas_call x1, Pallas kernels, local_few(): pl.pallas_call(functools.partial(prepare_kernel, tiles, slots), out_shape...  1.51 us
    pallas_call x4, Pallas kernels, on_vmem(): pl.pallas_call(kernel, out_shape=out_shape, in_specs=[VMEM] * len(args),...  1.4 us
    pallas_call x1, Pallas kernels, local_few(): pl.pallas_call(functools.partial(pack_kernel, tiles, slots), out_shape=[j...  1 us
  transfers between devices with their start and end apart: 10, of which 3 were waited for; matrix products, arithmetic and copies ran while one was open for 0% of the time, Pallas kernels for 10%

profile of v14, /device:TPU:1, one launch (start us, length us, event | category | flops | bytes accessed | tf_op | source)
XLA Modules:
  0.0 22.1 jit_solution(3475091091648987928)
XLA Ops:
  0.0 1.0 %pack.1 = (bf16[128,512]{1,0:T(8,128)(2,1)S(1)}, bf16[64,512]{1,0:T(8,128)(2,1)S(1)}, bf16[64,512]{1,0:T(8,128)(2,1)S(1)}) custom-call(s32[4,8]{1,0:T(4,128)} %kept.3, bf16[128,1024]{1,0:T(8,128)(2,1)} %doubles.1), custom_call_target="tpu_custom_call" | custom-call | tf_op jit(solution)/shard_map/pack/pallas_call | solution.py:167
  1.0 3.2 %collective-permute-start.1 = (bf16[64,512]{1,0:T(8,128)(2,1)S(1)}, bf16[64,512]{1,0:T(8,128)(2,1)S(1)}, u32[]{:S(2)}, u32[]{:S(2)}) collective-permute-start(bf16[64,512]{1,0:T(8,128)(2,1)S(1)} %get-tuple-element.21), channel_id=1, source_target_pairs={{0,8},{4,12},{8,0},{12,4},{1,9},{5,13},{9,1},{13,5},{2,10},{6,14},... | collective-permute-start | bytes 196616 | tf_op jit(solution)/shard_map/ppermute | solution.py:150
  4.2 1.3 %collective-permute-start = (bf16[128,512]{1,0:T(8,128)(2,1)S(1)}, bf16[128,512]{1,0:T(8,128)(2,1)S(1)}, u32[]{:S(2)}, u32[]{:S(2)}) collective-permute-start(bf16[128,512]{1,0:T(8,128)(2,1)S(1)} %get-tuple-element.18.own), channel_id=1, source_target_pairs={{0,4},{4,0},{8,12},{12,8},{1,5},{5,1},{9,13},{13,9},{2,6},{6,2},{1... | collective-permute-start | bytes 393224 | tf_op jit(solution)/shard_map/ppermute | solution.py:150
  5.5 0.0 collective-permute-start.2
  5.5 1.3 %collective-permute-start.5 = (bf16[64,512]{1,0:T(8,128)(2,1)S(1)}, bf16[64,512]{1,0:T(8,128)(2,1)S(1)}, u32[]{:S(2)}, u32[]{:S(2)}) collective-permute-start(bf16[64,512]{1,0:T(8,128)(2,1)S(1)} %get-tuple-element.22), channel_id=1, source_target_pairs={{0,8},{4,12},{8,0},{12,4},{1,9},{5,13},{9,1},{13,5},{2,10},{6,14},... | collective-permute-start | bytes 196616 | tf_op jit(solution)/shard_map/ppermute | solution.py:150
  6.9 0.0 collective-permute-done.1.near
  6.9 2.2 %collective-permute-start.6 = (bf16[64,512]{1,0:T(8,128)(2,1)S(1)}, bf16[64,512]{1,0:T(8,128)(2,1)S(1)}, u32[]{:S(2)}, u32[]{:S(2)}) collective-permute-start(bf16[64,512]{1,0:T(8,128)(2,1)S(1)} %collective-permute-done.1.near), channel_id=1, source_target_pairs={{0,4},{4,0},{8,12},{12,8},{1,5},{5,1},{9,13},{13,9},{2,6},{6,2},{1... | collective-permute-start | bytes 196616 | tf_op jit(solution)/shard_map/ppermute | solution.py:150
  9.1 1.5 %prepare.1 = (bf16[4,512,256]{2,1,0:T(8,128)(2,1)S(1)}, f32[128,256]{1,0:T(8,128)S(1)}) custom-call(s32[4,8]{1,0:T(4,128)} %kept.3, s32[2,8]{1,0:T(2,128)} %bitcast.1, bf16[1024,256]{1,0:T(8,128)(2,1)} %integrals.1, bf16[128,512]{1,0:T(8,128)(2,1)S(1)} %get-tuple-element.18.own), custom_call_target="tpu_custom_call" | custom-call | flops 1000000000 | bytes 1024 | tf_op jit(solution)/shard_map/prepare/pallas_call | solution.py:186
  10.6 0.7 %collective-permute-done.2.far = bf16[64,512]{1,0:T(8,128)(2,1)S(1)} collective-permute-done((bf16[64,512]{1,0:T(8,128)(2,1)S(1)}, bf16[64,512]{1,0:T(8,128)(2,1)S(1)}, u32[]{:S(2)}, u32[]{:S(2)}) %collective-permute-start.2) | collective-permute-done | bytes 65568 | tf_op jit(solution)/shard_map/ppermute | solution.py:150
  11.3 0.0 collective-permute-done.pair
  11.3 0.3 %early.1 = (f32[64,256]{1,0:T(8,128)S(1)}, f32[64,256]{1,0:T(8,128)S(1)}, s16[144,128]{1,0:T(8,128)(2,1)S(1)}, s16[144,128]{1,0:T(8,128)(2,1)S(1)}) custom-call(f32[128,256]{1,0:T(8,128)S(1)} %get-tuple-element.19.product, bf16[4,512,256]{2,1,0:T(8,128)(2,1)S(1)} %get-tuple-element.20.gathered, bf16[128,512]{1,0:T(8,128)(2,1)S(1)} %collective-permute-done.pair, ...), custom_call_target="tpu_custom_call" | custom-call | bytes 1024 | tf_op jit(solution)/shard_map/early/pallas_call | solution.py:204
  11.6 1.3 %collective-permute-start.3 = (s16[144,128]{1,0:T(8,128)(2,1)S(1)}, s16[144,128]{1,0:T(8,128)(2,1)S(1)}, u32[]{:S(2)}, u32[]{:S(2)}) collective-permute-start(s16[144,128]{1,0:T(8,128)(2,1)S(1)} %get-tuple-element.24), channel_id=1, source_target_pairs={{0,2},{1,3},{2,0},{3,1},{4,6},{5,7},{6,4},{7,5},{8,10},{9,11},{10,... | collective-permute-start | bytes 110600 | tf_op jit(solution)/shard_map/ppermute | solution.py:150
  12.9 3.0 %collective-permute-start.4 = (s16[144,128]{1,0:T(8,128)(2,1)S(1)}, s16[144,128]{1,0:T(8,128)(2,1)S(1)}, u32[]{:S(2)}, u32[]{:S(2)}) collective-permute-start(s16[144,128]{1,0:T(8,128)(2,1)S(1)} %get-tuple-element.25), channel_id=1, source_target_pairs={{0,3},{1,2},{2,1},{3,0},{4,7},{5,6},{6,5},{7,4},{8,11},{9,10},{10,... | collective-permute-start | bytes 110600 | tf_op jit(solution)/shard_map/ppermute | solution.py:150
  15.9 0.0 collective-permute-done.5.near
  15.9 0.0 collective-permute-done.6.far
  15.9 0.0 copy-start
  15.9 0.3 %late.1 = (f32[64,256]{1,0:T(8,128)S(1)}, s16[288,128]{1,0:T(8,128)(2,1)S(1)}, s16[144,128]{1,0:T(8,128)(2,1)S(1)}, s16[144,128]{1,0:T(8,128)(2,1)S(1)}) custom-call(f32[64,256]{1,0:T(8,128)S(1)} %get-tuple-element.26.core_sums, f32[128,256]{1,0:T(8,128)S(1)} %get-tuple-element.19.product, bf16[4,512,256]{2,1,0:T(8,128)(2,1)S(1)} %get-tuple-element.20.gathered, ...), custom_call_target="tpu_custom_call" | custom-call | flops 99999997952 | bytes 1024 | tf_op jit(solution)/shard_map/late/pallas_call | solution.py:204
  16.2 1.7 %collective-permute-start.7 = (s16[144,128]{1,0:T(8,128)(2,1)S(1)}, s16[144,128]{1,0:T(8,128)(2,1)S(1)}, u32[]{:S(2)}, u32[]{:S(2)}) collective-permute-start(s16[144,128]{1,0:T(8,128)(2,1)S(1)} %get-tuple-element.28), channel_id=1, source_target_pairs={{0,2},{1,3},{2,0},{3,1},{4,6},{5,7},{6,4},{7,5},{8,10},{9,11},{10,... | collective-permute-start | bytes 110600 | tf_op jit(solution)/shard_map/ppermute | solution.py:150
  18.0 0.3 %collective-permute-start.8 = (s16[144,128]{1,0:T(8,128)(2,1)S(1)}, s16[144,128]{1,0:T(8,128)(2,1)S(1)}, u32[]{:S(2)}, u32[]{:S(2)}) collective-permute-start(s16[144,128]{1,0:T(8,128)(2,1)S(1)} %get-tuple-element.29), channel_id=1, source_target_pairs={{0,3},{1,2},{2,1},{3,0},{4,7},{5,6},{6,5},{7,4},{8,11},{9,10},{10,... | collective-permute-start | bytes 110600 | tf_op jit(solution)/shard_map/ppermute | solution.py:150
  18.3 0.2 collective-permute-start.9
  18.5 0.0 collective-permute-done.3.two
  18.5 0.0 collective-permute-done.4.three
  18.5 0.0 copy-done
  18.5 0.8 %collective-permute-done.7.two = s16[144,128]{1,0:T(8,128)(2,1)S(1)} collective-permute-done((s16[144,128]{1,0:T(8,128)(2,1)S(1)}, s16[144,128]{1,0:T(8,128)(2,1)S(1)}, u32[]{:S(2)}, u32[]{:S(2)}) %collective-permute-start.7) | collective-permute-done | bytes 36896 | tf_op jit(solution)/shard_map/ppermute | solution.py:150
  19.3 2.0 %collective-permute-done.8.three = s16[144,128]{1,0:T(8,128)(2,1)S(1)} collective-permute-done((s16[144,128]{1,0:T(8,128)(2,1)S(1)}, s16[144,128]{1,0:T(8,128)(2,1)S(1)}, u32[]{:S(2)}, u32[]{:S(2)}) %collective-permute-start.8) | collective-permute-done | bytes 36896 | tf_op jit(solution)/shard_map/ppermute | solution.py:150
  21.4 0.0 collective-permute-done.9.one
  21.4 0.7 %last.1 = f32[128,256]{1,0:T(8,128)} custom-call(f32[128,256]{1,0:T(8,128)S(1)} %first.1.base, f32[64,256]{1,0:T(8,128)S(1)} %get-tuple-element.27.own_sums, s16[144,128]{1,0:T(8,128)(2,1)S(1)} %collective-permute-done.7.two, s16[144,128]{1,0:T(8,128)(2,1)S(1)} %collective-permute-done.8.three, s16[288,128]{1,0:T(8,128)(2,1)S(1)} %collective-permute-done.9.one), custom_call_target="tpu_custom_call" | custom-call | bytes 1024 | tf_op jit(solution)/shard_map/last/pallas_call | solution.py:204
  (1 shorter events, 0.0 us)
Async XLA Ops:
  1.0 5.9 %collective-permute-start.1 = (bf16[64,512]{1,0:T(8,128)(2,1)S(1)}, bf16[64,512]{1,0:T(8,128)(2,1)S(1)}, u32[]{:S(2)}, u32[]{:S(2)}) collective-permute-start(bf16[64,512]{1,0:T(8,128)(2,1)S(1)} %get-tuple-element.21), channel_id=1, source_target_pairs={{0,8},{4,12},{8,0},{12,4},{1,9},{5,13},{9,1},{13,5},{2,10},{6,14},... | collective-permute-start | bytes 196616 | tf_op jit(solution)/shard_map/ppermute | solution.py:150
  4.2 7.1 %collective-permute-start = (bf16[128,512]{1,0:T(8,128)(2,1)S(1)}, bf16[128,512]{1,0:T(8,128)(2,1)S(1)}, u32[]{:S(2)}, u32[]{:S(2)}) collective-permute-start(bf16[128,512]{1,0:T(8,128)(2,1)S(1)} %get-tuple-element.18.own), channel_id=1, source_target_pairs={{0,4},{4,0},{8,12},{12,8},{1,5},{5,1},{9,13},{13,9},{2,6},{6,2},{1... | collective-permute-start | bytes 393224 | tf_op jit(solution)/shard_map/ppermute | solution.py:150
  5.5 5.8 %collective-permute-start.2 = (bf16[64,512]{1,0:T(8,128)(2,1)S(1)}, bf16[64,512]{1,0:T(8,128)(2,1)S(1)}, u32[]{:S(2)}, u32[]{:S(2)}) collective-permute-start(bf16[64,512]{1,0:T(8,128)(2,1)S(1)} %get-tuple-element.22), channel_id=1, source_target_pairs={{0,12},{4,8},{8,4},{12,0},{1,13},{5,9},{9,5},{13,1},{2,14},{6,10},... | collective-permute-start | bytes 196616 | tf_op jit(solution)/shard_map/ppermute | solution.py:150
  5.5 10.4 %collective-permute-start.5 = (bf16[64,512]{1,0:T(8,128)(2,1)S(1)}, bf16[64,512]{1,0:T(8,128)(2,1)S(1)}, u32[]{:S(2)}, u32[]{:S(2)}) collective-permute-start(bf16[64,512]{1,0:T(8,128)(2,1)S(1)} %get-tuple-element.22), channel_id=1, source_target_pairs={{0,8},{4,12},{8,0},{12,4},{1,9},{5,13},{9,1},{13,5},{2,10},{6,14},... | collective-permute-start | bytes 196616 | tf_op jit(solution)/shard_map/ppermute | solution.py:150
  6.9 9.0 %collective-permute-start.6 = (bf16[64,512]{1,0:T(8,128)(2,1)S(1)}, bf16[64,512]{1,0:T(8,128)(2,1)S(1)}, u32[]{:S(2)}, u32[]{:S(2)}) collective-permute-start(bf16[64,512]{1,0:T(8,128)(2,1)S(1)} %collective-permute-done.1.near), channel_id=1, source_target_pairs={{0,4},{4,0},{8,12},{12,8},{1,5},{5,1},{9,13},{13,9},{2,6},{6,2},{1... | collective-permute-start | bytes 196616 | tf_op jit(solution)/shard_map/ppermute | solution.py:150
  11.6 6.9 %collective-permute-start.3 = (s16[144,128]{1,0:T(8,128)(2,1)S(1)}, s16[144,128]{1,0:T(8,128)(2,1)S(1)}, u32[]{:S(2)}, u32[]{:S(2)}) collective-permute-start(s16[144,128]{1,0:T(8,128)(2,1)S(1)} %get-tuple-element.24), channel_id=1, source_target_pairs={{0,2},{1,3},{2,0},{3,1},{4,6},{5,7},{6,4},{7,5},{8,10},{9,11},{10,... | collective-permute-start | bytes 110600 | tf_op jit(solution)/shard_map/ppermute | solution.py:150
  12.9 5.6 %collective-permute-start.4 = (s16[144,128]{1,0:T(8,128)(2,1)S(1)}, s16[144,128]{1,0:T(8,128)(2,1)S(1)}, u32[]{:S(2)}, u32[]{:S(2)}) collective-permute-start(s16[144,128]{1,0:T(8,128)(2,1)S(1)} %get-tuple-element.25), channel_id=1, source_target_pairs={{0,3},{1,2},{2,1},{3,0},{4,7},{5,6},{6,5},{7,4},{8,11},{9,10},{10,... | collective-permute-start | bytes 110600 | tf_op jit(solution)/shard_map/ppermute | solution.py:150
  15.9 2.6 %copy-start = (f32[128,256]{1,0:T(8,128)S(1)}, f32[128,256]{1,0:T(8,128)}, u32[]{:S(2)}) copy-start(f32[128,256]{1,0:T(8,128)} %residual.1) | copy-start | bytes 393220
  16.2 3.1 %collective-permute-start.7 = (s16[144,128]{1,0:T(8,128)(2,1)S(1)}, s16[144,128]{1,0:T(8,128)(2,1)S(1)}, u32[]{:S(2)}, u32[]{:S(2)}) collective-permute-start(s16[144,128]{1,0:T(8,128)(2,1)S(1)} %get-tuple-element.28), channel_id=1, source_target_pairs={{0,2},{1,3},{2,0},{3,1},{4,6},{5,7},{6,4},{7,5},{8,10},{9,11},{10,... | collective-permute-start | bytes 110600 | tf_op jit(solution)/shard_map/ppermute | solution.py:150
  18.0 3.4 %collective-permute-start.8 = (s16[144,128]{1,0:T(8,128)(2,1)S(1)}, s16[144,128]{1,0:T(8,128)(2,1)S(1)}, u32[]{:S(2)}, u32[]{:S(2)}) collective-permute-start(s16[144,128]{1,0:T(8,128)(2,1)S(1)} %get-tuple-element.29), channel_id=1, source_target_pairs={{0,3},{1,2},{2,1},{3,0},{4,7},{5,6},{6,5},{7,4},{8,11},{9,10},{10,... | collective-permute-start | bytes 110600 | tf_op jit(solution)/shard_map/ppermute | solution.py:150
  18.3 3.1 %collective-permute-start.9 = (s16[288,128]{1,0:T(8,128)(2,1)S(1)}, s16[288,128]{1,0:T(8,128)(2,1)S(1)}, u32[]{:S(2)}, u32[]{:S(2)}) collective-permute-start(s16[288,128]{1,0:T(8,128)(2,1)S(1)} %get-tuple-element.30), channel_id=1, source_target_pairs={{0,1},{1,0},{2,3},{3,2},{4,5},{5,4},{6,7},{7,6},{8,9},{9,8},{10,11... | collective-permute-start | bytes 221192 | tf_op jit(solution)/shard_map/ppermute | solution.py:150

commit v15 on v14

--- a/solution.py
+++ b/solution.py
@@ -16,6 +16,7 @@
 VMEM = pl.BlockSpec(memory_space=pltpu.VMEM)
 HBM = pl.BlockSpec(memory_space=pltpu.HBM)
 PARAMS = pltpu.CompilerParams(vmem_limit_bytes=8 * 1024 * 1024)
+
 ROWS = 4
 
 
@@ -30,7 +31,7 @@
         at = at + kept[row, tile]
 
 
-def pack_kernel(tiles, slots, kept, doubles, packed, first, second, table, block, places, sems):
+def pack_kernel(tiles, slots, kept, doubles, first, second, table, block, places, sems):
     table_copy = pltpu.make_async_copy(kept, table, sems.at[0])
     block_copy = pltpu.make_async_copy(doubles, block, sems.at[1])
     table_copy.start()
@@ -40,14 +41,13 @@
     block_copy.wait()
     half = first.shape[0]
     for slot in range(slots):
-        tile = block[:, pl.ds(pl.multiple_of(places[slot] * TILE, TILE), TILE)]
+        tile = pl.ds(pl.multiple_of(places[slot] * TILE, TILE), TILE)
         to = slice(slot * TILE, (slot + 1) * TILE)
-        packed[:, to] = tile
-        first[:, to] = tile[:half]
-        second[:, to] = tile[half:]
-
-
-def prepare_kernel(tiles, slots, kept, int_kept, integrals, own, gathered, product, table, int_table, held, places, sems):
+        first[:, to] = block[:half, tile]
+        second[:, to] = block[half:, tile]
+
+
+def prepare_kernel(tiles, slots, kept, int_kept, integrals, first, second, gathered, product, table, int_table, held, places, sems):
     copies = [
         pltpu.make_async_copy(*pair, sems.at[i])
         for i, pair in enumerate(((kept, table), (int_kept, int_table), (integrals, held)))
@@ -67,7 +67,11 @@
                 part = held[pl.ds(start, TILE), ab * TILE : (ab + 1) * TILE]
                 on = (int_table[ab, tile] != 0).astype(jnp.float32).astype(part.dtype)
                 gathered[n, slot * TILE : (slot + 1) * TILE, ab * TILE : (ab + 1) * TILE] = part * on
-    product[...] = jnp.dot(own[...], gathered[row ^ col], preferred_element_type=jnp.float32)
+    half = first.shape[0]
+    for start, own in ((0, first), (half, second)):
+        product[start : start + half, :] = jnp.dot(
+            own[...], gathered[row ^ col], preferred_element_type=jnp.float32
+        )
 
 
 def encode(x, out):
@@ -104,25 +108,25 @@
     return 1 - step % 2
 
 
-def half_sums(late, product, gathered, pair, near, far, sums):
+def half_sums(late, product, gathered, near, far, pair, sums):
     mine = lax.axis_index("rows") ^ lax.axis_index("cols")
     half = product.shape[0] // 2
-    rows = [slice(h * half, (h + 1) * half) for h in (early_half(step) ^ late for step in range(2))]
-    sums[mine] = product[rows[0], :]
-    for step, block in enumerate((pair[rows[1], :], near[...], far[...]), 1):
-        sums[mine ^ step] = jnp.dot(block, gathered[mine ^ step], preferred_element_type=jnp.float32)
-
-
-def early_kernel(product, gathered, pair, near, far, own_sums, core_sums, two, three, sums):
-    half_sums(0, product, gathered, pair, near, far, sums)
+    start = (early_half(0) ^ late) * half
+    sums[mine] = product[start : start + half, :]
+    for step, block in zip((2, 3, 1), (near, far, pair)):
+        sums[mine ^ step] = jnp.dot(block[...], gathered[mine ^ step], preferred_element_type=jnp.float32)
+
+
+def early_kernel(product, gathered, near, far, pair, own_sums, core_sums, two, three, sums):
+    half_sums(0, product, gathered, near, far, pair, sums)
     own_sums[...] = sums[0]
     core_sums[...] = sums[1]
     encode(sums[2], two)
     encode(sums[3], three)
 
 
-def late_kernel(core_sums, product, gathered, pair, near, far, own_sums, one, two, three, sums):
-    half_sums(1, product, gathered, pair, near, far, sums)
+def late_kernel(core_sums, product, gathered, near, far, pair, own_sums, one, two, three, sums):
+    half_sums(1, product, gathered, near, far, pair, sums)
     own_sums[...] = sums[0]
     encode(sums[2], two)
     encode(sums[3], three)
@@ -164,11 +168,11 @@
     doubles, doubles_kept, integrals, integral_kept = (
         pltpu.with_memory_space_constraint(x, pltpu.HBM) for x in (doubles, doubles_kept, integrals, integral_kept.T)
     )
-    packed, first, second = pl.pallas_call(
+    first, second = pl.pallas_call(
         functools.partial(pack_kernel, tiles, slots),
-        out_shape=[jax.ShapeDtypeStruct((pairs, slots * TILE), doubles.dtype), half_block, half_block],
+        out_shape=[half_block] * 2,
         in_specs=[HBM, HBM],
-        out_specs=[VMEM] * 3,
+        out_specs=[VMEM] * 2,
         scratch_shapes=[
             pltpu.SMEM(doubles_kept.shape, jnp.int32),
             pltpu.VMEM(doubles.shape, doubles.dtype),
@@ -179,14 +183,15 @@
         name="pack",
     )(doubles_kept, doubles)
     near_second = swap(second, "rows", 2)
-    pair = swap(packed, "rows", 1)
     far_first = swap(first, "rows", 3)
+    pair_first = swap(first, "rows", 1)
     near_first = swap(first, "rows", 2)
+    pair_second = swap(second, "rows", 1)
     far_second = swap(near_second, "rows", 1)
     gathered, product = pl.pallas_call(
         functools.partial(prepare_kernel, tiles, slots),
         out_shape=[jax.ShapeDtypeStruct((ROWS, slots * TILE, width), integrals.dtype), sums_shape],
-        in_specs=[HBM, HBM, HBM, VMEM],
+        in_specs=[HBM] * 3 + [VMEM] * 2,
         out_specs=[VMEM] * 2,
         scratch_shapes=[
             pltpu.SMEM(doubles_kept.shape, jnp.int32),
@@ -196,9 +201,9 @@
             pltpu.SemaphoreType.DMA((3,)),
         ],
         compiler_params=PARAMS,
-        cost_estimate=cost(10**9),
+        cost_estimate=cost(0),
         name="prepare",
-    )(doubles_kept, integral_kept, integrals, packed)
+    )(doubles_kept, integral_kept, integrals, first, second)
 
     def on_vmem(kernel, name, flops, out_shape, *args, scratch=()):
         return pl.pallas_call(
@@ -220,9 +225,9 @@
         [half_shape] * 2 + [message] * 2,
         product,
         gathered,
-        pair,
         near_second,
         far_first,
+        pair_first,
         scratch=sums,
     )
     two, three = swap(two, "cols", 2), swap(three, "cols", 3)
@@ -234,9 +239,9 @@
         core_early,
         product,
         gathered,
-        pair,
         near_first,
         far_second,
+        pair_second,
         scratch=sums,
     )
     two_late, three_late = swap(two_late, "cols", 2), swap(three_late, "cols", 3)

time: 22.2 us -> 22.1 us (level)
  the two profiles are of different devices: /device:TPU:1 before, /device:TPU:0 now
where the time goes in v15:
time: 22.1 us; the launch traced here: 22 us
  starting transfers between devices  14.3 us (65%)
  Pallas kernels  3.92 us (18%)
  waiting for transfers between devices  3.68 us (17%)
    ppermute x11, starting transfers between devices, swap(): return lax.ppermute(x, axis, [(i, i ^ step) for i in range(ROWS)])  14.3 us
    ppermute x11, waiting for transfers between devices, swap(): return lax.ppermute(x, axis, [(i, i ^ step) for i in range(ROWS)])  3.68 us
    pallas_call x1, Pallas kernels, local_few(): pl.pallas_call(functools.partial(prepare_kernel, tiles, slots), out_shape...  1.53 us
    pallas_call x4, Pallas kernels, on_vmem(): pl.pallas_call(kernel, out_shape=out_shape, in_specs=[VMEM] * len(args),...  1.39 us
    pallas_call x1, Pallas kernels, local_few(): pl.pallas_call(functools.partial(pack_kernel, tiles, slots), out_shape=[h...  1 us
  transfers between devices with their start and end apart: 11, of which 4 were waited for; matrix products, arithmetic and copies ran while one was open for 0% of the time, Pallas kernels for 10%

profile of v15, /device:TPU:0, one launch (start us, length us, event | category | flops | bytes accessed | tf_op | source)
XLA Modules:
  0.0 22.0 jit_solution(16994441855757933353)
XLA Ops:
  0.0 1.0 %pack.1 = (bf16[64,512]{1,0:T(8,128)(2,1)S(1)}, bf16[64,512]{1,0:T(8,128)(2,1)S(1)}) custom-call(s32[4,8]{1,0:T(4,128)} %kept.3, bf16[128,1024]{1,0:T(8,128)(2,1)} %doubles.1), custom_call_target="tpu_custom_call" | custom-call | tf_op jit(solution)/shard_map/pack/pallas_call | solution.py:171
  1.0 4.1 %collective-permute-start = (bf16[64,512]{1,0:T(8,128)(2,1)S(1)}, bf16[64,512]{1,0:T(8,128)(2,1)S(1)}, u32[]{:S(2)}, u32[]{:S(2)}) collective-permute-start(bf16[64,512]{1,0:T(8,128)(2,1)S(1)} %get-tuple-element.18.second), channel_id=1, source_target_pairs={{0,8},{4,12},{8,0},{12,4},{1,9},{5,13},{9,1},{13,5},{2,10},{6,14},... | collective-permute-start | bytes 196616 | tf_op jit(solution)/shard_map/ppermute | solution.py:154
  5.1 1.3 %collective-permute-start.1 = (bf16[64,512]{1,0:T(8,128)(2,1)S(1)}, bf16[64,512]{1,0:T(8,128)(2,1)S(1)}, u32[]{:S(2)}, u32[]{:S(2)}) collective-permute-start(bf16[64,512]{1,0:T(8,128)(2,1)S(1)} %get-tuple-element.17.first), channel_id=1, source_target_pairs={{0,12},{4,8},{8,4},{12,0},{1,13},{5,9},{9,5},{13,1},{2,14},{6,10},... | collective-permute-start | bytes 196616 | tf_op jit(solution)/shard_map/ppermute | solution.py:154
  6.5 0.2 %collective-permute-start.2 = (bf16[64,512]{1,0:T(8,128)(2,1)S(1)}, bf16[64,512]{1,0:T(8,128)(2,1)S(1)}, u32[]{:S(2)}, u32[]{:S(2)}) collective-permute-start(bf16[64,512]{1,0:T(8,128)(2,1)S(1)} %get-tuple-element.17.first), channel_id=1, source_target_pairs={{0,4},{4,0},{8,12},{12,8},{1,5},{5,1},{9,13},{13,9},{2,6},{6,2},{1... | collective-permute-start | bytes 196616 | tf_op jit(solution)/shard_map/ppermute | solution.py:154
  6.7 2.8 %collective-permute-start.5 = (bf16[64,512]{1,0:T(8,128)(2,1)S(1)}, bf16[64,512]{1,0:T(8,128)(2,1)S(1)}, u32[]{:S(2)}, u32[]{:S(2)}) collective-permute-start(bf16[64,512]{1,0:T(8,128)(2,1)S(1)} %get-tuple-element.17.first), channel_id=1, source_target_pairs={{0,8},{4,12},{8,0},{12,4},{1,9},{5,13},{9,1},{13,5},{2,10},{6,14},... | collective-permute-start | bytes 196616 | tf_op jit(solution)/shard_map/ppermute | solution.py:154
  9.5 0.7 %collective-permute-start.7 = (bf16[64,512]{1,0:T(8,128)(2,1)S(1)}, bf16[64,512]{1,0:T(8,128)(2,1)S(1)}, u32[]{:S(2)}, u32[]{:S(2)}) collective-permute-start(bf16[64,512]{1,0:T(8,128)(2,1)S(1)} %get-tuple-element.18.second), channel_id=1, source_target_pairs={{0,4},{4,0},{8,12},{12,8},{1,5},{5,1},{9,13},{13,9},{2,6},{6,2},{1... | collective-permute-start | bytes 196616 | tf_op jit(solution)/shard_map/ppermute | solution.py:154
  10.2 0.0 collective-permute-done.near
  10.2 1.3 %collective-permute-start.6 = (bf16[64,512]{1,0:T(8,128)(2,1)S(1)}, bf16[64,512]{1,0:T(8,128)(2,1)S(1)}, u32[]{:S(2)}, u32[]{:S(2)}) collective-permute-start(bf16[64,512]{1,0:T(8,128)(2,1)S(1)} %collective-permute-done.near), channel_id=1, source_target_pairs={{0,4},{4,0},{8,12},{12,8},{1,5},{5,1},{9,13},{13,9},{2,6},{6,2},{1... | collective-permute-start | bytes 196616 | tf_op jit(solution)/shard_map/ppermute | solution.py:154
  11.5 1.5 %prepare.1 = (bf16[4,512,256]{2,1,0:T(8,128)(2,1)S(1)}, f32[128,256]{1,0:T(8,128)S(1)}) custom-call(s32[4,8]{1,0:T(4,128)} %kept.3, s32[2,8]{1,0:T(2,128)} %bitcast.1, bf16[1024,256]{1,0:T(8,128)(2,1)} %integrals.1, bf16[64,512]{1,0:T(8,128)(2,1)S(1)} %get-tuple-element.17.first, bf16[64,512]{1,0:T(8,128)(2,1)S(1)} %get-tuple-element.18.second), custom_call_target="tpu_custom_call" | custom-call | bytes 1024 | tf_op jit(solution)/shard_map/prepare/pallas_call | solution.py:191
  13.1 0.0 collective-permute-done.1.far
  13.1 0.0 collective-permute-done.2.pair
  13.1 0.3 %early.1 = (f32[64,256]{1,0:T(8,128)S(1)}, f32[64,256]{1,0:T(8,128)S(1)}, s16[144,128]{1,0:T(8,128)(2,1)S(1)}, s16[144,128]{1,0:T(8,128)(2,1)S(1)}) custom-call(f32[128,256]{1,0:T(8,128)S(1)} %get-tuple-element.19.product, bf16[4,512,256]{2,1,0:T(8,128)(2,1)S(1)} %get-tuple-element.20.gathered, bf16[64,512]{1,0:T(8,128)(2,1)S(1)} %collective-permute-done.near, ...), custom_call_target="tpu_custom_call" | custom-call | bytes 1024 | tf_op jit(solution)/shard_map/early/pallas_call | solution.py:209
  13.4 1.6 %collective-permute-start.3 = (s16[144,128]{1,0:T(8,128)(2,1)S(1)}, s16[144,128]{1,0:T(8,128)(2,1)S(1)}, u32[]{:S(2)}, u32[]{:S(2)}) collective-permute-start(s16[144,128]{1,0:T(8,128)(2,1)S(1)} %get-tuple-element.22), channel_id=1, source_target_pairs={{0,2},{1,3},{2,0},{3,1},{4,6},{5,7},{6,4},{7,5},{8,10},{9,11},{10,... | collective-permute-start | bytes 110600 | tf_op jit(solution)/shard_map/ppermute | solution.py:154
  15.0 0.0 collective-permute-start.4
  15.0 0.0 collective-permute-done.5.near
  15.0 0.0 collective-permute-done.7.pair
  15.0 0.6 %collective-permute-done.6.far = bf16[64,512]{1,0:T(8,128)(2,1)S(1)} collective-permute-done((bf16[64,512]{1,0:T(8,128)(2,1)S(1)}, bf16[64,512]{1,0:T(8,128)(2,1)S(1)}, u32[]{:S(2)}, u32[]{:S(2)}) %collective-permute-start.6) | collective-permute-done | bytes 65568 | tf_op jit(solution)/shard_map/ppermute | solution.py:154
  15.6 0.0 copy-start
  15.6 0.3 %late.1 = (f32[64,256]{1,0:T(8,128)S(1)}, s16[288,128]{1,0:T(8,128)(2,1)S(1)}, s16[144,128]{1,0:T(8,128)(2,1)S(1)}, s16[144,128]{1,0:T(8,128)(2,1)S(1)}) custom-call(f32[64,256]{1,0:T(8,128)S(1)} %get-tuple-element.24.core_sums, f32[128,256]{1,0:T(8,128)S(1)} %get-tuple-element.19.product, bf16[4,512,256]{2,1,0:T(8,128)(2,1)S(1)} %get-tuple-element.20.gathered, ...), custom_call_target="tpu_custom_call" | custom-call | flops 99999997952 | bytes 1024 | tf_op jit(solution)/shard_map/late/pallas_call | solution.py:209
  16.0 1.6 %collective-permute-start.8 = (s16[144,128]{1,0:T(8,128)(2,1)S(1)}, s16[144,128]{1,0:T(8,128)(2,1)S(1)}, u32[]{:S(2)}, u32[]{:S(2)}) collective-permute-start(s16[144,128]{1,0:T(8,128)(2,1)S(1)} %get-tuple-element.26), channel_id=1, source_target_pairs={{0,2},{1,3},{2,0},{3,1},{4,6},{5,7},{6,4},{7,5},{8,10},{9,11},{10,... | collective-permute-start | bytes 110600 | tf_op jit(solution)/shard_map/ppermute | solution.py:154
  17.5 0.0 collective-permute-start.9
  17.5 0.6 %collective-permute-start.10 = (s16[288,128]{1,0:T(8,128)(2,1)S(1)}, s16[288,128]{1,0:T(8,128)(2,1)S(1)}, u32[]{:S(2)}, u32[]{:S(2)}) collective-permute-start(s16[288,128]{1,0:T(8,128)(2,1)S(1)} %get-tuple-element.28), channel_id=1, source_target_pairs={{0,1},{1,0},{2,3},{3,2},{4,5},{5,4},{6,7},{7,6},{8,9},{9,8},{10,11... | collective-permute-start | bytes 221192 | tf_op jit(solution)/shard_map/ppermute | solution.py:154
  18.2 0.0 collective-permute-done.3.two
  18.2 0.2 collective-permute-done.4.three
  18.4 0.0 copy-done
  18.4 1.6 %collective-permute-done.8.two = s16[144,128]{1,0:T(8,128)(2,1)S(1)} collective-permute-done((s16[144,128]{1,0:T(8,128)(2,1)S(1)}, s16[144,128]{1,0:T(8,128)(2,1)S(1)}, u32[]{:S(2)}, u32[]{:S(2)}) %collective-permute-start.8) | collective-permute-done | bytes 36896 | tf_op jit(solution)/shard_map/ppermute | solution.py:154
  20.0 1.2 %collective-permute-done.9.three = s16[144,128]{1,0:T(8,128)(2,1)S(1)} collective-permute-done((s16[144,128]{1,0:T(8,128)(2,1)S(1)}, s16[144,128]{1,0:T(8,128)(2,1)S(1)}, u32[]{:S(2)}, u32[]{:S(2)}) %collective-permute-start.9) | collective-permute-done | bytes 36896 | tf_op jit(solution)/shard_map/ppermute | solution.py:154
  21.2 0.0 collective-permute-done.10.one
  21.2 0.7 %last.1 = f32[128,256]{1,0:T(8,128)} custom-call(f32[128,256]{1,0:T(8,128)S(1)} %first.1.base, f32[64,256]{1,0:T(8,128)S(1)} %get-tuple-element.25.own_sums, s16[144,128]{1,0:T(8,128)(2,1)S(1)} %collective-permute-done.8.two, s16[144,128]{1,0:T(8,128)(2,1)S(1)} %collective-permute-done.9.three, s16[288,128]{1,0:T(8,128)(2,1)S(1)} %collective-permute-done.10.one), custom_call_target="tpu_custom_call" | custom-call | bytes 1024 | tf_op jit(solution)/shard_map/last/pallas_call | solution.py:209
  (1 shorter events, 0.0 us)
Async XLA Ops:
  1.0 9.2 %collective-permute-start = (bf16[64,512]{1,0:T(8,128)(2,1)S(1)}, bf16[64,512]{1,0:T(8,128)(2,1)S(1)}, u32[]{:S(2)}, u32[]{:S(2)}) collective-permute-start(bf16[64,512]{1,0:T(8,128)(2,1)S(1)} %get-tuple-element.18.second), channel_id=1, source_target_pairs={{0,8},{4,12},{8,0},{12,4},{1,9},{5,13},{9,1},{13,5},{2,10},{6,14},... | collective-permute-start | bytes 196616 | tf_op jit(solution)/shard_map/ppermute | solution.py:154
  5.1 8.0 %collective-permute-start.1 = (bf16[64,512]{1,0:T(8,128)(2,1)S(1)}, bf16[64,512]{1,0:T(8,128)(2,1)S(1)}, u32[]{:S(2)}, u32[]{:S(2)}) collective-permute-start(bf16[64,512]{1,0:T(8,128)(2,1)S(1)} %get-tuple-element.17.first), channel_id=1, source_target_pairs={{0,12},{4,8},{8,4},{12,0},{1,13},{5,9},{9,5},{13,1},{2,14},{6,10},... | collective-permute-start | bytes 196616 | tf_op jit(solution)/shard_map/ppermute | solution.py:154
  6.5 6.6 %collective-permute-start.2 = (bf16[64,512]{1,0:T(8,128)(2,1)S(1)}, bf16[64,512]{1,0:T(8,128)(2,1)S(1)}, u32[]{:S(2)}, u32[]{:S(2)}) collective-permute-start(bf16[64,512]{1,0:T(8,128)(2,1)S(1)} %get-tuple-element.17.first), channel_id=1, source_target_pairs={{0,4},{4,0},{8,12},{12,8},{1,5},{5,1},{9,13},{13,9},{2,6},{6,2},{1... | collective-permute-start | bytes 196616 | tf_op jit(solution)/shard_map/ppermute | solution.py:154
  6.7 8.3 %collective-permute-start.5 = (bf16[64,512]{1,0:T(8,128)(2,1)S(1)}, bf16[64,512]{1,0:T(8,128)(2,1)S(1)}, u32[]{:S(2)}, u32[]{:S(2)}) collective-permute-start(bf16[64,512]{1,0:T(8,128)(2,1)S(1)} %get-tuple-element.17.first), channel_id=1, source_target_pairs={{0,8},{4,12},{8,0},{12,4},{1,9},{5,13},{9,1},{13,5},{2,10},{6,14},... | collective-permute-start | bytes 196616 | tf_op jit(solution)/shard_map/ppermute | solution.py:154
  9.5 5.5 %collective-permute-start.7 = (bf16[64,512]{1,0:T(8,128)(2,1)S(1)}, bf16[64,512]{1,0:T(8,128)(2,1)S(1)}, u32[]{:S(2)}, u32[]{:S(2)}) collective-permute-start(bf16[64,512]{1,0:T(8,128)(2,1)S(1)} %get-tuple-element.18.second), channel_id=1, source_target_pairs={{0,4},{4,0},{8,12},{12,8},{1,5},{5,1},{9,13},{13,9},{2,6},{6,2},{1... | collective-permute-start | bytes 196616 | tf_op jit(solution)/shard_map/ppermute | solution.py:154
  10.2 5.5 %collective-permute-start.6 = (bf16[64,512]{1,0:T(8,128)(2,1)S(1)}, bf16[64,512]{1,0:T(8,128)(2,1)S(1)}, u32[]{:S(2)}, u32[]{:S(2)}) collective-permute-start(bf16[64,512]{1,0:T(8,128)(2,1)S(1)} %collective-permute-done.near), channel_id=1, source_target_pairs={{0,4},{4,0},{8,12},{12,8},{1,5},{5,1},{9,13},{13,9},{2,6},{6,2},{1... | collective-permute-start | bytes 196616 | tf_op jit(solution)/shard_map/ppermute | solution.py:154
  13.4 4.8 %collective-permute-start.3 = (s16[144,128]{1,0:T(8,128)(2,1)S(1)}, s16[144,128]{1,0:T(8,128)(2,1)S(1)}, u32[]{:S(2)}, u32[]{:S(2)}) collective-permute-start(s16[144,128]{1,0:T(8,128)(2,1)S(1)} %get-tuple-element.22), channel_id=1, source_target_pairs={{0,2},{1,3},{2,0},{3,1},{4,6},{5,7},{6,4},{7,5},{8,10},{9,11},{10,... | collective-permute-start | bytes 110600 | tf_op jit(solution)/shard_map/ppermute | solution.py:154
  15.0 3.4 %collective-permute-start.4 = (s16[144,128]{1,0:T(8,128)(2,1)S(1)}, s16[144,128]{1,0:T(8,128)(2,1)S(1)}, u32[]{:S(2)}, u32[]{:S(2)}) collective-permute-start(s16[144,128]{1,0:T(8,128)(2,1)S(1)} %get-tuple-element.23), channel_id=1, source_target_pairs={{0,3},{1,2},{2,1},{3,0},{4,7},{5,6},{6,5},{7,4},{8,11},{9,10},{10,... | collective-permute-start | bytes 110600 | tf_op jit(solution)/shard_map/ppermute | solution.py:154
  15.6 2.7 %copy-start = (f32[128,256]{1,0:T(8,128)S(1)}, f32[128,256]{1,0:T(8,128)}, u32[]{:S(2)}) copy-start(f32[128,256]{1,0:T(8,128)} %residual.1) | copy-start | bytes 393220
  16.0 4.0 %collective-permute-start.8 = (s16[144,128]{1,0:T(8,128)(2,1)S(1)}, s16[144,128]{1,0:T(8,128)(2,1)S(1)}, u32[]{:S(2)}, u32[]{:S(2)}) collective-permute-start(s16[144,128]{1,0:T(8,128)(2,1)S(1)} %get-tuple-element.26), channel_id=1, source_target_pairs={{0,2},{1,3},{2,0},{3,1},{4,6},{5,7},{6,4},{7,5},{8,10},{9,11},{10,... | collective-permute-start | bytes 110600 | tf_op jit(solution)/shard_map/ppermute | solution.py:154
  17.5 3.7 %collective-permute-start.9 = (s16[144,128]{1,0:T(8,128)(2,1)S(1)}, s16[144,128]{1,0:T(8,128)(2,1)S(1)}, u32[]{:S(2)}, u32[]{:S(2)}) collective-permute-start(s16[144,128]{1,0:T(8,128)(2,1)S(1)} %get-tuple-element.27), channel_id=1, source_target_pairs={{0,3},{1,2},{2,1},{3,0},{4,7},{5,6},{6,5},{7,4},{8,11},{9,10},{10,... | collective-permute-start | bytes 110600 | tf_op jit(solution)/shard_map/ppermute | solution.py:154
  17.5 3.7 %collective-permute-start.10 = (s16[288,128]{1,0:T(8,128)(2,1)S(1)}, s16[288,128]{1,0:T(8,128)(2,1)S(1)}, u32[]{:S(2)}, u32[]{:S(2)}) collective-permute-start(s16[288,128]{1,0:T(8,128)(2,1)S(1)} %get-tuple-element.28), channel_id=1, source_target_pairs={{0,1},{1,0},{2,3},{3,2},{4,5},{5,4},{6,7},{7,6},{8,9},{9,8},{10,11... | collective-permute-start | bytes 221192 | tf_op jit(solution)/shard_map/ppermute | solution.py:154

commit v16 on v15

--- a/solution.py
+++ b/solution.py
@@ -31,7 +31,7 @@
         at = at + kept[row, tile]
 
 
-def pack_kernel(tiles, slots, kept, doubles, first, second, table, block, places, sems):
+def pack_kernel(tiles, slots, kept, doubles, first, second, second_too, table, block, places, sems):
     table_copy = pltpu.make_async_copy(kept, table, sems.at[0])
     block_copy = pltpu.make_async_copy(doubles, block, sems.at[1])
     table_copy.start()
@@ -45,6 +45,7 @@
         to = slice(slot * TILE, (slot + 1) * TILE)
         first[:, to] = block[:half, tile]
         second[:, to] = block[half:, tile]
+        second_too[:, to] = block[half:, tile]
 
 
 def prepare_kernel(tiles, slots, kept, int_kept, integrals, first, second, gathered, product, table, int_table, held, places, sems):
@@ -74,6 +75,10 @@
         )
 
 
+def after_kernel(token, x, out):
+    pass
+
+
 def encode(x, out):
     pairs, width = x.shape
     largest = jnp.max(jnp.abs(x), axis=0, keepdims=True)
@@ -148,6 +153,19 @@
     half_of(out, early)[...] = half_of(base, early)[...] + decode(half_of(one, 0), half)
     total = half_of(base, 1 - early)[...] + own_sums[...] + decode(half_of(one, 1), half)
     half_of(out, 1 - early)[...] = total + decode(two, half) + decode(three, half)
+
+
+def after(token, x):
+    return pl.pallas_call(
+        after_kernel,
+        out_shape=jax.ShapeDtypeStruct(x.shape, x.dtype),
+        in_specs=[pl.BlockSpec(memory_space=pl.ANY)] * 2,
+        out_specs=pl.BlockSpec(memory_space=pl.ANY),
+        input_output_aliases={1: 0},
+        compiler_params=PARAMS,
+        cost_estimate=cost(0),
+        name="after",
+    )(token, x)
 
 
 def swap(x, axis, step):
@@ -168,11 +186,11 @@
     doubles, doubles_kept, integrals, integral_kept = (
         pltpu.with_memory_space_constraint(x, pltpu.HBM) for x in (doubles, doubles_kept, integrals, integral_kept.T)
     )
-    first, second = pl.pallas_call(
+    first, second, second_too = pl.pallas_call(
         functools.partial(pack_kernel, tiles, slots),
-        out_shape=[half_block] * 2,
+        out_shape=[half_block] * 3,
         in_specs=[HBM, HBM],
-        out_specs=[VMEM] * 2,
+        out_specs=[VMEM] * 3,
         scratch_shapes=[
             pltpu.SMEM(doubles_kept.shape, jnp.int32),
             pltpu.VMEM(doubles.shape, doubles.dtype),
@@ -186,8 +204,8 @@
     far_first = swap(first, "rows", 3)
     pair_first = swap(first, "rows", 1)
     near_first = swap(first, "rows", 2)
-    pair_second = swap(second, "rows", 1)
     far_second = swap(near_second, "rows", 1)
+    pair_second = swap(after(near_second, second_too), "rows", 1)
     gathered, product = pl.pallas_call(
         functools.partial(prepare_kernel, tiles, slots),
         out_shape=[jax.ShapeDtypeStruct((ROWS, slots * TILE, width), integrals.dtype), sums_shape],

time: 22.1 us -> 22.5 us (1.018)
  starting transfers between devices: 14.3 us -> 14.7 us
    ppermute x11, starting transfers between devices: 14.3 us -> 14.7 us  [swap(): return lax.ppermute(x, axis, [(i, i ^ step) for i in range(ROWS)])]
where the time goes in v16:
time: 22.5 us; the launch traced here: 22.4 us
  starting transfers between devices  14.7 us (65%)
  Pallas kernels  3.93 us (17%)
  waiting for transfers between devices  3.68 us (16%)
    ppermute x11, starting transfers between devices, swap(): return lax.ppermute(x, axis, [(i, i ^ step) for i in range(ROWS)])  14.7 us
    ppermute x11, waiting for transfers between devices, swap(): return lax.ppermute(x, axis, [(i, i ^ step) for i in range(ROWS)])  3.68 us
    pallas_call x1, Pallas kernels, local_few(): pl.pallas_call(functools.partial(prepare_kernel, tiles, slots), out_shape...  1.53 us
    pallas_call x4, Pallas kernels, on_vmem(): pl.pallas_call(kernel, out_shape=out_shape, in_specs=[VMEM] * len(args),...  1.4 us
    pallas_call x1, Pallas kernels, local_few(): pl.pallas_call(functools.partial(pack_kernel, tiles, slots), out_shape=[h...  1 us
  transfers between devices with their start and end apart: 11, of which 4 were waited for; matrix products, arithmetic and copies ran while one was open for 0% of the time, Pallas kernels for 10%

profile of v16, /device:TPU:0, one launch (start us, length us, event | category | flops | bytes accessed | tf_op | source)
XLA Modules:
  0.0 22.4 jit_solution(15652539593192320834)
XLA Ops:
  0.0 1.0 %pack.1 = (bf16[64,512]{1,0:T(8,128)(2,1)S(1)}, bf16[64,512]{1,0:T(8,128)(2,1)S(1)}, bf16[64,512]{1,0:T(8,128)(2,1)S(1)}) custom-call(s32[4,8]{1,0:T(4,128)} %kept.3, bf16[128,1024]{1,0:T(8,128)(2,1)} %doubles.1), custom_call_target="tpu_custom_call" | custom-call | tf_op jit(solution)/shard_map/pack/pallas_call | solution.py:189
  1.0 4.1 %collective-permute-start = (bf16[64,512]{1,0:T(8,128)(2,1)S(1)}, bf16[64,512]{1,0:T(8,128)(2,1)S(1)}, u32[]{:S(2)}, u32[]{:S(2)}) collective-permute-start(bf16[64,512]{1,0:T(8,128)(2,1)S(1)} %get-tuple-element.19.second), channel_id=1, source_target_pairs={{0,8},{4,12},{8,0},{12,4},{1,9},{5,13},{9,1},{13,5},{2,10},{6,14},... | collective-permute-start | bytes 196616 | tf_op jit(solution)/shard_map/ppermute | solution.py:172
  5.1 1.3 %collective-permute-start.1 = (bf16[64,512]{1,0:T(8,128)(2,1)S(1)}, bf16[64,512]{1,0:T(8,128)(2,1)S(1)}, u32[]{:S(2)}, u32[]{:S(2)}) collective-permute-start(bf16[64,512]{1,0:T(8,128)(2,1)S(1)} %get-tuple-element.18.first), channel_id=1, source_target_pairs={{0,12},{4,8},{8,4},{12,0},{1,13},{5,9},{9,5},{13,1},{2,14},{6,10},... | collective-permute-start | bytes 196616 | tf_op jit(solution)/shard_map/ppermute | solution.py:172
  6.5 0.2 %collective-permute-start.2 = (bf16[64,512]{1,0:T(8,128)(2,1)S(1)}, bf16[64,512]{1,0:T(8,128)(2,1)S(1)}, u32[]{:S(2)}, u32[]{:S(2)}) collective-permute-start(bf16[64,512]{1,0:T(8,128)(2,1)S(1)} %get-tuple-element.18.first), channel_id=1, source_target_pairs={{0,4},{4,0},{8,12},{12,8},{1,5},{5,1},{9,13},{13,9},{2,6},{6,2},{1... | collective-permute-start | bytes 196616 | tf_op jit(solution)/shard_map/ppermute | solution.py:172
  6.7 2.8 %collective-permute-start.5 = (bf16[64,512]{1,0:T(8,128)(2,1)S(1)}, bf16[64,512]{1,0:T(8,128)(2,1)S(1)}, u32[]{:S(2)}, u32[]{:S(2)}) collective-permute-start(bf16[64,512]{1,0:T(8,128)(2,1)S(1)} %get-tuple-element.18.first), channel_id=1, source_target_pairs={{0,8},{4,12},{8,0},{12,4},{1,9},{5,13},{9,1},{13,5},{2,10},{6,14},... | collective-permute-start | bytes 196616 | tf_op jit(solution)/shard_map/ppermute | solution.py:172
  9.5 0.0 collective-permute-done.near.token
  9.5 2.0 %collective-permute-start.6 = (bf16[64,512]{1,0:T(8,128)(2,1)S(1)}, bf16[64,512]{1,0:T(8,128)(2,1)S(1)}, u32[]{:S(2)}, u32[]{:S(2)}) collective-permute-start(bf16[64,512]{1,0:T(8,128)(2,1)S(1)} %collective-permute-done.near.token), channel_id=1, source_target_pairs={{0,4},{4,0},{8,12},{12,8},{1,5},{5,1},{9,13},{13,9},{2,6},{6,2},{1... | collective-permute-start | bytes 196616 | tf_op jit(solution)/shard_map/ppermute | solution.py:172
  11.5 0.0 collective-permute-start.7
  11.5 1.5 %prepare.1 = (bf16[4,512,256]{2,1,0:T(8,128)(2,1)S(1)}, f32[128,256]{1,0:T(8,128)S(1)}) custom-call(s32[4,8]{1,0:T(4,128)} %kept.3, s32[2,8]{1,0:T(2,128)} %bitcast.1, bf16[1024,256]{1,0:T(8,128)(2,1)} %integrals.1, bf16[64,512]{1,0:T(8,128)(2,1)S(1)} %get-tuple-element.18.first, bf16[64,512]{1,0:T(8,128)(2,1)S(1)} %get-tuple-element.19.second), custom_call_target="tpu_custom_call" | custom-call | bytes 1024 | tf_op jit(solution)/shard_map/prepare/pallas_call | solution.py:209
  13.1 0.0 collective-permute-done.1.far
  13.1 0.0 collective-permute-done.2.pair
  13.1 0.3 %early.1 = (f32[64,256]{1,0:T(8,128)S(1)}, f32[64,256]{1,0:T(8,128)S(1)}, s16[144,128]{1,0:T(8,128)(2,1)S(1)}, s16[144,128]{1,0:T(8,128)(2,1)S(1)}) custom-call(f32[128,256]{1,0:T(8,128)S(1)} %get-tuple-element.20.product, bf16[4,512,256]{2,1,0:T(8,128)(2,1)S(1)} %get-tuple-element.21.gathered, bf16[64,512]{1,0:T(8,128)(2,1)S(1)} %collective-permute-done.near.token, ...), custom_call_target="tpu_custom_call" | custom-call | bytes 1024 | tf_op jit(solution)/shard_map/early/pallas_call | solution.py:227
  13.4 2.0 %collective-permute-start.3 = (s16[144,128]{1,0:T(8,128)(2,1)S(1)}, s16[144,128]{1,0:T(8,128)(2,1)S(1)}, u32[]{:S(2)}, u32[]{:S(2)}) collective-permute-start(s16[144,128]{1,0:T(8,128)(2,1)S(1)} %get-tuple-element.23), channel_id=1, source_target_pairs={{0,2},{1,3},{2,0},{3,1},{4,6},{5,7},{6,4},{7,5},{8,10},{9,11},{10,... | collective-permute-start | bytes 110600 | tf_op jit(solution)/shard_map/ppermute | solution.py:172
  15.4 0.0 collective-permute-start.4
  15.4 0.0 collective-permute-done.5.near
  15.4 0.0 collective-permute-done.6.far
  15.4 0.3 %collective-permute-done.7.pair = bf16[64,512]{1,0:T(8,128)(2,1)S(1)} collective-permute-done((bf16[64,512]{1,0:T(8,128)(2,1)S(1)}, bf16[64,512]{1,0:T(8,128)(2,1)S(1)}, u32[]{:S(2)}, u32[]{:S(2)}) %collective-permute-start.7) | collective-permute-done | bytes 65568 | tf_op jit(solution)/shard_map/ppermute | solution.py:172
  15.8 0.0 copy-start
  15.8 0.3 %late.1 = (f32[64,256]{1,0:T(8,128)S(1)}, s16[288,128]{1,0:T(8,128)(2,1)S(1)}, s16[144,128]{1,0:T(8,128)(2,1)S(1)}, s16[144,128]{1,0:T(8,128)(2,1)S(1)}) custom-call(f32[64,256]{1,0:T(8,128)S(1)} %get-tuple-element.25.core_sums, f32[128,256]{1,0:T(8,128)S(1)} %get-tuple-element.20.product, bf16[4,512,256]{2,1,0:T(8,128)(2,1)S(1)} %get-tuple-element.21.gathered, ...), custom_call_target="tpu_custom_call" | custom-call | flops 99999997952 | bytes 1024 | tf_op jit(solution)/shard_map/late/pallas_call | solution.py:227
  16.1 1.8 %collective-permute-start.8 = (s16[144,128]{1,0:T(8,128)(2,1)S(1)}, s16[144,128]{1,0:T(8,128)(2,1)S(1)}, u32[]{:S(2)}, u32[]{:S(2)}) collective-permute-start(s16[144,128]{1,0:T(8,128)(2,1)S(1)} %get-tuple-element.28), channel_id=1, source_target_pairs={{0,2},{1,3},{2,0},{3,1},{4,6},{5,7},{6,4},{7,5},{8,10},{9,11},{10,... | collective-permute-start | bytes 110600 | tf_op jit(solution)/shard_map/ppermute | solution.py:172
  17.9 0.0 collective-permute-start.9
  17.9 0.4 %collective-permute-start.10 = (s16[288,128]{1,0:T(8,128)(2,1)S(1)}, s16[288,128]{1,0:T(8,128)(2,1)S(1)}, u32[]{:S(2)}, u32[]{:S(2)}) collective-permute-start(s16[288,128]{1,0:T(8,128)(2,1)S(1)} %get-tuple-element.30), channel_id=1, source_target_pairs={{0,1},{1,0},{2,3},{3,2},{4,5},{5,4},{6,7},{7,6},{8,9},{9,8},{10,11... | collective-permute-start | bytes 221192 | tf_op jit(solution)/shard_map/ppermute | solution.py:172
  18.3 0.0 collective-permute-done.3.two
  18.3 0.5 %collective-permute-done.4.three = s16[144,128]{1,0:T(8,128)(2,1)S(1)} collective-permute-done((s16[144,128]{1,0:T(8,128)(2,1)S(1)}, s16[144,128]{1,0:T(8,128)(2,1)S(1)}, u32[]{:S(2)}, u32[]{:S(2)}) %collective-permute-start.4) | collective-permute-done | bytes 36896 | tf_op jit(solution)/shard_map/ppermute | solution.py:172
  18.8 0.0 copy-done
  18.8 1.3 %collective-permute-done.8.two = s16[144,128]{1,0:T(8,128)(2,1)S(1)} collective-permute-done((s16[144,128]{1,0:T(8,128)(2,1)S(1)}, s16[144,128]{1,0:T(8,128)(2,1)S(1)}, u32[]{:S(2)}, u32[]{:S(2)}) %collective-permute-start.8) | collective-permute-done | bytes 36896 | tf_op jit(solution)/shard_map/ppermute | solution.py:172
  20.1 1.5 %collective-permute-done.9.three = s16[144,128]{1,0:T(8,128)(2,1)S(1)} collective-permute-done((s16[144,128]{1,0:T(8,128)(2,1)S(1)}, s16[144,128]{1,0:T(8,128)(2,1)S(1)}, u32[]{:S(2)}, u32[]{:S(2)}) %collective-permute-start.9) | collective-permute-done | bytes 36896 | tf_op jit(solution)/shard_map/ppermute | solution.py:172
  21.6 0.0 collective-permute-done.10.one
  21.6 0.7 %last.1 = f32[128,256]{1,0:T(8,128)} custom-call(f32[128,256]{1,0:T(8,128)S(1)} %first.1.base, f32[64,256]{1,0:T(8,128)S(1)} %get-tuple-element.27.own_sums, s16[144,128]{1,0:T(8,128)(2,1)S(1)} %collective-permute-done.8.two, s16[144,128]{1,0:T(8,128)(2,1)S(1)} %collective-permute-done.9.three, s16[288,128]{1,0:T(8,128)(2,1)S(1)} %collective-permute-done.10.one), custom_call_target="tpu_custom_call" | custom-call | bytes 1024 | tf_op jit(solution)/shard_map/last/pallas_call | solution.py:227
  (2 shorter events, 0.0 us)
Async XLA Ops:
  1.0 8.5 %collective-permute-start = (bf16[64,512]{1,0:T(8,128)(2,1)S(1)}, bf16[64,512]{1,0:T(8,128)(2,1)S(1)}, u32[]{:S(2)}, u32[]{:S(2)}) collective-permute-start(bf16[64,512]{1,0:T(8,128)(2,1)S(1)} %get-tuple-element.19.second), channel_id=1, source_target_pairs={{0,8},{4,12},{8,0},{12,4},{1,9},{5,13},{9,1},{13,5},{2,10},{6,14},... | collective-permute-start | bytes 196616 | tf_op jit(solution)/shard_map/ppermute | solution.py:172
  5.1 8.0 %collective-permute-start.1 = (bf16[64,512]{1,0:T(8,128)(2,1)S(1)}, bf16[64,512]{1,0:T(8,128)(2,1)S(1)}, u32[]{:S(2)}, u32[]{:S(2)}) collective-permute-start(bf16[64,512]{1,0:T(8,128)(2,1)S(1)} %get-tuple-element.18.first), channel_id=1, source_target_pairs={{0,12},{4,8},{8,4},{12,0},{1,13},{5,9},{9,5},{13,1},{2,14},{6,10},... | collective-permute-start | bytes 196616 | tf_op jit(solution)/shard_map/ppermute | solution.py:172
  6.5 6.6 %collective-permute-start.2 = (bf16[64,512]{1,0:T(8,128)(2,1)S(1)}, bf16[64,512]{1,0:T(8,128)(2,1)S(1)}, u32[]{:S(2)}, u32[]{:S(2)}) collective-permute-start(bf16[64,512]{1,0:T(8,128)(2,1)S(1)} %get-tuple-element.18.first), channel_id=1, source_target_pairs={{0,4},{4,0},{8,12},{12,8},{1,5},{5,1},{9,13},{13,9},{2,6},{6,2},{1... | collective-permute-start | bytes 196616 | tf_op jit(solution)/shard_map/ppermute | solution.py:172
  6.7 8.7 %collective-permute-start.5 = (bf16[64,512]{1,0:T(8,128)(2,1)S(1)}, bf16[64,512]{1,0:T(8,128)(2,1)S(1)}, u32[]{:S(2)}, u32[]{:S(2)}) collective-permute-start(bf16[64,512]{1,0:T(8,128)(2,1)S(1)} %get-tuple-element.18.first), channel_id=1, source_target_pairs={{0,8},{4,12},{8,0},{12,4},{1,9},{5,13},{9,1},{13,5},{2,10},{6,14},... | collective-permute-start | bytes 196616 | tf_op jit(solution)/shard_map/ppermute | solution.py:172
  9.5 5.9 %collective-permute-start.6 = (bf16[64,512]{1,0:T(8,128)(2,1)S(1)}, bf16[64,512]{1,0:T(8,128)(2,1)S(1)}, u32[]{:S(2)}, u32[]{:S(2)}) collective-permute-start(bf16[64,512]{1,0:T(8,128)(2,1)S(1)} %collective-permute-done.near.token), channel_id=1, source_target_pairs={{0,4},{4,0},{8,12},{12,8},{1,5},{5,1},{9,13},{13,9},{2,6},{6,2},{1... | collective-permute-start | bytes 196616 | tf_op jit(solution)/shard_map/ppermute | solution.py:172
  11.5 4.3 %collective-permute-start.7 = (bf16[64,512]{1,0:T(8,128)(2,1)S(1)}, bf16[64,512]{1,0:T(8,128)(2,1)S(1)}, u32[]{:S(2)}, u32[]{:S(2)}) collective-permute-start(bf16[64,512]{1,0:T(8,128)(2,1)S(1)} %after.1), channel_id=1, source_target_pairs={{0,4},{4,0},{8,12},{12,8},{1,5},{5,1},{9,13},{13,9},{2,6},{6,2},{1... | collective-permute-start | bytes 196616 | tf_op jit(solution)/shard_map/ppermute | solution.py:172
  13.4 4.9 %collective-permute-start.3 = (s16[144,128]{1,0:T(8,128)(2,1)S(1)}, s16[144,128]{1,0:T(8,128)(2,1)S(1)}, u32[]{:S(2)}, u32[]{:S(2)}) collective-permute-start(s16[144,128]{1,0:T(8,128)(2,1)S(1)} %get-tuple-element.23), channel_id=1, source_target_pairs={{0,2},{1,3},{2,0},{3,1},{4,6},{5,7},{6,4},{7,5},{8,10},{9,11},{10,... | collective-permute-start | bytes 110600 | tf_op jit(solution)/shard_map/ppermute | solution.py:172
  15.4 3.4 %collective-permute-start.4 = (s16[144,128]{1,0:T(8,128)(2,1)S(1)}, s16[144,128]{1,0:T(8,128)(2,1)S(1)}, u32[]{:S(2)}, u32[]{:S(2)}) collective-permute-start(s16[144,128]{1,0:T(8,128)(2,1)S(1)} %get-tuple-element.24), channel_id=1, source_target_pairs={{0,3},{1,2},{2,1},{3,0},{4,7},{5,6},{6,5},{7,4},{8,11},{9,10},{10,... | collective-permute-start | bytes 110600 | tf_op jit(solution)/shard_map/ppermute | solution.py:172
  15.8 3.0 %copy-start = (f32[128,256]{1,0:T(8,128)S(1)}, f32[128,256]{1,0:T(8,128)}, u32[]{:S(2)}) copy-start(f32[128,256]{1,0:T(8,128)} %residual.1) | copy-start | bytes 393220
  16.1 4.0 %collective-permute-start.8 = (s16[144,128]{1,0:T(8,128)(2,1)S(1)}, s16[144,128]{1,0:T(8,128)(2,1)S(1)}, u32[]{:S(2)}, u32[]{:S(2)}) collective-permute-start(s16[144,128]{1,0:T(8,128)(2,1)S(1)} %get-tuple-element.28), channel_id=1, source_target_pairs={{0,2},{1,3},{2,0},{3,1},{4,6},{5,7},{6,4},{7,5},{8,10},{9,11},{10,... | collective-permute-start | bytes 110600 | tf_op jit(solution)/shard_map/ppermute | solution.py:172
  17.9 3.8 %collective-permute-start.9 = (s16[144,128]{1,0:T(8,128)(2,1)S(1)}, s16[144,128]{1,0:T(8,128)(2,1)S(1)}, u32[]{:S(2)}, u32[]{:S(2)}) collective-permute-start(s16[144,128]{1,0:T(8,128)(2,1)S(1)} %get-tuple-element.29), channel_id=1, source_target_pairs={{0,3},{1,2},{2,1},{3,0},{4,7},{5,6},{6,5},{7,4},{8,11},{9,10},{10,... | collective-permute-start | bytes 110600 | tf_op jit(solution)/shard_map/ppermute | solution.py:172
  17.9 3.8 %collective-permute-start.10 = (s16[288,128]{1,0:T(8,128)(2,1)S(1)}, s16[288,128]{1,0:T(8,128)(2,1)S(1)}, u32[]{:S(2)}, u32[]{:S(2)}) collective-permute-start(s16[288,128]{1,0:T(8,128)(2,1)S(1)} %get-tuple-element.30), channel_id=1, source_target_pairs={{0,1},{1,0},{2,3},{3,2},{4,5},{5,4},{6,7},{7,6},{8,9},{9,8},{10,11... | collective-permute-start | bytes 221192 | tf_op jit(solution)/shard_map/ppermute | solution.py:172

commit v17 on v13

--- a/solution.py
+++ b/solution.py
@@ -95,27 +95,56 @@
     return jnp.concatenate(parts, axis=1)
 
 
-def ladder_kernel(product, gathered, pair, near_first, near_second, far_first, far_second, kept_sums, *rest):
-    outs, sums = rest[:-1], rest[-1]
-    mine = lax.axis_index("rows") ^ lax.axis_index("cols")
-    half = near_first.shape[0]
+def place():
+    return lax.axis_index("rows") ^ lax.axis_index("cols")
+
+
+def early_kernel(product, gathered, pair, near_second, far_first, sums):
+    mine = place()
+    half = near_second.shape[0]
     sums[mine] = product[...]
     sums[mine ^ 1] = jnp.dot(pair[...], gathered[mine ^ 1], preferred_element_type=jnp.float32)
-    for step, start, block in ((2, 0, near_first), (3, 0, far_first), (2, half, near_second), (3, half, far_second)):
+    for step, start, block in ((2, half, near_second), (3, 0, far_first)):
         sums[mine ^ step, start : start + half, :] = jnp.dot(
             block[...], gathered[mine ^ step], preferred_element_type=jnp.float32
         )
-    kept_sums[...] = sums[0]
-    for n, out in enumerate(outs, 1):
-        encode(sums[n], out)
-
-
-def finish_kernel(residual, kept_sums, *rest):
-    messages, out = rest[:-1], rest[-1]
-    total = residual[...] + kept_sums[...]
-    for message in messages:
-        total = total + decode(message, total.shape[0])
-    out[...] = total
+
+
+def whole(n, early, near_sums, far_sums, out):
+    half = near_sums.shape[0]
+    step = place() ^ n
+    out[...] = early[n]
+
+    @pl.when(step == 2)
+    def _():
+        out[:half, :] = near_sums[...]
+
+    @pl.when(step == 3)
+    def _():
+        out[half:, :] = far_sums[...]
+
+
+def late_kernel(early, gathered, near_first, far_second, near_sums, far_sums, two, held):
+    mine = place()
+    near_sums[...] = jnp.dot(near_first[...], gathered[mine ^ 2], preferred_element_type=jnp.float32)
+    far_sums[...] = jnp.dot(far_second[...], gathered[mine ^ 3], preferred_element_type=jnp.float32)
+    whole(2, early, near_sums, far_sums, held)
+    encode(held[...], two)
+
+
+def rest_kernel(early, near_sums, far_sums, one, three, kept_sums, held):
+    for n, out in ((3, three), (1, one)):
+        whole(n, early, near_sums, far_sums, held)
+        encode(held[...], out)
+    whole(0, early, near_sums, far_sums, kept_sums)
+
+
+def first_kernel(residual, kept_sums, two, out):
+    out[...] = residual[...] + kept_sums[...] + decode(two, out.shape[0])
+
+
+def last_kernel(base, three, one, out):
+    out[...] = base[...] + decode(three, out.shape[0]) + decode(one, out.shape[0])
 
 
 def swap(x, axis, step):
@@ -166,28 +195,35 @@
             pltpu.SemaphoreType.DMA((3,)),
         ],
         compiler_params=PARAMS,
-        cost_estimate=cost(0),
+        cost_estimate=cost(10**9),
         name="prepare",
     )(doubles_kept, integral_kept, integrals, packed)
-    kept_sums, *messages = pl.pallas_call(
-        ladder_kernel,
-        out_shape=[sums_shape] + [message] * (ROWS - 1),
-        in_specs=[VMEM] * 7,
-        out_specs=[VMEM] * ROWS,
-        scratch_shapes=[pltpu.VMEM((ROWS, pairs, width), jnp.float32)],
-        compiler_params=PARAMS,
-        cost_estimate=cost(10**11),
-        name="ladder",
-    )(product, gathered, pair, near_first, near_second, far_first, far_second)
-    messages = [swap(messages[step - 1], "cols", step) for step in (2, 3, 1)]
-    return pl.pallas_call(
-        finish_kernel,
-        out_shape=sums_shape,
-        in_specs=[VMEM] * (ROWS + 1),
-        out_specs=VMEM,
-        compiler_params=PARAMS,
-        name="finish",
-    )(residual, kept_sums, *messages)
+
+    def on_vmem(kernel, name, flops, out_shape, *args, scratch=()):
+        return pl.pallas_call(
+            kernel,
+            out_shape=out_shape,
+            in_specs=[VMEM] * len(args),
+            out_specs=jax.tree.map(lambda _: VMEM, out_shape),
+            scratch_shapes=scratch,
+            compiler_params=PARAMS,
+            cost_estimate=cost(flops),
+            name=name,
+        )(*args)
+
+    held = [pltpu.VMEM((pairs, width), jnp.float32)]
+    half_sums = jax.ShapeDtypeStruct((pairs // 2, width), jnp.float32)
+    all_sums = jax.ShapeDtypeStruct((ROWS, pairs, width), jnp.float32)
+    early = on_vmem(early_kernel, "early", 0, all_sums, product, gathered, pair, near_second, far_first)
+    near_sums, far_sums, two = on_vmem(
+        late_kernel, "late", 10**11, [half_sums] * 2 + [message], early, gathered, near_first, far_second, scratch=held
+    )
+    one, three, kept_sums = on_vmem(
+        rest_kernel, "rest", 0, [message] * 2 + [sums_shape], early, near_sums, far_sums, scratch=held
+    )
+    two, three, one = swap(two, "cols", 2), swap(three, "cols", 3), swap(one, "cols", 1)
+    base = on_vmem(first_kernel, "first", 0, sums_shape, residual, kept_sums, two)
+    return on_vmem(last_kernel, "last", 0, sums_shape, base, three, one)
 
 
 def local_many(doubles, doubles_kept, integrals, integral_kept, residual):

time: 21.9 us -> 21.7 us (level)
  waiting for transfers between devices: 5.74 us -> 5.23 us
    ppermute x8, waiting for transfers between devices: 5.74 us -> 5.23 us  [swap(): return lax.ppermute(x, axis, [(i, i ^ step) for i in range(ROWS)])]
    pallas_call x2 -> x5, Pallas kernels: 1.16 us -> 1.37 us  [on_vmem(): pl.pallas_call(kernel, out_shape=out_shape, in_specs=[VMEM] * len(args),...]
  transfers between devices with their start and end apart: 8 -> 8, of which waited for: 5 -> 5; matrix products, arithmetic and copies ran while one was open for 0% -> 0% of each run, Pallas kernels for 7% -> 9%
where the time goes in v17:
time: 21.7 us; the launch traced here: 21.5 us
  starting transfers between devices  12.3 us (57%)
  waiting for transfers between devices  5.23 us (24%)
  Pallas kernels  3.89 us (18%)
    ppermute x8, starting transfers between devices, swap(): return lax.ppermute(x, axis, [(i, i ^ step) for i in range(ROWS)])  12.3 us
    ppermute x8, waiting for transfers between devices, swap(): return lax.ppermute(x, axis, [(i, i ^ step) for i in range(ROWS)])  5.23 us
    pallas_call x1, Pallas kernels, local_few(): pl.pallas_call(functools.partial(prepare_kernel, tiles, slots), out_shape...  1.52 us
    pallas_call x5, Pallas kernels, on_vmem(): pl.pallas_call(kernel, out_shape=out_shape, in_specs=[VMEM] * len(args),...  1.37 us
    pallas_call x1, Pallas kernels, local_few(): pl.pallas_call(functools.partial(pack_kernel, tiles, slots), out_shape=[j...  1 us
  transfers between devices with their start and end apart: 8, of which 5 were waited for; matrix products, arithmetic and copies ran while one was open for 0% of the time, Pallas kernels for 9%

profile of v17, /device:TPU:0, one launch (start us, length us, event | category | flops | bytes accessed | tf_op | source)
XLA Modules:
  0.0 21.5 jit_solution(6287232125096390123)
XLA Ops:
  0.0 1.0 %pack.1 = (bf16[128,512]{1,0:T(8,128)(2,1)S(1)}, bf16[64,512]{1,0:T(8,128)(2,1)S(1)}, bf16[64,512]{1,0:T(8,128)(2,1)S(1)}) custom-call(s32[4,8]{1,0:T(4,128)} %kept.3, bf16[128,1024]{1,0:T(8,128)(2,1)} %doubles.1), custom_call_target="tpu_custom_call" | custom-call | tf_op jit(solution)/shard_map/pack/pallas_call | solution.py:166
  1.0 4.1 %collective-permute-start.1 = (bf16[64,512]{1,0:T(8,128)(2,1)S(1)}, bf16[64,512]{1,0:T(8,128)(2,1)S(1)}, u32[]{:S(2)}, u32[]{:S(2)}) collective-permute-start(bf16[64,512]{1,0:T(8,128)(2,1)S(1)} %get-tuple-element.19), channel_id=1, source_target_pairs={{0,8},{4,12},{8,0},{12,4},{1,9},{5,13},{9,1},{13,5},{2,10},{6,14},... | collective-permute-start | bytes 196616 | tf_op jit(solution)/shard_map/ppermute | solution.py:151
  5.1 1.6 %collective-permute-start = (bf16[128,512]{1,0:T(8,128)(2,1)S(1)}, bf16[128,512]{1,0:T(8,128)(2,1)S(1)}, u32[]{:S(2)}, u32[]{:S(2)}) collective-permute-start(bf16[128,512]{1,0:T(8,128)(2,1)S(1)} %get-tuple-element.16.own), channel_id=1, source_target_pairs={{0,4},{4,0},{8,12},{12,8},{1,5},{5,1},{9,13},{13,9},{2,6},{6,2},{1... | collective-permute-start | bytes 393224 | tf_op jit(solution)/shard_map/ppermute | solution.py:151
  6.7 0.0 collective-permute-start.2
  6.7 1.9 %collective-permute-start.3 = (bf16[64,512]{1,0:T(8,128)(2,1)S(1)}, bf16[64,512]{1,0:T(8,128)(2,1)S(1)}, u32[]{:S(2)}, u32[]{:S(2)}) collective-permute-start(bf16[64,512]{1,0:T(8,128)(2,1)S(1)} %get-tuple-element.20), channel_id=1, source_target_pairs={{0,8},{4,12},{8,0},{12,4},{1,9},{5,13},{9,1},{13,5},{2,10},{6,14},... | collective-permute-start | bytes 196616 | tf_op jit(solution)/shard_map/ppermute | solution.py:151
  8.6 0.0 collective-permute-done.1.near_second
  8.6 2.5 %collective-permute-start.4 = (bf16[64,512]{1,0:T(8,128)(2,1)S(1)}, bf16[64,512]{1,0:T(8,128)(2,1)S(1)}, u32[]{:S(2)}, u32[]{:S(2)}) collective-permute-start(bf16[64,512]{1,0:T(8,128)(2,1)S(1)} %collective-permute-done.1.near_second), channel_id=1, source_target_pairs={{0,4},{4,0},{8,12},{12,8},{1,5},{5,1},{9,13},{13,9},{2,6},{6,2},{1... | collective-permute-start | bytes 196616 | tf_op jit(solution)/shard_map/ppermute | solution.py:151
  11.1 1.5 %prepare.1 = (bf16[4,512,256]{2,1,0:T(8,128)(2,1)S(1)}, f32[128,256]{1,0:T(8,128)S(1)}) custom-call(s32[4,8]{1,0:T(4,128)} %kept.3, s32[2,8]{1,0:T(2,128)} %bitcast.1, bf16[1024,256]{1,0:T(8,128)(2,1)} %integrals.1, bf16[128,512]{1,0:T(8,128)(2,1)S(1)} %get-tuple-element.16.own), custom_call_target="tpu_custom_call" | custom-call | flops 1000000000 | bytes 1024 | tf_op jit(solution)/shard_map/prepare/pallas_call | solution.py:185
  12.6 1.0 %collective-permute-done.2.far_first = bf16[64,512]{1,0:T(8,128)(2,1)S(1)} collective-permute-done((bf16[64,512]{1,0:T(8,128)(2,1)S(1)}, bf16[64,512]{1,0:T(8,128)(2,1)S(1)}, u32[]{:S(2)}, u32[]{:S(2)}) %collective-permute-start.2) | collective-permute-done | bytes 65568 | tf_op jit(solution)/shard_map/ppermute | solution.py:151
  13.6 0.0 collective-permute-done.pair
  13.6 0.3 %early.1 = f32[4,128,256]{2,1,0:T(8,128)S(1)} custom-call(f32[128,256]{1,0:T(8,128)S(1)} %get-tuple-element.17.product, bf16[4,512,256]{2,1,0:T(8,128)(2,1)S(1)} %get-tuple-element.18.gathered, bf16[128,512]{1,0:T(8,128)(2,1)S(1)} %collective-permute-done.pair, bf16[64,512]{1,0:T(8,128)(2,1)S(1)} %collective-permute-done.1.near_second, ...), custom_call_target="tpu_custom_call" | custom-call | bytes 1024 | tf_op jit(solution)/shard_map/early/pallas_call | solution.py:203
  13.9 0.3 %collective-permute-done.3.near_first = bf16[64,512]{1,0:T(8,128)(2,1)S(1)} collective-permute-done((bf16[64,512]{1,0:T(8,128)(2,1)S(1)}, bf16[64,512]{1,0:T(8,128)(2,1)S(1)}, u32[]{:S(2)}, u32[]{:S(2)}) %collective-permute-start.3) | collective-permute-done | bytes 65568 | tf_op jit(solution)/shard_map/ppermute | solution.py:151
  14.1 0.5 %collective-permute-done.4.far_second = bf16[64,512]{1,0:T(8,128)(2,1)S(1)} collective-permute-done((bf16[64,512]{1,0:T(8,128)(2,1)S(1)}, bf16[64,512]{1,0:T(8,128)(2,1)S(1)}, u32[]{:S(2)}, u32[]{:S(2)}) %collective-permute-start.4) | collective-permute-done | bytes 65568 | tf_op jit(solution)/shard_map/ppermute | solution.py:151
  14.7 0.3 %late.1 = (f32[64,256]{1,0:T(8,128)S(1)}, f32[64,256]{1,0:T(8,128)S(1)}, s16[272,128]{1,0:T(8,128)(2,1)S(1)}) custom-call(f32[4,128,256]{2,1,0:T(8,128)S(1)} %early.1, bf16[4,512,256]{2,1,0:T(8,128)(2,1)S(1)} %get-tuple-element.18.gathered, bf16[64,512]{1,0:T(8,128)(2,1)S(1)} %collective-permute-done.3.near_first, ...), custom_call_target="tpu_custom_call" | custom-call | flops 99999997952 | bytes 1024 | tf_op jit(solution)/shard_map/late/pallas_call | solution.py:203
  15.0 1.8 %collective-permute-start.5 = (s16[272,128]{1,0:T(8,128)(2,1)S(1)}, s16[272,128]{1,0:T(8,128)(2,1)S(1)}, u32[]{:S(2)}, u32[]{:S(2)}) collective-permute-start(s16[272,128]{1,0:T(8,128)(2,1)S(1)} %get-tuple-element.24), channel_id=1, source_target_pairs={{0,2},{1,3},{2,0},{3,1},{4,6},{5,7},{6,4},{7,5},{8,10},{9,11},{10,... | collective-permute-start | bytes 208904 | tf_op jit(solution)/shard_map/ppermute | solution.py:151
  16.8 0.0 copy-start
  16.8 0.1 rest.1
  16.9 0.1 collective-permute-start.6
  17.0 0.4 %collective-permute-start.7 = (s16[272,128]{1,0:T(8,128)(2,1)S(1)}, s16[272,128]{1,0:T(8,128)(2,1)S(1)}, u32[]{:S(2)}, u32[]{:S(2)}) collective-permute-start(s16[272,128]{1,0:T(8,128)(2,1)S(1)} %get-tuple-element.26), channel_id=1, source_target_pairs={{0,1},{1,0},{2,3},{3,2},{4,5},{5,4},{6,7},{7,6},{8,9},{9,8},{10,11... | collective-permute-start | bytes 208904 | tf_op jit(solution)/shard_map/ppermute | solution.py:151
  17.4 2.0 %collective-permute-done.5.two = s16[272,128]{1,0:T(8,128)(2,1)S(1)} collective-permute-done((s16[272,128]{1,0:T(8,128)(2,1)S(1)}, s16[272,128]{1,0:T(8,128)(2,1)S(1)}, u32[]{:S(2)}, u32[]{:S(2)}) %collective-permute-start.5) | collective-permute-done | bytes 69664 | tf_op jit(solution)/shard_map/ppermute | solution.py:151
  19.3 0.0 copy-done
  19.4 1.5 %collective-permute-done.6.three = s16[272,128]{1,0:T(8,128)(2,1)S(1)} collective-permute-done((s16[272,128]{1,0:T(8,128)(2,1)S(1)}, s16[272,128]{1,0:T(8,128)(2,1)S(1)}, u32[]{:S(2)}, u32[]{:S(2)}) %collective-permute-start.6) | collective-permute-done | bytes 69664 | tf_op jit(solution)/shard_map/ppermute | solution.py:151
  20.8 0.0 collective-permute-done.7.one
  20.8 0.7 %last.1 = f32[128,256]{1,0:T(8,128)} custom-call(f32[128,256]{1,0:T(8,128)S(1)} %first.1.base, s16[272,128]{1,0:T(8,128)(2,1)S(1)} %collective-permute-done.6.three, s16[272,128]{1,0:T(8,128)(2,1)S(1)} %collective-permute-done.7.one), custom_call_target="tpu_custom_call" | custom-call | bytes 1024 | tf_op jit(solution)/shard_map/last/pallas_call | solution.py:203
  (1 shorter events, 0.0 us)
Async XLA Ops:
  1.0 7.6 %collective-permute-start.1 = (bf16[64,512]{1,0:T(8,128)(2,1)S(1)}, bf16[64,512]{1,0:T(8,128)(2,1)S(1)}, u32[]{:S(2)}, u32[]{:S(2)}) collective-permute-start(bf16[64,512]{1,0:T(8,128)(2,1)S(1)} %get-tuple-element.19), channel_id=1, source_target_pairs={{0,8},{4,12},{8,0},{12,4},{1,9},{5,13},{9,1},{13,5},{2,10},{6,14},... | collective-permute-start | bytes 196616 | tf_op jit(solution)/shard_map/ppermute | solution.py:151
  5.1 8.5 %collective-permute-start = (bf16[128,512]{1,0:T(8,128)(2,1)S(1)}, bf16[128,512]{1,0:T(8,128)(2,1)S(1)}, u32[]{:S(2)}, u32[]{:S(2)}) collective-permute-start(bf16[128,512]{1,0:T(8,128)(2,1)S(1)} %get-tuple-element.16.own), channel_id=1, source_target_pairs={{0,4},{4,0},{8,12},{12,8},{1,5},{5,1},{9,13},{13,9},{2,6},{6,2},{1... | collective-permute-start | bytes 393224 | tf_op jit(solution)/shard_map/ppermute | solution.py:151
  6.7 6.9 %collective-permute-start.2 = (bf16[64,512]{1,0:T(8,128)(2,1)S(1)}, bf16[64,512]{1,0:T(8,128)(2,1)S(1)}, u32[]{:S(2)}, u32[]{:S(2)}) collective-permute-start(bf16[64,512]{1,0:T(8,128)(2,1)S(1)} %get-tuple-element.20), channel_id=1, source_target_pairs={{0,12},{4,8},{8,4},{12,0},{1,13},{5,9},{9,5},{13,1},{2,14},{6,10},... | collective-permute-start | bytes 196616 | tf_op jit(solution)/shard_map/ppermute | solution.py:151
  6.7 7.4 %collective-permute-start.3 = (bf16[64,512]{1,0:T(8,128)(2,1)S(1)}, bf16[64,512]{1,0:T(8,128)(2,1)S(1)}, u32[]{:S(2)}, u32[]{:S(2)}) collective-permute-start(bf16[64,512]{1,0:T(8,128)(2,1)S(1)} %get-tuple-element.20), channel_id=1, source_target_pairs={{0,8},{4,12},{8,0},{12,4},{1,9},{5,13},{9,1},{13,5},{2,10},{6,14},... | collective-permute-start | bytes 196616 | tf_op jit(solution)/shard_map/ppermute | solution.py:151
  8.6 6.1 %collective-permute-start.4 = (bf16[64,512]{1,0:T(8,128)(2,1)S(1)}, bf16[64,512]{1,0:T(8,128)(2,1)S(1)}, u32[]{:S(2)}, u32[]{:S(2)}) collective-permute-start(bf16[64,512]{1,0:T(8,128)(2,1)S(1)} %collective-permute-done.1.near_second), channel_id=1, source_target_pairs={{0,4},{4,0},{8,12},{12,8},{1,5},{5,1},{9,13},{13,9},{2,6},{6,2},{1... | collective-permute-start | bytes 196616 | tf_op jit(solution)/shard_map/ppermute | solution.py:151
  15.0 4.4 %collective-permute-start.5 = (s16[272,128]{1,0:T(8,128)(2,1)S(1)}, s16[272,128]{1,0:T(8,128)(2,1)S(1)}, u32[]{:S(2)}, u32[]{:S(2)}) collective-permute-start(s16[272,128]{1,0:T(8,128)(2,1)S(1)} %get-tuple-element.24), channel_id=1, source_target_pairs={{0,2},{1,3},{2,0},{3,1},{4,6},{5,7},{6,4},{7,5},{8,10},{9,11},{10,... | collective-permute-start | bytes 208904 | tf_op jit(solution)/shard_map/ppermute | solution.py:151
  16.8 2.5 %copy-start = (f32[128,256]{1,0:T(8,128)S(1)}, f32[128,256]{1,0:T(8,128)}, u32[]{:S(2)}) copy-start(f32[128,256]{1,0:T(8,128)} %residual.1) | copy-start | bytes 393220
  16.9 3.9 %collective-permute-start.6 = (s16[272,128]{1,0:T(8,128)(2,1)S(1)}, s16[272,128]{1,0:T(8,128)(2,1)S(1)}, u32[]{:S(2)}, u32[]{:S(2)}) collective-permute-start(s16[272,128]{1,0:T(8,128)(2,1)S(1)} %get-tuple-element.25), channel_id=1, source_target_pairs={{0,3},{1,2},{2,1},{3,0},{4,7},{5,6},{6,5},{7,4},{8,11},{9,10},{10,... | collective-permute-start | bytes 208904 | tf_op jit(solution)/shard_map/ppermute | solution.py:151
  17.0 3.8 %collective-permute-start.7 = (s16[272,128]{1,0:T(8,128)(2,1)S(1)}, s16[272,128]{1,0:T(8,128)(2,1)S(1)}, u32[]{:S(2)}, u32[]{:S(2)}) collective-permute-start(s16[272,128]{1,0:T(8,128)(2,1)S(1)} %get-tuple-element.26), channel_id=1, source_target_pairs={{0,1},{1,0},{2,3},{3,2},{4,5},{5,4},{6,7},{7,6},{8,9},{9,8},{10,11... | collective-permute-start | bytes 208904 | tf_op jit(solution)/shard_map/ppermute | solution.py:151

commit v18 on v17

--- a/solution.py
+++ b/solution.py
@@ -16,6 +16,7 @@
 VMEM = pl.BlockSpec(memory_space=pltpu.VMEM)
 HBM = pl.BlockSpec(memory_space=pltpu.HBM)
 PARAMS = pltpu.CompilerParams(vmem_limit_bytes=8 * 1024 * 1024)
+PIECES = 4
 ROWS = 4
 
 
@@ -30,14 +31,22 @@
         at = at + kept[row, tile]
 
 
+def copies(source, target, sems):
+    size = source.shape[0] // PIECES
+    rows = [pl.ds(i * size, size) for i in range(PIECES)]
+    return [pltpu.make_async_copy(source.at[r], target.at[r], sems.at[i]) for i, r in enumerate(rows)]
+
+
 def pack_kernel(tiles, slots, kept, doubles, packed, first, second, table, block, places, sems):
-    table_copy = pltpu.make_async_copy(kept, table, sems.at[0])
-    block_copy = pltpu.make_async_copy(doubles, block, sems.at[1])
+    table_copy = pltpu.make_async_copy(kept, table, sems.at[PIECES])
+    block_copies = copies(doubles, block, sems)
     table_copy.start()
-    block_copy.start()
+    for copy in block_copies:
+        copy.start()
     table_copy.wait()
     list_kept(table, lax.axis_index("rows"), tiles, places)
-    block_copy.wait()
+    for copy in block_copies:
+        copy.wait()
     half = first.shape[0]
     for slot in range(slots):
         tile = block[:, pl.ds(pl.multiple_of(places[slot] * TILE, TILE), TILE)]
@@ -48,13 +57,12 @@
 
 
 def prepare_kernel(tiles, slots, kept, int_kept, integrals, own, gathered, product, table, int_table, held, places, sems):
-    copies = [
-        pltpu.make_async_copy(*pair, sems.at[i])
-        for i, pair in enumerate(((kept, table), (int_kept, int_table), (integrals, held)))
-    ]
-    for copy in copies:
+    started = copies(integrals, held, sems)
+    for i, pair in enumerate(((kept, table), (int_kept, int_table)), PIECES):
+        started.append(pltpu.make_async_copy(*pair, sems.at[i]))
+    for copy in started:
         copy.start()
-    for copy in copies:
+    for copy in started:
         copy.wait()
     row, col = lax.axis_index("rows"), lax.axis_index("cols")
     tiles_ab = integrals.shape[1] // TILE
@@ -84,14 +92,15 @@
     out[bands * pairs :, :] = head.astype(jnp.int16)
 
 
-def decode(message, pairs):
+def decode(message, pairs, start, stop):
     bands = (message.shape[0] - HEAD) // pairs
     each = HEAD // bands
     head = message[bands * pairs :, :].astype(jnp.int32).astype(jnp.float32)
     parts = []
     for band in range(bands):
         scale = jnp.exp2(head[band * each : band * each + 1, :] * (-1.0 / STEPS))
-        parts.append(message[band * pairs : (band + 1) * pairs, :].astype(jnp.int32).astype(jnp.float32) * scale)
+        code = message[band * pairs + start : band * pairs + stop, :]
+        parts.append(code.astype(jnp.int32).astype(jnp.float32) * scale)
     return jnp.concatenate(parts, axis=1)
 
 
@@ -140,11 +149,20 @@
 
 
 def first_kernel(residual, kept_sums, two, out):
-    out[...] = residual[...] + kept_sums[...] + decode(two, out.shape[0])
-
-
-def last_kernel(base, three, one, out):
-    out[...] = base[...] + decode(three, out.shape[0]) + decode(one, out.shape[0])
+    pairs = out.shape[0]
+    out[...] = residual[...] + kept_sums[...] + decode(two, pairs, 0, pairs)
+
+
+def last_kernel(base, three, one, out, total, sems):
+    pairs = total.shape[0]
+    size = pairs // PIECES
+    started = copies(total, out, sems)
+    for i, copy in enumerate(started):
+        rows = (i * size, (i + 1) * size)
+        total[rows[0] : rows[1], :] = base[rows[0] : rows[1], :] + decode(three, pairs, *rows) + decode(one, pairs, *rows)
+        copy.start()
+    for copy in started:
+        copy.wait()
 
 
 def swap(x, axis, step):
@@ -172,7 +190,7 @@
             pltpu.SMEM(doubles_kept.shape, jnp.int32),
             pltpu.VMEM(doubles.shape, doubles.dtype),
             places,
-            pltpu.SemaphoreType.DMA((2,)),
+            pltpu.SemaphoreType.DMA((PIECES + 1,)),
         ],
         compiler_params=PARAMS,
         name="pack",
@@ -192,7 +210,7 @@
             pltpu.SMEM(integral_kept.shape, jnp.int32),
             pltpu.VMEM(integrals.shape, integrals.dtype),
             places,
-            pltpu.SemaphoreType.DMA((3,)),
+            pltpu.SemaphoreType.DMA((PIECES + 2,)),
         ],
         compiler_params=PARAMS,
         cost_estimate=cost(10**9),
@@ -223,7 +241,16 @@
     )
     two, three, one = swap(two, "cols", 2), swap(three, "cols", 3), swap(one, "cols", 1)
     base = on_vmem(first_kernel, "first", 0, sums_shape, residual, kept_sums, two)
-    return on_vmem(last_kernel, "last", 0, sums_shape, base, three, one)
+    return pl.pallas_call(
+        last_kernel,
+        out_shape=sums_shape,
+        in_specs=[VMEM] * 3,
+        out_specs=HBM,
+        scratch_shapes=[pltpu.VMEM((pairs, width), jnp.float32), pltpu.SemaphoreType.DMA((PIECES,))],
+        compiler_params=PARAMS,
+        cost_estimate=cost(0),
+        name="last",
+    )(base, three, one)
 
 
 def local_many(doubles, doubles_kept, integrals, integral_kept, residual):

time: 21.7 us -> 21.7 us (level)
    pallas_call x0 -> x1, Pallas kernels: none -> 0.7 us  [local_few(): pl.pallas_call(last_kernel, out_shape=sums_shape, in_specs=[VMEM] * 3, ou...]
    pallas_call x5 -> x4, Pallas kernels: 1.37 us -> 0.68 us  [on_vmem(): pl.pallas_call(kernel, out_shape=out_shape, in_specs=[VMEM] * len(args),...]
  transfers between devices with their start and end apart: 8 -> 8, of which waited for: 5 -> 5; matrix products, arithmetic and copies ran while one was open for 0% -> 0% of each run, Pallas kernels for 9% -> 10%
where the time goes in v18:
time: 21.7 us; the launch traced here: 21.5 us
  starting transfers between devices  12.3 us (57%)
  waiting for transfers between devices  5.11 us (24%)
  Pallas kernels  4.03 us (19%)
    ppermute x8, starting transfers between devices, swap(): return lax.ppermute(x, axis, [(i, i ^ step) for i in range(ROWS)])  12.3 us
    ppermute x8, waiting for transfers between devices, swap(): return lax.ppermute(x, axis, [(i, i ^ step) for i in range(ROWS)])  5.11 us
    pallas_call x1, Pallas kernels, local_few(): pl.pallas_call(functools.partial(prepare_kernel, tiles, slots), out_shape...  1.64 us
    pallas_call x1, Pallas kernels, local_few(): pl.pallas_call(functools.partial(pack_kernel, tiles, slots), out_shape=[j...  1.01 us
    pallas_call x1, Pallas kernels, local_few(): pl.pallas_call(last_kernel, out_shape=sums_shape, in_specs=[VMEM] * 3, ou...  0.7 us
    pallas_call x4, Pallas kernels, on_vmem(): pl.pallas_call(kernel, out_shape=out_shape, in_specs=[VMEM] * len(args),...  0.68 us
  transfers between devices with their start and end apart: 8, of which 5 were waited for; matrix products, arithmetic and copies ran while one was open for 0% of the time, Pallas kernels for 10%

profile of v18, /device:TPU:0, one launch (start us, length us, event | category | flops | bytes accessed | tf_op | source)
XLA Modules:
  0.0 21.5 jit_solution(14245893927805657974)
XLA Ops:
  0.0 1.0 %pack.1 = (bf16[128,512]{1,0:T(8,128)(2,1)S(1)}, bf16[64,512]{1,0:T(8,128)(2,1)S(1)}, bf16[64,512]{1,0:T(8,128)(2,1)S(1)}) custom-call(s32[4,8]{1,0:T(4,128)} %kept.3, bf16[128,1024]{1,0:T(8,128)(2,1)} %doubles.1), custom_call_target="tpu_custom_call" | custom-call | tf_op jit(solution)/shard_map/pack/pallas_call | solution.py:184
  1.0 4.1 %collective-permute-start.1 = (bf16[64,512]{1,0:T(8,128)(2,1)S(1)}, bf16[64,512]{1,0:T(8,128)(2,1)S(1)}, u32[]{:S(2)}, u32[]{:S(2)}) collective-permute-start(bf16[64,512]{1,0:T(8,128)(2,1)S(1)} %get-tuple-element.19), channel_id=1, source_target_pairs={{0,8},{4,12},{8,0},{12,4},{1,9},{5,13},{9,1},{13,5},{2,10},{6,14},... | collective-permute-start | bytes 196616 | tf_op jit(solution)/shard_map/ppermute | solution.py:169
  5.1 1.6 %collective-permute-start = (bf16[128,512]{1,0:T(8,128)(2,1)S(1)}, bf16[128,512]{1,0:T(8,128)(2,1)S(1)}, u32[]{:S(2)}, u32[]{:S(2)}) collective-permute-start(bf16[128,512]{1,0:T(8,128)(2,1)S(1)} %get-tuple-element.16.own), channel_id=1, source_target_pairs={{0,4},{4,0},{8,12},{12,8},{1,5},{5,1},{9,13},{13,9},{2,6},{6,2},{1... | collective-permute-start | bytes 393224 | tf_op jit(solution)/shard_map/ppermute | solution.py:169
  6.7 0.0 collective-permute-start.2
  6.7 1.9 %collective-permute-start.3 = (bf16[64,512]{1,0:T(8,128)(2,1)S(1)}, bf16[64,512]{1,0:T(8,128)(2,1)S(1)}, u32[]{:S(2)}, u32[]{:S(2)}) collective-permute-start(bf16[64,512]{1,0:T(8,128)(2,1)S(1)} %get-tuple-element.20), channel_id=1, source_target_pairs={{0,8},{4,12},{8,0},{12,4},{1,9},{5,13},{9,1},{13,5},{2,10},{6,14},... | collective-permute-start | bytes 196616 | tf_op jit(solution)/shard_map/ppermute | solution.py:169
  8.6 0.0 collective-permute-done.1.near_second
  8.6 2.5 %collective-permute-start.4 = (bf16[64,512]{1,0:T(8,128)(2,1)S(1)}, bf16[64,512]{1,0:T(8,128)(2,1)S(1)}, u32[]{:S(2)}, u32[]{:S(2)}) collective-permute-start(bf16[64,512]{1,0:T(8,128)(2,1)S(1)} %collective-permute-done.1.near_second), channel_id=1, source_target_pairs={{0,4},{4,0},{8,12},{12,8},{1,5},{5,1},{9,13},{13,9},{2,6},{6,2},{1... | collective-permute-start | bytes 196616 | tf_op jit(solution)/shard_map/ppermute | solution.py:169
  11.1 1.6 %prepare.1 = (bf16[4,512,256]{2,1,0:T(8,128)(2,1)S(1)}, f32[128,256]{1,0:T(8,128)S(1)}) custom-call(s32[4,8]{1,0:T(4,128)} %kept.3, s32[2,8]{1,0:T(2,128)} %bitcast.1, bf16[1024,256]{1,0:T(8,128)(2,1)} %integrals.1, bf16[128,512]{1,0:T(8,128)(2,1)S(1)} %get-tuple-element.16.own), custom_call_target="tpu_custom_call" | custom-call | flops 1000000000 | bytes 1024 | tf_op jit(solution)/shard_map/prepare/pallas_call | solution.py:203
  12.7 0.9 %collective-permute-done.2.far_first = bf16[64,512]{1,0:T(8,128)(2,1)S(1)} collective-permute-done((bf16[64,512]{1,0:T(8,128)(2,1)S(1)}, bf16[64,512]{1,0:T(8,128)(2,1)S(1)}, u32[]{:S(2)}, u32[]{:S(2)}) %collective-permute-start.2) | collective-permute-done | bytes 65568 | tf_op jit(solution)/shard_map/ppermute | solution.py:169
  13.6 0.0 collective-permute-done.pair
  13.6 0.3 %early.1 = f32[4,128,256]{2,1,0:T(8,128)S(1)} custom-call(f32[128,256]{1,0:T(8,128)S(1)} %get-tuple-element.17.product, bf16[4,512,256]{2,1,0:T(8,128)(2,1)S(1)} %get-tuple-element.18.gathered, bf16[128,512]{1,0:T(8,128)(2,1)S(1)} %collective-permute-done.pair, bf16[64,512]{1,0:T(8,128)(2,1)S(1)} %collective-permute-done.1.near_second, ...), custom_call_target="tpu_custom_call" | custom-call | bytes 1024 | tf_op jit(solution)/shard_map/early/pallas_call | solution.py:221
  13.9 0.3 %collective-permute-done.3.near_first = bf16[64,512]{1,0:T(8,128)(2,1)S(1)} collective-permute-done((bf16[64,512]{1,0:T(8,128)(2,1)S(1)}, bf16[64,512]{1,0:T(8,128)(2,1)S(1)}, u32[]{:S(2)}, u32[]{:S(2)}) %collective-permute-start.3) | collective-permute-done | bytes 65568 | tf_op jit(solution)/shard_map/ppermute | solution.py:169
  14.1 0.5 %collective-permute-done.4.far_second = bf16[64,512]{1,0:T(8,128)(2,1)S(1)} collective-permute-done((bf16[64,512]{1,0:T(8,128)(2,1)S(1)}, bf16[64,512]{1,0:T(8,128)(2,1)S(1)}, u32[]{:S(2)}, u32[]{:S(2)}) %collective-permute-start.4) | collective-permute-done | bytes 65568 | tf_op jit(solution)/shard_map/ppermute | solution.py:169
  14.7 0.3 %late.1 = (f32[64,256]{1,0:T(8,128)S(1)}, f32[64,256]{1,0:T(8,128)S(1)}, s16[272,128]{1,0:T(8,128)(2,1)S(1)}) custom-call(f32[4,128,256]{2,1,0:T(8,128)S(1)} %early.1, bf16[4,512,256]{2,1,0:T(8,128)(2,1)S(1)} %get-tuple-element.18.gathered, bf16[64,512]{1,0:T(8,128)(2,1)S(1)} %collective-permute-done.3.near_first, ...), custom_call_target="tpu_custom_call" | custom-call | flops 99999997952 | bytes 1024 | tf_op jit(solution)/shard_map/late/pallas_call | solution.py:221
  15.0 1.8 %collective-permute-start.5 = (s16[272,128]{1,0:T(8,128)(2,1)S(1)}, s16[272,128]{1,0:T(8,128)(2,1)S(1)}, u32[]{:S(2)}, u32[]{:S(2)}) collective-permute-start(s16[272,128]{1,0:T(8,128)(2,1)S(1)} %get-tuple-element.24), channel_id=1, source_target_pairs={{0,2},{1,3},{2,0},{3,1},{4,6},{5,7},{6,4},{7,5},{8,10},{9,11},{10,... | collective-permute-start | bytes 208904 | tf_op jit(solution)/shard_map/ppermute | solution.py:169
  16.8 0.0 copy-start
  16.8 0.1 rest.1
  16.9 0.1 collective-permute-start.6
  17.0 0.4 %collective-permute-start.7 = (s16[272,128]{1,0:T(8,128)(2,1)S(1)}, s16[272,128]{1,0:T(8,128)(2,1)S(1)}, u32[]{:S(2)}, u32[]{:S(2)}) collective-permute-start(s16[272,128]{1,0:T(8,128)(2,1)S(1)} %get-tuple-element.26), channel_id=1, source_target_pairs={{0,1},{1,0},{2,3},{3,2},{4,5},{5,4},{6,7},{7,6},{8,9},{9,8},{10,11... | collective-permute-start | bytes 208904 | tf_op jit(solution)/shard_map/ppermute | solution.py:169
  17.4 2.0 %collective-permute-done.5.two = s16[272,128]{1,0:T(8,128)(2,1)S(1)} collective-permute-done((s16[272,128]{1,0:T(8,128)(2,1)S(1)}, s16[272,128]{1,0:T(8,128)(2,1)S(1)}, u32[]{:S(2)}, u32[]{:S(2)}) %collective-permute-start.5) | collective-permute-done | bytes 69664 | tf_op jit(solution)/shard_map/ppermute | solution.py:169
  19.3 0.0 copy-done
  19.4 1.5 %collective-permute-done.6.three = s16[272,128]{1,0:T(8,128)(2,1)S(1)} collective-permute-done((s16[272,128]{1,0:T(8,128)(2,1)S(1)}, s16[272,128]{1,0:T(8,128)(2,1)S(1)}, u32[]{:S(2)}, u32[]{:S(2)}) %collective-permute-start.6) | collective-permute-done | bytes 69664 | tf_op jit(solution)/shard_map/ppermute | solution.py:169
  20.8 0.0 collective-permute-done.7.one
  20.8 0.7 %last.1 = f32[128,256]{1,0:T(8,128)} custom-call(f32[128,256]{1,0:T(8,128)S(1)} %first.1.base, s16[272,128]{1,0:T(8,128)(2,1)S(1)} %collective-permute-done.6.three, s16[272,128]{1,0:T(8,128)(2,1)S(1)} %collective-permute-done.7.one), custom_call_target="tpu_custom_call" | custom-call | bytes 1024 | tf_op jit(solution)/shard_map/last/pallas_call | solution.py:244
  (1 shorter events, 0.0 us)
Async XLA Ops:
  1.0 7.6 %collective-permute-start.1 = (bf16[64,512]{1,0:T(8,128)(2,1)S(1)}, bf16[64,512]{1,0:T(8,128)(2,1)S(1)}, u32[]{:S(2)}, u32[]{:S(2)}) collective-permute-start(bf16[64,512]{1,0:T(8,128)(2,1)S(1)} %get-tuple-element.19), channel_id=1, source_target_pairs={{0,8},{4,12},{8,0},{12,4},{1,9},{5,13},{9,1},{13,5},{2,10},{6,14},... | collective-permute-start | bytes 196616 | tf_op jit(solution)/shard_map/ppermute | solution.py:169
  5.1 8.5 %collective-permute-start = (bf16[128,512]{1,0:T(8,128)(2,1)S(1)}, bf16[128,512]{1,0:T(8,128)(2,1)S(1)}, u32[]{:S(2)}, u32[]{:S(2)}) collective-permute-start(bf16[128,512]{1,0:T(8,128)(2,1)S(1)} %get-tuple-element.16.own), channel_id=1, source_target_pairs={{0,4},{4,0},{8,12},{12,8},{1,5},{5,1},{9,13},{13,9},{2,6},{6,2},{1... | collective-permute-start | bytes 393224 | tf_op jit(solution)/shard_map/ppermute | solution.py:169
  6.7 6.9 %collective-permute-start.2 = (bf16[64,512]{1,0:T(8,128)(2,1)S(1)}, bf16[64,512]{1,0:T(8,128)(2,1)S(1)}, u32[]{:S(2)}, u32[]{:S(2)}) collective-permute-start(bf16[64,512]{1,0:T(8,128)(2,1)S(1)} %get-tuple-element.20), channel_id=1, source_target_pairs={{0,12},{4,8},{8,4},{12,0},{1,13},{5,9},{9,5},{13,1},{2,14},{6,10},... | collective-permute-start | bytes 196616 | tf_op jit(solution)/shard_map/ppermute | solution.py:169
  6.7 7.4 %collective-permute-start.3 = (bf16[64,512]{1,0:T(8,128)(2,1)S(1)}, bf16[64,512]{1,0:T(8,128)(2,1)S(1)}, u32[]{:S(2)}, u32[]{:S(2)}) collective-permute-start(bf16[64,512]{1,0:T(8,128)(2,1)S(1)} %get-tuple-element.20), channel_id=1, source_target_pairs={{0,8},{4,12},{8,0},{12,4},{1,9},{5,13},{9,1},{13,5},{2,10},{6,14},... | collective-permute-start | bytes 196616 | tf_op jit(solution)/shard_map/ppermute | solution.py:169
  8.6 6.1 %collective-permute-start.4 = (bf16[64,512]{1,0:T(8,128)(2,1)S(1)}, bf16[64,512]{1,0:T(8,128)(2,1)S(1)}, u32[]{:S(2)}, u32[]{:S(2)}) collective-permute-start(bf16[64,512]{1,0:T(8,128)(2,1)S(1)} %collective-permute-done.1.near_second), channel_id=1, source_target_pairs={{0,4},{4,0},{8,12},{12,8},{1,5},{5,1},{9,13},{13,9},{2,6},{6,2},{1... | collective-permute-start | bytes 196616 | tf_op jit(solution)/shard_map/ppermute | solution.py:169
  15.0 4.4 %collective-permute-start.5 = (s16[272,128]{1,0:T(8,128)(2,1)S(1)}, s16[272,128]{1,0:T(8,128)(2,1)S(1)}, u32[]{:S(2)}, u32[]{:S(2)}) collective-permute-start(s16[272,128]{1,0:T(8,128)(2,1)S(1)} %get-tuple-element.24), channel_id=1, source_target_pairs={{0,2},{1,3},{2,0},{3,1},{4,6},{5,7},{6,4},{7,5},{8,10},{9,11},{10,... | collective-permute-start | bytes 208904 | tf_op jit(solution)/shard_map/ppermute | solution.py:169
  16.8 2.5 %copy-start = (f32[128,256]{1,0:T(8,128)S(1)}, f32[128,256]{1,0:T(8,128)}, u32[]{:S(2)}) copy-start(f32[128,256]{1,0:T(8,128)} %residual.1) | copy-start | bytes 393220
  16.9 3.9 %collective-permute-start.6 = (s16[272,128]{1,0:T(8,128)(2,1)S(1)}, s16[272,128]{1,0:T(8,128)(2,1)S(1)}, u32[]{:S(2)}, u32[]{:S(2)}) collective-permute-start(s16[272,128]{1,0:T(8,128)(2,1)S(1)} %get-tuple-element.25), channel_id=1, source_target_pairs={{0,3},{1,2},{2,1},{3,0},{4,7},{5,6},{6,5},{7,4},{8,11},{9,10},{10,... | collective-permute-start | bytes 208904 | tf_op jit(solution)/shard_map/ppermute | solution.py:169
  17.0 3.8 %collective-permute-start.7 = (s16[272,128]{1,0:T(8,128)(2,1)S(1)}, s16[272,128]{1,0:T(8,128)(2,1)S(1)}, u32[]{:S(2)}, u32[]{:S(2)}) collective-permute-start(s16[272,128]{1,0:T(8,128)(2,1)S(1)} %get-tuple-element.26), channel_id=1, source_target_pairs={{0,1},{1,0},{2,3},{3,2},{4,5},{5,4},{6,7},{7,6},{8,9},{9,8},{10,11... | collective-permute-start | bytes 208904 | tf_op jit(solution)/shard_map/ppermute | solution.py:169

commit v19 on v18

--- a/solution.py
+++ b/solution.py
@@ -37,7 +37,7 @@
     return [pltpu.make_async_copy(source.at[r], target.at[r], sems.at[i]) for i, r in enumerate(rows)]
 
 
-def pack_kernel(tiles, slots, kept, doubles, packed, first, second, table, block, places, sems):
+def pack_kernel(tiles, slots, kept, doubles, packed, packed_too, first, second, table, block, places, sems):
     table_copy = pltpu.make_async_copy(kept, table, sems.at[PIECES])
     block_copies = copies(doubles, block, sems)
     table_copy.start()
@@ -52,6 +52,7 @@
         tile = block[:, pl.ds(pl.multiple_of(places[slot] * TILE, TILE), TILE)]
         to = slice(slot * TILE, (slot + 1) * TILE)
         packed[:, to] = tile
+        packed_too[:, to] = tile
         first[:, to] = tile[:half]
         second[:, to] = tile[half:]
 
@@ -78,6 +79,10 @@
     product[...] = jnp.dot(own[...], gathered[row ^ col], preferred_element_type=jnp.float32)
 
 
+def after_kernel(token, x, out):
+    pass
+
+
 def encode(x, out):
     pairs, width = x.shape
     largest = jnp.max(jnp.abs(x), axis=0, keepdims=True)
@@ -108,21 +113,33 @@
     return lax.axis_index("rows") ^ lax.axis_index("cols")
 
 
-def early_kernel(product, gathered, pair, near_second, far_first, sums):
+def early_kernel(product, gathered, pair_down, near_second, far_first, sums):
     mine = place()
     half = near_second.shape[0]
     sums[mine] = product[...]
-    sums[mine ^ 1] = jnp.dot(pair[...], gathered[mine ^ 1], preferred_element_type=jnp.float32)
+
+    @pl.when(lax.axis_index("rows") % 2 == 0)
+    def _():
+        sums[mine ^ 1] = jnp.dot(pair_down[...], gathered[mine ^ 1], preferred_element_type=jnp.float32)
+
     for step, start, block in ((2, half, near_second), (3, 0, far_first)):
         sums[mine ^ step, start : start + half, :] = jnp.dot(
             block[...], gathered[mine ^ step], preferred_element_type=jnp.float32
         )
 
 
-def whole(n, early, near_sums, far_sums, out):
+def whole(n, early, pair_sums, near_sums, far_sums, out):
     half = near_sums.shape[0]
     step = place() ^ n
-    out[...] = early[n]
+    up = (step == 1) & (lax.axis_index("rows") % 2 == 1)
+
+    @pl.when(jnp.logical_not(up))
+    def _():
+        out[...] = early[n]
+
+    @pl.when(up)
+    def _():
+        out[...] = pair_sums[...]
 
     @pl.when(step == 2)
     def _():
@@ -133,19 +150,24 @@
         out[half:, :] = far_sums[...]
 
 
-def late_kernel(early, gathered, near_first, far_second, near_sums, far_sums, two, held):
+def late_kernel(early, gathered, near_first, far_second, pair_up, pair_sums, near_sums, far_sums, two, held):
     mine = place()
+
+    @pl.when(lax.axis_index("rows") % 2 == 1)
+    def _():
+        pair_sums[...] = jnp.dot(pair_up[...], gathered[mine ^ 1], preferred_element_type=jnp.float32)
+
     near_sums[...] = jnp.dot(near_first[...], gathered[mine ^ 2], preferred_element_type=jnp.float32)
     far_sums[...] = jnp.dot(far_second[...], gathered[mine ^ 3], preferred_element_type=jnp.float32)
-    whole(2, early, near_sums, far_sums, held)
+    whole(2, early, pair_sums, near_sums, far_sums, held)
     encode(held[...], two)
 
 
-def rest_kernel(early, near_sums, far_sums, one, three, kept_sums, held):
+def rest_kernel(early, pair_sums, near_sums, far_sums, one, three, kept_sums, held):
     for n, out in ((3, three), (1, one)):
-        whole(n, early, near_sums, far_sums, held)
+        whole(n, early, pair_sums, near_sums, far_sums, held)
         encode(held[...], out)
-    whole(0, early, near_sums, far_sums, kept_sums)
+    whole(0, early, pair_sums, near_sums, far_sums, kept_sums)
 
 
 def first_kernel(residual, kept_sums, two, out):
@@ -163,6 +185,19 @@
         copy.start()
     for copy in started:
         copy.wait()
+
+
+def after(token, x):
+    return pl.pallas_call(
+        after_kernel,
+        out_shape=jax.ShapeDtypeStruct(x.shape, x.dtype),
+        in_specs=[pl.BlockSpec(memory_space=pl.ANY)] * 2,
+        out_specs=pl.BlockSpec(memory_space=pl.ANY),
+        input_output_aliases={1: 0},
+        compiler_params=PARAMS,
+        cost_estimate=cost(0),
+        name="after",
+    )(token, x)
 
 
 def swap(x, axis, step):
@@ -181,11 +216,11 @@
     doubles, doubles_kept, integrals, integral_kept = (
         pltpu.with_memory_space_constraint(x, pltpu.HBM) for x in (doubles, doubles_kept, integrals, integral_kept.T)
     )
-    packed, first, second = pl.pallas_call(
+    packed, packed_too, first, second = pl.pallas_call(
         functools.partial(pack_kernel, tiles, slots),
-        out_shape=[jax.ShapeDtypeStruct((pairs, slots * TILE), doubles.dtype), half_block, half_block],
+        out_shape=[jax.ShapeDtypeStruct((pairs, slots * TILE), doubles.dtype)] * 2 + [half_block] * 2,
         in_specs=[HBM, HBM],
-        out_specs=[VMEM] * 3,
+        out_specs=[VMEM] * 4,
         scratch_shapes=[
             pltpu.SMEM(doubles_kept.shape, jnp.int32),
             pltpu.VMEM(doubles.shape, doubles.dtype),
@@ -196,10 +231,12 @@
         name="pack",
     )(doubles_kept, doubles)
     near_second = swap(second, "rows", 2)
-    pair = swap(packed, "rows", 1)
+    pair_down = lax.ppermute(packed, "rows", [(i + 1, i) for i in range(0, ROWS, 2)])
     far_first = swap(first, "rows", 3)
     near_first = swap(first, "rows", 2)
+    near_second = after(pair_down, near_second)
     far_second = swap(near_second, "rows", 1)
+    pair_up = lax.ppermute(after(near_second, packed_too), "rows", [(i, i + 1) for i in range(0, ROWS, 2)])
     gathered, product = pl.pallas_call(
         functools.partial(prepare_kernel, tiles, slots),
         out_shape=[jax.ShapeDtypeStruct((ROWS, slots * TILE, width), integrals.dtype), sums_shape],
@@ -213,7 +250,7 @@
             pltpu.SemaphoreType.DMA((PIECES + 2,)),
         ],
         compiler_params=PARAMS,
-        cost_estimate=cost(10**9),
+        cost_estimate=cost(10**11),
         name="prepare",
     )(doubles_kept, integral_kept, integrals, packed)
 
@@ -232,12 +269,29 @@
     held = [pltpu.VMEM((pairs, width), jnp.float32)]
     half_sums = jax.ShapeDtypeStruct((pairs // 2, width), jnp.float32)
     all_sums = jax.ShapeDtypeStruct((ROWS, pairs, width), jnp.float32)
-    early = on_vmem(early_kernel, "early", 0, all_sums, product, gathered, pair, near_second, far_first)
-    near_sums, far_sums, two = on_vmem(
-        late_kernel, "late", 10**11, [half_sums] * 2 + [message], early, gathered, near_first, far_second, scratch=held
+    early = on_vmem(early_kernel, "early", 0, all_sums, product, gathered, pair_down, near_second, far_first)
+    pair_sums, near_sums, far_sums, two = on_vmem(
+        late_kernel,
+        "late",
+        10**11,
+        [sums_shape] + [half_sums] * 2 + [message],
+        early,
+        gathered,
+        near_first,
+        far_second,
+        pair_up,
+        scratch=held,
     )
     one, three, kept_sums = on_vmem(
-        rest_kernel, "rest", 0, [message] * 2 + [sums_shape], early, near_sums, far_sums, scratch=held
+        rest_kernel,
+        "rest",
+        0,
+        [message] * 2 + [sums_shape],
+        early,
+        pair_sums,
+        near_sums,
+        far_sums,
+        scratch=held,
     )
     two, three, one = swap(two, "cols", 2), swap(three, "cols", 3), swap(one, "cols", 1)
     base = on_vmem(first_kernel, "first", 0, sums_shape, residual, kept_sums, two)

time: 21.7 us -> 26.4 us (1.22)
  starting transfers between devices: 12.3 us -> 18 us
  waiting for transfers between devices: 5.11 us -> 3.82 us
    ppermute x0 -> x2, starting transfers between devices: none -> 3.21 us  [the longest x1 1.92 us: local_few(): lax.ppermute(after(near_second, packed_too), 'rows', [(i, i + 1) for i in...]
    ppermute x8 -> x7, starting transfers between devices: 12.3 us -> 14.8 us  [swap(): return lax.ppermute(x, axis, [(i, i ^ step) for i in range(ROWS)])]
    ppermute x8 -> x7, waiting for transfers between devices: 5.11 us -> 3.42 us  [swap(): return lax.ppermute(x, axis, [(i, i ^ step) for i in range(ROWS)])]
    ppermute x0 -> x2, waiting for transfers between devices: none -> 0.39 us  [the longest x1 0.39 us: local_few(): lax.ppermute(after(near_second, packed_too), 'rows', [(i, i + 1) for i in...]
  transfers between devices with their start and end apart: 8 -> 9, of which waited for: 5 -> 3; matrix products, arithmetic and copies ran while one was open for 0% -> 0% of each run, Pallas kernels for 10% -> 9%
where the time goes in v19:
time: 26.4 us; the launch traced here: 26.1 us
  starting transfers between devices  18 us (68%)
  Pallas kernels  4.23 us (16%)
  waiting for transfers between devices  3.82 us (14%)
    ppermute x7, starting transfers between devices, swap(): return lax.ppermute(x, axis, [(i, i ^ step) for i in range(ROWS)])  14.8 us
    ppermute x7, waiting for transfers between devices, swap(): return lax.ppermute(x, axis, [(i, i ^ step) for i in range(ROWS)])  3.42 us
    ppermute x1, starting transfers between devices, local_few(): lax.ppermute(after(near_second, packed_too), 'rows', [(i, i + 1) for i in...  1.92 us
    pallas_call x1, Pallas kernels, local_few(): pl.pallas_call(functools.partial(prepare_kernel, tiles, slots), out_shape...  1.64 us
    ppermute x1, starting transfers between devices, local_few(): lax.ppermute(packed, 'rows', [(i + 1, i) for i in range(0, ROWS, 2)])  1.29 us
    pallas_call x1, Pallas kernels, local_few(): pl.pallas_call(functools.partial(pack_kernel, tiles, slots), out_shape=[j...  1.04 us
    pallas_call x4, Pallas kernels, on_vmem(): pl.pallas_call(kernel, out_shape=out_shape, in_specs=[VMEM] * len(args),...  0.85 us
    pallas_call x1, Pallas kernels, local_few(): pl.pallas_call(last_kernel, out_shape=sums_shape, in_specs=[VMEM] * 3, ou...  0.7 us
  transfers between devices with their start and end apart: 9, of which 3 were waited for; matrix products, arithmetic and copies ran while one was open for 0% of the time, Pallas kernels for 9%

profile of v19, /device:TPU:0, one launch (start us, length us, event | category | flops | bytes accessed | tf_op | source)
XLA Modules:
  0.0 26.1 jit_solution(430322815420705866)
XLA Ops:
  0.0 1.0 %pack.1 = (bf16[128,512]{1,0:T(8,128)(2,1)S(1)}, bf16[128,512]{1,0:T(8,128)(2,1)S(1)}, bf16[64,512]{1,0:T(8,128)(2,1)S(1)}, bf16[64,512]{1,0:T(8,128)(2,1)S(1)}) custom-call(s32[4,8]{1,0:T(4,128)} %kept.3, bf16[128,1024]{1,0:T(8,128)(2,1)} %doubles.1), custom_call_target="tpu_custom_call" | custom-call | tf_op jit(solution)/shard_map/pack/pallas_call | solution.py:219
  1.0 1.3 %collective-permute-start = (bf16[128,512]{1,0:T(8,128)(2,1)S(1)}, bf16[128,512]{1,0:T(8,128)(2,1)S(1)}, u32[]{:S(2)}, u32[]{:S(2)}) collective-permute-start(bf16[128,512]{1,0:T(8,128)(2,1)S(1)} %get-tuple-element.18.own), channel_id=1, source_target_pairs={{4,0},{12,8},{5,1},{13,9},{6,2},{14,10},{7,3},{15,11},{20,16},{28,... | collective-permute-start | bytes 393224 | tf_op jit(solution)/shard_map/ppermute | solution.py:234
  2.3 4.1 %collective-permute-start.1 = (bf16[64,512]{1,0:T(8,128)(2,1)S(1)}, bf16[64,512]{1,0:T(8,128)(2,1)S(1)}, u32[]{:S(2)}, u32[]{:S(2)}) collective-permute-start(bf16[64,512]{1,0:T(8,128)(2,1)S(1)} %get-tuple-element.21), channel_id=1, source_target_pairs={{0,8},{4,12},{8,0},{12,4},{1,9},{5,13},{9,1},{13,5},{2,10},{6,14},... | collective-permute-start | bytes 196616 | tf_op jit(solution)/shard_map/ppermute | solution.py:204
  6.4 2.2 %collective-permute-start.2 = (bf16[64,512]{1,0:T(8,128)(2,1)S(1)}, bf16[64,512]{1,0:T(8,128)(2,1)S(1)}, u32[]{:S(2)}, u32[]{:S(2)}) collective-permute-start(bf16[64,512]{1,0:T(8,128)(2,1)S(1)} %get-tuple-element.22), channel_id=1, source_target_pairs={{0,12},{4,8},{8,4},{12,0},{1,13},{5,9},{9,5},{13,1},{2,14},{6,10},... | collective-permute-start | bytes 196616 | tf_op jit(solution)/shard_map/ppermute | solution.py:204
  8.6 1.9 %collective-permute-start.3 = (bf16[64,512]{1,0:T(8,128)(2,1)S(1)}, bf16[64,512]{1,0:T(8,128)(2,1)S(1)}, u32[]{:S(2)}, u32[]{:S(2)}) collective-permute-start(bf16[64,512]{1,0:T(8,128)(2,1)S(1)} %get-tuple-element.22), channel_id=1, source_target_pairs={{0,8},{4,12},{8,0},{12,4},{1,9},{5,13},{9,1},{13,5},{2,10},{6,14},... | collective-permute-start | bytes 196616 | tf_op jit(solution)/shard_map/ppermute | solution.py:204
  10.6 0.0 collective-permute-done.1.x
  10.6 0.0 collective-permute-done.token.pair_down
  10.6 4.3 %collective-permute-start.4 = (bf16[64,512]{1,0:T(8,128)(2,1)S(1)}, bf16[64,512]{1,0:T(8,128)(2,1)S(1)}, u32[]{:S(2)}, u32[]{:S(2)}) collective-permute-start(bf16[64,512]{1,0:T(8,128)(2,1)S(1)} %after.2.near_second.token), channel_id=1, source_target_pairs={{0,4},{4,0},{8,12},{12,8},{1,5},{5,1},{9,13},{13,9},{2,6},{6,2},{1... | collective-permute-start | bytes 196616 | tf_op jit(solution)/shard_map/ppermute | solution.py:204
  14.9 1.9 %collective-permute-start.5 = (bf16[128,512]{1,0:T(8,128)(2,1)S(1)}, bf16[128,512]{1,0:T(8,128)(2,1)S(1)}, u32[]{:S(2)}, u32[]{:S(2)}) collective-permute-start(bf16[128,512]{1,0:T(8,128)(2,1)S(1)} %after.3), channel_id=1, source_target_pairs={{0,4},{8,12},{1,5},{9,13},{2,6},{10,14},{3,7},{11,15},{16,20},{24,... | collective-permute-start | bytes 393224 | tf_op jit(solution)/shard_map/ppermute | solution.py:239
  16.8 1.6 %prepare.1 = (bf16[4,512,256]{2,1,0:T(8,128)(2,1)S(1)}, f32[128,256]{1,0:T(8,128)S(1)}) custom-call(s32[4,8]{1,0:T(4,128)} %kept.3, s32[2,8]{1,0:T(2,128)} %bitcast.1, bf16[1024,256]{1,0:T(8,128)(2,1)} %integrals.1, bf16[128,512]{1,0:T(8,128)(2,1)S(1)} %get-tuple-element.18.own), custom_call_target="tpu_custom_call" | custom-call | flops 99999997952 | bytes 1024 | tf_op jit(solution)/shard_map/prepare/pallas_call | solution.py:240
  18.5 0.0 collective-permute-done.2.far_first
  18.5 0.4 %early.1 = f32[4,128,256]{2,1,0:T(8,128)S(1)} custom-call(f32[128,256]{1,0:T(8,128)S(1)} %get-tuple-element.19.product, bf16[4,512,256]{2,1,0:T(8,128)(2,1)S(1)} %get-tuple-element.20.gathered, bf16[128,512]{1,0:T(8,128)(2,1)S(1)} %collective-permute-done.token.pair_down, bf16[64,512]{1,0:T(8,128)(2,1)S(1)} %after.2.near_second.token, ...), custom_call_target="tpu_custom_call" | custom-call | bytes 1024 | tf_op jit(solution)/shard_map/early/pallas_call | solution.py:258
  18.9 0.0 collective-permute-done.3.near_first
  18.9 0.0 collective-permute-done.4.far_second
  18.9 0.4 %collective-permute-done.5.pair_up = bf16[128,512]{1,0:T(8,128)(2,1)S(1)} collective-permute-done((bf16[128,512]{1,0:T(8,128)(2,1)S(1)}, bf16[128,512]{1,0:T(8,128)(2,1)S(1)}, u32[]{:S(2)}, u32[]{:S(2)}) %collective-permute-start.5) | collective-permute-done | bytes 131104 | tf_op jit(solution)/shard_map/ppermute | solution.py:239
  19.3 0.3 %late.1 = (f32[128,256]{1,0:T(8,128)S(1)}, f32[64,256]{1,0:T(8,128)S(1)}, f32[64,256]{1,0:T(8,128)S(1)}, s16[272,128]{1,0:T(8,128)(2,1)S(1)}) custom-call(f32[4,128,256]{2,1,0:T(8,128)S(1)} %early.1, bf16[4,512,256]{2,1,0:T(8,128)(2,1)S(1)} %get-tuple-element.20.gathered, bf16[64,512]{1,0:T(8,128)(2,1)S(1)} %collective-permute-done.3.near_first, ...), custom_call_target="tpu_custom_call" | custom-call | flops 99999997952 | bytes 1024 | tf_op jit(solution)/shard_map/late/pallas_call | solution.py:258
  19.6 1.6 %collective-permute-start.6 = (s16[272,128]{1,0:T(8,128)(2,1)S(1)}, s16[272,128]{1,0:T(8,128)(2,1)S(1)}, u32[]{:S(2)}, u32[]{:S(2)}) collective-permute-start(s16[272,128]{1,0:T(8,128)(2,1)S(1)} %get-tuple-element.28), channel_id=1, source_target_pairs={{0,2},{1,3},{2,0},{3,1},{4,6},{5,7},{6,4},{7,5},{8,10},{9,11},{10,... | collective-permute-start | bytes 208904 | tf_op jit(solution)/shard_map/ppermute | solution.py:204
  21.1 0.0 copy-start
  21.1 0.1 rest.1
  21.3 0.1 collective-permute-start.7
  21.4 0.6 %collective-permute-start.8 = (s16[272,128]{1,0:T(8,128)(2,1)S(1)}, s16[272,128]{1,0:T(8,128)(2,1)S(1)}, u32[]{:S(2)}, u32[]{:S(2)}) collective-permute-start(s16[272,128]{1,0:T(8,128)(2,1)S(1)} %get-tuple-element.30), channel_id=1, source_target_pairs={{0,1},{1,0},{2,3},{3,2},{4,5},{5,4},{6,7},{7,6},{8,9},{9,8},{10,11... | collective-permute-start | bytes 208904 | tf_op jit(solution)/shard_map/ppermute | solution.py:204
  22.0 2.0 %collective-permute-done.6.two = s16[272,128]{1,0:T(8,128)(2,1)S(1)} collective-permute-done((s16[272,128]{1,0:T(8,128)(2,1)S(1)}, s16[272,128]{1,0:T(8,128)(2,1)S(1)}, u32[]{:S(2)}, u32[]{:S(2)}) %collective-permute-start.6) | collective-permute-done | bytes 69664 | tf_op jit(solution)/shard_map/ppermute | solution.py:204
  23.9 0.0 copy-done
  24.0 1.5 %collective-permute-done.7.three = s16[272,128]{1,0:T(8,128)(2,1)S(1)} collective-permute-done((s16[272,128]{1,0:T(8,128)(2,1)S(1)}, s16[272,128]{1,0:T(8,128)(2,1)S(1)}, u32[]{:S(2)}, u32[]{:S(2)}) %collective-permute-start.7) | collective-permute-done | bytes 69664 | tf_op jit(solution)/shard_map/ppermute | solution.py:204
  25.4 0.0 collective-permute-done.8.one
  25.4 0.7 %last.1 = f32[128,256]{1,0:T(8,128)} custom-call(f32[128,256]{1,0:T(8,128)S(1)} %first.1.base, s16[272,128]{1,0:T(8,128)(2,1)S(1)} %collective-permute-done.7.three, s16[272,128]{1,0:T(8,128)(2,1)S(1)} %collective-permute-done.8.one), custom_call_target="tpu_custom_call" | custom-call | bytes 1024 | tf_op jit(solution)/shard_map/last/pallas_call | solution.py:298
  (3 shorter events, 0.0 us)
Async XLA Ops:
  1.0 9.5 %collective-permute-start = (bf16[128,512]{1,0:T(8,128)(2,1)S(1)}, bf16[128,512]{1,0:T(8,128)(2,1)S(1)}, u32[]{:S(2)}, u32[]{:S(2)}) collective-permute-start(bf16[128,512]{1,0:T(8,128)(2,1)S(1)} %get-tuple-element.18.own), channel_id=1, source_target_pairs={{4,0},{12,8},{5,1},{13,9},{6,2},{14,10},{7,3},{15,11},{20,16},{28,... | collective-permute-start | bytes 393224 | tf_op jit(solution)/shard_map/ppermute | solution.py:234
  2.3 8.2 %collective-permute-start.1 = (bf16[64,512]{1,0:T(8,128)(2,1)S(1)}, bf16[64,512]{1,0:T(8,128)(2,1)S(1)}, u32[]{:S(2)}, u32[]{:S(2)}) collective-permute-start(bf16[64,512]{1,0:T(8,128)(2,1)S(1)} %get-tuple-element.21), channel_id=1, source_target_pairs={{0,8},{4,12},{8,0},{12,4},{1,9},{5,13},{9,1},{13,5},{2,10},{6,14},... | collective-permute-start | bytes 196616 | tf_op jit(solution)/shard_map/ppermute | solution.py:204
  6.4 12.0 %collective-permute-start.2 = (bf16[64,512]{1,0:T(8,128)(2,1)S(1)}, bf16[64,512]{1,0:T(8,128)(2,1)S(1)}, u32[]{:S(2)}, u32[]{:S(2)}) collective-permute-start(bf16[64,512]{1,0:T(8,128)(2,1)S(1)} %get-tuple-element.22), channel_id=1, source_target_pairs={{0,12},{4,8},{8,4},{12,0},{1,13},{5,9},{9,5},{13,1},{2,14},{6,10},... | collective-permute-start | bytes 196616 | tf_op jit(solution)/shard_map/ppermute | solution.py:204
  8.6 10.3 %collective-permute-start.3 = (bf16[64,512]{1,0:T(8,128)(2,1)S(1)}, bf16[64,512]{1,0:T(8,128)(2,1)S(1)}, u32[]{:S(2)}, u32[]{:S(2)}) collective-permute-start(bf16[64,512]{1,0:T(8,128)(2,1)S(1)} %get-tuple-element.22), channel_id=1, source_target_pairs={{0,8},{4,12},{8,0},{12,4},{1,9},{5,13},{9,1},{13,5},{2,10},{6,14},... | collective-permute-start | bytes 196616 | tf_op jit(solution)/shard_map/ppermute | solution.py:204
  10.6 8.3 %collective-permute-start.4 = (bf16[64,512]{1,0:T(8,128)(2,1)S(1)}, bf16[64,512]{1,0:T(8,128)(2,1)S(1)}, u32[]{:S(2)}, u32[]{:S(2)}) collective-permute-start(bf16[64,512]{1,0:T(8,128)(2,1)S(1)} %after.2.near_second.token), channel_id=1, source_target_pairs={{0,4},{4,0},{8,12},{12,8},{1,5},{5,1},{9,13},{13,9},{2,6},{6,2},{1... | collective-permute-start | bytes 196616 | tf_op jit(solution)/shard_map/ppermute | solution.py:204
  14.9 4.4 %collective-permute-start.5 = (bf16[128,512]{1,0:T(8,128)(2,1)S(1)}, bf16[128,512]{1,0:T(8,128)(2,1)S(1)}, u32[]{:S(2)}, u32[]{:S(2)}) collective-permute-start(bf16[128,512]{1,0:T(8,128)(2,1)S(1)} %after.3), channel_id=1, source_target_pairs={{0,4},{8,12},{1,5},{9,13},{2,6},{10,14},{3,7},{11,15},{16,20},{24,... | collective-permute-start | bytes 393224 | tf_op jit(solution)/shard_map/ppermute | solution.py:239
  19.6 4.4 %collective-permute-start.6 = (s16[272,128]{1,0:T(8,128)(2,1)S(1)}, s16[272,128]{1,0:T(8,128)(2,1)S(1)}, u32[]{:S(2)}, u32[]{:S(2)}) collective-permute-start(s16[272,128]{1,0:T(8,128)(2,1)S(1)} %get-tuple-element.28), channel_id=1, source_target_pairs={{0,2},{1,3},{2,0},{3,1},{4,6},{5,7},{6,4},{7,5},{8,10},{9,11},{10,... | collective-permute-start | bytes 208904 | tf_op jit(solution)/shard_map/ppermute | solution.py:204
  21.1 2.8 %copy-start = (f32[128,256]{1,0:T(8,128)S(1)}, f32[128,256]{1,0:T(8,128)}, u32[]{:S(2)}) copy-start(f32[128,256]{1,0:T(8,128)} %residual.1) | copy-start | bytes 393220
  21.3 4.2 %collective-permute-start.7 = (s16[272,128]{1,0:T(8,128)(2,1)S(1)}, s16[272,128]{1,0:T(8,128)(2,1)S(1)}, u32[]{:S(2)}, u32[]{:S(2)}) collective-permute-start(s16[272,128]{1,0:T(8,128)(2,1)S(1)} %get-tuple-element.29), channel_id=1, source_target_pairs={{0,3},{1,2},{2,1},{3,0},{4,7},{5,6},{6,5},{7,4},{8,11},{9,10},{10,... | collective-permute-start | bytes 208904 | tf_op jit(solution)/shard_map/ppermute | solution.py:204
  21.4 4.1 %collective-permute-start.8 = (s16[272,128]{1,0:T(8,128)(2,1)S(1)}, s16[272,128]{1,0:T(8,128)(2,1)S(1)}, u32[]{:S(2)}, u32[]{:S(2)}) collective-permute-start(s16[272,128]{1,0:T(8,128)(2,1)S(1)} %get-tuple-element.30), channel_id=1, source_target_pairs={{0,1},{1,0},{2,3},{3,2},{4,5},{5,4},{6,7},{7,6},{8,9},{9,8},{10,11... | collective-permute-start | bytes 208904 | tf_op jit(solution)/shard_map/ppermute | solution.py:204

commit v20 on v18

--- a/solution.py
+++ b/solution.py
@@ -16,6 +16,7 @@
 VMEM = pl.BlockSpec(memory_space=pltpu.VMEM)
 HBM = pl.BlockSpec(memory_space=pltpu.HBM)
 PARAMS = pltpu.CompilerParams(vmem_limit_bytes=8 * 1024 * 1024)
+DIRECT = 48
 PIECES = 4
 ROWS = 4
 
@@ -47,13 +48,13 @@
     list_kept(table, lax.axis_index("rows"), tiles, places)
     for copy in block_copies:
         copy.wait()
-    half = first.shape[0]
+    cut = first.shape[0]
     for slot in range(slots):
         tile = block[:, pl.ds(pl.multiple_of(places[slot] * TILE, TILE), TILE)]
         to = slice(slot * TILE, (slot + 1) * TILE)
         packed[:, to] = tile
-        first[:, to] = tile[:half]
-        second[:, to] = tile[half:]
+        first[:, to] = tile[:cut]
+        second[:, to] = tile[cut:]
 
 
 def prepare_kernel(tiles, slots, kept, int_kept, integrals, own, gathered, product, table, int_table, held, places, sems):
@@ -110,27 +111,27 @@
 
 def early_kernel(product, gathered, pair, near_second, far_first, sums):
     mine = place()
-    half = near_second.shape[0]
+    cut = far_first.shape[0]
     sums[mine] = product[...]
     sums[mine ^ 1] = jnp.dot(pair[...], gathered[mine ^ 1], preferred_element_type=jnp.float32)
-    for step, start, block in ((2, half, near_second), (3, 0, far_first)):
-        sums[mine ^ step, start : start + half, :] = jnp.dot(
+    for step, start, block in ((2, cut, near_second), (3, 0, far_first)):
+        sums[mine ^ step, start : start + block.shape[0], :] = jnp.dot(
             block[...], gathered[mine ^ step], preferred_element_type=jnp.float32
         )
 
 
 def whole(n, early, near_sums, far_sums, out):
-    half = near_sums.shape[0]
+    cut = near_sums.shape[0]
     step = place() ^ n
     out[...] = early[n]
 
     @pl.when(step == 2)
     def _():
-        out[:half, :] = near_sums[...]
+        out[:cut, :] = near_sums[...]
 
     @pl.when(step == 3)
     def _():
-        out[half:, :] = far_sums[...]
+        out[cut:, :] = far_sums[...]
 
 
 def late_kernel(early, gathered, near_first, far_second, near_sums, far_sums, two, held):
@@ -176,14 +177,15 @@
     slots = tiles // GROUP * KEEP
     places = pltpu.SMEM((tiles + 1,), jnp.int32)
     sums_shape = jax.ShapeDtypeStruct((pairs, width), jnp.float32)
-    half_block = jax.ShapeDtypeStruct((pairs // 2, slots * TILE), doubles.dtype)
+    parts = (DIRECT, pairs - DIRECT)
+    blocks = [jax.ShapeDtypeStruct((rows, slots * TILE), doubles.dtype) for rows in parts]
     message = jax.ShapeDtypeStruct((pairs * width // TILE + HEAD, TILE), jnp.int16)
     doubles, doubles_kept, integrals, integral_kept = (
         pltpu.with_memory_space_constraint(x, pltpu.HBM) for x in (doubles, doubles_kept, integrals, integral_kept.T)
     )
     packed, first, second = pl.pallas_call(
         functools.partial(pack_kernel, tiles, slots),
-        out_shape=[jax.ShapeDtypeStruct((pairs, slots * TILE), doubles.dtype), half_block, half_block],
+        out_shape=[jax.ShapeDtypeStruct((pairs, slots * TILE), doubles.dtype)] + blocks,
         in_specs=[HBM, HBM],
         out_specs=[VMEM] * 3,
         scratch_shapes=[
@@ -213,7 +215,7 @@
             pltpu.SemaphoreType.DMA((PIECES + 2,)),
         ],
         compiler_params=PARAMS,
-        cost_estimate=cost(10**9),
+        cost_estimate=cost(115 * 10**7),
         name="prepare",
     )(doubles_kept, integral_kept, integrals, packed)
 
@@ -230,11 +232,11 @@
         )(*args)
 
     held = [pltpu.VMEM((pairs, width), jnp.float32)]
-    half_sums = jax.ShapeDtypeStruct((pairs // 2, width), jnp.float32)
+    part_sums = [jax.ShapeDtypeStruct((rows, width), jnp.float32) for rows in parts]
     all_sums = jax.ShapeDtypeStruct((ROWS, pairs, width), jnp.float32)
     early = on_vmem(early_kernel, "early", 0, all_sums, product, gathered, pair, near_second, far_first)
     near_sums, far_sums, two = on_vmem(
-        late_kernel, "late", 10**11, [half_sums] * 2 + [message], early, gathered, near_first, far_second, scratch=held
+        late_kernel, "late", 10**11, part_sums + [message], early, gathered, near_first, far_second, scratch=held
     )
     one, three, kept_sums = on_vmem(
         rest_kernel, "rest", 0, [message] * 2 + [sums_shape], early, near_sums, far_sums, scratch=held

time: 21.7 us -> 21.6 us (level)
  starting transfers between devices: 12.3 us -> 11.8 us
  waiting for transfers between devices: 5.11 us -> 5.47 us
    ppermute x8, starting transfers between devices: 12.3 us -> 11.8 us  [swap(): return lax.ppermute(x, axis, [(i, i ^ step) for i in range(ROWS)])]
    ppermute x8, waiting for transfers between devices: 5.11 us -> 5.47 us  [swap(): return lax.ppermute(x, axis, [(i, i ^ step) for i in range(ROWS)])]
  transfers between devices with their start and end apart: 8 -> 8, of which waited for: 5 -> 6; matrix products, arithmetic and copies ran while one was open for 0% -> 0% of each run, Pallas kernels for 10% -> 10%
where the time goes in v20:
time: 21.6 us; the launch traced here: 21.4 us
  starting transfers between devices  11.8 us (55%)
  waiting for transfers between devices  5.47 us (25%)
  Pallas kernels  4.02 us (19%)
    ppermute x8, starting transfers between devices, swap(): return lax.ppermute(x, axis, [(i, i ^ step) for i in range(ROWS)])  11.8 us
    ppermute x8, waiting for transfers between devices, swap(): return lax.ppermute(x, axis, [(i, i ^ step) for i in range(ROWS)])  5.47 us
    pallas_call x1, Pallas kernels, local_few(): pl.pallas_call(functools.partial(prepare_kernel, tiles, slots), out_shape...  1.64 us
    pallas_call x1, Pallas kernels, local_few(): pl.pallas_call(functools.partial(pack_kernel, tiles, slots), out_shape=[j...  1.01 us
    pallas_call x1, Pallas kernels, local_few(): pl.pallas_call(last_kernel, out_shape=sums_shape, in_specs=[VMEM] * 3, ou...  0.7 us
    pallas_call x4, Pallas kernels, on_vmem(): pl.pallas_call(kernel, out_shape=out_shape, in_specs=[VMEM] * len(args),...  0.67 us
  transfers between devices with their start and end apart: 8, of which 6 were waited for; matrix products, arithmetic and copies ran while one was open for 0% of the time, Pallas kernels for 10%

profile of v20, /device:TPU:0, one launch (start us, length us, event | category | flops | bytes accessed | tf_op | source)
XLA Modules:
  0.0 21.4 jit_solution(2392280045019482857)
XLA Ops:
  0.0 1.0 %pack.1 = (bf16[128,512]{1,0:T(8,128)(2,1)S(1)}, bf16[48,512]{1,0:T(8,128)(2,1)S(1)}, bf16[80,512]{1,0:T(8,128)(2,1)S(1)}) custom-call(s32[4,8]{1,0:T(4,128)} %kept.3, bf16[128,1024]{1,0:T(8,128)(2,1)} %doubles.1), custom_call_target="tpu_custom_call" | custom-call | tf_op jit(solution)/shard_map/pack/pallas_call | solution.py:186
  1.0 4.1 %collective-permute-start.1 = (bf16[80,512]{1,0:T(8,128)(2,1)S(1)}, bf16[80,512]{1,0:T(8,128)(2,1)S(1)}, u32[]{:S(2)}, u32[]{:S(2)}) collective-permute-start(bf16[80,512]{1,0:T(8,128)(2,1)S(1)} %get-tuple-element.19), channel_id=1, source_target_pairs={{0,8},{4,12},{8,0},{12,4},{1,9},{5,13},{9,1},{13,5},{2,10},{6,14},... | collective-permute-start | bytes 245768 | tf_op jit(solution)/shard_map/ppermute | solution.py:170
  5.1 1.6 %collective-permute-start = (bf16[128,512]{1,0:T(8,128)(2,1)S(1)}, bf16[128,512]{1,0:T(8,128)(2,1)S(1)}, u32[]{:S(2)}, u32[]{:S(2)}) collective-permute-start(bf16[128,512]{1,0:T(8,128)(2,1)S(1)} %get-tuple-element.16.own), channel_id=1, source_target_pairs={{0,4},{4,0},{8,12},{12,8},{1,5},{5,1},{9,13},{13,9},{2,6},{6,2},{1... | collective-permute-start | bytes 393224 | tf_op jit(solution)/shard_map/ppermute | solution.py:170
  6.7 0.0 collective-permute-start.2
  6.7 1.9 %collective-permute-start.3 = (bf16[48,512]{1,0:T(8,128)(2,1)S(1)}, bf16[48,512]{1,0:T(8,128)(2,1)S(1)}, u32[]{:S(2)}, u32[]{:S(2)}) collective-permute-start(bf16[48,512]{1,0:T(8,128)(2,1)S(1)} %get-tuple-element.20), channel_id=1, source_target_pairs={{0,8},{4,12},{8,0},{12,4},{1,9},{5,13},{9,1},{13,5},{2,10},{6,14},... | collective-permute-start | bytes 147464 | tf_op jit(solution)/shard_map/ppermute | solution.py:170
  8.6 0.5 %collective-permute-done.1.near_second = bf16[80,512]{1,0:T(8,128)(2,1)S(1)} collective-permute-done((bf16[80,512]{1,0:T(8,128)(2,1)S(1)}, bf16[80,512]{1,0:T(8,128)(2,1)S(1)}, u32[]{:S(2)}, u32[]{:S(2)}) %collective-permute-start.1) | collective-permute-done | bytes 81952 | tf_op jit(solution)/shard_map/ppermute | solution.py:170
  9.1 2.0 %collective-permute-start.4 = (bf16[80,512]{1,0:T(8,128)(2,1)S(1)}, bf16[80,512]{1,0:T(8,128)(2,1)S(1)}, u32[]{:S(2)}, u32[]{:S(2)}) collective-permute-start(bf16[80,512]{1,0:T(8,128)(2,1)S(1)} %collective-permute-done.1.near_second), channel_id=1, source_target_pairs={{0,4},{4,0},{8,12},{12,8},{1,5},{5,1},{9,13},{13,9},{2,6},{6,2},{1... | collective-permute-start | bytes 245768 | tf_op jit(solution)/shard_map/ppermute | solution.py:170
  11.1 1.6 %prepare.1 = (bf16[4,512,256]{2,1,0:T(8,128)(2,1)S(1)}, f32[128,256]{1,0:T(8,128)S(1)}) custom-call(s32[4,8]{1,0:T(4,128)} %kept.3, s32[2,8]{1,0:T(2,128)} %bitcast.1, bf16[1024,256]{1,0:T(8,128)(2,1)} %integrals.1, bf16[128,512]{1,0:T(8,128)(2,1)S(1)} %get-tuple-element.16.own), custom_call_target="tpu_custom_call" | custom-call | flops 1150000000 | bytes 1024 | tf_op jit(solution)/shard_map/prepare/pallas_call | solution.py:205
  12.7 0.3 %collective-permute-done.2.far_first = bf16[48,512]{1,0:T(8,128)(2,1)S(1)} collective-permute-done((bf16[48,512]{1,0:T(8,128)(2,1)S(1)}, bf16[48,512]{1,0:T(8,128)(2,1)S(1)}, u32[]{:S(2)}, u32[]{:S(2)}) %collective-permute-start.2) | collective-permute-done | bytes 49184 | tf_op jit(solution)/shard_map/ppermute | solution.py:170
  13.1 0.3 %collective-permute-done.pair = bf16[128,512]{1,0:T(8,128)(2,1)S(1)} collective-permute-done((bf16[128,512]{1,0:T(8,128)(2,1)S(1)}, bf16[128,512]{1,0:T(8,128)(2,1)S(1)}, u32[]{:S(2)}, u32[]{:S(2)}) %collective-permute-start) | collective-permute-done | bytes 131104 | tf_op jit(solution)/shard_map/ppermute | solution.py:170
  13.4 0.2 %early.1 = f32[4,128,256]{2,1,0:T(8,128)S(1)} custom-call(f32[128,256]{1,0:T(8,128)S(1)} %get-tuple-element.17.product, bf16[4,512,256]{2,1,0:T(8,128)(2,1)S(1)} %get-tuple-element.18.gathered, bf16[128,512]{1,0:T(8,128)(2,1)S(1)} %collective-permute-done.pair, bf16[80,512]{1,0:T(8,128)(2,1)S(1)} %collective-permute-done.1.near_second, ...), custom_call_target="tpu_custom_call" | custom-call | bytes 1024 | tf_op jit(solution)/shard_map/early/pallas_call | solution.py:223
  13.6 0.0 collective-permute-done.3.near_first
  13.6 0.9 %collective-permute-done.4.far_second = bf16[80,512]{1,0:T(8,128)(2,1)S(1)} collective-permute-done((bf16[80,512]{1,0:T(8,128)(2,1)S(1)}, bf16[80,512]{1,0:T(8,128)(2,1)S(1)}, u32[]{:S(2)}, u32[]{:S(2)}) %collective-permute-start.4) | collective-permute-done | bytes 81952 | tf_op jit(solution)/shard_map/ppermute | solution.py:170
  14.5 0.3 %late.1 = (f32[48,256]{1,0:T(8,128)S(1)}, f32[80,256]{1,0:T(8,128)S(1)}, s16[272,128]{1,0:T(8,128)(2,1)S(1)}) custom-call(f32[4,128,256]{2,1,0:T(8,128)S(1)} %early.1, bf16[4,512,256]{2,1,0:T(8,128)(2,1)S(1)} %get-tuple-element.18.gathered, bf16[48,512]{1,0:T(8,128)(2,1)S(1)} %collective-permute-done.3.near_first, ...), custom_call_target="tpu_custom_call" | custom-call | flops 99999997952 | bytes 1024 | tf_op jit(solution)/shard_map/late/pallas_call | solution.py:223
  14.8 1.8 %collective-permute-start.5 = (s16[272,128]{1,0:T(8,128)(2,1)S(1)}, s16[272,128]{1,0:T(8,128)(2,1)S(1)}, u32[]{:S(2)}, u32[]{:S(2)}) collective-permute-start(s16[272,128]{1,0:T(8,128)(2,1)S(1)} %get-tuple-element.24), channel_id=1, source_target_pairs={{0,2},{1,3},{2,0},{3,1},{4,6},{5,7},{6,4},{7,5},{8,10},{9,11},{10,... | collective-permute-start | bytes 208904 | tf_op jit(solution)/shard_map/ppermute | solution.py:170
  16.6 0.0 copy-start
  16.6 0.1 rest.1
  16.8 0.1 collective-permute-start.6
  16.8 0.4 %collective-permute-start.7 = (s16[272,128]{1,0:T(8,128)(2,1)S(1)}, s16[272,128]{1,0:T(8,128)(2,1)S(1)}, u32[]{:S(2)}, u32[]{:S(2)}) collective-permute-start(s16[272,128]{1,0:T(8,128)(2,1)S(1)} %get-tuple-element.26), channel_id=1, source_target_pairs={{0,1},{1,0},{2,3},{3,2},{4,5},{5,4},{6,7},{7,6},{8,9},{9,8},{10,11... | collective-permute-start | bytes 208904 | tf_op jit(solution)/shard_map/ppermute | solution.py:170
  17.2 2.0 %collective-permute-done.5.two = s16[272,128]{1,0:T(8,128)(2,1)S(1)} collective-permute-done((s16[272,128]{1,0:T(8,128)(2,1)S(1)}, s16[272,128]{1,0:T(8,128)(2,1)S(1)}, u32[]{:S(2)}, u32[]{:S(2)}) %collective-permute-start.5) | collective-permute-done | bytes 69664 | tf_op jit(solution)/shard_map/ppermute | solution.py:170
  19.2 0.0 copy-done
  19.2 1.5 %collective-permute-done.6.three = s16[272,128]{1,0:T(8,128)(2,1)S(1)} collective-permute-done((s16[272,128]{1,0:T(8,128)(2,1)S(1)}, s16[272,128]{1,0:T(8,128)(2,1)S(1)}, u32[]{:S(2)}, u32[]{:S(2)}) %collective-permute-start.6) | collective-permute-done | bytes 69664 | tf_op jit(solution)/shard_map/ppermute | solution.py:170
  20.7 0.0 collective-permute-done.7.one
  20.7 0.7 %last.1 = f32[128,256]{1,0:T(8,128)} custom-call(f32[128,256]{1,0:T(8,128)S(1)} %first.1.base, s16[272,128]{1,0:T(8,128)(2,1)S(1)} %collective-permute-done.6.three, s16[272,128]{1,0:T(8,128)(2,1)S(1)} %collective-permute-done.7.one), custom_call_target="tpu_custom_call" | custom-call | bytes 1024 | tf_op jit(solution)/shard_map/last/pallas_call | solution.py:246
  (1 shorter events, 0.0 us)
Async XLA Ops:
  1.0 8.1 %collective-permute-start.1 = (bf16[80,512]{1,0:T(8,128)(2,1)S(1)}, bf16[80,512]{1,0:T(8,128)(2,1)S(1)}, u32[]{:S(2)}, u32[]{:S(2)}) collective-permute-start(bf16[80,512]{1,0:T(8,128)(2,1)S(1)} %get-tuple-element.19), channel_id=1, source_target_pairs={{0,8},{4,12},{8,0},{12,4},{1,9},{5,13},{9,1},{13,5},{2,10},{6,14},... | collective-permute-start | bytes 245768 | tf_op jit(solution)/shard_map/ppermute | solution.py:170
  5.1 8.2 %collective-permute-start = (bf16[128,512]{1,0:T(8,128)(2,1)S(1)}, bf16[128,512]{1,0:T(8,128)(2,1)S(1)}, u32[]{:S(2)}, u32[]{:S(2)}) collective-permute-start(bf16[128,512]{1,0:T(8,128)(2,1)S(1)} %get-tuple-element.16.own), channel_id=1, source_target_pairs={{0,4},{4,0},{8,12},{12,8},{1,5},{5,1},{9,13},{13,9},{2,6},{6,2},{1... | collective-permute-start | bytes 393224 | tf_op jit(solution)/shard_map/ppermute | solution.py:170
  6.7 6.4 %collective-permute-start.2 = (bf16[48,512]{1,0:T(8,128)(2,1)S(1)}, bf16[48,512]{1,0:T(8,128)(2,1)S(1)}, u32[]{:S(2)}, u32[]{:S(2)}) collective-permute-start(bf16[48,512]{1,0:T(8,128)(2,1)S(1)} %get-tuple-element.20), channel_id=1, source_target_pairs={{0,12},{4,8},{8,4},{12,0},{1,13},{5,9},{9,5},{13,1},{2,14},{6,10},... | collective-permute-start | bytes 147464 | tf_op jit(solution)/shard_map/ppermute | solution.py:170
  6.7 6.9 %collective-permute-start.3 = (bf16[48,512]{1,0:T(8,128)(2,1)S(1)}, bf16[48,512]{1,0:T(8,128)(2,1)S(1)}, u32[]{:S(2)}, u32[]{:S(2)}) collective-permute-start(bf16[48,512]{1,0:T(8,128)(2,1)S(1)} %get-tuple-element.20), channel_id=1, source_target_pairs={{0,8},{4,12},{8,0},{12,4},{1,9},{5,13},{9,1},{13,5},{2,10},{6,14},... | collective-permute-start | bytes 147464 | tf_op jit(solution)/shard_map/ppermute | solution.py:170
  9.1 5.4 %collective-permute-start.4 = (bf16[80,512]{1,0:T(8,128)(2,1)S(1)}, bf16[80,512]{1,0:T(8,128)(2,1)S(1)}, u32[]{:S(2)}, u32[]{:S(2)}) collective-permute-start(bf16[80,512]{1,0:T(8,128)(2,1)S(1)} %collective-permute-done.1.near_second), channel_id=1, source_target_pairs={{0,4},{4,0},{8,12},{12,8},{1,5},{5,1},{9,13},{13,9},{2,6},{6,2},{1... | collective-permute-start | bytes 245768 | tf_op jit(solution)/shard_map/ppermute | solution.py:170
  14.8 4.4 %collective-permute-start.5 = (s16[272,128]{1,0:T(8,128)(2,1)S(1)}, s16[272,128]{1,0:T(8,128)(2,1)S(1)}, u32[]{:S(2)}, u32[]{:S(2)}) collective-permute-start(s16[272,128]{1,0:T(8,128)(2,1)S(1)} %get-tuple-element.24), channel_id=1, source_target_pairs={{0,2},{1,3},{2,0},{3,1},{4,6},{5,7},{6,4},{7,5},{8,10},{9,11},{10,... | collective-permute-start | bytes 208904 | tf_op jit(solution)/shard_map/ppermute | solution.py:170
  16.6 2.6 %copy-start = (f32[128,256]{1,0:T(8,128)S(1)}, f32[128,256]{1,0:T(8,128)}, u32[]{:S(2)}) copy-start(f32[128,256]{1,0:T(8,128)} %residual.1) | copy-start | bytes 393220
  16.8 3.9 %collective-permute-start.6 = (s16[272,128]{1,0:T(8,128)(2,1)S(1)}, s16[272,128]{1,0:T(8,128)(2,1)S(1)}, u32[]{:S(2)}, u32[]{:S(2)}) collective-permute-start(s16[272,128]{1,0:T(8,128)(2,1)S(1)} %get-tuple-element.25), channel_id=1, source_target_pairs={{0,3},{1,2},{2,1},{3,0},{4,7},{5,6},{6,5},{7,4},{8,11},{9,10},{10,... | collective-permute-start | bytes 208904 | tf_op jit(solution)/shard_map/ppermute | solution.py:170
  16.8 3.8 %collective-permute-start.7 = (s16[272,128]{1,0:T(8,128)(2,1)S(1)}, s16[272,128]{1,0:T(8,128)(2,1)S(1)}, u32[]{:S(2)}, u32[]{:S(2)}) collective-permute-start(s16[272,128]{1,0:T(8,128)(2,1)S(1)} %get-tuple-element.26), channel_id=1, source_target_pairs={{0,1},{1,0},{2,3},{3,2},{4,5},{5,4},{6,7},{7,6},{8,9},{9,8},{10,11... | collective-permute-start | bytes 208904 | tf_op jit(solution)/shard_map/ppermute | solution.py:170

commit v21 on v20

--- a/solution.py
+++ b/solution.py
@@ -134,33 +134,33 @@
         out[cut:, :] = far_sums[...]
 
 
-def late_kernel(early, gathered, near_first, far_second, near_sums, far_sums, two, held):
+def late_kernel(early, gathered, near_first, far_second, near_sums, far_sums, three, held):
     mine = place()
     near_sums[...] = jnp.dot(near_first[...], gathered[mine ^ 2], preferred_element_type=jnp.float32)
     far_sums[...] = jnp.dot(far_second[...], gathered[mine ^ 3], preferred_element_type=jnp.float32)
-    whole(2, early, near_sums, far_sums, held)
-    encode(held[...], two)
-
-
-def rest_kernel(early, near_sums, far_sums, one, three, kept_sums, held):
-    for n, out in ((3, three), (1, one)):
+    whole(3, early, near_sums, far_sums, held)
+    encode(held[...], three)
+
+
+def rest_kernel(early, near_sums, far_sums, one, two, kept_sums, held):
+    for n, out in ((2, two), (1, one)):
         whole(n, early, near_sums, far_sums, held)
         encode(held[...], out)
     whole(0, early, near_sums, far_sums, kept_sums)
 
 
-def first_kernel(residual, kept_sums, two, out):
+def first_kernel(residual, kept_sums, three, out):
     pairs = out.shape[0]
-    out[...] = residual[...] + kept_sums[...] + decode(two, pairs, 0, pairs)
-
-
-def last_kernel(base, three, one, out, total, sems):
+    out[...] = residual[...] + kept_sums[...] + decode(three, pairs, 0, pairs)
+
+
+def last_kernel(base, two, one, out, total, sems):
     pairs = total.shape[0]
     size = pairs // PIECES
     started = copies(total, out, sems)
     for i, copy in enumerate(started):
         rows = (i * size, (i + 1) * size)
-        total[rows[0] : rows[1], :] = base[rows[0] : rows[1], :] + decode(three, pairs, *rows) + decode(one, pairs, *rows)
+        total[rows[0] : rows[1], :] = base[rows[0] : rows[1], :] + decode(two, pairs, *rows) + decode(one, pairs, *rows)
         copy.start()
     for copy in started:
         copy.wait()
@@ -235,14 +235,14 @@
     part_sums = [jax.ShapeDtypeStruct((rows, width), jnp.float32) for rows in parts]
     all_sums = jax.ShapeDtypeStruct((ROWS, pairs, width), jnp.float32)
     early = on_vmem(early_kernel, "early", 0, all_sums, product, gathered, pair, near_second, far_first)
-    near_sums, far_sums, two = on_vmem(
+    near_sums, far_sums, three = on_vmem(
         late_kernel, "late", 10**11, part_sums + [message], early, gathered, near_first, far_second, scratch=held
     )
-    one, three, kept_sums = on_vmem(
+    one, two, kept_sums = on_vmem(
         rest_kernel, "rest", 0, [message] * 2 + [sums_shape], early, near_sums, far_sums, scratch=held
     )
     two, three, one = swap(two, "cols", 2), swap(three, "cols", 3), swap(one, "cols", 1)
-    base = on_vmem(first_kernel, "first", 0, sums_shape, residual, kept_sums, two)
+    base = on_vmem(first_kernel, "first", 0, sums_shape, residual, kept_sums, three)
     return pl.pallas_call(
         last_kernel,
         out_shape=sums_shape,
@@ -252,7 +252,7 @@
         compiler_params=PARAMS,
         cost_estimate=cost(0),
         name="last",
-    )(base, three, one)
+    )(base, two, one)
 
 
 def local_many(doubles, doubles_kept, integrals, integral_kept, residual):

time: 21.6 us -> 21.7 us (level)
  waiting for transfers between devices: 5.47 us -> 5.82 us
    ppermute x8, waiting for transfers between devices: 5.47 us -> 5.82 us  [swap(): return lax.ppermute(x, axis, [(i, i ^ step) for i in range(ROWS)])]
  transfers between devices with their start and end apart: 8 -> 8, of which waited for: 6 -> 6; matrix products, arithmetic and copies ran while one was open for 0% -> 0% of each run, Pallas kernels for 10% -> 9%
where the time goes in v21:
time: 21.7 us; the launch traced here: 21.5 us
  starting transfers between devices  11.6 us (53%)
  waiting for transfers between devices  5.82 us (27%)
  Pallas kernels  4.02 us (19%)
    ppermute x8, starting transfers between devices, swap(): return lax.ppermute(x, axis, [(i, i ^ step) for i in range(ROWS)])  11.6 us
    ppermute x8, waiting for transfers between devices, swap(): return lax.ppermute(x, axis, [(i, i ^ step) for i in range(ROWS)])  5.82 us
    pallas_call x1, Pallas kernels, local_few(): pl.pallas_call(functools.partial(prepare_kernel, tiles, slots), out_shape...  1.64 us
    pallas_call x1, Pallas kernels, local_few(): pl.pallas_call(functools.partial(pack_kernel, tiles, slots), out_shape=[j...  1.01 us
    pallas_call x1, Pallas kernels, local_few(): pl.pallas_call(last_kernel, out_shape=sums_shape, in_specs=[VMEM] * 3, ou...  0.7 us
    pallas_call x4, Pallas kernels, on_vmem(): pl.pallas_call(kernel, out_shape=out_shape, in_specs=[VMEM] * len(args),...  0.67 us
  transfers between devices with their start and end apart: 8, of which 6 were waited for; matrix products, arithmetic and copies ran while one was open for 0% of the time, Pallas kernels for 9%

profile of v21, /device:TPU:0, one launch (start us, length us, event | category | flops | bytes accessed | tf_op | source)
XLA Modules:
  0.0 21.5 jit_solution(4622137617988885359)
XLA Ops:
  0.0 1.0 %pack.1 = (bf16[128,512]{1,0:T(8,128)(2,1)S(1)}, bf16[48,512]{1,0:T(8,128)(2,1)S(1)}, bf16[80,512]{1,0:T(8,128)(2,1)S(1)}) custom-call(s32[4,8]{1,0:T(4,128)} %kept.3, bf16[128,1024]{1,0:T(8,128)(2,1)} %doubles.1), custom_call_target="tpu_custom_call" | custom-call | tf_op jit(solution)/shard_map/pack/pallas_call | solution.py:186
  1.0 4.1 %collective-permute-start.1 = (bf16[80,512]{1,0:T(8,128)(2,1)S(1)}, bf16[80,512]{1,0:T(8,128)(2,1)S(1)}, u32[]{:S(2)}, u32[]{:S(2)}) collective-permute-start(bf16[80,512]{1,0:T(8,128)(2,1)S(1)} %get-tuple-element.19), channel_id=1, source_target_pairs={{0,8},{4,12},{8,0},{12,4},{1,9},{5,13},{9,1},{13,5},{2,10},{6,14},... | collective-permute-start | bytes 245768 | tf_op jit(solution)/shard_map/ppermute | solution.py:170
  5.1 1.6 %collective-permute-start = (bf16[128,512]{1,0:T(8,128)(2,1)S(1)}, bf16[128,512]{1,0:T(8,128)(2,1)S(1)}, u32[]{:S(2)}, u32[]{:S(2)}) collective-permute-start(bf16[128,512]{1,0:T(8,128)(2,1)S(1)} %get-tuple-element.16.own), channel_id=1, source_target_pairs={{0,4},{4,0},{8,12},{12,8},{1,5},{5,1},{9,13},{13,9},{2,6},{6,2},{1... | collective-permute-start | bytes 393224 | tf_op jit(solution)/shard_map/ppermute | solution.py:170
  6.7 0.0 collective-permute-start.2
  6.7 1.9 %collective-permute-start.3 = (bf16[48,512]{1,0:T(8,128)(2,1)S(1)}, bf16[48,512]{1,0:T(8,128)(2,1)S(1)}, u32[]{:S(2)}, u32[]{:S(2)}) collective-permute-start(bf16[48,512]{1,0:T(8,128)(2,1)S(1)} %get-tuple-element.20), channel_id=1, source_target_pairs={{0,8},{4,12},{8,0},{12,4},{1,9},{5,13},{9,1},{13,5},{2,10},{6,14},... | collective-permute-start | bytes 147464 | tf_op jit(solution)/shard_map/ppermute | solution.py:170
  8.6 0.5 %collective-permute-done.1.near_second = bf16[80,512]{1,0:T(8,128)(2,1)S(1)} collective-permute-done((bf16[80,512]{1,0:T(8,128)(2,1)S(1)}, bf16[80,512]{1,0:T(8,128)(2,1)S(1)}, u32[]{:S(2)}, u32[]{:S(2)}) %collective-permute-start.1) | collective-permute-done | bytes 81952 | tf_op jit(solution)/shard_map/ppermute | solution.py:170
  9.1 2.0 %collective-permute-start.4 = (bf16[80,512]{1,0:T(8,128)(2,1)S(1)}, bf16[80,512]{1,0:T(8,128)(2,1)S(1)}, u32[]{:S(2)}, u32[]{:S(2)}) collective-permute-start(bf16[80,512]{1,0:T(8,128)(2,1)S(1)} %collective-permute-done.1.near_second), channel_id=1, source_target_pairs={{0,4},{4,0},{8,12},{12,8},{1,5},{5,1},{9,13},{13,9},{2,6},{6,2},{1... | collective-permute-start | bytes 245768 | tf_op jit(solution)/shard_map/ppermute | solution.py:170
  11.1 1.6 %prepare.1 = (bf16[4,512,256]{2,1,0:T(8,128)(2,1)S(1)}, f32[128,256]{1,0:T(8,128)S(1)}) custom-call(s32[4,8]{1,0:T(4,128)} %kept.3, s32[2,8]{1,0:T(2,128)} %bitcast.1, bf16[1024,256]{1,0:T(8,128)(2,1)} %integrals.1, bf16[128,512]{1,0:T(8,128)(2,1)S(1)} %get-tuple-element.16.own), custom_call_target="tpu_custom_call" | custom-call | flops 1150000000 | bytes 1024 | tf_op jit(solution)/shard_map/prepare/pallas_call | solution.py:205
  12.7 0.3 %collective-permute-done.2.far_first = bf16[48,512]{1,0:T(8,128)(2,1)S(1)} collective-permute-done((bf16[48,512]{1,0:T(8,128)(2,1)S(1)}, bf16[48,512]{1,0:T(8,128)(2,1)S(1)}, u32[]{:S(2)}, u32[]{:S(2)}) %collective-permute-start.2) | collective-permute-done | bytes 49184 | tf_op jit(solution)/shard_map/ppermute | solution.py:170
  13.1 0.3 %collective-permute-done.pair = bf16[128,512]{1,0:T(8,128)(2,1)S(1)} collective-permute-done((bf16[128,512]{1,0:T(8,128)(2,1)S(1)}, bf16[128,512]{1,0:T(8,128)(2,1)S(1)}, u32[]{:S(2)}, u32[]{:S(2)}) %collective-permute-start) | collective-permute-done | bytes 131104 | tf_op jit(solution)/shard_map/ppermute | solution.py:170
  13.4 0.2 %early.1 = f32[4,128,256]{2,1,0:T(8,128)S(1)} custom-call(f32[128,256]{1,0:T(8,128)S(1)} %get-tuple-element.17.product, bf16[4,512,256]{2,1,0:T(8,128)(2,1)S(1)} %get-tuple-element.18.gathered, bf16[128,512]{1,0:T(8,128)(2,1)S(1)} %collective-permute-done.pair, bf16[80,512]{1,0:T(8,128)(2,1)S(1)} %collective-permute-done.1.near_second, ...), custom_call_target="tpu_custom_call" | custom-call | bytes 1024 | tf_op jit(solution)/shard_map/early/pallas_call | solution.py:223
  13.6 0.0 collective-permute-done.3.near_first
  13.6 0.9 %collective-permute-done.4.far_second = bf16[80,512]{1,0:T(8,128)(2,1)S(1)} collective-permute-done((bf16[80,512]{1,0:T(8,128)(2,1)S(1)}, bf16[80,512]{1,0:T(8,128)(2,1)S(1)}, u32[]{:S(2)}, u32[]{:S(2)}) %collective-permute-start.4) | collective-permute-done | bytes 81952 | tf_op jit(solution)/shard_map/ppermute | solution.py:170
  14.5 0.3 %late.1 = (f32[48,256]{1,0:T(8,128)S(1)}, f32[80,256]{1,0:T(8,128)S(1)}, s16[272,128]{1,0:T(8,128)(2,1)S(1)}) custom-call(f32[4,128,256]{2,1,0:T(8,128)S(1)} %early.1, bf16[4,512,256]{2,1,0:T(8,128)(2,1)S(1)} %get-tuple-element.18.gathered, bf16[48,512]{1,0:T(8,128)(2,1)S(1)} %collective-permute-done.3.near_first, ...), custom_call_target="tpu_custom_call" | custom-call | flops 99999997952 | bytes 1024 | tf_op jit(solution)/shard_map/late/pallas_call | solution.py:223
  14.8 0.9 %collective-permute-start.5 = (s16[272,128]{1,0:T(8,128)(2,1)S(1)}, s16[272,128]{1,0:T(8,128)(2,1)S(1)}, u32[]{:S(2)}, u32[]{:S(2)}) collective-permute-start(s16[272,128]{1,0:T(8,128)(2,1)S(1)} %get-tuple-element.24), channel_id=1, source_target_pairs={{0,3},{1,2},{2,1},{3,0},{4,7},{5,6},{6,5},{7,4},{8,11},{9,10},{10,... | collective-permute-start | bytes 208904 | tf_op jit(solution)/shard_map/ppermute | solution.py:170
  15.7 0.0 copy-start
  15.7 0.1 rest.1
  15.8 1.1 %collective-permute-start.6 = (s16[272,128]{1,0:T(8,128)(2,1)S(1)}, s16[272,128]{1,0:T(8,128)(2,1)S(1)}, u32[]{:S(2)}, u32[]{:S(2)}) collective-permute-start(s16[272,128]{1,0:T(8,128)(2,1)S(1)} %get-tuple-element.25), channel_id=1, source_target_pairs={{0,2},{1,3},{2,0},{3,1},{4,6},{5,7},{6,4},{7,5},{8,10},{9,11},{10,... | collective-permute-start | bytes 208904 | tf_op jit(solution)/shard_map/ppermute | solution.py:170
  16.9 0.1 collective-permute-start.7
  17.0 2.0 %collective-permute-done.5.three = s16[272,128]{1,0:T(8,128)(2,1)S(1)} collective-permute-done((s16[272,128]{1,0:T(8,128)(2,1)S(1)}, s16[272,128]{1,0:T(8,128)(2,1)S(1)}, u32[]{:S(2)}, u32[]{:S(2)}) %collective-permute-start.5) | collective-permute-done | bytes 69664 | tf_op jit(solution)/shard_map/ppermute | solution.py:170
  19.1 0.0 copy-done
  19.1 1.7 %collective-permute-done.6.two = s16[272,128]{1,0:T(8,128)(2,1)S(1)} collective-permute-done((s16[272,128]{1,0:T(8,128)(2,1)S(1)}, s16[272,128]{1,0:T(8,128)(2,1)S(1)}, u32[]{:S(2)}, u32[]{:S(2)}) %collective-permute-start.6) | collective-permute-done | bytes 69664 | tf_op jit(solution)/shard_map/ppermute | solution.py:170
  20.8 0.0 collective-permute-done.7.one
  20.8 0.7 %last.1 = f32[128,256]{1,0:T(8,128)} custom-call(f32[128,256]{1,0:T(8,128)S(1)} %first.1.base, s16[272,128]{1,0:T(8,128)(2,1)S(1)} %collective-permute-done.6.two, s16[272,128]{1,0:T(8,128)(2,1)S(1)} %collective-permute-done.7.one), custom_call_target="tpu_custom_call" | custom-call | bytes 1024 | tf_op jit(solution)/shard_map/last/pallas_call | solution.py:246
  (1 shorter events, 0.0 us)
Async XLA Ops:
  1.0 8.1 %collective-permute-start.1 = (bf16[80,512]{1,0:T(8,128)(2,1)S(1)}, bf16[80,512]{1,0:T(8,128)(2,1)S(1)}, u32[]{:S(2)}, u32[]{:S(2)}) collective-permute-start(bf16[80,512]{1,0:T(8,128)(2,1)S(1)} %get-tuple-element.19), channel_id=1, source_target_pairs={{0,8},{4,12},{8,0},{12,4},{1,9},{5,13},{9,1},{13,5},{2,10},{6,14},... | collective-permute-start | bytes 245768 | tf_op jit(solution)/shard_map/ppermute | solution.py:170
  5.1 8.2 %collective-permute-start = (bf16[128,512]{1,0:T(8,128)(2,1)S(1)}, bf16[128,512]{1,0:T(8,128)(2,1)S(1)}, u32[]{:S(2)}, u32[]{:S(2)}) collective-permute-start(bf16[128,512]{1,0:T(8,128)(2,1)S(1)} %get-tuple-element.16.own), channel_id=1, source_target_pairs={{0,4},{4,0},{8,12},{12,8},{1,5},{5,1},{9,13},{13,9},{2,6},{6,2},{1... | collective-permute-start | bytes 393224 | tf_op jit(solution)/shard_map/ppermute | solution.py:170
  6.7 6.4 %collective-permute-start.2 = (bf16[48,512]{1,0:T(8,128)(2,1)S(1)}, bf16[48,512]{1,0:T(8,128)(2,1)S(1)}, u32[]{:S(2)}, u32[]{:S(2)}) collective-permute-start(bf16[48,512]{1,0:T(8,128)(2,1)S(1)} %get-tuple-element.20), channel_id=1, source_target_pairs={{0,12},{4,8},{8,4},{12,0},{1,13},{5,9},{9,5},{13,1},{2,14},{6,10},... | collective-permute-start | bytes 147464 | tf_op jit(solution)/shard_map/ppermute | solution.py:170
  6.7 6.9 %collective-permute-start.3 = (bf16[48,512]{1,0:T(8,128)(2,1)S(1)}, bf16[48,512]{1,0:T(8,128)(2,1)S(1)}, u32[]{:S(2)}, u32[]{:S(2)}) collective-permute-start(bf16[48,512]{1,0:T(8,128)(2,1)S(1)} %get-tuple-element.20), channel_id=1, source_target_pairs={{0,8},{4,12},{8,0},{12,4},{1,9},{5,13},{9,1},{13,5},{2,10},{6,14},... | collective-permute-start | bytes 147464 | tf_op jit(solution)/shard_map/ppermute | solution.py:170
  9.1 5.4 %collective-permute-start.4 = (bf16[80,512]{1,0:T(8,128)(2,1)S(1)}, bf16[80,512]{1,0:T(8,128)(2,1)S(1)}, u32[]{:S(2)}, u32[]{:S(2)}) collective-permute-start(bf16[80,512]{1,0:T(8,128)(2,1)S(1)} %collective-permute-done.1.near_second), channel_id=1, source_target_pairs={{0,4},{4,0},{8,12},{12,8},{1,5},{5,1},{9,13},{13,9},{2,6},{6,2},{1... | collective-permute-start | bytes 245768 | tf_op jit(solution)/shard_map/ppermute | solution.py:170
  14.8 4.2 %collective-permute-start.5 = (s16[272,128]{1,0:T(8,128)(2,1)S(1)}, s16[272,128]{1,0:T(8,128)(2,1)S(1)}, u32[]{:S(2)}, u32[]{:S(2)}) collective-permute-start(s16[272,128]{1,0:T(8,128)(2,1)S(1)} %get-tuple-element.24), channel_id=1, source_target_pairs={{0,3},{1,2},{2,1},{3,0},{4,7},{5,6},{6,5},{7,4},{8,11},{9,10},{10,... | collective-permute-start | bytes 208904 | tf_op jit(solution)/shard_map/ppermute | solution.py:170
  15.7 3.4 %copy-start = (f32[128,256]{1,0:T(8,128)S(1)}, f32[128,256]{1,0:T(8,128)}, u32[]{:S(2)}) copy-start(f32[128,256]{1,0:T(8,128)} %residual.1) | copy-start | bytes 393220
  15.8 5.0 %collective-permute-start.6 = (s16[272,128]{1,0:T(8,128)(2,1)S(1)}, s16[272,128]{1,0:T(8,128)(2,1)S(1)}, u32[]{:S(2)}, u32[]{:S(2)}) collective-permute-start(s16[272,128]{1,0:T(8,128)(2,1)S(1)} %get-tuple-element.25), channel_id=1, source_target_pairs={{0,2},{1,3},{2,0},{3,1},{4,6},{5,7},{6,4},{7,5},{8,10},{9,11},{10,... | collective-permute-start | bytes 208904 | tf_op jit(solution)/shard_map/ppermute | solution.py:170
  16.9 4.0 %collective-permute-start.7 = (s16[272,128]{1,0:T(8,128)(2,1)S(1)}, s16[272,128]{1,0:T(8,128)(2,1)S(1)}, u32[]{:S(2)}, u32[]{:S(2)}) collective-permute-start(s16[272,128]{1,0:T(8,128)(2,1)S(1)} %get-tuple-element.26), channel_id=1, source_target_pairs={{0,1},{1,0},{2,3},{3,2},{4,5},{5,4},{6,7},{7,6},{8,9},{9,8},{10,11... | collective-permute-start | bytes 208904 | tf_op jit(solution)/shard_map/ppermute | solution.py:170

commit v22 on v20

--- a/solution.py
+++ b/solution.py
@@ -16,7 +16,7 @@
 VMEM = pl.BlockSpec(memory_space=pltpu.VMEM)
 HBM = pl.BlockSpec(memory_space=pltpu.HBM)
 PARAMS = pltpu.CompilerParams(vmem_limit_bytes=8 * 1024 * 1024)
-DIRECT = 48
+DIRECT = 32
 PIECES = 4
 ROWS = 4
 

time: 21.6 us -> 22.5 us (1.042)
  waiting for transfers between devices: 5.47 us -> 8.07 us
  starting transfers between devices: 11.8 us -> 10.1 us
    ppermute x8, waiting for transfers between devices: 5.47 us -> 8.07 us  [swap(): return lax.ppermute(x, axis, [(i, i ^ step) for i in range(ROWS)])]
    ppermute x8, starting transfers between devices: 11.8 us -> 10.1 us  [swap(): return lax.ppermute(x, axis, [(i, i ^ step) for i in range(ROWS)])]
  transfers between devices with their start and end apart: 8 -> 8, of which waited for: 6 -> 5; matrix products, arithmetic and copies ran while one was open for 0% -> 0% of each run, Pallas kernels for 10% -> 9%
where the time goes in v22:
time: 22.5 us; the launch traced here: 22.3 us
  starting transfers between devices  10.1 us (45%)
  waiting for transfers between devices  8.07 us (36%)
  Pallas kernels  4.02 us (18%)
    ppermute x8, starting transfers between devices, swap(): return lax.ppermute(x, axis, [(i, i ^ step) for i in range(ROWS)])  10.1 us
    ppermute x8, waiting for transfers between devices, swap(): return lax.ppermute(x, axis, [(i, i ^ step) for i in range(ROWS)])  8.07 us
    pallas_call x1, Pallas kernels, local_few(): pl.pallas_call(functools.partial(prepare_kernel, tiles, slots), out_shape...  1.64 us
    pallas_call x1, Pallas kernels, local_few(): pl.pallas_call(functools.partial(pack_kernel, tiles, slots), out_shape=[j...  1.01 us
    pallas_call x1, Pallas kernels, local_few(): pl.pallas_call(last_kernel, out_shape=sums_shape, in_specs=[VMEM] * 3, ou...  0.7 us
    pallas_call x4, Pallas kernels, on_vmem(): pl.pallas_call(kernel, out_shape=out_shape, in_specs=[VMEM] * len(args),...  0.67 us
  transfers between devices with their start and end apart: 8, of which 5 were waited for; matrix products, arithmetic and copies ran while one was open for 0% of the time, Pallas kernels for 9%

profile of v22, /device:TPU:0, one launch (start us, length us, event | category | flops | bytes accessed | tf_op | source)
XLA Modules:
  0.0 22.3 jit_solution(8762658985166798735)
XLA Ops:
  0.0 1.0 %pack.1 = (bf16[128,512]{1,0:T(8,128)(2,1)S(1)}, bf16[32,512]{1,0:T(8,128)(2,1)S(1)}, bf16[96,512]{1,0:T(8,128)(2,1)S(1)}) custom-call(s32[4,8]{1,0:T(4,128)} %kept.3, bf16[128,1024]{1,0:T(8,128)(2,1)} %doubles.1), custom_call_target="tpu_custom_call" | custom-call | tf_op jit(solution)/shard_map/pack/pallas_call | solution.py:186
  1.0 4.1 %collective-permute-start.1 = (bf16[96,512]{1,0:T(8,128)(2,1)S(1)}, bf16[96,512]{1,0:T(8,128)(2,1)S(1)}, u32[]{:S(2)}, u32[]{:S(2)}) collective-permute-start(bf16[96,512]{1,0:T(8,128)(2,1)S(1)} %get-tuple-element.19), channel_id=1, source_target_pairs={{0,8},{4,12},{8,0},{12,4},{1,9},{5,13},{9,1},{13,5},{2,10},{6,14},... | collective-permute-start | bytes 294920 | tf_op jit(solution)/shard_map/ppermute | solution.py:170
  5.1 1.6 %collective-permute-start = (bf16[128,512]{1,0:T(8,128)(2,1)S(1)}, bf16[128,512]{1,0:T(8,128)(2,1)S(1)}, u32[]{:S(2)}, u32[]{:S(2)}) collective-permute-start(bf16[128,512]{1,0:T(8,128)(2,1)S(1)} %get-tuple-element.16.own), channel_id=1, source_target_pairs={{0,4},{4,0},{8,12},{12,8},{1,5},{5,1},{9,13},{13,9},{2,6},{6,2},{1... | collective-permute-start | bytes 393224 | tf_op jit(solution)/shard_map/ppermute | solution.py:170
  6.7 0.0 collective-permute-start.2
  6.7 1.9 %collective-permute-start.3 = (bf16[32,512]{1,0:T(8,128)(2,1)S(1)}, bf16[32,512]{1,0:T(8,128)(2,1)S(1)}, u32[]{:S(2)}, u32[]{:S(2)}) collective-permute-start(bf16[32,512]{1,0:T(8,128)(2,1)S(1)} %get-tuple-element.20), channel_id=1, source_target_pairs={{0,8},{4,12},{8,0},{12,4},{1,9},{5,13},{9,1},{13,5},{2,10},{6,14},... | collective-permute-start | bytes 98312 | tf_op jit(solution)/shard_map/ppermute | solution.py:170
  8.6 2.2 %collective-permute-done.1.near_second = bf16[96,512]{1,0:T(8,128)(2,1)S(1)} collective-permute-done((bf16[96,512]{1,0:T(8,128)(2,1)S(1)}, bf16[96,512]{1,0:T(8,128)(2,1)S(1)}, u32[]{:S(2)}, u32[]{:S(2)}) %collective-permute-start.1) | collective-permute-done | bytes 98336 | tf_op jit(solution)/shard_map/ppermute | solution.py:170
  10.8 0.3 %collective-permute-start.4 = (bf16[96,512]{1,0:T(8,128)(2,1)S(1)}, bf16[96,512]{1,0:T(8,128)(2,1)S(1)}, u32[]{:S(2)}, u32[]{:S(2)}) collective-permute-start(bf16[96,512]{1,0:T(8,128)(2,1)S(1)} %collective-permute-done.1.near_second), channel_id=1, source_target_pairs={{0,4},{4,0},{8,12},{12,8},{1,5},{5,1},{9,13},{13,9},{2,6},{6,2},{1... | collective-permute-start | bytes 294920 | tf_op jit(solution)/shard_map/ppermute | solution.py:170
  11.1 1.6 %prepare.1 = (bf16[4,512,256]{2,1,0:T(8,128)(2,1)S(1)}, f32[128,256]{1,0:T(8,128)S(1)}) custom-call(s32[4,8]{1,0:T(4,128)} %kept.3, s32[2,8]{1,0:T(2,128)} %bitcast.1, bf16[1024,256]{1,0:T(8,128)(2,1)} %integrals.1, bf16[128,512]{1,0:T(8,128)(2,1)S(1)} %get-tuple-element.16.own), custom_call_target="tpu_custom_call" | custom-call | flops 1150000000 | bytes 1024 | tf_op jit(solution)/shard_map/prepare/pallas_call | solution.py:205
  12.7 0.2 collective-permute-done.2.far_first
  12.9 0.0 collective-permute-done.pair
  12.9 0.2 %early.1 = f32[4,128,256]{2,1,0:T(8,128)S(1)} custom-call(f32[128,256]{1,0:T(8,128)S(1)} %get-tuple-element.17.product, bf16[4,512,256]{2,1,0:T(8,128)(2,1)S(1)} %get-tuple-element.18.gathered, bf16[128,512]{1,0:T(8,128)(2,1)S(1)} %collective-permute-done.pair, bf16[96,512]{1,0:T(8,128)(2,1)S(1)} %collective-permute-done.1.near_second, ...), custom_call_target="tpu_custom_call" | custom-call | bytes 1024 | tf_op jit(solution)/shard_map/early/pallas_call | solution.py:223
  13.2 0.0 collective-permute-done.3.near_first
  13.2 2.2 %collective-permute-done.4.far_second = bf16[96,512]{1,0:T(8,128)(2,1)S(1)} collective-permute-done((bf16[96,512]{1,0:T(8,128)(2,1)S(1)}, bf16[96,512]{1,0:T(8,128)(2,1)S(1)}, u32[]{:S(2)}, u32[]{:S(2)}) %collective-permute-start.4) | collective-permute-done | bytes 98336 | tf_op jit(solution)/shard_map/ppermute | solution.py:170
  15.4 0.3 %late.1 = (f32[32,256]{1,0:T(8,128)S(1)}, f32[96,256]{1,0:T(8,128)S(1)}, s16[272,128]{1,0:T(8,128)(2,1)S(1)}) custom-call(f32[4,128,256]{2,1,0:T(8,128)S(1)} %early.1, bf16[4,512,256]{2,1,0:T(8,128)(2,1)S(1)} %get-tuple-element.18.gathered, bf16[32,512]{1,0:T(8,128)(2,1)S(1)} %collective-permute-done.3.near_first, ...), custom_call_target="tpu_custom_call" | custom-call | flops 99999997952 | bytes 1024 | tf_op jit(solution)/shard_map/late/pallas_call | solution.py:223
  15.7 1.7 %collective-permute-start.5 = (s16[272,128]{1,0:T(8,128)(2,1)S(1)}, s16[272,128]{1,0:T(8,128)(2,1)S(1)}, u32[]{:S(2)}, u32[]{:S(2)}) collective-permute-start(s16[272,128]{1,0:T(8,128)(2,1)S(1)} %get-tuple-element.24), channel_id=1, source_target_pairs={{0,2},{1,3},{2,0},{3,1},{4,6},{5,7},{6,4},{7,5},{8,10},{9,11},{10,... | collective-permute-start | bytes 208904 | tf_op jit(solution)/shard_map/ppermute | solution.py:170
  17.5 0.0 copy-start
  17.5 0.1 rest.1
  17.6 0.1 collective-permute-start.6
  17.7 0.5 %collective-permute-start.7 = (s16[272,128]{1,0:T(8,128)(2,1)S(1)}, s16[272,128]{1,0:T(8,128)(2,1)S(1)}, u32[]{:S(2)}, u32[]{:S(2)}) collective-permute-start(s16[272,128]{1,0:T(8,128)(2,1)S(1)} %get-tuple-element.26), channel_id=1, source_target_pairs={{0,1},{1,0},{2,3},{3,2},{4,5},{5,4},{6,7},{7,6},{8,9},{9,8},{10,11... | collective-permute-start | bytes 208904 | tf_op jit(solution)/shard_map/ppermute | solution.py:170
  18.1 2.0 %collective-permute-done.5.two = s16[272,128]{1,0:T(8,128)(2,1)S(1)} collective-permute-done((s16[272,128]{1,0:T(8,128)(2,1)S(1)}, s16[272,128]{1,0:T(8,128)(2,1)S(1)}, u32[]{:S(2)}, u32[]{:S(2)}) %collective-permute-start.5) | collective-permute-done | bytes 69664 | tf_op jit(solution)/shard_map/ppermute | solution.py:170
  20.1 0.0 copy-done
  20.1 1.5 %collective-permute-done.6.three = s16[272,128]{1,0:T(8,128)(2,1)S(1)} collective-permute-done((s16[272,128]{1,0:T(8,128)(2,1)S(1)}, s16[272,128]{1,0:T(8,128)(2,1)S(1)}, u32[]{:S(2)}, u32[]{:S(2)}) %collective-permute-start.6) | collective-permute-done | bytes 69664 | tf_op jit(solution)/shard_map/ppermute | solution.py:170
  21.6 0.0 collective-permute-done.7.one
  21.6 0.7 %last.1 = f32[128,256]{1,0:T(8,128)} custom-call(f32[128,256]{1,0:T(8,128)S(1)} %first.1.base, s16[272,128]{1,0:T(8,128)(2,1)S(1)} %collective-permute-done.6.three, s16[272,128]{1,0:T(8,128)(2,1)S(1)} %collective-permute-done.7.one), custom_call_target="tpu_custom_call" | custom-call | bytes 1024 | tf_op jit(solution)/shard_map/last/pallas_call | solution.py:246
  (1 shorter events, 0.0 us)
Async XLA Ops:
  1.0 9.8 %collective-permute-start.1 = (bf16[96,512]{1,0:T(8,128)(2,1)S(1)}, bf16[96,512]{1,0:T(8,128)(2,1)S(1)}, u32[]{:S(2)}, u32[]{:S(2)}) collective-permute-start(bf16[96,512]{1,0:T(8,128)(2,1)S(1)} %get-tuple-element.19), channel_id=1, source_target_pairs={{0,8},{4,12},{8,0},{12,4},{1,9},{5,13},{9,1},{13,5},{2,10},{6,14},... | collective-permute-start | bytes 294920 | tf_op jit(solution)/shard_map/ppermute | solution.py:170
  5.1 7.8 %collective-permute-start = (bf16[128,512]{1,0:T(8,128)(2,1)S(1)}, bf16[128,512]{1,0:T(8,128)(2,1)S(1)}, u32[]{:S(2)}, u32[]{:S(2)}) collective-permute-start(bf16[128,512]{1,0:T(8,128)(2,1)S(1)} %get-tuple-element.16.own), channel_id=1, source_target_pairs={{0,4},{4,0},{8,12},{12,8},{1,5},{5,1},{9,13},{13,9},{2,6},{6,2},{1... | collective-permute-start | bytes 393224 | tf_op jit(solution)/shard_map/ppermute | solution.py:170
  6.7 6.2 %collective-permute-start.2 = (bf16[32,512]{1,0:T(8,128)(2,1)S(1)}, bf16[32,512]{1,0:T(8,128)(2,1)S(1)}, u32[]{:S(2)}, u32[]{:S(2)}) collective-permute-start(bf16[32,512]{1,0:T(8,128)(2,1)S(1)} %get-tuple-element.20), channel_id=1, source_target_pairs={{0,12},{4,8},{8,4},{12,0},{1,13},{5,9},{9,5},{13,1},{2,14},{6,10},... | collective-permute-start | bytes 98312 | tf_op jit(solution)/shard_map/ppermute | solution.py:170
  6.7 6.5 %collective-permute-start.3 = (bf16[32,512]{1,0:T(8,128)(2,1)S(1)}, bf16[32,512]{1,0:T(8,128)(2,1)S(1)}, u32[]{:S(2)}, u32[]{:S(2)}) collective-permute-start(bf16[32,512]{1,0:T(8,128)(2,1)S(1)} %get-tuple-element.20), channel_id=1, source_target_pairs={{0,8},{4,12},{8,0},{12,4},{1,9},{5,13},{9,1},{13,5},{2,10},{6,14},... | collective-permute-start | bytes 98312 | tf_op jit(solution)/shard_map/ppermute | solution.py:170
  10.8 4.6 %collective-permute-start.4 = (bf16[96,512]{1,0:T(8,128)(2,1)S(1)}, bf16[96,512]{1,0:T(8,128)(2,1)S(1)}, u32[]{:S(2)}, u32[]{:S(2)}) collective-permute-start(bf16[96,512]{1,0:T(8,128)(2,1)S(1)} %collective-permute-done.1.near_second), channel_id=1, source_target_pairs={{0,4},{4,0},{8,12},{12,8},{1,5},{5,1},{9,13},{13,9},{2,6},{6,2},{1... | collective-permute-start | bytes 294920 | tf_op jit(solution)/shard_map/ppermute | solution.py:170
  15.7 4.4 %collective-permute-start.5 = (s16[272,128]{1,0:T(8,128)(2,1)S(1)}, s16[272,128]{1,0:T(8,128)(2,1)S(1)}, u32[]{:S(2)}, u32[]{:S(2)}) collective-permute-start(s16[272,128]{1,0:T(8,128)(2,1)S(1)} %get-tuple-element.24), channel_id=1, source_target_pairs={{0,2},{1,3},{2,0},{3,1},{4,6},{5,7},{6,4},{7,5},{8,10},{9,11},{10,... | collective-permute-start | bytes 208904 | tf_op jit(solution)/shard_map/ppermute | solution.py:170
  17.5 2.6 %copy-start = (f32[128,256]{1,0:T(8,128)S(1)}, f32[128,256]{1,0:T(8,128)}, u32[]{:S(2)}) copy-start(f32[128,256]{1,0:T(8,128)} %residual.1) | copy-start | bytes 393220
  17.6 4.0 %collective-permute-start.6 = (s16[272,128]{1,0:T(8,128)(2,1)S(1)}, s16[272,128]{1,0:T(8,128)(2,1)S(1)}, u32[]{:S(2)}, u32[]{:S(2)}) collective-permute-start(s16[272,128]{1,0:T(8,128)(2,1)S(1)} %get-tuple-element.25), channel_id=1, source_target_pairs={{0,3},{1,2},{2,1},{3,0},{4,7},{5,6},{6,5},{7,4},{8,11},{9,10},{10,... | collective-permute-start | bytes 208904 | tf_op jit(solution)/shard_map/ppermute | solution.py:170
  17.7 3.9 %collective-permute-start.7 = (s16[272,128]{1,0:T(8,128)(2,1)S(1)}, s16[272,128]{1,0:T(8,128)(2,1)S(1)}, u32[]{:S(2)}, u32[]{:S(2)}) collective-permute-start(s16[272,128]{1,0:T(8,128)(2,1)S(1)} %get-tuple-element.26), channel_id=1, source_target_pairs={{0,1},{1,0},{2,3},{3,2},{4,5},{5,4},{6,7},{7,6},{8,9},{9,8},{10,11... | collective-permute-start | bytes 208904 | tf_op jit(solution)/shard_map/ppermute | solution.py:170

commit v23 on v21

--- a/solution.py
+++ b/solution.py
@@ -109,6 +109,10 @@
     return lax.axis_index("rows") ^ lax.axis_index("cols")
 
 
+def far_steps(col):
+    return 3 - col // 2, 2 + col // 2
+
+
 def early_kernel(product, gathered, pair, near_second, far_first, sums):
     mine = place()
     cut = far_first.shape[0]
@@ -134,33 +138,33 @@
         out[cut:, :] = far_sums[...]
 
 
-def late_kernel(early, gathered, near_first, far_second, near_sums, far_sums, three, held):
+def late_kernel(early, gathered, near_first, far_second, near_sums, far_sums, one_far, held):
     mine = place()
     near_sums[...] = jnp.dot(near_first[...], gathered[mine ^ 2], preferred_element_type=jnp.float32)
     far_sums[...] = jnp.dot(far_second[...], gathered[mine ^ 3], preferred_element_type=jnp.float32)
-    whole(3, early, near_sums, far_sums, held)
-    encode(held[...], three)
-
-
-def rest_kernel(early, near_sums, far_sums, one, two, kept_sums, held):
-    for n, out in ((2, two), (1, one)):
+    whole(far_steps(lax.axis_index("cols"))[0], early, near_sums, far_sums, held)
+    encode(held[...], one_far)
+
+
+def rest_kernel(early, near_sums, far_sums, one, other_far, kept_sums, held):
+    for n, out in ((far_steps(lax.axis_index("cols"))[1], other_far), (1, one)):
         whole(n, early, near_sums, far_sums, held)
         encode(held[...], out)
     whole(0, early, near_sums, far_sums, kept_sums)
 
 
-def first_kernel(residual, kept_sums, three, out):
+def first_kernel(residual, kept_sums, one_far, out):
     pairs = out.shape[0]
-    out[...] = residual[...] + kept_sums[...] + decode(three, pairs, 0, pairs)
-
-
-def last_kernel(base, two, one, out, total, sems):
+    out[...] = residual[...] + kept_sums[...] + decode(one_far, pairs, 0, pairs)
+
+
+def last_kernel(base, other_far, one, out, total, sems):
     pairs = total.shape[0]
     size = pairs // PIECES
     started = copies(total, out, sems)
     for i, copy in enumerate(started):
         rows = (i * size, (i + 1) * size)
-        total[rows[0] : rows[1], :] = base[rows[0] : rows[1], :] + decode(two, pairs, *rows) + decode(one, pairs, *rows)
+        total[rows[0] : rows[1], :] = base[rows[0] : rows[1], :] + decode(other_far, pairs, *rows) + decode(one, pairs, *rows)
         copy.start()
     for copy in started:
         copy.wait()
@@ -235,14 +239,18 @@
     part_sums = [jax.ShapeDtypeStruct((rows, width), jnp.float32) for rows in parts]
     all_sums = jax.ShapeDtypeStruct((ROWS, pairs, width), jnp.float32)
     early = on_vmem(early_kernel, "early", 0, all_sums, product, gathered, pair, near_second, far_first)
-    near_sums, far_sums, three = on_vmem(
+    near_sums, far_sums, one_far = on_vmem(
         late_kernel, "late", 10**11, part_sums + [message], early, gathered, near_first, far_second, scratch=held
     )
-    one, two, kept_sums = on_vmem(
+    one, other_far, kept_sums = on_vmem(
         rest_kernel, "rest", 0, [message] * 2 + [sums_shape], early, near_sums, far_sums, scratch=held
     )
-    two, three, one = swap(two, "cols", 2), swap(three, "cols", 3), swap(one, "cols", 1)
-    base = on_vmem(first_kernel, "first", 0, sums_shape, residual, kept_sums, three)
+    one_far, other_far = (
+        lax.ppermute(x, "cols", [(col, col ^ far_steps(col)[i]) for col in range(ROWS)])
+        for i, x in enumerate((one_far, other_far))
+    )
+    one = swap(one, "cols", 1)
+    base = on_vmem(first_kernel, "first", 0, sums_shape, residual, kept_sums, one_far)
     return pl.pallas_call(
         last_kernel,
         out_shape=sums_shape,
@@ -252,7 +260,7 @@
         compiler_params=PARAMS,
         cost_estimate=cost(0),
         name="last",
-    )(base, two, one)
+    )(base, other_far, one)
 
 
 def local_many(doubles, doubles_kept, integrals, integral_kept, residual):

time: 21.7 us -> 21.1 us (0.972)
  the two profiles are of different devices: /device:TPU:0 before, /device:TPU:1 now
where the time goes in v23:
time: 21.1 us; the launch traced here: 20.9 us
  starting transfers between devices  11.2 us (53%)
  waiting for transfers between devices  5.65 us (27%)
  Pallas kernels  4.02 us (19%)
    ppermute x6, starting transfers between devices, swap(): return lax.ppermute(x, axis, [(i, i ^ step) for i in range(ROWS)])  8.7 us
    ppermute x2, waiting for transfers between devices, local_few(): lax.ppermute(x, 'cols', [(col, col ^ far_steps(col)[i]) for col in range(...  3.02 us
    ppermute x6, waiting for transfers between devices, swap(): return lax.ppermute(x, axis, [(i, i ^ step) for i in range(ROWS)])  2.62 us
    ppermute x2, starting transfers between devices, local_few(): lax.ppermute(x, 'cols', [(col, col ^ far_steps(col)[i]) for col in range(...  2.46 us
    pallas_call x1, Pallas kernels, local_few(): pl.pallas_call(functools.partial(prepare_kernel, tiles, slots), out_shape...  1.64 us
    pallas_call x1, Pallas kernels, local_few(): pl.pallas_call(functools.partial(pack_kernel, tiles, slots), out_shape=[j...  1.01 us
    pallas_call x1, Pallas kernels, local_few(): pl.pallas_call(last_kernel, out_shape=sums_shape, in_specs=[VMEM] * 3, ou...  0.7 us
    pallas_call x4, Pallas kernels, on_vmem(): pl.pallas_call(kernel, out_shape=out_shape, in_specs=[VMEM] * len(args),...  0.67 us
  transfers between devices with their start and end apart: 8, of which 4 were waited for; matrix products, arithmetic and copies ran while one was open for 0% of the time, Pallas kernels for 10%

profile of v23, /device:TPU:1, one launch (start us, length us, event | category | flops | bytes accessed | tf_op | source)
XLA Modules:
  0.0 20.9 jit_solution(11400615880783864109)
XLA Ops:
  0.0 1.0 %pack.1 = (bf16[128,512]{1,0:T(8,128)(2,1)S(1)}, bf16[48,512]{1,0:T(8,128)(2,1)S(1)}, bf16[80,512]{1,0:T(8,128)(2,1)S(1)}) custom-call(s32[4,8]{1,0:T(4,128)} %kept.3, bf16[128,1024]{1,0:T(8,128)(2,1)} %doubles.1), custom_call_target="tpu_custom_call" | custom-call | tf_op jit(solution)/shard_map/pack/pallas_call | solution.py:190
  1.0 3.2 %collective-permute-start.1 = (bf16[80,512]{1,0:T(8,128)(2,1)S(1)}, bf16[80,512]{1,0:T(8,128)(2,1)S(1)}, u32[]{:S(2)}, u32[]{:S(2)}) collective-permute-start(bf16[80,512]{1,0:T(8,128)(2,1)S(1)} %get-tuple-element.19), channel_id=1, source_target_pairs={{0,8},{4,12},{8,0},{12,4},{1,9},{5,13},{9,1},{13,5},{2,10},{6,14},... | collective-permute-start | bytes 245768 | tf_op jit(solution)/shard_map/ppermute | solution.py:174
  4.2 1.3 %collective-permute-start = (bf16[128,512]{1,0:T(8,128)(2,1)S(1)}, bf16[128,512]{1,0:T(8,128)(2,1)S(1)}, u32[]{:S(2)}, u32[]{:S(2)}) collective-permute-start(bf16[128,512]{1,0:T(8,128)(2,1)S(1)} %get-tuple-element.16.own), channel_id=1, source_target_pairs={{0,4},{4,0},{8,12},{12,8},{1,5},{5,1},{9,13},{13,9},{2,6},{6,2},{1... | collective-permute-start | bytes 393224 | tf_op jit(solution)/shard_map/ppermute | solution.py:174
  5.5 0.0 collective-permute-start.2
  5.5 1.3 %collective-permute-start.3 = (bf16[48,512]{1,0:T(8,128)(2,1)S(1)}, bf16[48,512]{1,0:T(8,128)(2,1)S(1)}, u32[]{:S(2)}, u32[]{:S(2)}) collective-permute-start(bf16[48,512]{1,0:T(8,128)(2,1)S(1)} %get-tuple-element.20), channel_id=1, source_target_pairs={{0,8},{4,12},{8,0},{12,4},{1,9},{5,13},{9,1},{13,5},{2,10},{6,14},... | collective-permute-start | bytes 147464 | tf_op jit(solution)/shard_map/ppermute | solution.py:174
  6.9 0.0 collective-permute-done.1.near_second
  6.9 2.2 %collective-permute-start.4 = (bf16[80,512]{1,0:T(8,128)(2,1)S(1)}, bf16[80,512]{1,0:T(8,128)(2,1)S(1)}, u32[]{:S(2)}, u32[]{:S(2)}) collective-permute-start(bf16[80,512]{1,0:T(8,128)(2,1)S(1)} %collective-permute-done.1.near_second), channel_id=1, source_target_pairs={{0,4},{4,0},{8,12},{12,8},{1,5},{5,1},{9,13},{13,9},{2,6},{6,2},{1... | collective-permute-start | bytes 245768 | tf_op jit(solution)/shard_map/ppermute | solution.py:174
  9.1 1.6 %prepare.1 = (bf16[4,512,256]{2,1,0:T(8,128)(2,1)S(1)}, f32[128,256]{1,0:T(8,128)S(1)}) custom-call(s32[4,8]{1,0:T(4,128)} %kept.3, s32[2,8]{1,0:T(2,128)} %bitcast.1, bf16[1024,256]{1,0:T(8,128)(2,1)} %integrals.1, bf16[128,512]{1,0:T(8,128)(2,1)S(1)} %get-tuple-element.16.own), custom_call_target="tpu_custom_call" | custom-call | flops 1150000000 | bytes 1024 | tf_op jit(solution)/shard_map/prepare/pallas_call | solution.py:209
  10.7 0.1 collective-permute-done.2.far_first
  10.9 0.0 collective-permute-done.pair
  10.9 0.3 %early.1 = f32[4,128,256]{2,1,0:T(8,128)S(1)} custom-call(f32[128,256]{1,0:T(8,128)S(1)} %get-tuple-element.17.product, bf16[4,512,256]{2,1,0:T(8,128)(2,1)S(1)} %get-tuple-element.18.gathered, bf16[128,512]{1,0:T(8,128)(2,1)S(1)} %collective-permute-done.pair, bf16[80,512]{1,0:T(8,128)(2,1)S(1)} %collective-permute-done.1.near_second, ...), custom_call_target="tpu_custom_call" | custom-call | bytes 1024 | tf_op jit(solution)/shard_map/early/pallas_call | solution.py:227
  11.1 0.0 collective-permute-done.3.near_first
  11.1 2.5 %collective-permute-done.4.far_second = bf16[80,512]{1,0:T(8,128)(2,1)S(1)} collective-permute-done((bf16[80,512]{1,0:T(8,128)(2,1)S(1)}, bf16[80,512]{1,0:T(8,128)(2,1)S(1)}, u32[]{:S(2)}, u32[]{:S(2)}) %collective-permute-start.4) | collective-permute-done | bytes 81952 | tf_op jit(solution)/shard_map/ppermute | solution.py:174
  13.6 0.3 %late.1 = (f32[48,256]{1,0:T(8,128)S(1)}, f32[80,256]{1,0:T(8,128)S(1)}, s16[272,128]{1,0:T(8,128)(2,1)S(1)}) custom-call(f32[4,128,256]{2,1,0:T(8,128)S(1)} %early.1, bf16[4,512,256]{2,1,0:T(8,128)(2,1)S(1)} %get-tuple-element.18.gathered, bf16[48,512]{1,0:T(8,128)(2,1)S(1)} %collective-permute-done.3.near_first, ...), custom_call_target="tpu_custom_call" | custom-call | flops 99999997952 | bytes 1024 | tf_op jit(solution)/shard_map/late/pallas_call | solution.py:227
  13.9 2.4 %collective-permute-start.5 = (s16[272,128]{1,0:T(8,128)(2,1)S(1)}, s16[272,128]{1,0:T(8,128)(2,1)S(1)}, u32[]{:S(2)}, u32[]{:S(2)}) collective-permute-start(s16[272,128]{1,0:T(8,128)(2,1)S(1)} %get-tuple-element.24), channel_id=1, source_target_pairs={{0,3},{1,2},{2,0},{3,1},{4,7},{5,6},{6,4},{7,5},{8,11},{9,10},{10,... | collective-permute-start | bytes 208904 | tf_op jit(solution)/shard_map/ppermute | solution.py:249
  16.3 0.0 copy-start
  16.3 0.1 rest.1
  16.4 0.1 collective-permute-start.6
  16.5 0.7 %collective-permute-start.7 = (s16[272,128]{1,0:T(8,128)(2,1)S(1)}, s16[272,128]{1,0:T(8,128)(2,1)S(1)}, u32[]{:S(2)}, u32[]{:S(2)}) collective-permute-start(s16[272,128]{1,0:T(8,128)(2,1)S(1)} %get-tuple-element.26), channel_id=1, source_target_pairs={{0,1},{1,0},{2,3},{3,2},{4,5},{5,4},{6,7},{7,6},{8,9},{9,8},{10,11... | collective-permute-start | bytes 208904 | tf_op jit(solution)/shard_map/ppermute | solution.py:174
  17.1 0.8 %collective-permute-done.5.one_far = s16[272,128]{1,0:T(8,128)(2,1)S(1)} collective-permute-done((s16[272,128]{1,0:T(8,128)(2,1)S(1)}, s16[272,128]{1,0:T(8,128)(2,1)S(1)}, u32[]{:S(2)}, u32[]{:S(2)}) %collective-permute-start.5) | collective-permute-done | bytes 69664 | tf_op jit(solution)/shard_map/ppermute | solution.py:249
  17.9 0.0 copy-done
  17.9 2.3 %collective-permute-done.6.other_far = s16[272,128]{1,0:T(8,128)(2,1)S(1)} collective-permute-done((s16[272,128]{1,0:T(8,128)(2,1)S(1)}, s16[272,128]{1,0:T(8,128)(2,1)S(1)}, u32[]{:S(2)}, u32[]{:S(2)}) %collective-permute-start.6) | collective-permute-done | bytes 69664 | tf_op jit(solution)/shard_map/ppermute | solution.py:249
  20.2 0.0 collective-permute-done.7.one
  20.2 0.7 %last.1 = f32[128,256]{1,0:T(8,128)} custom-call(f32[128,256]{1,0:T(8,128)S(1)} %first.1.base, s16[272,128]{1,0:T(8,128)(2,1)S(1)} %collective-permute-done.6.other_far, s16[272,128]{1,0:T(8,128)(2,1)S(1)} %collective-permute-done.7.one), custom_call_target="tpu_custom_call" | custom-call | bytes 1024 | tf_op jit(solution)/shard_map/last/pallas_call | solution.py:254
  (1 shorter events, 0.0 us)
Async XLA Ops:
  1.0 5.9 %collective-permute-start.1 = (bf16[80,512]{1,0:T(8,128)(2,1)S(1)}, bf16[80,512]{1,0:T(8,128)(2,1)S(1)}, u32[]{:S(2)}, u32[]{:S(2)}) collective-permute-start(bf16[80,512]{1,0:T(8,128)(2,1)S(1)} %get-tuple-element.19), channel_id=1, source_target_pairs={{0,8},{4,12},{8,0},{12,4},{1,9},{5,13},{9,1},{13,5},{2,10},{6,14},... | collective-permute-start | bytes 245768 | tf_op jit(solution)/shard_map/ppermute | solution.py:174
  4.2 6.6 %collective-permute-start = (bf16[128,512]{1,0:T(8,128)(2,1)S(1)}, bf16[128,512]{1,0:T(8,128)(2,1)S(1)}, u32[]{:S(2)}, u32[]{:S(2)}) collective-permute-start(bf16[128,512]{1,0:T(8,128)(2,1)S(1)} %get-tuple-element.16.own), channel_id=1, source_target_pairs={{0,4},{4,0},{8,12},{12,8},{1,5},{5,1},{9,13},{13,9},{2,6},{6,2},{1... | collective-permute-start | bytes 393224 | tf_op jit(solution)/shard_map/ppermute | solution.py:174
  5.5 5.3 %collective-permute-start.2 = (bf16[48,512]{1,0:T(8,128)(2,1)S(1)}, bf16[48,512]{1,0:T(8,128)(2,1)S(1)}, u32[]{:S(2)}, u32[]{:S(2)}) collective-permute-start(bf16[48,512]{1,0:T(8,128)(2,1)S(1)} %get-tuple-element.20), channel_id=1, source_target_pairs={{0,12},{4,8},{8,4},{12,0},{1,13},{5,9},{9,5},{13,1},{2,14},{6,10},... | collective-permute-start | bytes 147464 | tf_op jit(solution)/shard_map/ppermute | solution.py:174
  5.5 5.6 %collective-permute-start.3 = (bf16[48,512]{1,0:T(8,128)(2,1)S(1)}, bf16[48,512]{1,0:T(8,128)(2,1)S(1)}, u32[]{:S(2)}, u32[]{:S(2)}) collective-permute-start(bf16[48,512]{1,0:T(8,128)(2,1)S(1)} %get-tuple-element.20), channel_id=1, source_target_pairs={{0,8},{4,12},{8,0},{12,4},{1,9},{5,13},{9,1},{13,5},{2,10},{6,14},... | collective-permute-start | bytes 147464 | tf_op jit(solution)/shard_map/ppermute | solution.py:174
  6.9 6.7 %collective-permute-start.4 = (bf16[80,512]{1,0:T(8,128)(2,1)S(1)}, bf16[80,512]{1,0:T(8,128)(2,1)S(1)}, u32[]{:S(2)}, u32[]{:S(2)}) collective-permute-start(bf16[80,512]{1,0:T(8,128)(2,1)S(1)} %collective-permute-done.1.near_second), channel_id=1, source_target_pairs={{0,4},{4,0},{8,12},{12,8},{1,5},{5,1},{9,13},{13,9},{2,6},{6,2},{1... | collective-permute-start | bytes 245768 | tf_op jit(solution)/shard_map/ppermute | solution.py:174
  13.9 4.0 %collective-permute-start.5 = (s16[272,128]{1,0:T(8,128)(2,1)S(1)}, s16[272,128]{1,0:T(8,128)(2,1)S(1)}, u32[]{:S(2)}, u32[]{:S(2)}) collective-permute-start(s16[272,128]{1,0:T(8,128)(2,1)S(1)} %get-tuple-element.24), channel_id=1, source_target_pairs={{0,3},{1,2},{2,0},{3,1},{4,7},{5,6},{6,4},{7,5},{8,11},{9,10},{10,... | collective-permute-start | bytes 208904 | tf_op jit(solution)/shard_map/ppermute | solution.py:249
  16.3 1.6 %copy-start = (f32[128,256]{1,0:T(8,128)S(1)}, f32[128,256]{1,0:T(8,128)}, u32[]{:S(2)}) copy-start(f32[128,256]{1,0:T(8,128)} %residual.1) | copy-start | bytes 393220
  16.4 3.8 %collective-permute-start.6 = (s16[272,128]{1,0:T(8,128)(2,1)S(1)}, s16[272,128]{1,0:T(8,128)(2,1)S(1)}, u32[]{:S(2)}, u32[]{:S(2)}) collective-permute-start(s16[272,128]{1,0:T(8,128)(2,1)S(1)} %get-tuple-element.25), channel_id=1, source_target_pairs={{0,2},{1,3},{2,1},{3,0},{4,6},{5,7},{6,5},{7,4},{8,10},{9,11},{10,... | collective-permute-start | bytes 208904 | tf_op jit(solution)/shard_map/ppermute | solution.py:249
  16.5 3.7 %collective-permute-start.7 = (s16[272,128]{1,0:T(8,128)(2,1)S(1)}, s16[272,128]{1,0:T(8,128)(2,1)S(1)}, u32[]{:S(2)}, u32[]{:S(2)}) collective-permute-start(s16[272,128]{1,0:T(8,128)(2,1)S(1)} %get-tuple-element.26), channel_id=1, source_target_pairs={{0,1},{1,0},{2,3},{3,2},{4,5},{5,4},{6,7},{7,6},{8,9},{9,8},{10,11... | collective-permute-start | bytes 208904 | tf_op jit(solution)/shard_map/ppermute | solution.py:174

commit v24 on v23

--- a/solution.py
+++ b/solution.py
@@ -16,7 +16,7 @@
 VMEM = pl.BlockSpec(memory_space=pltpu.VMEM)
 HBM = pl.BlockSpec(memory_space=pltpu.HBM)
 PARAMS = pltpu.CompilerParams(vmem_limit_bytes=8 * 1024 * 1024)
-DIRECT = 48
+DIRECT = 64
 PIECES = 4
 ROWS = 4
 
@@ -219,7 +219,7 @@
             pltpu.SemaphoreType.DMA((PIECES + 2,)),
         ],
         compiler_params=PARAMS,
-        cost_estimate=cost(115 * 10**7),
+        cost_estimate=cost(10**9),
         name="prepare",
     )(doubles_kept, integral_kept, integrals, packed)
 

time: 21.1 us -> 21.2 us (level)
  no operation moved by 1% of the time
where the time goes in v24:
time: 21.2 us; the launch traced here: 21.1 us
  starting transfers between devices  11.2 us (53%)
  waiting for transfers between devices  5.81 us (27%)
  Pallas kernels  4.03 us (19%)
    ppermute x6, starting transfers between devices, swap(): return lax.ppermute(x, axis, [(i, i ^ step) for i in range(ROWS)])  8.69 us
    ppermute x2, waiting for transfers between devices, local_few(): lax.ppermute(x, 'cols', [(col, col ^ far_steps(col)[i]) for col in range(...  3.04 us
    ppermute x6, waiting for transfers between devices, swap(): return lax.ppermute(x, axis, [(i, i ^ step) for i in range(ROWS)])  2.77 us
    ppermute x2, starting transfers between devices, local_few(): lax.ppermute(x, 'cols', [(col, col ^ far_steps(col)[i]) for col in range(...  2.47 us
    pallas_call x1, Pallas kernels, local_few(): pl.pallas_call(functools.partial(prepare_kernel, tiles, slots), out_shape...  1.64 us
    pallas_call x1, Pallas kernels, local_few(): pl.pallas_call(functools.partial(pack_kernel, tiles, slots), out_shape=[j...  1.01 us
    pallas_call x1, Pallas kernels, local_few(): pl.pallas_call(last_kernel, out_shape=sums_shape, in_specs=[VMEM] * 3, ou...  0.7 us
    pallas_call x4, Pallas kernels, on_vmem(): pl.pallas_call(kernel, out_shape=out_shape, in_specs=[VMEM] * len(args),...  0.67 us
  transfers between devices with their start and end apart: 8, of which 4 were waited for; matrix products, arithmetic and copies ran while one was open for 0% of the time, Pallas kernels for 10%

profile of v24, /device:TPU:1, one launch (start us, length us, event | category | flops | bytes accessed | tf_op | source)
XLA Modules:
  0.0 21.1 jit_solution(14809990367776673835)
XLA Ops:
  0.0 1.0 %pack.1 = (bf16[128,512]{1,0:T(8,128)(2,1)S(1)}, bf16[64,512]{1,0:T(8,128)(2,1)S(1)}, bf16[64,512]{1,0:T(8,128)(2,1)S(1)}) custom-call(s32[4,8]{1,0:T(4,128)} %kept.3, bf16[128,1024]{1,0:T(8,128)(2,1)} %doubles.1), custom_call_target="tpu_custom_call" | custom-call | tf_op jit(solution)/shard_map/pack/pallas_call | solution.py:190
  1.0 3.2 %collective-permute-start.1 = (bf16[64,512]{1,0:T(8,128)(2,1)S(1)}, bf16[64,512]{1,0:T(8,128)(2,1)S(1)}, u32[]{:S(2)}, u32[]{:S(2)}) collective-permute-start(bf16[64,512]{1,0:T(8,128)(2,1)S(1)} %get-tuple-element.19), channel_id=1, source_target_pairs={{0,8},{4,12},{8,0},{12,4},{1,9},{5,13},{9,1},{13,5},{2,10},{6,14},... | collective-permute-start | bytes 196616 | tf_op jit(solution)/shard_map/ppermute | solution.py:174
  4.2 1.3 %collective-permute-start = (bf16[128,512]{1,0:T(8,128)(2,1)S(1)}, bf16[128,512]{1,0:T(8,128)(2,1)S(1)}, u32[]{:S(2)}, u32[]{:S(2)}) collective-permute-start(bf16[128,512]{1,0:T(8,128)(2,1)S(1)} %get-tuple-element.16.own), channel_id=1, source_target_pairs={{0,4},{4,0},{8,12},{12,8},{1,5},{5,1},{9,13},{13,9},{2,6},{6,2},{1... | collective-permute-start | bytes 393224 | tf_op jit(solution)/shard_map/ppermute | solution.py:174
  5.5 0.0 collective-permute-start.2
  5.5 1.3 %collective-permute-start.3 = (bf16[64,512]{1,0:T(8,128)(2,1)S(1)}, bf16[64,512]{1,0:T(8,128)(2,1)S(1)}, u32[]{:S(2)}, u32[]{:S(2)}) collective-permute-start(bf16[64,512]{1,0:T(8,128)(2,1)S(1)} %get-tuple-element.20), channel_id=1, source_target_pairs={{0,8},{4,12},{8,0},{12,4},{1,9},{5,13},{9,1},{13,5},{2,10},{6,14},... | collective-permute-start | bytes 196616 | tf_op jit(solution)/shard_map/ppermute | solution.py:174
  6.9 0.0 collective-permute-done.1.near_second
  6.9 2.2 %collective-permute-start.4 = (bf16[64,512]{1,0:T(8,128)(2,1)S(1)}, bf16[64,512]{1,0:T(8,128)(2,1)S(1)}, u32[]{:S(2)}, u32[]{:S(2)}) collective-permute-start(bf16[64,512]{1,0:T(8,128)(2,1)S(1)} %collective-permute-done.1.near_second), channel_id=1, source_target_pairs={{0,4},{4,0},{8,12},{12,8},{1,5},{5,1},{9,13},{13,9},{2,6},{6,2},{1... | collective-permute-start | bytes 196616 | tf_op jit(solution)/shard_map/ppermute | solution.py:174
  9.1 1.6 %prepare.1 = (bf16[4,512,256]{2,1,0:T(8,128)(2,1)S(1)}, f32[128,256]{1,0:T(8,128)S(1)}) custom-call(s32[4,8]{1,0:T(4,128)} %kept.3, s32[2,8]{1,0:T(2,128)} %bitcast.1, bf16[1024,256]{1,0:T(8,128)(2,1)} %integrals.1, bf16[128,512]{1,0:T(8,128)(2,1)S(1)} %get-tuple-element.16.own), custom_call_target="tpu_custom_call" | custom-call | flops 1000000000 | bytes 1024 | tf_op jit(solution)/shard_map/prepare/pallas_call | solution.py:209
  10.7 0.6 %collective-permute-done.2.far_first = bf16[64,512]{1,0:T(8,128)(2,1)S(1)} collective-permute-done((bf16[64,512]{1,0:T(8,128)(2,1)S(1)}, bf16[64,512]{1,0:T(8,128)(2,1)S(1)}, u32[]{:S(2)}, u32[]{:S(2)}) %collective-permute-start.2) | collective-permute-done | bytes 65568 | tf_op jit(solution)/shard_map/ppermute | solution.py:174
  11.3 0.0 collective-permute-done.pair
  11.3 0.3 %early.1 = f32[4,128,256]{2,1,0:T(8,128)S(1)} custom-call(f32[128,256]{1,0:T(8,128)S(1)} %get-tuple-element.17.product, bf16[4,512,256]{2,1,0:T(8,128)(2,1)S(1)} %get-tuple-element.18.gathered, bf16[128,512]{1,0:T(8,128)(2,1)S(1)} %collective-permute-done.pair, bf16[64,512]{1,0:T(8,128)(2,1)S(1)} %collective-permute-done.1.near_second, ...), custom_call_target="tpu_custom_call" | custom-call | bytes 1024 | tf_op jit(solution)/shard_map/early/pallas_call | solution.py:227
  11.5 0.0 collective-permute-done.3.near_first
  11.6 2.2 %collective-permute-done.4.far_second = bf16[64,512]{1,0:T(8,128)(2,1)S(1)} collective-permute-done((bf16[64,512]{1,0:T(8,128)(2,1)S(1)}, bf16[64,512]{1,0:T(8,128)(2,1)S(1)}, u32[]{:S(2)}, u32[]{:S(2)}) %collective-permute-start.4) | collective-permute-done | bytes 65568 | tf_op jit(solution)/shard_map/ppermute | solution.py:174
  13.8 0.3 %late.1 = (f32[64,256]{1,0:T(8,128)S(1)}, f32[64,256]{1,0:T(8,128)S(1)}, s16[272,128]{1,0:T(8,128)(2,1)S(1)}) custom-call(f32[4,128,256]{2,1,0:T(8,128)S(1)} %early.1, bf16[4,512,256]{2,1,0:T(8,128)(2,1)S(1)} %get-tuple-element.18.gathered, bf16[64,512]{1,0:T(8,128)(2,1)S(1)} %collective-permute-done.3.near_first, ...), custom_call_target="tpu_custom_call" | custom-call | flops 99999997952 | bytes 1024 | tf_op jit(solution)/shard_map/late/pallas_call | solution.py:227
  14.0 2.4 %collective-permute-start.5 = (s16[272,128]{1,0:T(8,128)(2,1)S(1)}, s16[272,128]{1,0:T(8,128)(2,1)S(1)}, u32[]{:S(2)}, u32[]{:S(2)}) collective-permute-start(s16[272,128]{1,0:T(8,128)(2,1)S(1)} %get-tuple-element.24), channel_id=1, source_target_pairs={{0,3},{1,2},{2,0},{3,1},{4,7},{5,6},{6,4},{7,5},{8,11},{9,10},{10,... | collective-permute-start | bytes 208904 | tf_op jit(solution)/shard_map/ppermute | solution.py:249
  16.4 0.0 copy-start
  16.4 0.1 rest.1
  16.6 0.1 collective-permute-start.6
  16.6 0.6 %collective-permute-start.7 = (s16[272,128]{1,0:T(8,128)(2,1)S(1)}, s16[272,128]{1,0:T(8,128)(2,1)S(1)}, u32[]{:S(2)}, u32[]{:S(2)}) collective-permute-start(s16[272,128]{1,0:T(8,128)(2,1)S(1)} %get-tuple-element.26), channel_id=1, source_target_pairs={{0,1},{1,0},{2,3},{3,2},{4,5},{5,4},{6,7},{7,6},{8,9},{9,8},{10,11... | collective-permute-start | bytes 208904 | tf_op jit(solution)/shard_map/ppermute | solution.py:174
  17.3 0.6 %collective-permute-done.5.one_far = s16[272,128]{1,0:T(8,128)(2,1)S(1)} collective-permute-done((s16[272,128]{1,0:T(8,128)(2,1)S(1)}, s16[272,128]{1,0:T(8,128)(2,1)S(1)}, u32[]{:S(2)}, u32[]{:S(2)}) %collective-permute-start.5) | collective-permute-done | bytes 69664 | tf_op jit(solution)/shard_map/ppermute | solution.py:249
  17.9 0.0 copy-done
  17.9 2.4 %collective-permute-done.6.other_far = s16[272,128]{1,0:T(8,128)(2,1)S(1)} collective-permute-done((s16[272,128]{1,0:T(8,128)(2,1)S(1)}, s16[272,128]{1,0:T(8,128)(2,1)S(1)}, u32[]{:S(2)}, u32[]{:S(2)}) %collective-permute-start.6) | collective-permute-done | bytes 69664 | tf_op jit(solution)/shard_map/ppermute | solution.py:249
  20.4 0.0 collective-permute-done.7.one
  20.4 0.7 %last.1 = f32[128,256]{1,0:T(8,128)} custom-call(f32[128,256]{1,0:T(8,128)S(1)} %first.1.base, s16[272,128]{1,0:T(8,128)(2,1)S(1)} %collective-permute-done.6.other_far, s16[272,128]{1,0:T(8,128)(2,1)S(1)} %collective-permute-done.7.one), custom_call_target="tpu_custom_call" | custom-call | bytes 1024 | tf_op jit(solution)/shard_map/last/pallas_call | solution.py:254
  (1 shorter events, 0.0 us)
Async XLA Ops:
  1.0 5.9 %collective-permute-start.1 = (bf16[64,512]{1,0:T(8,128)(2,1)S(1)}, bf16[64,512]{1,0:T(8,128)(2,1)S(1)}, u32[]{:S(2)}, u32[]{:S(2)}) collective-permute-start(bf16[64,512]{1,0:T(8,128)(2,1)S(1)} %get-tuple-element.19), channel_id=1, source_target_pairs={{0,8},{4,12},{8,0},{12,4},{1,9},{5,13},{9,1},{13,5},{2,10},{6,14},... | collective-permute-start | bytes 196616 | tf_op jit(solution)/shard_map/ppermute | solution.py:174
  4.2 7.1 %collective-permute-start = (bf16[128,512]{1,0:T(8,128)(2,1)S(1)}, bf16[128,512]{1,0:T(8,128)(2,1)S(1)}, u32[]{:S(2)}, u32[]{:S(2)}) collective-permute-start(bf16[128,512]{1,0:T(8,128)(2,1)S(1)} %get-tuple-element.16.own), channel_id=1, source_target_pairs={{0,4},{4,0},{8,12},{12,8},{1,5},{5,1},{9,13},{13,9},{2,6},{6,2},{1... | collective-permute-start | bytes 393224 | tf_op jit(solution)/shard_map/ppermute | solution.py:174
  5.5 5.8 %collective-permute-start.2 = (bf16[64,512]{1,0:T(8,128)(2,1)S(1)}, bf16[64,512]{1,0:T(8,128)(2,1)S(1)}, u32[]{:S(2)}, u32[]{:S(2)}) collective-permute-start(bf16[64,512]{1,0:T(8,128)(2,1)S(1)} %get-tuple-element.20), channel_id=1, source_target_pairs={{0,12},{4,8},{8,4},{12,0},{1,13},{5,9},{9,5},{13,1},{2,14},{6,10},... | collective-permute-start | bytes 196616 | tf_op jit(solution)/shard_map/ppermute | solution.py:174
  5.5 6.0 %collective-permute-start.3 = (bf16[64,512]{1,0:T(8,128)(2,1)S(1)}, bf16[64,512]{1,0:T(8,128)(2,1)S(1)}, u32[]{:S(2)}, u32[]{:S(2)}) collective-permute-start(bf16[64,512]{1,0:T(8,128)(2,1)S(1)} %get-tuple-element.20), channel_id=1, source_target_pairs={{0,8},{4,12},{8,0},{12,4},{1,9},{5,13},{9,1},{13,5},{2,10},{6,14},... | collective-permute-start | bytes 196616 | tf_op jit(solution)/shard_map/ppermute | solution.py:174
  6.9 6.9 %collective-permute-start.4 = (bf16[64,512]{1,0:T(8,128)(2,1)S(1)}, bf16[64,512]{1,0:T(8,128)(2,1)S(1)}, u32[]{:S(2)}, u32[]{:S(2)}) collective-permute-start(bf16[64,512]{1,0:T(8,128)(2,1)S(1)} %collective-permute-done.1.near_second), channel_id=1, source_target_pairs={{0,4},{4,0},{8,12},{12,8},{1,5},{5,1},{9,13},{13,9},{2,6},{6,2},{1... | collective-permute-start | bytes 196616 | tf_op jit(solution)/shard_map/ppermute | solution.py:174
  14.0 3.9 %collective-permute-start.5 = (s16[272,128]{1,0:T(8,128)(2,1)S(1)}, s16[272,128]{1,0:T(8,128)(2,1)S(1)}, u32[]{:S(2)}, u32[]{:S(2)}) collective-permute-start(s16[272,128]{1,0:T(8,128)(2,1)S(1)} %get-tuple-element.24), channel_id=1, source_target_pairs={{0,3},{1,2},{2,0},{3,1},{4,7},{5,6},{6,4},{7,5},{8,11},{9,10},{10,... | collective-permute-start | bytes 208904 | tf_op jit(solution)/shard_map/ppermute | solution.py:249
  16.4 1.5 %copy-start = (f32[128,256]{1,0:T(8,128)S(1)}, f32[128,256]{1,0:T(8,128)}, u32[]{:S(2)}) copy-start(f32[128,256]{1,0:T(8,128)} %residual.1) | copy-start | bytes 393220
  16.6 3.8 %collective-permute-start.6 = (s16[272,128]{1,0:T(8,128)(2,1)S(1)}, s16[272,128]{1,0:T(8,128)(2,1)S(1)}, u32[]{:S(2)}, u32[]{:S(2)}) collective-permute-start(s16[272,128]{1,0:T(8,128)(2,1)S(1)} %get-tuple-element.25), channel_id=1, source_target_pairs={{0,2},{1,3},{2,1},{3,0},{4,6},{5,7},{6,5},{7,4},{8,10},{9,11},{10,... | collective-permute-start | bytes 208904 | tf_op jit(solution)/shard_map/ppermute | solution.py:249
  16.6 3.7 %collective-permute-start.7 = (s16[272,128]{1,0:T(8,128)(2,1)S(1)}, s16[272,128]{1,0:T(8,128)(2,1)S(1)}, u32[]{:S(2)}, u32[]{:S(2)}) collective-permute-start(s16[272,128]{1,0:T(8,128)(2,1)S(1)} %get-tuple-element.26), channel_id=1, source_target_pairs={{0,1},{1,0},{2,3},{3,2},{4,5},{5,4},{6,7},{7,6},{8,9},{9,8},{10,11... | collective-permute-start | bytes 208904 | tf_op jit(solution)/shard_map/ppermute | solution.py:174

commit v25 on v23

--- a/solution.py
+++ b/solution.py
@@ -113,44 +113,36 @@
     return 3 - col // 2, 2 + col // 2
 
 
-def early_kernel(product, gathered, pair, near_second, far_first, sums):
+def early_kernel(product, gathered, pair, near_second, far_first, near_first, sums):
     mine = place()
     cut = far_first.shape[0]
     sums[mine] = product[...]
     sums[mine ^ 1] = jnp.dot(pair[...], gathered[mine ^ 1], preferred_element_type=jnp.float32)
-    for step, start, block in ((2, cut, near_second), (3, 0, far_first)):
+    for step, start, block in ((2, cut, near_second), (3, 0, far_first), (2, 0, near_first)):
         sums[mine ^ step, start : start + block.shape[0], :] = jnp.dot(
             block[...], gathered[mine ^ step], preferred_element_type=jnp.float32
         )
 
 
-def whole(n, early, near_sums, far_sums, out):
-    cut = near_sums.shape[0]
-    step = place() ^ n
+def whole(n, early, far_sums, out):
     out[...] = early[n]
 
-    @pl.when(step == 2)
+    @pl.when((place() ^ n) == 3)
     def _():
-        out[:cut, :] = near_sums[...]
-
-    @pl.when(step == 3)
-    def _():
-        out[cut:, :] = far_sums[...]
-
-
-def late_kernel(early, gathered, near_first, far_second, near_sums, far_sums, one_far, held):
-    mine = place()
-    near_sums[...] = jnp.dot(near_first[...], gathered[mine ^ 2], preferred_element_type=jnp.float32)
-    far_sums[...] = jnp.dot(far_second[...], gathered[mine ^ 3], preferred_element_type=jnp.float32)
-    whole(far_steps(lax.axis_index("cols"))[0], early, near_sums, far_sums, held)
+        out[out.shape[0] - far_sums.shape[0] :, :] = far_sums[...]
+
+
+def late_kernel(early, gathered, far_second, far_sums, one_far, held):
+    far_sums[...] = jnp.dot(far_second[...], gathered[place() ^ 3], preferred_element_type=jnp.float32)
+    whole(far_steps(lax.axis_index("cols"))[0], early, far_sums, held)
     encode(held[...], one_far)
 
 
-def rest_kernel(early, near_sums, far_sums, one, other_far, kept_sums, held):
+def rest_kernel(early, far_sums, one, other_far, kept_sums, held):
     for n, out in ((far_steps(lax.axis_index("cols"))[1], other_far), (1, one)):
-        whole(n, early, near_sums, far_sums, held)
+        whole(n, early, far_sums, held)
         encode(held[...], out)
-    whole(0, early, near_sums, far_sums, kept_sums)
+    whole(0, early, far_sums, kept_sums)
 
 
 def first_kernel(residual, kept_sums, one_far, out):
@@ -236,14 +228,14 @@
         )(*args)
 
     held = [pltpu.VMEM((pairs, width), jnp.float32)]
-    part_sums = [jax.ShapeDtypeStruct((rows, width), jnp.float32) for rows in parts]
+    late_sums = jax.ShapeDtypeStruct((parts[1], width), jnp.float32)
     all_sums = jax.ShapeDtypeStruct((ROWS, pairs, width), jnp.float32)
-    early = on_vmem(early_kernel, "early", 0, all_sums, product, gathered, pair, near_second, far_first)
-    near_sums, far_sums, one_far = on_vmem(
-        late_kernel, "late", 10**11, part_sums + [message], early, gathered, near_first, far_second, scratch=held
+    early = on_vmem(early_kernel, "early", 0, all_sums, product, gathered, pair, near_second, far_first, near_first)
+    far_sums, one_far = on_vmem(
+        late_kernel, "late", 10**11, [late_sums, message], early, gathered, far_second, scratch=held
     )
     one, other_far, kept_sums = on_vmem(
-        rest_kernel, "rest", 0, [message] * 2 + [sums_shape], early, near_sums, far_sums, scratch=held
+        rest_kernel, "rest", 0, [message] * 2 + [sums_shape], early, far_sums, scratch=held
     )
     one_far, other_far = (
         lax.ppermute(x, "cols", [(col, col ^ far_steps(col)[i]) for col in range(ROWS)])

time: 21.1 us -> 21 us (level)
  transfers between devices with their start and end apart: 8 -> 8, of which waited for: 4 -> 5; matrix products, arithmetic and copies ran while one was open for 0% -> 0% of each run, Pallas kernels for 10% -> 10%
where the time goes in v25:
time: 21 us; the launch traced here: 20.9 us
  starting transfers between devices  11.2 us (53%)
  waiting for transfers between devices  5.63 us (27%)
  Pallas kernels  4 us (19%)
    ppermute x6, starting transfers between devices, swap(): return lax.ppermute(x, axis, [(i, i ^ step) for i in range(ROWS)])  8.71 us
    ppermute x2, waiting for transfers between devices, local_few(): lax.ppermute(x, 'cols', [(col, col ^ far_steps(col)[i]) for col in range(...  3.03 us
    ppermute x6, waiting for transfers between devices, swap(): return lax.ppermute(x, axis, [(i, i ^ step) for i in range(ROWS)])  2.6 us
    ppermute x2, starting transfers between devices, local_few(): lax.ppermute(x, 'cols', [(col, col ^ far_steps(col)[i]) for col in range(...  2.45 us
    pallas_call x1, Pallas kernels, local_few(): pl.pallas_call(functools.partial(prepare_kernel, tiles, slots), out_shape...  1.64 us
    pallas_call x1, Pallas kernels, local_few(): pl.pallas_call(functools.partial(pack_kernel, tiles, slots), out_shape=[j...  1.01 us
    pallas_call x1, Pallas kernels, local_few(): pl.pallas_call(last_kernel, out_shape=sums_shape, in_specs=[VMEM] * 3, ou...  0.7 us
    pallas_call x4, Pallas kernels, on_vmem(): pl.pallas_call(kernel, out_shape=out_shape, in_specs=[VMEM] * len(args),...  0.64 us
  transfers between devices with their start and end apart: 8, of which 5 were waited for; matrix products, arithmetic and copies ran while one was open for 0% of the time, Pallas kernels for 10%

profile of v25, /device:TPU:1, one launch (start us, length us, event | category | flops | bytes accessed | tf_op | source)
XLA Modules:
  0.0 20.9 jit_solution(18212801469483377674)
XLA Ops:
  0.0 1.0 %pack.1 = (bf16[128,512]{1,0:T(8,128)(2,1)S(1)}, bf16[48,512]{1,0:T(8,128)(2,1)S(1)}, bf16[80,512]{1,0:T(8,128)(2,1)S(1)}) custom-call(s32[4,8]{1,0:T(4,128)} %kept.3, bf16[128,1024]{1,0:T(8,128)(2,1)} %doubles.1), custom_call_target="tpu_custom_call" | custom-call | tf_op jit(solution)/shard_map/pack/pallas_call | solution.py:182
  1.0 3.2 %collective-permute-start.1 = (bf16[80,512]{1,0:T(8,128)(2,1)S(1)}, bf16[80,512]{1,0:T(8,128)(2,1)S(1)}, u32[]{:S(2)}, u32[]{:S(2)}) collective-permute-start(bf16[80,512]{1,0:T(8,128)(2,1)S(1)} %get-tuple-element.18), channel_id=1, source_target_pairs={{0,8},{4,12},{8,0},{12,4},{1,9},{5,13},{9,1},{13,5},{2,10},{6,14},... | collective-permute-start | bytes 245768 | tf_op jit(solution)/shard_map/ppermute | solution.py:166
  4.2 1.3 %collective-permute-start = (bf16[128,512]{1,0:T(8,128)(2,1)S(1)}, bf16[128,512]{1,0:T(8,128)(2,1)S(1)}, u32[]{:S(2)}, u32[]{:S(2)}) collective-permute-start(bf16[128,512]{1,0:T(8,128)(2,1)S(1)} %get-tuple-element.15.own), channel_id=1, source_target_pairs={{0,4},{4,0},{8,12},{12,8},{1,5},{5,1},{9,13},{13,9},{2,6},{6,2},{1... | collective-permute-start | bytes 393224 | tf_op jit(solution)/shard_map/ppermute | solution.py:166
  5.5 0.0 collective-permute-start.2
  5.5 1.3 %collective-permute-start.3 = (bf16[48,512]{1,0:T(8,128)(2,1)S(1)}, bf16[48,512]{1,0:T(8,128)(2,1)S(1)}, u32[]{:S(2)}, u32[]{:S(2)}) collective-permute-start(bf16[48,512]{1,0:T(8,128)(2,1)S(1)} %get-tuple-element.19), channel_id=1, source_target_pairs={{0,8},{4,12},{8,0},{12,4},{1,9},{5,13},{9,1},{13,5},{2,10},{6,14},... | collective-permute-start | bytes 147464 | tf_op jit(solution)/shard_map/ppermute | solution.py:166
  6.9 0.0 collective-permute-done.1.near_second
  6.9 2.2 %collective-permute-start.4 = (bf16[80,512]{1,0:T(8,128)(2,1)S(1)}, bf16[80,512]{1,0:T(8,128)(2,1)S(1)}, u32[]{:S(2)}, u32[]{:S(2)}) collective-permute-start(bf16[80,512]{1,0:T(8,128)(2,1)S(1)} %collective-permute-done.1.near_second), channel_id=1, source_target_pairs={{0,4},{4,0},{8,12},{12,8},{1,5},{5,1},{9,13},{13,9},{2,6},{6,2},{1... | collective-permute-start | bytes 245768 | tf_op jit(solution)/shard_map/ppermute | solution.py:166
  9.1 1.6 %prepare.1 = (bf16[4,512,256]{2,1,0:T(8,128)(2,1)S(1)}, f32[128,256]{1,0:T(8,128)S(1)}) custom-call(s32[4,8]{1,0:T(4,128)} %kept.3, s32[2,8]{1,0:T(2,128)} %bitcast.1, bf16[1024,256]{1,0:T(8,128)(2,1)} %integrals.1, bf16[128,512]{1,0:T(8,128)(2,1)S(1)} %get-tuple-element.15.own), custom_call_target="tpu_custom_call" | custom-call | flops 1150000000 | bytes 1024 | tf_op jit(solution)/shard_map/prepare/pallas_call | solution.py:201
  10.7 0.1 collective-permute-done.2.far_first
  10.9 0.1 collective-permute-done.3.near_first
  10.9 0.0 collective-permute-done.pair
  10.9 0.3 %early.1 = f32[4,128,256]{2,1,0:T(8,128)S(1)} custom-call(f32[128,256]{1,0:T(8,128)S(1)} %get-tuple-element.16.product, bf16[4,512,256]{2,1,0:T(8,128)(2,1)S(1)} %get-tuple-element.17.gathered, bf16[128,512]{1,0:T(8,128)(2,1)S(1)} %collective-permute-done.pair, bf16[80,512]{1,0:T(8,128)(2,1)S(1)} %collective-permute-done.1.near_second, ...), custom_call_target="tpu_custom_call" | custom-call | bytes 1024 | tf_op jit(solution)/shard_map/early/pallas_call | solution.py:219
  11.2 2.4 %collective-permute-done.4.far_second = bf16[80,512]{1,0:T(8,128)(2,1)S(1)} collective-permute-done((bf16[80,512]{1,0:T(8,128)(2,1)S(1)}, bf16[80,512]{1,0:T(8,128)(2,1)S(1)}, u32[]{:S(2)}, u32[]{:S(2)}) %collective-permute-start.4) | collective-permute-done | bytes 81952 | tf_op jit(solution)/shard_map/ppermute | solution.py:166
  13.6 0.2 %late.1 = (f32[80,256]{1,0:T(8,128)S(1)}, s16[272,128]{1,0:T(8,128)(2,1)S(1)}) custom-call(f32[4,128,256]{2,1,0:T(8,128)S(1)} %early.1, bf16[4,512,256]{2,1,0:T(8,128)(2,1)S(1)} %get-tuple-element.17.gathered, bf16[80,512]{1,0:T(8,128)(2,1)S(1)} %collective-permute-done.4.far_second), custom_call_target="tpu_custom_call" | custom-call | flops 99999997952 | bytes 1024 | tf_op jit(solution)/shard_map/late/pallas_call | solution.py:219
  13.8 2.4 %collective-permute-start.5 = (s16[272,128]{1,0:T(8,128)(2,1)S(1)}, s16[272,128]{1,0:T(8,128)(2,1)S(1)}, u32[]{:S(2)}, u32[]{:S(2)}) collective-permute-start(s16[272,128]{1,0:T(8,128)(2,1)S(1)} %get-tuple-element.22), channel_id=1, source_target_pairs={{0,3},{1,2},{2,0},{3,1},{4,7},{5,6},{6,4},{7,5},{8,11},{9,10},{10,... | collective-permute-start | bytes 208904 | tf_op jit(solution)/shard_map/ppermute | solution.py:241
  16.2 0.0 copy-start
  16.2 0.1 rest.1
  16.4 0.1 collective-permute-start.6
  16.4 0.7 %collective-permute-start.7 = (s16[272,128]{1,0:T(8,128)(2,1)S(1)}, s16[272,128]{1,0:T(8,128)(2,1)S(1)}, u32[]{:S(2)}, u32[]{:S(2)}) collective-permute-start(s16[272,128]{1,0:T(8,128)(2,1)S(1)} %get-tuple-element.24), channel_id=1, source_target_pairs={{0,1},{1,0},{2,3},{3,2},{4,5},{5,4},{6,7},{7,6},{8,9},{9,8},{10,11... | collective-permute-start | bytes 208904 | tf_op jit(solution)/shard_map/ppermute | solution.py:166
  17.1 0.8 %collective-permute-done.5.one_far = s16[272,128]{1,0:T(8,128)(2,1)S(1)} collective-permute-done((s16[272,128]{1,0:T(8,128)(2,1)S(1)}, s16[272,128]{1,0:T(8,128)(2,1)S(1)}, u32[]{:S(2)}, u32[]{:S(2)}) %collective-permute-start.5) | collective-permute-done | bytes 69664 | tf_op jit(solution)/shard_map/ppermute | solution.py:241
  17.9 0.0 copy-done
  17.9 2.3 %collective-permute-done.6.other_far = s16[272,128]{1,0:T(8,128)(2,1)S(1)} collective-permute-done((s16[272,128]{1,0:T(8,128)(2,1)S(1)}, s16[272,128]{1,0:T(8,128)(2,1)S(1)}, u32[]{:S(2)}, u32[]{:S(2)}) %collective-permute-start.6) | collective-permute-done | bytes 69664 | tf_op jit(solution)/shard_map/ppermute | solution.py:241
  20.1 0.0 collective-permute-done.7.one
  20.1 0.7 %last.1 = f32[128,256]{1,0:T(8,128)} custom-call(f32[128,256]{1,0:T(8,128)S(1)} %first.1.base, s16[272,128]{1,0:T(8,128)(2,1)S(1)} %collective-permute-done.6.other_far, s16[272,128]{1,0:T(8,128)(2,1)S(1)} %collective-permute-done.7.one), custom_call_target="tpu_custom_call" | custom-call | bytes 1024 | tf_op jit(solution)/shard_map/last/pallas_call | solution.py:246
  (1 shorter events, 0.0 us)
Async XLA Ops:
  1.0 5.9 %collective-permute-start.1 = (bf16[80,512]{1,0:T(8,128)(2,1)S(1)}, bf16[80,512]{1,0:T(8,128)(2,1)S(1)}, u32[]{:S(2)}, u32[]{:S(2)}) collective-permute-start(bf16[80,512]{1,0:T(8,128)(2,1)S(1)} %get-tuple-element.18), channel_id=1, source_target_pairs={{0,8},{4,12},{8,0},{12,4},{1,9},{5,13},{9,1},{13,5},{2,10},{6,14},... | collective-permute-start | bytes 245768 | tf_op jit(solution)/shard_map/ppermute | solution.py:166
  4.2 6.7 %collective-permute-start = (bf16[128,512]{1,0:T(8,128)(2,1)S(1)}, bf16[128,512]{1,0:T(8,128)(2,1)S(1)}, u32[]{:S(2)}, u32[]{:S(2)}) collective-permute-start(bf16[128,512]{1,0:T(8,128)(2,1)S(1)} %get-tuple-element.15.own), channel_id=1, source_target_pairs={{0,4},{4,0},{8,12},{12,8},{1,5},{5,1},{9,13},{13,9},{2,6},{6,2},{1... | collective-permute-start | bytes 393224 | tf_op jit(solution)/shard_map/ppermute | solution.py:166
  5.5 5.3 %collective-permute-start.2 = (bf16[48,512]{1,0:T(8,128)(2,1)S(1)}, bf16[48,512]{1,0:T(8,128)(2,1)S(1)}, u32[]{:S(2)}, u32[]{:S(2)}) collective-permute-start(bf16[48,512]{1,0:T(8,128)(2,1)S(1)} %get-tuple-element.19), channel_id=1, source_target_pairs={{0,12},{4,8},{8,4},{12,0},{1,13},{5,9},{9,5},{13,1},{2,14},{6,10},... | collective-permute-start | bytes 147464 | tf_op jit(solution)/shard_map/ppermute | solution.py:166
  5.5 5.4 %collective-permute-start.3 = (bf16[48,512]{1,0:T(8,128)(2,1)S(1)}, bf16[48,512]{1,0:T(8,128)(2,1)S(1)}, u32[]{:S(2)}, u32[]{:S(2)}) collective-permute-start(bf16[48,512]{1,0:T(8,128)(2,1)S(1)} %get-tuple-element.19), channel_id=1, source_target_pairs={{0,8},{4,12},{8,0},{12,4},{1,9},{5,13},{9,1},{13,5},{2,10},{6,14},... | collective-permute-start | bytes 147464 | tf_op jit(solution)/shard_map/ppermute | solution.py:166
  6.9 6.7 %collective-permute-start.4 = (bf16[80,512]{1,0:T(8,128)(2,1)S(1)}, bf16[80,512]{1,0:T(8,128)(2,1)S(1)}, u32[]{:S(2)}, u32[]{:S(2)}) collective-permute-start(bf16[80,512]{1,0:T(8,128)(2,1)S(1)} %collective-permute-done.1.near_second), channel_id=1, source_target_pairs={{0,4},{4,0},{8,12},{12,8},{1,5},{5,1},{9,13},{13,9},{2,6},{6,2},{1... | collective-permute-start | bytes 245768 | tf_op jit(solution)/shard_map/ppermute | solution.py:166
  13.8 4.0 %collective-permute-start.5 = (s16[272,128]{1,0:T(8,128)(2,1)S(1)}, s16[272,128]{1,0:T(8,128)(2,1)S(1)}, u32[]{:S(2)}, u32[]{:S(2)}) collective-permute-start(s16[272,128]{1,0:T(8,128)(2,1)S(1)} %get-tuple-element.22), channel_id=1, source_target_pairs={{0,3},{1,2},{2,0},{3,1},{4,7},{5,6},{6,4},{7,5},{8,11},{9,10},{10,... | collective-permute-start | bytes 208904 | tf_op jit(solution)/shard_map/ppermute | solution.py:241
  16.2 1.6 %copy-start = (f32[128,256]{1,0:T(8,128)S(1)}, f32[128,256]{1,0:T(8,128)}, u32[]{:S(2)}) copy-start(f32[128,256]{1,0:T(8,128)} %residual.1) | copy-start | bytes 393220
  16.4 3.8 %collective-permute-start.6 = (s16[272,128]{1,0:T(8,128)(2,1)S(1)}, s16[272,128]{1,0:T(8,128)(2,1)S(1)}, u32[]{:S(2)}, u32[]{:S(2)}) collective-permute-start(s16[272,128]{1,0:T(8,128)(2,1)S(1)} %get-tuple-element.23), channel_id=1, source_target_pairs={{0,2},{1,3},{2,1},{3,0},{4,6},{5,7},{6,5},{7,4},{8,10},{9,11},{10,... | collective-permute-start | bytes 208904 | tf_op jit(solution)/shard_map/ppermute | solution.py:241
  16.4 3.7 %collective-permute-start.7 = (s16[272,128]{1,0:T(8,128)(2,1)S(1)}, s16[272,128]{1,0:T(8,128)(2,1)S(1)}, u32[]{:S(2)}, u32[]{:S(2)}) collective-permute-start(s16[272,128]{1,0:T(8,128)(2,1)S(1)} %get-tuple-element.24), channel_id=1, source_target_pairs={{0,1},{1,0},{2,3},{3,2},{4,5},{5,4},{6,7},{7,6},{8,9},{9,8},{10,11... | collective-permute-start | bytes 208904 | tf_op jit(solution)/shard_map/ppermute | solution.py:166

commit v26 on v23

--- a/solution.py
+++ b/solution.py
@@ -46,15 +46,17 @@
         copy.start()
     table_copy.wait()
     list_kept(table, lax.axis_index("rows"), tiles, places)
-    for copy in block_copies:
+    cut, size = first.shape[0], block.shape[0] // PIECES
+    tiles_kept = [pl.ds(pl.multiple_of(places[slot] * TILE, TILE), TILE) for slot in range(slots)]
+    for i, copy in enumerate(block_copies):
         copy.wait()
-    cut = first.shape[0]
-    for slot in range(slots):
-        tile = block[:, pl.ds(pl.multiple_of(places[slot] * TILE, TILE), TILE)]
-        to = slice(slot * TILE, (slot + 1) * TILE)
-        packed[:, to] = tile
-        first[:, to] = tile[:cut]
-        second[:, to] = tile[cut:]
+        begin, end = i * size, (i + 1) * size
+        for slot, tile in enumerate(tiles_kept):
+            to = slice(slot * TILE, (slot + 1) * TILE)
+            for target, low, high in ((packed, 0, block.shape[0]), (first, 0, cut), (second, cut, block.shape[0])):
+                start, stop = max(begin, low), min(end, high)
+                if start < stop:
+                    target[start - low : stop - low, to] = block[start:stop, tile]
 
 
 def prepare_kernel(tiles, slots, kept, int_kept, integrals, own, gathered, product, table, int_table, held, places, sems):

time: 21.1 us -> 21 us (level)
  no operation moved by 1% of the time
where the time goes in v26:
time: 21 us; the launch traced here: 20.9 us
  starting transfers between devices  11.2 us (53%)
  waiting for transfers between devices  5.64 us (27%)
  Pallas kernels  3.99 us (19%)
    ppermute x6, starting transfers between devices, swap(): return lax.ppermute(x, axis, [(i, i ^ step) for i in range(ROWS)])  8.71 us
    ppermute x2, waiting for transfers between devices, local_few(): lax.ppermute(x, 'cols', [(col, col ^ far_steps(col)[i]) for col in range(...  3.02 us
    ppermute x6, waiting for transfers between devices, swap(): return lax.ppermute(x, axis, [(i, i ^ step) for i in range(ROWS)])  2.63 us
    ppermute x2, starting transfers between devices, local_few(): lax.ppermute(x, 'cols', [(col, col ^ far_steps(col)[i]) for col in range(...  2.45 us
    pallas_call x1, Pallas kernels, local_few(): pl.pallas_call(functools.partial(prepare_kernel, tiles, slots), out_shape...  1.64 us
    pallas_call x1, Pallas kernels, local_few(): pl.pallas_call(functools.partial(pack_kernel, tiles, slots), out_shape=[j...  0.98 us
    pallas_call x1, Pallas kernels, local_few(): pl.pallas_call(last_kernel, out_shape=sums_shape, in_specs=[VMEM] * 3, ou...  0.7 us
    pallas_call x4, Pallas kernels, on_vmem(): pl.pallas_call(kernel, out_shape=out_shape, in_specs=[VMEM] * len(args),...  0.67 us
  transfers between devices with their start and end apart: 8, of which 4 were waited for; matrix products, arithmetic and copies ran while one was open for 0% of the time, Pallas kernels for 10%

profile of v26, /device:TPU:1, one launch (start us, length us, event | category | flops | bytes accessed | tf_op | source)
XLA Modules:
  0.0 20.9 jit_solution(7159454990056520356)
XLA Ops:
  0.0 1.0 %pack.1 = (bf16[128,512]{1,0:T(8,128)(2,1)S(1)}, bf16[48,512]{1,0:T(8,128)(2,1)S(1)}, bf16[80,512]{1,0:T(8,128)(2,1)S(1)}) custom-call(s32[4,8]{1,0:T(4,128)} %kept.3, bf16[128,1024]{1,0:T(8,128)(2,1)} %doubles.1), custom_call_target="tpu_custom_call" | custom-call | tf_op jit(solution)/shard_map/pack/pallas_call | solution.py:192
  1.0 3.2 %collective-permute-start.1 = (bf16[80,512]{1,0:T(8,128)(2,1)S(1)}, bf16[80,512]{1,0:T(8,128)(2,1)S(1)}, u32[]{:S(2)}, u32[]{:S(2)}) collective-permute-start(bf16[80,512]{1,0:T(8,128)(2,1)S(1)} %get-tuple-element.19), channel_id=1, source_target_pairs={{0,8},{4,12},{8,0},{12,4},{1,9},{5,13},{9,1},{13,5},{2,10},{6,14},... | collective-permute-start | bytes 245768 | tf_op jit(solution)/shard_map/ppermute | solution.py:176
  4.2 1.3 %collective-permute-start = (bf16[128,512]{1,0:T(8,128)(2,1)S(1)}, bf16[128,512]{1,0:T(8,128)(2,1)S(1)}, u32[]{:S(2)}, u32[]{:S(2)}) collective-permute-start(bf16[128,512]{1,0:T(8,128)(2,1)S(1)} %get-tuple-element.16.own), channel_id=1, source_target_pairs={{0,4},{4,0},{8,12},{12,8},{1,5},{5,1},{9,13},{13,9},{2,6},{6,2},{1... | collective-permute-start | bytes 393224 | tf_op jit(solution)/shard_map/ppermute | solution.py:176
  5.5 0.0 collective-permute-start.2
  5.5 1.3 %collective-permute-start.3 = (bf16[48,512]{1,0:T(8,128)(2,1)S(1)}, bf16[48,512]{1,0:T(8,128)(2,1)S(1)}, u32[]{:S(2)}, u32[]{:S(2)}) collective-permute-start(bf16[48,512]{1,0:T(8,128)(2,1)S(1)} %get-tuple-element.20), channel_id=1, source_target_pairs={{0,8},{4,12},{8,0},{12,4},{1,9},{5,13},{9,1},{13,5},{2,10},{6,14},... | collective-permute-start | bytes 147464 | tf_op jit(solution)/shard_map/ppermute | solution.py:176
  6.8 0.0 collective-permute-done.1.near_second
  6.8 2.2 %collective-permute-start.4 = (bf16[80,512]{1,0:T(8,128)(2,1)S(1)}, bf16[80,512]{1,0:T(8,128)(2,1)S(1)}, u32[]{:S(2)}, u32[]{:S(2)}) collective-permute-start(bf16[80,512]{1,0:T(8,128)(2,1)S(1)} %collective-permute-done.1.near_second), channel_id=1, source_target_pairs={{0,4},{4,0},{8,12},{12,8},{1,5},{5,1},{9,13},{13,9},{2,6},{6,2},{1... | collective-permute-start | bytes 245768 | tf_op jit(solution)/shard_map/ppermute | solution.py:176
  9.0 1.6 %prepare.1 = (bf16[4,512,256]{2,1,0:T(8,128)(2,1)S(1)}, f32[128,256]{1,0:T(8,128)S(1)}) custom-call(s32[4,8]{1,0:T(4,128)} %kept.3, s32[2,8]{1,0:T(2,128)} %bitcast.1, bf16[1024,256]{1,0:T(8,128)(2,1)} %integrals.1, bf16[128,512]{1,0:T(8,128)(2,1)S(1)} %get-tuple-element.16.own), custom_call_target="tpu_custom_call" | custom-call | flops 1150000000 | bytes 1024 | tf_op jit(solution)/shard_map/prepare/pallas_call | solution.py:211
  10.7 0.1 collective-permute-done.2.far_first
  10.8 0.0 collective-permute-done.pair
  10.8 0.2 %early.1 = f32[4,128,256]{2,1,0:T(8,128)S(1)} custom-call(f32[128,256]{1,0:T(8,128)S(1)} %get-tuple-element.17.product, bf16[4,512,256]{2,1,0:T(8,128)(2,1)S(1)} %get-tuple-element.18.gathered, bf16[128,512]{1,0:T(8,128)(2,1)S(1)} %collective-permute-done.pair, bf16[80,512]{1,0:T(8,128)(2,1)S(1)} %collective-permute-done.1.near_second, ...), custom_call_target="tpu_custom_call" | custom-call | bytes 1024 | tf_op jit(solution)/shard_map/early/pallas_call | solution.py:229
  11.1 0.0 collective-permute-done.3.near_first
  11.1 2.5 %collective-permute-done.4.far_second = bf16[80,512]{1,0:T(8,128)(2,1)S(1)} collective-permute-done((bf16[80,512]{1,0:T(8,128)(2,1)S(1)}, bf16[80,512]{1,0:T(8,128)(2,1)S(1)}, u32[]{:S(2)}, u32[]{:S(2)}) %collective-permute-start.4) | collective-permute-done | bytes 81952 | tf_op jit(solution)/shard_map/ppermute | solution.py:176
  13.6 0.3 %late.1 = (f32[48,256]{1,0:T(8,128)S(1)}, f32[80,256]{1,0:T(8,128)S(1)}, s16[272,128]{1,0:T(8,128)(2,1)S(1)}) custom-call(f32[4,128,256]{2,1,0:T(8,128)S(1)} %early.1, bf16[4,512,256]{2,1,0:T(8,128)(2,1)S(1)} %get-tuple-element.18.gathered, bf16[48,512]{1,0:T(8,128)(2,1)S(1)} %collective-permute-done.3.near_first, ...), custom_call_target="tpu_custom_call" | custom-call | flops 99999997952 | bytes 1024 | tf_op jit(solution)/shard_map/late/pallas_call | solution.py:229
  13.8 2.4 %collective-permute-start.5 = (s16[272,128]{1,0:T(8,128)(2,1)S(1)}, s16[272,128]{1,0:T(8,128)(2,1)S(1)}, u32[]{:S(2)}, u32[]{:S(2)}) collective-permute-start(s16[272,128]{1,0:T(8,128)(2,1)S(1)} %get-tuple-element.24), channel_id=1, source_target_pairs={{0,3},{1,2},{2,0},{3,1},{4,7},{5,6},{6,4},{7,5},{8,11},{9,10},{10,... | collective-permute-start | bytes 208904 | tf_op jit(solution)/shard_map/ppermute | solution.py:251
  16.2 0.0 copy-start
  16.2 0.1 rest.1
  16.4 0.1 collective-permute-start.6
  16.4 0.7 %collective-permute-start.7 = (s16[272,128]{1,0:T(8,128)(2,1)S(1)}, s16[272,128]{1,0:T(8,128)(2,1)S(1)}, u32[]{:S(2)}, u32[]{:S(2)}) collective-permute-start(s16[272,128]{1,0:T(8,128)(2,1)S(1)} %get-tuple-element.26), channel_id=1, source_target_pairs={{0,1},{1,0},{2,3},{3,2},{4,5},{5,4},{6,7},{7,6},{8,9},{9,8},{10,11... | collective-permute-start | bytes 208904 | tf_op jit(solution)/shard_map/ppermute | solution.py:176
  17.1 0.8 %collective-permute-done.5.one_far = s16[272,128]{1,0:T(8,128)(2,1)S(1)} collective-permute-done((s16[272,128]{1,0:T(8,128)(2,1)S(1)}, s16[272,128]{1,0:T(8,128)(2,1)S(1)}, u32[]{:S(2)}, u32[]{:S(2)}) %collective-permute-start.5) | collective-permute-done | bytes 69664 | tf_op jit(solution)/shard_map/ppermute | solution.py:251
  17.9 0.0 copy-done
  17.9 2.3 %collective-permute-done.6.other_far = s16[272,128]{1,0:T(8,128)(2,1)S(1)} collective-permute-done((s16[272,128]{1,0:T(8,128)(2,1)S(1)}, s16[272,128]{1,0:T(8,128)(2,1)S(1)}, u32[]{:S(2)}, u32[]{:S(2)}) %collective-permute-start.6) | collective-permute-done | bytes 69664 | tf_op jit(solution)/shard_map/ppermute | solution.py:251
  20.2 0.0 collective-permute-done.7.one
  20.2 0.7 %last.1 = f32[128,256]{1,0:T(8,128)} custom-call(f32[128,256]{1,0:T(8,128)S(1)} %first.1.base, s16[272,128]{1,0:T(8,128)(2,1)S(1)} %collective-permute-done.6.other_far, s16[272,128]{1,0:T(8,128)(2,1)S(1)} %collective-permute-done.7.one), custom_call_target="tpu_custom_call" | custom-call | bytes 1024 | tf_op jit(solution)/shard_map/last/pallas_call | solution.py:256
  (1 shorter events, 0.0 us)
Async XLA Ops:
  1.0 5.9 %collective-permute-start.1 = (bf16[80,512]{1,0:T(8,128)(2,1)S(1)}, bf16[80,512]{1,0:T(8,128)(2,1)S(1)}, u32[]{:S(2)}, u32[]{:S(2)}) collective-permute-start(bf16[80,512]{1,0:T(8,128)(2,1)S(1)} %get-tuple-element.19), channel_id=1, source_target_pairs={{0,8},{4,12},{8,0},{12,4},{1,9},{5,13},{9,1},{13,5},{2,10},{6,14},... | collective-permute-start | bytes 245768 | tf_op jit(solution)/shard_map/ppermute | solution.py:176
  4.2 6.6 %collective-permute-start = (bf16[128,512]{1,0:T(8,128)(2,1)S(1)}, bf16[128,512]{1,0:T(8,128)(2,1)S(1)}, u32[]{:S(2)}, u32[]{:S(2)}) collective-permute-start(bf16[128,512]{1,0:T(8,128)(2,1)S(1)} %get-tuple-element.16.own), channel_id=1, source_target_pairs={{0,4},{4,0},{8,12},{12,8},{1,5},{5,1},{9,13},{13,9},{2,6},{6,2},{1... | collective-permute-start | bytes 393224 | tf_op jit(solution)/shard_map/ppermute | solution.py:176
  5.5 5.3 %collective-permute-start.2 = (bf16[48,512]{1,0:T(8,128)(2,1)S(1)}, bf16[48,512]{1,0:T(8,128)(2,1)S(1)}, u32[]{:S(2)}, u32[]{:S(2)}) collective-permute-start(bf16[48,512]{1,0:T(8,128)(2,1)S(1)} %get-tuple-element.20), channel_id=1, source_target_pairs={{0,12},{4,8},{8,4},{12,0},{1,13},{5,9},{9,5},{13,1},{2,14},{6,10},... | collective-permute-start | bytes 147464 | tf_op jit(solution)/shard_map/ppermute | solution.py:176
  5.5 5.6 %collective-permute-start.3 = (bf16[48,512]{1,0:T(8,128)(2,1)S(1)}, bf16[48,512]{1,0:T(8,128)(2,1)S(1)}, u32[]{:S(2)}, u32[]{:S(2)}) collective-permute-start(bf16[48,512]{1,0:T(8,128)(2,1)S(1)} %get-tuple-element.20), channel_id=1, source_target_pairs={{0,8},{4,12},{8,0},{12,4},{1,9},{5,13},{9,1},{13,5},{2,10},{6,14},... | collective-permute-start | bytes 147464 | tf_op jit(solution)/shard_map/ppermute | solution.py:176
  6.8 6.7 %collective-permute-start.4 = (bf16[80,512]{1,0:T(8,128)(2,1)S(1)}, bf16[80,512]{1,0:T(8,128)(2,1)S(1)}, u32[]{:S(2)}, u32[]{:S(2)}) collective-permute-start(bf16[80,512]{1,0:T(8,128)(2,1)S(1)} %collective-permute-done.1.near_second), channel_id=1, source_target_pairs={{0,4},{4,0},{8,12},{12,8},{1,5},{5,1},{9,13},{13,9},{2,6},{6,2},{1... | collective-permute-start | bytes 245768 | tf_op jit(solution)/shard_map/ppermute | solution.py:176
  13.8 4.0 %collective-permute-start.5 = (s16[272,128]{1,0:T(8,128)(2,1)S(1)}, s16[272,128]{1,0:T(8,128)(2,1)S(1)}, u32[]{:S(2)}, u32[]{:S(2)}) collective-permute-start(s16[272,128]{1,0:T(8,128)(2,1)S(1)} %get-tuple-element.24), channel_id=1, source_target_pairs={{0,3},{1,2},{2,0},{3,1},{4,7},{5,6},{6,4},{7,5},{8,11},{9,10},{10,... | collective-permute-start | bytes 208904 | tf_op jit(solution)/shard_map/ppermute | solution.py:251
  16.2 1.6 %copy-start = (f32[128,256]{1,0:T(8,128)S(1)}, f32[128,256]{1,0:T(8,128)}, u32[]{:S(2)}) copy-start(f32[128,256]{1,0:T(8,128)} %residual.1) | copy-start | bytes 393220
  16.4 3.8 %collective-permute-start.6 = (s16[272,128]{1,0:T(8,128)(2,1)S(1)}, s16[272,128]{1,0:T(8,128)(2,1)S(1)}, u32[]{:S(2)}, u32[]{:S(2)}) collective-permute-start(s16[272,128]{1,0:T(8,128)(2,1)S(1)} %get-tuple-element.25), channel_id=1, source_target_pairs={{0,2},{1,3},{2,1},{3,0},{4,6},{5,7},{6,5},{7,4},{8,10},{9,11},{10,... | collective-permute-start | bytes 208904 | tf_op jit(solution)/shard_map/ppermute | solution.py:251
  16.4 3.7 %collective-permute-start.7 = (s16[272,128]{1,0:T(8,128)(2,1)S(1)}, s16[272,128]{1,0:T(8,128)(2,1)S(1)}, u32[]{:S(2)}, u32[]{:S(2)}) collective-permute-start(s16[272,128]{1,0:T(8,128)(2,1)S(1)} %get-tuple-element.26), channel_id=1, source_target_pairs={{0,1},{1,0},{2,3},{3,2},{4,5},{5,4},{6,7},{7,6},{8,9},{9,8},{10,11... | collective-permute-start | bytes 208904 | tf_op jit(solution)/shard_map/ppermute | solution.py:176

commit v27 on v24

--- a/solution.py
+++ b/solution.py
@@ -16,6 +16,7 @@
 VMEM = pl.BlockSpec(memory_space=pltpu.VMEM)
 HBM = pl.BlockSpec(memory_space=pltpu.HBM)
 PARAMS = pltpu.CompilerParams(vmem_limit_bytes=8 * 1024 * 1024)
+NEAR_LATE = 48
 DIRECT = 64
 PIECES = 4
 ROWS = 4
@@ -38,7 +39,7 @@
     return [pltpu.make_async_copy(source.at[r], target.at[r], sems.at[i]) for i, r in enumerate(rows)]
 
 
-def pack_kernel(tiles, slots, kept, doubles, packed, first, second, table, block, places, sems):
+def pack_kernel(tiles, slots, kept, doubles, packed, direct, first, second, table, block, places, sems):
     table_copy = pltpu.make_async_copy(kept, table, sems.at[PIECES])
     block_copies = copies(doubles, block, sems)
     table_copy.start()
@@ -53,6 +54,7 @@
         tile = block[:, pl.ds(pl.multiple_of(places[slot] * TILE, TILE), TILE)]
         to = slice(slot * TILE, (slot + 1) * TILE)
         packed[:, to] = tile
+        direct[:, to] = tile[: direct.shape[0]]
         first[:, to] = tile[:cut]
         second[:, to] = tile[cut:]
 
@@ -79,6 +81,10 @@
     product[...] = jnp.dot(own[...], gathered[row ^ col], preferred_element_type=jnp.float32)
 
 
+def tail_kernel(x, out):
+    out[...] = x[x.shape[0] - out.shape[0] :, :]
+
+
 def encode(x, out):
     pairs, width = x.shape
     largest = jnp.max(jnp.abs(x), axis=0, keepdims=True)
@@ -115,7 +121,7 @@
 
 def early_kernel(product, gathered, pair, near_second, far_first, sums):
     mine = place()
-    cut = far_first.shape[0]
+    cut = product.shape[0] - near_second.shape[0]
     sums[mine] = product[...]
     sums[mine ^ 1] = jnp.dot(pair[...], gathered[mine ^ 1], preferred_element_type=jnp.float32)
     for step, start, block in ((2, cut, near_second), (3, 0, far_first)):
@@ -125,17 +131,16 @@
 
 
 def whole(n, early, near_sums, far_sums, out):
-    cut = near_sums.shape[0]
     step = place() ^ n
     out[...] = early[n]
 
     @pl.when(step == 2)
     def _():
-        out[:cut, :] = near_sums[...]
+        out[: near_sums.shape[0], :] = near_sums[...]
 
     @pl.when(step == 3)
     def _():
-        out[cut:, :] = far_sums[...]
+        out[out.shape[0] - far_sums.shape[0] :, :] = far_sums[...]
 
 
 def late_kernel(early, gathered, near_first, far_second, near_sums, far_sums, one_far, held):
@@ -181,17 +186,18 @@
     slots = tiles // GROUP * KEEP
     places = pltpu.SMEM((tiles + 1,), jnp.int32)
     sums_shape = jax.ShapeDtypeStruct((pairs, width), jnp.float32)
-    parts = (DIRECT, pairs - DIRECT)
-    blocks = [jax.ShapeDtypeStruct((rows, slots * TILE), doubles.dtype) for rows in parts]
+    blocks = [
+        jax.ShapeDtypeStruct((rows, slots * TILE), doubles.dtype) for rows in (DIRECT, NEAR_LATE, pairs - NEAR_LATE)
+    ]
     message = jax.ShapeDtypeStruct((pairs * width // TILE + HEAD, TILE), jnp.int16)
     doubles, doubles_kept, integrals, integral_kept = (
         pltpu.with_memory_space_constraint(x, pltpu.HBM) for x in (doubles, doubles_kept, integrals, integral_kept.T)
     )
-    packed, first, second = pl.pallas_call(
+    packed, direct, first, second = pl.pallas_call(
         functools.partial(pack_kernel, tiles, slots),
         out_shape=[jax.ShapeDtypeStruct((pairs, slots * TILE), doubles.dtype)] + blocks,
         in_specs=[HBM, HBM],
-        out_specs=[VMEM] * 3,
+        out_specs=[VMEM] * 4,
         scratch_shapes=[
             pltpu.SMEM(doubles_kept.shape, jnp.int32),
             pltpu.VMEM(doubles.shape, doubles.dtype),
@@ -203,9 +209,18 @@
     )(doubles_kept, doubles)
     near_second = swap(second, "rows", 2)
     pair = swap(packed, "rows", 1)
-    far_first = swap(first, "rows", 3)
+    far_first = swap(direct, "rows", 3)
     near_first = swap(first, "rows", 2)
-    far_second = swap(near_second, "rows", 1)
+    handed_on = pl.pallas_call(
+        tail_kernel,
+        out_shape=jax.ShapeDtypeStruct((pairs - DIRECT, slots * TILE), doubles.dtype),
+        in_specs=[VMEM],
+        out_specs=VMEM,
+        compiler_params=PARAMS,
+        cost_estimate=cost(0),
+        name="tail",
+    )(near_second)
+    far_second = swap(handed_on, "rows", 1)
     gathered, product = pl.pallas_call(
         functools.partial(prepare_kernel, tiles, slots),
         out_shape=[jax.ShapeDtypeStruct((ROWS, slots * TILE, width), integrals.dtype), sums_shape],
@@ -219,7 +234,7 @@
             pltpu.SemaphoreType.DMA((PIECES + 2,)),
         ],
         compiler_params=PARAMS,
-        cost_estimate=cost(10**9),
+        cost_estimate=cost(115 * 10**7),
         name="prepare",
     )(doubles_kept, integral_kept, integrals, packed)
 
@@ -236,7 +251,7 @@
         )(*args)
 
     held = [pltpu.VMEM((pairs, width), jnp.float32)]
-    part_sums = [jax.ShapeDtypeStruct((rows, width), jnp.float32) for rows in parts]
+    part_sums = [jax.ShapeDtypeStruct((rows, width), jnp.float32) for rows in (NEAR_LATE, pairs - DIRECT)]
     all_sums = jax.ShapeDtypeStruct((ROWS, pairs, width), jnp.float32)
     early = on_vmem(early_kernel, "early", 0, all_sums, product, gathered, pair, near_second, far_first)
     near_sums, far_sums, one_far = on_vmem(

time: 21.2 us -> 21.1 us (level)
  waiting for transfers between devices: 5.81 us -> 5.44 us
    ppermute x6, waiting for transfers between devices: 2.77 us -> 2.42 us  [swap(): return lax.ppermute(x, axis, [(i, i ^ step) for i in range(ROWS)])]
where the time goes in v27:
time: 21.1 us; the launch traced here: 20.9 us
  starting transfers between devices  11.3 us (54%)
  waiting for transfers between devices  5.44 us (26%)
  Pallas kernels  4.03 us (19%)
    ppermute x6, starting transfers between devices, swap(): return lax.ppermute(x, axis, [(i, i ^ step) for i in range(ROWS)])  8.77 us
    ppermute x2, waiting for transfers between devices, local_few(): lax.ppermute(x, 'cols', [(col, col ^ far_steps(col)[i]) for col in range(...  3.02 us
    ppermute x2, starting transfers between devices, local_few(): lax.ppermute(x, 'cols', [(col, col ^ far_steps(col)[i]) for col in range(...  2.58 us
    ppermute x6, waiting for transfers between devices, swap(): return lax.ppermute(x, axis, [(i, i ^ step) for i in range(ROWS)])  2.42 us
    pallas_call x1, Pallas kernels, local_few(): pl.pallas_call(functools.partial(prepare_kernel, tiles, slots), out_shape...  1.64 us
    pallas_call x1, Pallas kernels, local_few(): pl.pallas_call(functools.partial(pack_kernel, tiles, slots), out_shape=[j...  1.02 us
    pallas_call x1, Pallas kernels, local_few(): pl.pallas_call(last_kernel, out_shape=sums_shape, in_specs=[VMEM] * 3, ou...  0.7 us
    pallas_call x4, Pallas kernels, on_vmem(): pl.pallas_call(kernel, out_shape=out_shape, in_specs=[VMEM] * len(args),...  0.67 us
  transfers between devices with their start and end apart: 8, of which 4 were waited for; matrix products, arithmetic and copies ran while one was open for 0% of the time, Pallas kernels for 10%

profile of v27, /device:TPU:1, one launch (start us, length us, event | category | flops | bytes accessed | tf_op | source)
XLA Modules:
  0.0 20.9 jit_solution(18030177390153506015)
XLA Ops:
  0.0 1.0 %pack.1 = (bf16[128,512]{1,0:T(8,128)(2,1)S(1)}, bf16[64,512]{1,0:T(8,128)(2,1)S(1)}, bf16[48,512]{1,0:T(8,128)(2,1)S(1)}, bf16[80,512]{1,0:T(8,128)(2,1)S(1)}) custom-call(s32[4,8]{1,0:T(4,128)} %kept.3, bf16[128,1024]{1,0:T(8,128)(2,1)} %doubles.1), custom_call_target="tpu_custom_call" | custom-call | tf_op jit(solution)/shard_map/pack/pallas_call | solution.py:196
  1.0 3.2 %collective-permute-start.1 = (bf16[80,512]{1,0:T(8,128)(2,1)S(1)}, bf16[80,512]{1,0:T(8,128)(2,1)S(1)}, u32[]{:S(2)}, u32[]{:S(2)}) collective-permute-start(bf16[80,512]{1,0:T(8,128)(2,1)S(1)} %get-tuple-element.20), channel_id=1, source_target_pairs={{0,8},{4,12},{8,0},{12,4},{1,9},{5,13},{9,1},{13,5},{2,10},{6,14},... | collective-permute-start | bytes 245768 | tf_op jit(solution)/shard_map/ppermute | solution.py:179
  4.2 1.3 %collective-permute-start = (bf16[128,512]{1,0:T(8,128)(2,1)S(1)}, bf16[128,512]{1,0:T(8,128)(2,1)S(1)}, u32[]{:S(2)}, u32[]{:S(2)}) collective-permute-start(bf16[128,512]{1,0:T(8,128)(2,1)S(1)} %get-tuple-element.17.own), channel_id=1, source_target_pairs={{0,4},{4,0},{8,12},{12,8},{1,5},{5,1},{9,13},{13,9},{2,6},{6,2},{1... | collective-permute-start | bytes 393224 | tf_op jit(solution)/shard_map/ppermute | solution.py:179
  5.5 0.0 collective-permute-start.2
  5.5 1.3 %collective-permute-start.3 = (bf16[48,512]{1,0:T(8,128)(2,1)S(1)}, bf16[48,512]{1,0:T(8,128)(2,1)S(1)}, u32[]{:S(2)}, u32[]{:S(2)}) collective-permute-start(bf16[48,512]{1,0:T(8,128)(2,1)S(1)} %get-tuple-element.22), channel_id=1, source_target_pairs={{0,8},{4,12},{8,0},{12,4},{1,9},{5,13},{9,1},{13,5},{2,10},{6,14},... | collective-permute-start | bytes 147464 | tf_op jit(solution)/shard_map/ppermute | solution.py:179
  6.9 0.0 collective-permute-done.1.near_second.x
  6.9 2.3 %collective-permute-start.4 = (bf16[64,512]{1,0:T(8,128)(2,1)S(1)}, bf16[64,512]{1,0:T(8,128)(2,1)S(1)}, u32[]{:S(2)}, u32[]{:S(2)}) collective-permute-start(bf16[64,512]{1,0:T(8,128)(2,1)S(1)} %tail.1), channel_id=1, source_target_pairs={{0,4},{4,0},{8,12},{12,8},{1,5},{5,1},{9,13},{13,9},{2,6},{6,2},{1... | collective-permute-start | bytes 196616 | tf_op jit(solution)/shard_map/ppermute | solution.py:179
  9.2 1.6 %prepare.1 = (bf16[4,512,256]{2,1,0:T(8,128)(2,1)S(1)}, f32[128,256]{1,0:T(8,128)S(1)}) custom-call(s32[4,8]{1,0:T(4,128)} %kept.3, s32[2,8]{1,0:T(2,128)} %bitcast.1, bf16[1024,256]{1,0:T(8,128)(2,1)} %integrals.1, bf16[128,512]{1,0:T(8,128)(2,1)S(1)} %get-tuple-element.17.own), custom_call_target="tpu_custom_call" | custom-call | flops 1150000000 | bytes 1024 | tf_op jit(solution)/shard_map/prepare/pallas_call | solution.py:224
  10.8 0.4 %collective-permute-done.2.far_first = bf16[64,512]{1,0:T(8,128)(2,1)S(1)} collective-permute-done((bf16[64,512]{1,0:T(8,128)(2,1)S(1)}, bf16[64,512]{1,0:T(8,128)(2,1)S(1)}, u32[]{:S(2)}, u32[]{:S(2)}) %collective-permute-start.2) | collective-permute-done | bytes 65568 | tf_op jit(solution)/shard_map/ppermute | solution.py:179
  11.2 0.0 collective-permute-done.pair
  11.2 0.3 %early.1 = f32[4,128,256]{2,1,0:T(8,128)S(1)} custom-call(f32[128,256]{1,0:T(8,128)S(1)} %get-tuple-element.18.product, bf16[4,512,256]{2,1,0:T(8,128)(2,1)S(1)} %get-tuple-element.19.gathered, bf16[128,512]{1,0:T(8,128)(2,1)S(1)} %collective-permute-done.pair, bf16[80,512]{1,0:T(8,128)(2,1)S(1)} %collective-permute-done.1.near_second.x, ...), custom_call_target="tpu_custom_call" | custom-call | bytes 1024 | tf_op jit(solution)/shard_map/early/pallas_call | solution.py:242
  11.5 0.0 collective-permute-done.3.near_first
  11.5 2.0 %collective-permute-done.4.far_second = bf16[64,512]{1,0:T(8,128)(2,1)S(1)} collective-permute-done((bf16[64,512]{1,0:T(8,128)(2,1)S(1)}, bf16[64,512]{1,0:T(8,128)(2,1)S(1)}, u32[]{:S(2)}, u32[]{:S(2)}) %collective-permute-start.4) | collective-permute-done | bytes 65568 | tf_op jit(solution)/shard_map/ppermute | solution.py:179
  13.5 0.3 %late.1 = (f32[48,256]{1,0:T(8,128)S(1)}, f32[64,256]{1,0:T(8,128)S(1)}, s16[272,128]{1,0:T(8,128)(2,1)S(1)}) custom-call(f32[4,128,256]{2,1,0:T(8,128)S(1)} %early.1, bf16[4,512,256]{2,1,0:T(8,128)(2,1)S(1)} %get-tuple-element.19.gathered, bf16[48,512]{1,0:T(8,128)(2,1)S(1)} %collective-permute-done.3.near_first, ...), custom_call_target="tpu_custom_call" | custom-call | flops 99999997952 | bytes 1024 | tf_op jit(solution)/shard_map/late/pallas_call | solution.py:242
  13.8 2.5 %collective-permute-start.5 = (s16[272,128]{1,0:T(8,128)(2,1)S(1)}, s16[272,128]{1,0:T(8,128)(2,1)S(1)}, u32[]{:S(2)}, u32[]{:S(2)}) collective-permute-start(s16[272,128]{1,0:T(8,128)(2,1)S(1)} %get-tuple-element.26), channel_id=1, source_target_pairs={{0,3},{1,2},{2,0},{3,1},{4,7},{5,6},{6,4},{7,5},{8,11},{9,10},{10,... | collective-permute-start | bytes 208904 | tf_op jit(solution)/shard_map/ppermute | solution.py:264
  16.3 0.0 copy-start
  16.3 0.1 rest.1
  16.4 0.1 collective-permute-start.6
  16.5 0.7 %collective-permute-start.7 = (s16[272,128]{1,0:T(8,128)(2,1)S(1)}, s16[272,128]{1,0:T(8,128)(2,1)S(1)}, u32[]{:S(2)}, u32[]{:S(2)}) collective-permute-start(s16[272,128]{1,0:T(8,128)(2,1)S(1)} %get-tuple-element.28), channel_id=1, source_target_pairs={{0,1},{1,0},{2,3},{3,2},{4,5},{5,4},{6,7},{7,6},{8,9},{9,8},{10,11... | collective-permute-start | bytes 208904 | tf_op jit(solution)/shard_map/ppermute | solution.py:179
  17.1 0.5 %collective-permute-done.5.one_far = s16[272,128]{1,0:T(8,128)(2,1)S(1)} collective-permute-done((s16[272,128]{1,0:T(8,128)(2,1)S(1)}, s16[272,128]{1,0:T(8,128)(2,1)S(1)}, u32[]{:S(2)}, u32[]{:S(2)}) %collective-permute-start.5) | collective-permute-done | bytes 69664 | tf_op jit(solution)/shard_map/ppermute | solution.py:264
  17.6 0.0 copy-done
  17.7 2.5 %collective-permute-done.6.other_far = s16[272,128]{1,0:T(8,128)(2,1)S(1)} collective-permute-done((s16[272,128]{1,0:T(8,128)(2,1)S(1)}, s16[272,128]{1,0:T(8,128)(2,1)S(1)}, u32[]{:S(2)}, u32[]{:S(2)}) %collective-permute-start.6) | collective-permute-done | bytes 69664 | tf_op jit(solution)/shard_map/ppermute | solution.py:264
  20.2 0.0 collective-permute-done.7.one
  20.2 0.7 %last.1 = f32[128,256]{1,0:T(8,128)} custom-call(f32[128,256]{1,0:T(8,128)S(1)} %first.1.base, s16[272,128]{1,0:T(8,128)(2,1)S(1)} %collective-permute-done.6.other_far, s16[272,128]{1,0:T(8,128)(2,1)S(1)} %collective-permute-done.7.one), custom_call_target="tpu_custom_call" | custom-call | bytes 1024 | tf_op jit(solution)/shard_map/last/pallas_call | solution.py:269
  (2 shorter events, 0.0 us)
Async XLA Ops:
  1.0 5.9 %collective-permute-start.1 = (bf16[80,512]{1,0:T(8,128)(2,1)S(1)}, bf16[80,512]{1,0:T(8,128)(2,1)S(1)}, u32[]{:S(2)}, u32[]{:S(2)}) collective-permute-start(bf16[80,512]{1,0:T(8,128)(2,1)S(1)} %get-tuple-element.20), channel_id=1, source_target_pairs={{0,8},{4,12},{8,0},{12,4},{1,9},{5,13},{9,1},{13,5},{2,10},{6,14},... | collective-permute-start | bytes 245768 | tf_op jit(solution)/shard_map/ppermute | solution.py:179
  4.2 7.0 %collective-permute-start = (bf16[128,512]{1,0:T(8,128)(2,1)S(1)}, bf16[128,512]{1,0:T(8,128)(2,1)S(1)}, u32[]{:S(2)}, u32[]{:S(2)}) collective-permute-start(bf16[128,512]{1,0:T(8,128)(2,1)S(1)} %get-tuple-element.17.own), channel_id=1, source_target_pairs={{0,4},{4,0},{8,12},{12,8},{1,5},{5,1},{9,13},{13,9},{2,6},{6,2},{1... | collective-permute-start | bytes 393224 | tf_op jit(solution)/shard_map/ppermute | solution.py:179
  5.5 5.7 %collective-permute-start.2 = (bf16[64,512]{1,0:T(8,128)(2,1)S(1)}, bf16[64,512]{1,0:T(8,128)(2,1)S(1)}, u32[]{:S(2)}, u32[]{:S(2)}) collective-permute-start(bf16[64,512]{1,0:T(8,128)(2,1)S(1)} %get-tuple-element.21), channel_id=1, source_target_pairs={{0,12},{4,8},{8,4},{12,0},{1,13},{5,9},{9,5},{13,1},{2,14},{6,10},... | collective-permute-start | bytes 196616 | tf_op jit(solution)/shard_map/ppermute | solution.py:179
  5.5 5.9 %collective-permute-start.3 = (bf16[48,512]{1,0:T(8,128)(2,1)S(1)}, bf16[48,512]{1,0:T(8,128)(2,1)S(1)}, u32[]{:S(2)}, u32[]{:S(2)}) collective-permute-start(bf16[48,512]{1,0:T(8,128)(2,1)S(1)} %get-tuple-element.22), channel_id=1, source_target_pairs={{0,8},{4,12},{8,0},{12,4},{1,9},{5,13},{9,1},{13,5},{2,10},{6,14},... | collective-permute-start | bytes 147464 | tf_op jit(solution)/shard_map/ppermute | solution.py:179
  6.9 6.6 %collective-permute-start.4 = (bf16[64,512]{1,0:T(8,128)(2,1)S(1)}, bf16[64,512]{1,0:T(8,128)(2,1)S(1)}, u32[]{:S(2)}, u32[]{:S(2)}) collective-permute-start(bf16[64,512]{1,0:T(8,128)(2,1)S(1)} %tail.1), channel_id=1, source_target_pairs={{0,4},{4,0},{8,12},{12,8},{1,5},{5,1},{9,13},{13,9},{2,6},{6,2},{1... | collective-permute-start | bytes 196616 | tf_op jit(solution)/shard_map/ppermute | solution.py:179
  13.8 3.9 %collective-permute-start.5 = (s16[272,128]{1,0:T(8,128)(2,1)S(1)}, s16[272,128]{1,0:T(8,128)(2,1)S(1)}, u32[]{:S(2)}, u32[]{:S(2)}) collective-permute-start(s16[272,128]{1,0:T(8,128)(2,1)S(1)} %get-tuple-element.26), channel_id=1, source_target_pairs={{0,3},{1,2},{2,0},{3,1},{4,7},{5,6},{6,4},{7,5},{8,11},{9,10},{10,... | collective-permute-start | bytes 208904 | tf_op jit(solution)/shard_map/ppermute | solution.py:264
  16.3 1.4 %copy-start = (f32[128,256]{1,0:T(8,128)S(1)}, f32[128,256]{1,0:T(8,128)}, u32[]{:S(2)}) copy-start(f32[128,256]{1,0:T(8,128)} %residual.1) | copy-start | bytes 393220
  16.4 3.8 %collective-permute-start.6 = (s16[272,128]{1,0:T(8,128)(2,1)S(1)}, s16[272,128]{1,0:T(8,128)(2,1)S(1)}, u32[]{:S(2)}, u32[]{:S(2)}) collective-permute-start(s16[272,128]{1,0:T(8,128)(2,1)S(1)} %get-tuple-element.27), channel_id=1, source_target_pairs={{0,2},{1,3},{2,1},{3,0},{4,6},{5,7},{6,5},{7,4},{8,10},{9,11},{10,... | collective-permute-start | bytes 208904 | tf_op jit(solution)/shard_map/ppermute | solution.py:264
  16.5 3.7 %collective-permute-start.7 = (s16[272,128]{1,0:T(8,128)(2,1)S(1)}, s16[272,128]{1,0:T(8,128)(2,1)S(1)}, u32[]{:S(2)}, u32[]{:S(2)}) collective-permute-start(s16[272,128]{1,0:T(8,128)(2,1)S(1)} %get-tuple-element.28), channel_id=1, source_target_pairs={{0,1},{1,0},{2,3},{3,2},{4,5},{5,4},{6,7},{7,6},{8,9},{9,8},{10,11... | collective-permute-start | bytes 208904 | tf_op jit(solution)/shard_map/ppermute | solution.py:179

commit v28 on v25

--- a/solution.py
+++ b/solution.py
@@ -109,39 +109,55 @@
     return lax.axis_index("rows") ^ lax.axis_index("cols")
 
 
-def far_steps(col):
-    return 3 - col // 2, 2 + col // 2
-
-
-def early_kernel(product, gathered, pair, near_second, far_first, near_first, sums):
+def near_step(col):
+    return 3 - col % 2
+
+
+def chip_steps(row, col):
+    odd = row % 2
+    own = row // 2 == col // 2
+    first = own * (3 - odd) + (1 - own) * (2 + odd)
+    return first, 5 - first
+
+
+def steps_here():
+    row, col = lax.axis_index("rows"), lax.axis_index("cols")
+    odd = row % 2
+    first = jnp.where(row // 2 == col // 2, 3 - odd, 2 + odd)
+    return first, 5 - first
+
+
+def early_kernel(product, gathered, pair, near_second, far_first, near_first, sums, one_far):
     mine = place()
+    near = near_step(lax.axis_index("cols"))
     cut = far_first.shape[0]
     sums[mine] = product[...]
     sums[mine ^ 1] = jnp.dot(pair[...], gathered[mine ^ 1], preferred_element_type=jnp.float32)
-    for step, start, block in ((2, cut, near_second), (3, 0, far_first), (2, 0, near_first)):
+    for step, start, block in ((near, cut, near_second), (5 - near, 0, far_first), (near, 0, near_first)):
         sums[mine ^ step, start : start + block.shape[0], :] = jnp.dot(
             block[...], gathered[mine ^ step], preferred_element_type=jnp.float32
         )
+    encode(sums[steps_here()[0]], one_far)
 
 
 def whole(n, early, far_sums, out):
     out[...] = early[n]
 
-    @pl.when((place() ^ n) == 3)
+    @pl.when((place() ^ n) == 5 - near_step(lax.axis_index("cols")))
     def _():
         out[out.shape[0] - far_sums.shape[0] :, :] = far_sums[...]
 
 
-def late_kernel(early, gathered, far_second, far_sums, one_far, held):
-    far_sums[...] = jnp.dot(far_second[...], gathered[place() ^ 3], preferred_element_type=jnp.float32)
-    whole(far_steps(lax.axis_index("cols"))[0], early, far_sums, held)
-    encode(held[...], one_far)
-
-
-def rest_kernel(early, far_sums, one, other_far, kept_sums, held):
-    for n, out in ((far_steps(lax.axis_index("cols"))[1], other_far), (1, one)):
-        whole(n, early, far_sums, held)
-        encode(held[...], out)
+def late_kernel(early, gathered, far_second, far_sums, other_far, held):
+    far = 5 - near_step(lax.axis_index("cols"))
+    far_sums[...] = jnp.dot(far_second[...], gathered[place() ^ far], preferred_element_type=jnp.float32)
+    whole(steps_here()[1], early, far_sums, held)
+    encode(held[...], other_far)
+
+
+def rest_kernel(early, far_sums, one, kept_sums, held):
+    whole(1, early, far_sums, held)
+    encode(held[...], one)
     whole(0, early, far_sums, kept_sums)
 
 
@@ -164,6 +180,15 @@
 
 def swap(x, axis, step):
     return lax.ppermute(x, axis, [(i, i ^ step) for i in range(ROWS)])
+
+
+def permute(x, target):
+    pairs = [(r * ROWS + c, target(r, c)) for r in range(ROWS) for c in range(ROWS)]
+    return lax.ppermute(x, ("rows", "cols"), [(i, r * ROWS + c) for i, (r, c) in pairs])
+
+
+def step_rows(x, step):
+    return permute(x, lambda row, col: (row ^ step(col), col))
 
 
 def local_few(doubles, doubles_kept, integrals, integral_kept, residual):
@@ -193,10 +218,10 @@
         compiler_params=PARAMS,
         name="pack",
     )(doubles_kept, doubles)
-    near_second = swap(second, "rows", 2)
+    near_second = step_rows(second, near_step)
     pair = swap(packed, "rows", 1)
-    far_first = swap(first, "rows", 3)
-    near_first = swap(first, "rows", 2)
+    far_first = step_rows(first, lambda col: 5 - near_step(col))
+    near_first = step_rows(first, near_step)
     far_second = swap(near_second, "rows", 1)
     gathered, product = pl.pallas_call(
         functools.partial(prepare_kernel, tiles, slots),
@@ -230,17 +255,24 @@
     held = [pltpu.VMEM((pairs, width), jnp.float32)]
     late_sums = jax.ShapeDtypeStruct((parts[1], width), jnp.float32)
     all_sums = jax.ShapeDtypeStruct((ROWS, pairs, width), jnp.float32)
-    early = on_vmem(early_kernel, "early", 0, all_sums, product, gathered, pair, near_second, far_first, near_first)
-    far_sums, one_far = on_vmem(
+    early, one_far = on_vmem(
+        early_kernel,
+        "early",
+        0,
+        [all_sums, message],
+        product,
+        gathered,
+        pair,
+        near_second,
+        far_first,
+        near_first,
+    )
+    one_far = permute(one_far, lambda row, col: (row, col ^ chip_steps(row, col)[0]))
+    far_sums, other_far = on_vmem(
         late_kernel, "late", 10**11, [late_sums, message], early, gathered, far_second, scratch=held
     )
-    one, other_far, kept_sums = on_vmem(
-        rest_kernel, "rest", 0, [message] * 2 + [sums_shape], early, far_sums, scratch=held
-    )
-    one_far, other_far = (
-        lax.ppermute(x, "cols", [(col, col ^ far_steps(col)[i]) for col in range(ROWS)])
-        for i, x in enumerate((one_far, other_far))
-    )
+    other_far = permute(other_far, lambda row, col: (row, col ^ chip_steps(row, col)[1]))
+    one, kept_sums = on_vmem(rest_kernel, "rest", 0, [message, sums_shape], early, far_sums, scratch=held)
     one = swap(one, "cols", 1)
     base = on_vmem(first_kernel, "first", 0, sums_shape, residual, kept_sums, one_far)
     return pl.pallas_call(

time: 21 us -> 21.6 us (1.029)
  the two profiles are of different devices: /device:TPU:1 before, /device:TPU:0 now
where the time goes in v28:
time: 21.6 us; the launch traced here: 21.4 us
  starting transfers between devices  11.3 us (52%)
  waiting for transfers between devices  5.98 us (28%)
  Pallas kernels  3.99 us (18%)
    ppermute x5, starting transfers between devices, permute(): lax.ppermute(x, ('rows', 'cols'), [(i, r * ROWS + c) for i, (r, c) in pai...  10 us
    ppermute x5, waiting for transfers between devices, permute(): lax.ppermute(x, ('rows', 'cols'), [(i, r * ROWS + c) for i, (r, c) in pai...  5.16 us
    pallas_call x1, Pallas kernels, local_few(): pl.pallas_call(functools.partial(prepare_kernel, tiles, slots), out_shape...  1.64 us
    ppermute x3, starting transfers between devices, swap(): return lax.ppermute(x, axis, [(i, i ^ step) for i in range(ROWS)])  1.3 us
    pallas_call x1, Pallas kernels, local_few(): pl.pallas_call(functools.partial(pack_kernel, tiles, slots), out_shape=[j...  1.01 us
    ppermute x3, waiting for transfers between devices, swap(): return lax.ppermute(x, axis, [(i, i ^ step) for i in range(ROWS)])  0.82 us
    pallas_call x1, Pallas kernels, local_few(): pl.pallas_call(last_kernel, out_shape=sums_shape, in_specs=[VMEM] * 3, ou...  0.7 us
    pallas_call x4, Pallas kernels, on_vmem(): pl.pallas_call(kernel, out_shape=out_shape, in_specs=[VMEM] * len(args),...  0.65 us
  transfers between devices with their start and end apart: 8, of which 6 were waited for; matrix products, arithmetic and copies ran while one was open for 0% of the time, Pallas kernels for 11%

profile of v28, /device:TPU:0, one launch (start us, length us, event | category | flops | bytes accessed | tf_op | source)
XLA Modules:
  0.0 21.4 jit_solution(16881277742513334832)
XLA Ops:
  0.0 1.0 %pack.1 = (bf16[128,512]{1,0:T(8,128)(2,1)S(1)}, bf16[48,512]{1,0:T(8,128)(2,1)S(1)}, bf16[80,512]{1,0:T(8,128)(2,1)S(1)}) custom-call(s32[4,8]{1,0:T(4,128)} %kept.3, bf16[128,1024]{1,0:T(8,128)(2,1)} %doubles.1), custom_call_target="tpu_custom_call" | custom-call | tf_op jit(solution)/shard_map/pack/pallas_call | solution.py:207
  1.0 5.1 %collective-permute-start.1 = (bf16[80,512]{1,0:T(8,128)(2,1)S(1)}, bf16[80,512]{1,0:T(8,128)(2,1)S(1)}, u32[]{:S(2)}, u32[]{:S(2)}) collective-permute-start(bf16[80,512]{1,0:T(8,128)(2,1)S(1)} %get-tuple-element.19), channel_id=1, source_target_pairs={{0,12},{1,9},{2,14},{3,11},{4,8},{5,13},{6,10},{7,15},{8,4},{9,1},... | collective-permute-start | bytes 245768 | tf_op jit(solution)/shard_map/ppermute | solution.py:187
  6.1 0.0 collective-permute-start
  6.1 0.6 %collective-permute-start.2 = (bf16[48,512]{1,0:T(8,128)(2,1)S(1)}, bf16[48,512]{1,0:T(8,128)(2,1)S(1)}, u32[]{:S(2)}, u32[]{:S(2)}) collective-permute-start(bf16[48,512]{1,0:T(8,128)(2,1)S(1)} %get-tuple-element.20), channel_id=1, source_target_pairs={{0,8},{1,13},{2,10},{3,15},{4,12},{5,9},{6,14},{7,11},{8,0},{9,5},... | collective-permute-start | bytes 147464 | tf_op jit(solution)/shard_map/ppermute | solution.py:187
  6.8 3.7 %collective-permute-start.3 = (bf16[48,512]{1,0:T(8,128)(2,1)S(1)}, bf16[48,512]{1,0:T(8,128)(2,1)S(1)}, u32[]{:S(2)}, u32[]{:S(2)}) collective-permute-start(bf16[48,512]{1,0:T(8,128)(2,1)S(1)} %get-tuple-element.20), channel_id=1, source_target_pairs={{0,12},{1,9},{2,14},{3,11},{4,8},{5,13},{6,10},{7,15},{8,4},{9,1},... | collective-permute-start | bytes 147464 | tf_op jit(solution)/shard_map/ppermute | solution.py:187
  10.5 0.0 collective-permute-done.1.near_second
  10.5 0.1 collective-permute-start.4
  10.6 1.6 %prepare.1 = (bf16[4,512,256]{2,1,0:T(8,128)(2,1)S(1)}, f32[128,256]{1,0:T(8,128)S(1)}) custom-call(s32[4,8]{1,0:T(4,128)} %kept.3, s32[2,8]{1,0:T(2,128)} %bitcast.1, bf16[1024,256]{1,0:T(8,128)(2,1)} %integrals.1, bf16[128,512]{1,0:T(8,128)(2,1)S(1)} %get-tuple-element.16.own), custom_call_target="tpu_custom_call" | custom-call | flops 1150000000 | bytes 1024 | tf_op jit(solution)/shard_map/prepare/pallas_call | solution.py:226
  12.3 0.2 %collective-permute-done.2.far_first = bf16[48,512]{1,0:T(8,128)(2,1)S(1)} collective-permute-done((bf16[48,512]{1,0:T(8,128)(2,1)S(1)}, bf16[48,512]{1,0:T(8,128)(2,1)S(1)}, u32[]{:S(2)}, u32[]{:S(2)}) %collective-permute-start.2) | collective-permute-done | bytes 49184 | tf_op jit(solution)/shard_map/ppermute | solution.py:187
  12.5 1.2 %collective-permute-done.3.near_first = bf16[48,512]{1,0:T(8,128)(2,1)S(1)} collective-permute-done((bf16[48,512]{1,0:T(8,128)(2,1)S(1)}, bf16[48,512]{1,0:T(8,128)(2,1)S(1)}, u32[]{:S(2)}, u32[]{:S(2)}) %collective-permute-start.3) | collective-permute-done | bytes 49184 | tf_op jit(solution)/shard_map/ppermute | solution.py:187
  13.8 0.3 %collective-permute-done.pair = bf16[128,512]{1,0:T(8,128)(2,1)S(1)} collective-permute-done((bf16[128,512]{1,0:T(8,128)(2,1)S(1)}, bf16[128,512]{1,0:T(8,128)(2,1)S(1)}, u32[]{:S(2)}, u32[]{:S(2)}) %collective-permute-start) | collective-permute-done | bytes 131104 | tf_op jit(solution)/shard_map/ppermute | solution.py:182
  14.1 0.3 %early.1 = (f32[4,128,256]{2,1,0:T(8,128)S(1)}, s16[272,128]{1,0:T(8,128)(2,1)S(1)}) custom-call(f32[128,256]{1,0:T(8,128)S(1)} %get-tuple-element.17.product, bf16[4,512,256]{2,1,0:T(8,128)(2,1)S(1)} %get-tuple-element.18.gathered, bf16[128,512]{1,0:T(8,128)(2,1)S(1)} %collective-permute-done.pair, bf16[80,512]{1,0:T(8,128)(2,1)S(1)} %collective-permute-done.1.near_second, ...), custom_call_target="tpu_custom_call" | custom-call | bytes 1024 | tf_op jit(solution)/shard_map/early/pallas_call | solution.py:244
  14.4 0.1 collective-permute-start.5
  14.5 0.5 %collective-permute-done.4.far_second = bf16[80,512]{1,0:T(8,128)(2,1)S(1)} collective-permute-done((bf16[80,512]{1,0:T(8,128)(2,1)S(1)}, bf16[80,512]{1,0:T(8,128)(2,1)S(1)}, u32[]{:S(2)}, u32[]{:S(2)}) %collective-permute-start.4) | collective-permute-done | bytes 81952 | tf_op jit(solution)/shard_map/ppermute | solution.py:182
  15.0 0.2 %late.1 = (f32[80,256]{1,0:T(8,128)S(1)}, s16[272,128]{1,0:T(8,128)(2,1)S(1)}) custom-call(f32[4,128,256]{2,1,0:T(8,128)S(1)} %get-tuple-element.21.early, bf16[4,512,256]{2,1,0:T(8,128)(2,1)S(1)} %get-tuple-element.18.gathered, bf16[80,512]{1,0:T(8,128)(2,1)S(1)} %collective-permute-done.4.far_second), custom_call_target="tpu_custom_call" | custom-call | flops 99999997952 | bytes 1024 | tf_op jit(solution)/shard_map/late/pallas_call | solution.py:244
  15.2 0.0 copy-start
  15.2 0.1 rest.1
  15.3 1.2 %collective-permute-start.7 = (s16[272,128]{1,0:T(8,128)(2,1)S(1)}, s16[272,128]{1,0:T(8,128)(2,1)S(1)}, u32[]{:S(2)}, u32[]{:S(2)}) collective-permute-start(s16[272,128]{1,0:T(8,128)(2,1)S(1)} %get-tuple-element.26), channel_id=1, source_target_pairs={{0,1},{1,0},{2,3},{3,2},{4,5},{5,4},{6,7},{7,6},{8,9},{9,8},{10,11... | collective-permute-start | bytes 208904 | tf_op jit(solution)/shard_map/ppermute | solution.py:182
  16.5 0.5 %collective-permute-start.6 = (s16[272,128]{1,0:T(8,128)(2,1)S(1)}, s16[272,128]{1,0:T(8,128)(2,1)S(1)}, u32[]{:S(2)}, u32[]{:S(2)}) collective-permute-start(s16[272,128]{1,0:T(8,128)(2,1)S(1)} %get-tuple-element.25), channel_id=1, source_target_pairs={{0,2},{1,3},{2,1},{3,0},{4,7},{5,6},{6,4},{7,5},{8,11},{9,10},{10,... | collective-permute-start | bytes 208904 | tf_op jit(solution)/shard_map/ppermute | solution.py:187
  17.0 1.8 %collective-permute-done.5.one_far = s16[272,128]{1,0:T(8,128)(2,1)S(1)} collective-permute-done((s16[272,128]{1,0:T(8,128)(2,1)S(1)}, s16[272,128]{1,0:T(8,128)(2,1)S(1)}, u32[]{:S(2)}, u32[]{:S(2)}) %collective-permute-start.5) | collective-permute-done | bytes 69664 | tf_op jit(solution)/shard_map/ppermute | solution.py:187
  18.8 0.0 copy-done
  18.8 0.0 collective-permute-done.7.one
  18.8 1.9 %collective-permute-done.6.other_far = s16[272,128]{1,0:T(8,128)(2,1)S(1)} collective-permute-done((s16[272,128]{1,0:T(8,128)(2,1)S(1)}, s16[272,128]{1,0:T(8,128)(2,1)S(1)}, u32[]{:S(2)}, u32[]{:S(2)}) %collective-permute-start.6) | collective-permute-done | bytes 69664 | tf_op jit(solution)/shard_map/ppermute | solution.py:187
  20.7 0.7 %last.1 = f32[128,256]{1,0:T(8,128)} custom-call(f32[128,256]{1,0:T(8,128)S(1)} %first.1.base, s16[272,128]{1,0:T(8,128)(2,1)S(1)} %collective-permute-done.6.other_far, s16[272,128]{1,0:T(8,128)(2,1)S(1)} %collective-permute-done.7.one), custom_call_target="tpu_custom_call" | custom-call | bytes 1024 | tf_op jit(solution)/shard_map/last/pallas_call | solution.py:278
  (1 shorter events, 0.0 us)
Async XLA Ops:
  1.0 9.5 %collective-permute-start.1 = (bf16[80,512]{1,0:T(8,128)(2,1)S(1)}, bf16[80,512]{1,0:T(8,128)(2,1)S(1)}, u32[]{:S(2)}, u32[]{:S(2)}) collective-permute-start(bf16[80,512]{1,0:T(8,128)(2,1)S(1)} %get-tuple-element.19), channel_id=1, source_target_pairs={{0,12},{1,9},{2,14},{3,11},{4,8},{5,13},{6,10},{7,15},{8,4},{9,1},... | collective-permute-start | bytes 245768 | tf_op jit(solution)/shard_map/ppermute | solution.py:187
  6.1 8.0 %collective-permute-start = (bf16[128,512]{1,0:T(8,128)(2,1)S(1)}, bf16[128,512]{1,0:T(8,128)(2,1)S(1)}, u32[]{:S(2)}, u32[]{:S(2)}) collective-permute-start(bf16[128,512]{1,0:T(8,128)(2,1)S(1)} %get-tuple-element.16.own), channel_id=1, source_target_pairs={{0,4},{4,0},{8,12},{12,8},{1,5},{5,1},{9,13},{13,9},{2,6},{6,2},{1... | collective-permute-start | bytes 393224 | tf_op jit(solution)/shard_map/ppermute | solution.py:182
  6.1 6.4 %collective-permute-start.2 = (bf16[48,512]{1,0:T(8,128)(2,1)S(1)}, bf16[48,512]{1,0:T(8,128)(2,1)S(1)}, u32[]{:S(2)}, u32[]{:S(2)}) collective-permute-start(bf16[48,512]{1,0:T(8,128)(2,1)S(1)} %get-tuple-element.20), channel_id=1, source_target_pairs={{0,8},{1,13},{2,10},{3,15},{4,12},{5,9},{6,14},{7,11},{8,0},{9,5},... | collective-permute-start | bytes 147464 | tf_op jit(solution)/shard_map/ppermute | solution.py:187
  6.8 7.0 %collective-permute-start.3 = (bf16[48,512]{1,0:T(8,128)(2,1)S(1)}, bf16[48,512]{1,0:T(8,128)(2,1)S(1)}, u32[]{:S(2)}, u32[]{:S(2)}) collective-permute-start(bf16[48,512]{1,0:T(8,128)(2,1)S(1)} %get-tuple-element.20), channel_id=1, source_target_pairs={{0,12},{1,9},{2,14},{3,11},{4,8},{5,13},{6,10},{7,15},{8,4},{9,1},... | collective-permute-start | bytes 147464 | tf_op jit(solution)/shard_map/ppermute | solution.py:187
  10.5 4.4 %collective-permute-start.4 = (bf16[80,512]{1,0:T(8,128)(2,1)S(1)}, bf16[80,512]{1,0:T(8,128)(2,1)S(1)}, u32[]{:S(2)}, u32[]{:S(2)}) collective-permute-start(bf16[80,512]{1,0:T(8,128)(2,1)S(1)} %collective-permute-done.1.near_second), channel_id=1, source_target_pairs={{0,4},{4,0},{8,12},{12,8},{1,5},{5,1},{9,13},{13,9},{2,6},{6,2},{1... | collective-permute-start | bytes 245768 | tf_op jit(solution)/shard_map/ppermute | solution.py:182
  14.4 4.4 %collective-permute-start.5 = (s16[272,128]{1,0:T(8,128)(2,1)S(1)}, s16[272,128]{1,0:T(8,128)(2,1)S(1)}, u32[]{:S(2)}, u32[]{:S(2)}) collective-permute-start(s16[272,128]{1,0:T(8,128)(2,1)S(1)} %get-tuple-element.24), channel_id=1, source_target_pairs={{0,3},{1,2},{2,0},{3,1},{4,6},{5,7},{6,5},{7,4},{8,10},{9,11},{10,... | collective-permute-start | bytes 208904 | tf_op jit(solution)/shard_map/ppermute | solution.py:187
  15.2 3.6 %copy-start = (f32[128,256]{1,0:T(8,128)S(1)}, f32[128,256]{1,0:T(8,128)}, u32[]{:S(2)}) copy-start(f32[128,256]{1,0:T(8,128)} %residual.1) | copy-start | bytes 393220
  15.3 3.5 %collective-permute-start.7 = (s16[272,128]{1,0:T(8,128)(2,1)S(1)}, s16[272,128]{1,0:T(8,128)(2,1)S(1)}, u32[]{:S(2)}, u32[]{:S(2)}) collective-permute-start(s16[272,128]{1,0:T(8,128)(2,1)S(1)} %get-tuple-element.26), channel_id=1, source_target_pairs={{0,1},{1,0},{2,3},{3,2},{4,5},{5,4},{6,7},{7,6},{8,9},{9,8},{10,11... | collective-permute-start | bytes 208904 | tf_op jit(solution)/shard_map/ppermute | solution.py:182
  16.5 4.2 %collective-permute-start.6 = (s16[272,128]{1,0:T(8,128)(2,1)S(1)}, s16[272,128]{1,0:T(8,128)(2,1)S(1)}, u32[]{:S(2)}, u32[]{:S(2)}) collective-permute-start(s16[272,128]{1,0:T(8,128)(2,1)S(1)} %get-tuple-element.25), channel_id=1, source_target_pairs={{0,2},{1,3},{2,1},{3,0},{4,7},{5,6},{6,4},{7,5},{8,11},{9,10},{10,... | collective-permute-start | bytes 208904 | tf_op jit(solution)/shard_map/ppermute | solution.py:187

commit v29 on v28

--- a/solution.py
+++ b/solution.py
@@ -148,14 +148,14 @@
         out[out.shape[0] - far_sums.shape[0] :, :] = far_sums[...]
 
 
-def late_kernel(early, gathered, far_second, far_sums, other_far, held):
+def late_kernel(early, gathered, far_second, far_sums):
     far = 5 - near_step(lax.axis_index("cols"))
     far_sums[...] = jnp.dot(far_second[...], gathered[place() ^ far], preferred_element_type=jnp.float32)
+
+
+def rest_kernel(early, far_sums, other_far, one, kept_sums, held):
     whole(steps_here()[1], early, far_sums, held)
     encode(held[...], other_far)
-
-
-def rest_kernel(early, far_sums, one, kept_sums, held):
     whole(1, early, far_sums, held)
     encode(held[...], one)
     whole(0, early, far_sums, kept_sums)
@@ -268,11 +268,11 @@
         near_first,
     )
     one_far = permute(one_far, lambda row, col: (row, col ^ chip_steps(row, col)[0]))
-    far_sums, other_far = on_vmem(
-        late_kernel, "late", 10**11, [late_sums, message], early, gathered, far_second, scratch=held
+    far_sums = on_vmem(late_kernel, "late", 10**11, late_sums, early, gathered, far_second)
+    other_far, one, kept_sums = on_vmem(
+        rest_kernel, "rest", 0, [message] * 2 + [sums_shape], early, far_sums, scratch=held
     )
     other_far = permute(other_far, lambda row, col: (row, col ^ chip_steps(row, col)[1]))
-    one, kept_sums = on_vmem(rest_kernel, "rest", 0, [message, sums_shape], early, far_sums, scratch=held)
     one = swap(one, "cols", 1)
     base = on_vmem(first_kernel, "first", 0, sums_shape, residual, kept_sums, one_far)
     return pl.pallas_call(

time: 21.6 us -> 20.6 us (0.954)
  waiting for transfers between devices: 5.98 us -> 4.88 us
    ppermute x3, starting transfers between devices: 1.3 us -> 0.12 us  [swap(): return lax.ppermute(x, axis, [(i, i ^ step) for i in range(ROWS)])]
    ppermute x5, starting transfers between devices: 10 us -> 11.1 us  [permute(): lax.ppermute(x, ('rows', 'cols'), [(i, r * ROWS + c) for i, (r, c) in pai...]
    ppermute x5, waiting for transfers between devices: 5.16 us -> 4.07 us  [permute(): lax.ppermute(x, ('rows', 'cols'), [(i, r * ROWS + c) for i, (r, c) in pai...]
where the time goes in v29:
time: 20.6 us; the launch traced here: 20.2 us
  starting transfers between devices  11.3 us (55%)
  waiting for transfers between devices  4.88 us (24%)
  Pallas kernels  4.02 us (20%)
    ppermute x5, starting transfers between devices, permute(): lax.ppermute(x, ('rows', 'cols'), [(i, r * ROWS + c) for i, (r, c) in pai...  11.1 us
    ppermute x5, waiting for transfers between devices, permute(): lax.ppermute(x, ('rows', 'cols'), [(i, r * ROWS + c) for i, (r, c) in pai...  4.07 us
    pallas_call x1, Pallas kernels, local_few(): pl.pallas_call(functools.partial(prepare_kernel, tiles, slots), out_shape...  1.64 us
    pallas_call x1, Pallas kernels, local_few(): pl.pallas_call(functools.partial(pack_kernel, tiles, slots), out_shape=[j...  1.01 us
    ppermute x3, waiting for transfers between devices, swap(): return lax.ppermute(x, axis, [(i, i ^ step) for i in range(ROWS)])  0.82 us
    pallas_call x1, Pallas kernels, local_few(): pl.pallas_call(last_kernel, out_shape=sums_shape, in_specs=[VMEM] * 3, ou...  0.7 us
    pallas_call x4, Pallas kernels, on_vmem(): pl.pallas_call(kernel, out_shape=out_shape, in_specs=[VMEM] * len(args),...  0.67 us
  transfers between devices with their start and end apart: 8, of which 6 were waited for; matrix products, arithmetic and copies ran while one was open for 0% of the time, Pallas kernels for 11%

profile of v29, /device:TPU:0, one launch (start us, length us, event | category | flops | bytes accessed | tf_op | source)
XLA Modules:
  0.0 20.2 jit_solution(15668699818939882910)
XLA Ops:
  0.0 1.0 %pack.1 = (bf16[128,512]{1,0:T(8,128)(2,1)S(1)}, bf16[48,512]{1,0:T(8,128)(2,1)S(1)}, bf16[80,512]{1,0:T(8,128)(2,1)S(1)}) custom-call(s32[4,8]{1,0:T(4,128)} %kept.3, bf16[128,1024]{1,0:T(8,128)(2,1)} %doubles.1), custom_call_target="tpu_custom_call" | custom-call | tf_op jit(solution)/shard_map/pack/pallas_call | solution.py:207
  1.0 5.1 %collective-permute-start.1 = (bf16[80,512]{1,0:T(8,128)(2,1)S(1)}, bf16[80,512]{1,0:T(8,128)(2,1)S(1)}, u32[]{:S(2)}, u32[]{:S(2)}) collective-permute-start(bf16[80,512]{1,0:T(8,128)(2,1)S(1)} %get-tuple-element.18), channel_id=1, source_target_pairs={{0,12},{1,9},{2,14},{3,11},{4,8},{5,13},{6,10},{7,15},{8,4},{9,1},... | collective-permute-start | bytes 245768 | tf_op jit(solution)/shard_map/ppermute | solution.py:187
  6.1 0.0 collective-permute-start
  6.1 0.6 %collective-permute-start.2 = (bf16[48,512]{1,0:T(8,128)(2,1)S(1)}, bf16[48,512]{1,0:T(8,128)(2,1)S(1)}, u32[]{:S(2)}, u32[]{:S(2)}) collective-permute-start(bf16[48,512]{1,0:T(8,128)(2,1)S(1)} %get-tuple-element.19), channel_id=1, source_target_pairs={{0,8},{1,13},{2,10},{3,15},{4,12},{5,9},{6,14},{7,11},{8,0},{9,5},... | collective-permute-start | bytes 147464 | tf_op jit(solution)/shard_map/ppermute | solution.py:187
  6.8 3.7 %collective-permute-start.3 = (bf16[48,512]{1,0:T(8,128)(2,1)S(1)}, bf16[48,512]{1,0:T(8,128)(2,1)S(1)}, u32[]{:S(2)}, u32[]{:S(2)}) collective-permute-start(bf16[48,512]{1,0:T(8,128)(2,1)S(1)} %get-tuple-element.19), channel_id=1, source_target_pairs={{0,12},{1,9},{2,14},{3,11},{4,8},{5,13},{6,10},{7,15},{8,4},{9,1},... | collective-permute-start | bytes 147464 | tf_op jit(solution)/shard_map/ppermute | solution.py:187
  10.5 0.0 collective-permute-done.1.near_second
  10.5 0.1 collective-permute-start.4
  10.6 1.6 %prepare.1 = (bf16[4,512,256]{2,1,0:T(8,128)(2,1)S(1)}, f32[128,256]{1,0:T(8,128)S(1)}) custom-call(s32[4,8]{1,0:T(4,128)} %kept.3, s32[2,8]{1,0:T(2,128)} %bitcast.1, bf16[1024,256]{1,0:T(8,128)(2,1)} %integrals.1, bf16[128,512]{1,0:T(8,128)(2,1)S(1)} %get-tuple-element.15.own), custom_call_target="tpu_custom_call" | custom-call | flops 1150000000 | bytes 1024 | tf_op jit(solution)/shard_map/prepare/pallas_call | solution.py:226
  12.3 0.2 %collective-permute-done.2.far_first = bf16[48,512]{1,0:T(8,128)(2,1)S(1)} collective-permute-done((bf16[48,512]{1,0:T(8,128)(2,1)S(1)}, bf16[48,512]{1,0:T(8,128)(2,1)S(1)}, u32[]{:S(2)}, u32[]{:S(2)}) %collective-permute-start.2) | collective-permute-done | bytes 49184 | tf_op jit(solution)/shard_map/ppermute | solution.py:187
  12.5 1.2 %collective-permute-done.3.near_first = bf16[48,512]{1,0:T(8,128)(2,1)S(1)} collective-permute-done((bf16[48,512]{1,0:T(8,128)(2,1)S(1)}, bf16[48,512]{1,0:T(8,128)(2,1)S(1)}, u32[]{:S(2)}, u32[]{:S(2)}) %collective-permute-start.3) | collective-permute-done | bytes 49184 | tf_op jit(solution)/shard_map/ppermute | solution.py:187
  13.8 0.3 %collective-permute-done.pair = bf16[128,512]{1,0:T(8,128)(2,1)S(1)} collective-permute-done((bf16[128,512]{1,0:T(8,128)(2,1)S(1)}, bf16[128,512]{1,0:T(8,128)(2,1)S(1)}, u32[]{:S(2)}, u32[]{:S(2)}) %collective-permute-start) | collective-permute-done | bytes 131104 | tf_op jit(solution)/shard_map/ppermute | solution.py:182
  14.1 0.3 %early.1 = (f32[4,128,256]{2,1,0:T(8,128)S(1)}, s16[272,128]{1,0:T(8,128)(2,1)S(1)}) custom-call(f32[128,256]{1,0:T(8,128)S(1)} %get-tuple-element.16.product, bf16[4,512,256]{2,1,0:T(8,128)(2,1)S(1)} %get-tuple-element.17.gathered, bf16[128,512]{1,0:T(8,128)(2,1)S(1)} %collective-permute-done.pair, bf16[80,512]{1,0:T(8,128)(2,1)S(1)} %collective-permute-done.1.near_second, ...), custom_call_target="tpu_custom_call" | custom-call | bytes 1024 | tf_op jit(solution)/shard_map/early/pallas_call | solution.py:244
  14.4 0.1 collective-permute-start.5
  14.5 0.5 %collective-permute-done.4.far_second = bf16[80,512]{1,0:T(8,128)(2,1)S(1)} collective-permute-done((bf16[80,512]{1,0:T(8,128)(2,1)S(1)}, bf16[80,512]{1,0:T(8,128)(2,1)S(1)}, u32[]{:S(2)}, u32[]{:S(2)}) %collective-permute-start.4) | collective-permute-done | bytes 81952 | tf_op jit(solution)/shard_map/ppermute | solution.py:182
  15.0 0.2 late.1.far_sums
  15.1 0.0 copy-start
  15.2 0.1 rest.1
  15.3 1.6 %collective-permute-start.6 = (s16[272,128]{1,0:T(8,128)(2,1)S(1)}, s16[272,128]{1,0:T(8,128)(2,1)S(1)}, u32[]{:S(2)}, u32[]{:S(2)}) collective-permute-start(s16[272,128]{1,0:T(8,128)(2,1)S(1)} %get-tuple-element.23), channel_id=1, source_target_pairs={{0,2},{1,3},{2,1},{3,0},{4,7},{5,6},{6,4},{7,5},{8,11},{9,10},{10,... | collective-permute-start | bytes 208904 | tf_op jit(solution)/shard_map/ppermute | solution.py:187
  16.9 0.0 collective-permute-start.7
  16.9 2.3 %collective-permute-done.5.one_far = s16[272,128]{1,0:T(8,128)(2,1)S(1)} collective-permute-done((s16[272,128]{1,0:T(8,128)(2,1)S(1)}, s16[272,128]{1,0:T(8,128)(2,1)S(1)}, u32[]{:S(2)}, u32[]{:S(2)}) %collective-permute-start.5) | collective-permute-done | bytes 69664 | tf_op jit(solution)/shard_map/ppermute | solution.py:187
  19.2 0.0 copy-done
  19.3 0.3 %collective-permute-done.6.other_far = s16[272,128]{1,0:T(8,128)(2,1)S(1)} collective-permute-done((s16[272,128]{1,0:T(8,128)(2,1)S(1)}, s16[272,128]{1,0:T(8,128)(2,1)S(1)}, u32[]{:S(2)}, u32[]{:S(2)}) %collective-permute-start.6) | collective-permute-done | bytes 69664 | tf_op jit(solution)/shard_map/ppermute | solution.py:187
  19.5 0.0 collective-permute-done.7.one
  19.5 0.7 %last.1 = f32[128,256]{1,0:T(8,128)} custom-call(f32[128,256]{1,0:T(8,128)S(1)} %first.1.base, s16[272,128]{1,0:T(8,128)(2,1)S(1)} %collective-permute-done.6.other_far, s16[272,128]{1,0:T(8,128)(2,1)S(1)} %collective-permute-done.7.one), custom_call_target="tpu_custom_call" | custom-call | bytes 1024 | tf_op jit(solution)/shard_map/last/pallas_call | solution.py:278
  (1 shorter events, 0.0 us)
Async XLA Ops:
  1.0 9.5 %collective-permute-start.1 = (bf16[80,512]{1,0:T(8,128)(2,1)S(1)}, bf16[80,512]{1,0:T(8,128)(2,1)S(1)}, u32[]{:S(2)}, u32[]{:S(2)}) collective-permute-start(bf16[80,512]{1,0:T(8,128)(2,1)S(1)} %get-tuple-element.18), channel_id=1, source_target_pairs={{0,12},{1,9},{2,14},{3,11},{4,8},{5,13},{6,10},{7,15},{8,4},{9,1},... | collective-permute-start | bytes 245768 | tf_op jit(solution)/shard_map/ppermute | solution.py:187
  6.1 8.0 %collective-permute-start = (bf16[128,512]{1,0:T(8,128)(2,1)S(1)}, bf16[128,512]{1,0:T(8,128)(2,1)S(1)}, u32[]{:S(2)}, u32[]{:S(2)}) collective-permute-start(bf16[128,512]{1,0:T(8,128)(2,1)S(1)} %get-tuple-element.15.own), channel_id=1, source_target_pairs={{0,4},{4,0},{8,12},{12,8},{1,5},{5,1},{9,13},{13,9},{2,6},{6,2},{1... | collective-permute-start | bytes 393224 | tf_op jit(solution)/shard_map/ppermute | solution.py:182
  6.1 6.4 %collective-permute-start.2 = (bf16[48,512]{1,0:T(8,128)(2,1)S(1)}, bf16[48,512]{1,0:T(8,128)(2,1)S(1)}, u32[]{:S(2)}, u32[]{:S(2)}) collective-permute-start(bf16[48,512]{1,0:T(8,128)(2,1)S(1)} %get-tuple-element.19), channel_id=1, source_target_pairs={{0,8},{1,13},{2,10},{3,15},{4,12},{5,9},{6,14},{7,11},{8,0},{9,5},... | collective-permute-start | bytes 147464 | tf_op jit(solution)/shard_map/ppermute | solution.py:187
  6.8 7.0 %collective-permute-start.3 = (bf16[48,512]{1,0:T(8,128)(2,1)S(1)}, bf16[48,512]{1,0:T(8,128)(2,1)S(1)}, u32[]{:S(2)}, u32[]{:S(2)}) collective-permute-start(bf16[48,512]{1,0:T(8,128)(2,1)S(1)} %get-tuple-element.19), channel_id=1, source_target_pairs={{0,12},{1,9},{2,14},{3,11},{4,8},{5,13},{6,10},{7,15},{8,4},{9,1},... | collective-permute-start | bytes 147464 | tf_op jit(solution)/shard_map/ppermute | solution.py:187
  10.5 4.4 %collective-permute-start.4 = (bf16[80,512]{1,0:T(8,128)(2,1)S(1)}, bf16[80,512]{1,0:T(8,128)(2,1)S(1)}, u32[]{:S(2)}, u32[]{:S(2)}) collective-permute-start(bf16[80,512]{1,0:T(8,128)(2,1)S(1)} %collective-permute-done.1.near_second), channel_id=1, source_target_pairs={{0,4},{4,0},{8,12},{12,8},{1,5},{5,1},{9,13},{13,9},{2,6},{6,2},{1... | collective-permute-start | bytes 245768 | tf_op jit(solution)/shard_map/ppermute | solution.py:182
  14.4 4.8 %collective-permute-start.5 = (s16[272,128]{1,0:T(8,128)(2,1)S(1)}, s16[272,128]{1,0:T(8,128)(2,1)S(1)}, u32[]{:S(2)}, u32[]{:S(2)}) collective-permute-start(s16[272,128]{1,0:T(8,128)(2,1)S(1)} %get-tuple-element.22), channel_id=1, source_target_pairs={{0,3},{1,2},{2,0},{3,1},{4,6},{5,7},{6,5},{7,4},{8,10},{9,11},{10,... | collective-permute-start | bytes 208904 | tf_op jit(solution)/shard_map/ppermute | solution.py:187
  15.1 4.1 %copy-start = (f32[128,256]{1,0:T(8,128)S(1)}, f32[128,256]{1,0:T(8,128)}, u32[]{:S(2)}) copy-start(f32[128,256]{1,0:T(8,128)} %residual.1) | copy-start | bytes 393220
  15.3 4.2 %collective-permute-start.6 = (s16[272,128]{1,0:T(8,128)(2,1)S(1)}, s16[272,128]{1,0:T(8,128)(2,1)S(1)}, u32[]{:S(2)}, u32[]{:S(2)}) collective-permute-start(s16[272,128]{1,0:T(8,128)(2,1)S(1)} %get-tuple-element.23), channel_id=1, source_target_pairs={{0,2},{1,3},{2,1},{3,0},{4,7},{5,6},{6,4},{7,5},{8,11},{9,10},{10,... | collective-permute-start | bytes 208904 | tf_op jit(solution)/shard_map/ppermute | solution.py:187
  16.9 2.6 %collective-permute-start.7 = (s16[272,128]{1,0:T(8,128)(2,1)S(1)}, s16[272,128]{1,0:T(8,128)(2,1)S(1)}, u32[]{:S(2)}, u32[]{:S(2)}) collective-permute-start(s16[272,128]{1,0:T(8,128)(2,1)S(1)} %get-tuple-element.24), channel_id=1, source_target_pairs={{0,1},{1,0},{2,3},{3,2},{4,5},{5,4},{6,7},{7,6},{8,9},{9,8},{10,11... | collective-permute-start | bytes 208904 | tf_op jit(solution)/shard_map/ppermute | solution.py:182

commit v30 on v29

--- a/solution.py
+++ b/solution.py
@@ -115,15 +115,14 @@
 
 def chip_steps(row, col):
     odd = row % 2
-    own = row // 2 == col // 2
-    first = own * (3 - odd) + (1 - own) * (2 + odd)
+    first = 3 - odd
     return first, 5 - first
 
 
 def steps_here():
     row, col = lax.axis_index("rows"), lax.axis_index("cols")
     odd = row % 2
-    first = jnp.where(row // 2 == col // 2, 3 - odd, 2 + odd)
+    first = 3 - odd
     return first, 5 - first
 
 

time: 20.6 us -> 21.2 us (1.029)
  waiting for transfers between devices: 4.88 us -> 5.66 us
    ppermute x5, waiting for transfers between devices: 4.07 us -> 4.86 us  [permute(): lax.ppermute(x, ('rows', 'cols'), [(i, r * ROWS + c) for i, (r, c) in pai...]
where the time goes in v30:
time: 21.2 us; the launch traced here: 21 us
  starting transfers between devices  11.2 us (53%)
  waiting for transfers between devices  5.66 us (27%)
  Pallas kernels  4.01 us (19%)
    ppermute x5, starting transfers between devices, permute(): lax.ppermute(x, ('rows', 'cols'), [(i, r * ROWS + c) for i, (r, c) in pai...  11.1 us
    ppermute x5, waiting for transfers between devices, permute(): lax.ppermute(x, ('rows', 'cols'), [(i, r * ROWS + c) for i, (r, c) in pai...  4.86 us
    pallas_call x1, Pallas kernels, local_few(): pl.pallas_call(functools.partial(prepare_kernel, tiles, slots), out_shape...  1.64 us
    pallas_call x1, Pallas kernels, local_few(): pl.pallas_call(functools.partial(pack_kernel, tiles, slots), out_shape=[j...  1.01 us
    ppermute x3, waiting for transfers between devices, swap(): return lax.ppermute(x, axis, [(i, i ^ step) for i in range(ROWS)])  0.8 us
    pallas_call x1, Pallas kernels, local_few(): pl.pallas_call(last_kernel, out_shape=sums_shape, in_specs=[VMEM] * 3, ou...  0.7 us
    pallas_call x4, Pallas kernels, on_vmem(): pl.pallas_call(kernel, out_shape=out_shape, in_specs=[VMEM] * len(args),...  0.66 us
  transfers between devices with their start and end apart: 8, of which 6 were waited for; matrix products, arithmetic and copies ran while one was open for 0% of the time, Pallas kernels for 11%

profile of v30, /device:TPU:0, one launch (start us, length us, event | category | flops | bytes accessed | tf_op | source)
XLA Modules:
  0.0 21.0 jit_solution(5066889622844734428)
XLA Ops:
  0.0 1.0 %pack.1 = (bf16[128,512]{1,0:T(8,128)(2,1)S(1)}, bf16[48,512]{1,0:T(8,128)(2,1)S(1)}, bf16[80,512]{1,0:T(8,128)(2,1)S(1)}) custom-call(s32[4,8]{1,0:T(4,128)} %kept.3, bf16[128,1024]{1,0:T(8,128)(2,1)} %doubles.1), custom_call_target="tpu_custom_call" | custom-call | tf_op jit(solution)/shard_map/pack/pallas_call | solution.py:206
  1.0 5.1 %collective-permute-start.1 = (bf16[80,512]{1,0:T(8,128)(2,1)S(1)}, bf16[80,512]{1,0:T(8,128)(2,1)S(1)}, u32[]{:S(2)}, u32[]{:S(2)}) collective-permute-start(bf16[80,512]{1,0:T(8,128)(2,1)S(1)} %get-tuple-element.18), channel_id=1, source_target_pairs={{0,12},{1,9},{2,14},{3,11},{4,8},{5,13},{6,10},{7,15},{8,4},{9,1},... | collective-permute-start | bytes 245768 | tf_op jit(solution)/shard_map/ppermute | solution.py:186
  6.1 0.0 collective-permute-start
  6.1 0.6 %collective-permute-start.2 = (bf16[48,512]{1,0:T(8,128)(2,1)S(1)}, bf16[48,512]{1,0:T(8,128)(2,1)S(1)}, u32[]{:S(2)}, u32[]{:S(2)}) collective-permute-start(bf16[48,512]{1,0:T(8,128)(2,1)S(1)} %get-tuple-element.19), channel_id=1, source_target_pairs={{0,8},{1,13},{2,10},{3,15},{4,12},{5,9},{6,14},{7,11},{8,0},{9,5},... | collective-permute-start | bytes 147464 | tf_op jit(solution)/shard_map/ppermute | solution.py:186
  6.8 3.7 %collective-permute-start.3 = (bf16[48,512]{1,0:T(8,128)(2,1)S(1)}, bf16[48,512]{1,0:T(8,128)(2,1)S(1)}, u32[]{:S(2)}, u32[]{:S(2)}) collective-permute-start(bf16[48,512]{1,0:T(8,128)(2,1)S(1)} %get-tuple-element.19), channel_id=1, source_target_pairs={{0,12},{1,9},{2,14},{3,11},{4,8},{5,13},{6,10},{7,15},{8,4},{9,1},... | collective-permute-start | bytes 147464 | tf_op jit(solution)/shard_map/ppermute | solution.py:186
  10.5 0.0 collective-permute-done.1.near_second
  10.5 0.1 collective-permute-start.4
  10.6 1.6 %prepare.1 = (bf16[4,512,256]{2,1,0:T(8,128)(2,1)S(1)}, f32[128,256]{1,0:T(8,128)S(1)}) custom-call(s32[4,8]{1,0:T(4,128)} %kept.3, s32[2,8]{1,0:T(2,128)} %bitcast.1, bf16[1024,256]{1,0:T(8,128)(2,1)} %integrals.1, bf16[128,512]{1,0:T(8,128)(2,1)S(1)} %get-tuple-element.15.own), custom_call_target="tpu_custom_call" | custom-call | flops 1150000000 | bytes 1024 | tf_op jit(solution)/shard_map/prepare/pallas_call | solution.py:225
  12.3 0.2 %collective-permute-done.2.far_first = bf16[48,512]{1,0:T(8,128)(2,1)S(1)} collective-permute-done((bf16[48,512]{1,0:T(8,128)(2,1)S(1)}, bf16[48,512]{1,0:T(8,128)(2,1)S(1)}, u32[]{:S(2)}, u32[]{:S(2)}) %collective-permute-start.2) | collective-permute-done | bytes 49184 | tf_op jit(solution)/shard_map/ppermute | solution.py:186
  12.5 1.2 %collective-permute-done.3.near_first = bf16[48,512]{1,0:T(8,128)(2,1)S(1)} collective-permute-done((bf16[48,512]{1,0:T(8,128)(2,1)S(1)}, bf16[48,512]{1,0:T(8,128)(2,1)S(1)}, u32[]{:S(2)}, u32[]{:S(2)}) %collective-permute-start.3) | collective-permute-done | bytes 49184 | tf_op jit(solution)/shard_map/ppermute | solution.py:186
  13.8 0.3 %collective-permute-done.pair = bf16[128,512]{1,0:T(8,128)(2,1)S(1)} collective-permute-done((bf16[128,512]{1,0:T(8,128)(2,1)S(1)}, bf16[128,512]{1,0:T(8,128)(2,1)S(1)}, u32[]{:S(2)}, u32[]{:S(2)}) %collective-permute-start) | collective-permute-done | bytes 131104 | tf_op jit(solution)/shard_map/ppermute | solution.py:181
  14.1 0.3 %early.1 = (f32[4,128,256]{2,1,0:T(8,128)S(1)}, s16[272,128]{1,0:T(8,128)(2,1)S(1)}) custom-call(f32[128,256]{1,0:T(8,128)S(1)} %get-tuple-element.16.product, bf16[4,512,256]{2,1,0:T(8,128)(2,1)S(1)} %get-tuple-element.17.gathered, bf16[128,512]{1,0:T(8,128)(2,1)S(1)} %collective-permute-done.pair, bf16[80,512]{1,0:T(8,128)(2,1)S(1)} %collective-permute-done.1.near_second, ...), custom_call_target="tpu_custom_call" | custom-call | bytes 1024 | tf_op jit(solution)/shard_map/early/pallas_call | solution.py:243
  14.4 0.1 collective-permute-start.5
  14.5 0.5 %collective-permute-done.4.far_second = bf16[80,512]{1,0:T(8,128)(2,1)S(1)} collective-permute-done((bf16[80,512]{1,0:T(8,128)(2,1)S(1)}, bf16[80,512]{1,0:T(8,128)(2,1)S(1)}, u32[]{:S(2)}, u32[]{:S(2)}) %collective-permute-start.4) | collective-permute-done | bytes 81952 | tf_op jit(solution)/shard_map/ppermute | solution.py:181
  15.0 0.2 late.1.far_sums
  15.1 0.0 copy-start
  15.2 0.1 rest.1
  15.3 1.6 %collective-permute-start.6 = (s16[272,128]{1,0:T(8,128)(2,1)S(1)}, s16[272,128]{1,0:T(8,128)(2,1)S(1)}, u32[]{:S(2)}, u32[]{:S(2)}) collective-permute-start(s16[272,128]{1,0:T(8,128)(2,1)S(1)} %get-tuple-element.23), channel_id=1, source_target_pairs={{0,2},{1,3},{2,0},{3,1},{4,7},{5,6},{6,5},{7,4},{8,10},{9,11},{10,... | collective-permute-start | bytes 208904 | tf_op jit(solution)/shard_map/ppermute | solution.py:186
  16.9 0.0 collective-permute-start.7
  16.9 2.1 %collective-permute-done.5.one_far = s16[272,128]{1,0:T(8,128)(2,1)S(1)} collective-permute-done((s16[272,128]{1,0:T(8,128)(2,1)S(1)}, s16[272,128]{1,0:T(8,128)(2,1)S(1)}, u32[]{:S(2)}, u32[]{:S(2)}) %collective-permute-start.5) | collective-permute-done | bytes 69664 | tf_op jit(solution)/shard_map/ppermute | solution.py:186
  18.9 0.0 copy-done
  19.0 1.3 %collective-permute-done.6.other_far = s16[272,128]{1,0:T(8,128)(2,1)S(1)} collective-permute-done((s16[272,128]{1,0:T(8,128)(2,1)S(1)}, s16[272,128]{1,0:T(8,128)(2,1)S(1)}, u32[]{:S(2)}, u32[]{:S(2)}) %collective-permute-start.6) | collective-permute-done | bytes 69664 | tf_op jit(solution)/shard_map/ppermute | solution.py:186
  20.3 0.0 collective-permute-done.7.one
  20.3 0.7 %last.1 = f32[128,256]{1,0:T(8,128)} custom-call(f32[128,256]{1,0:T(8,128)S(1)} %first.1.base, s16[272,128]{1,0:T(8,128)(2,1)S(1)} %collective-permute-done.6.other_far, s16[272,128]{1,0:T(8,128)(2,1)S(1)} %collective-permute-done.7.one), custom_call_target="tpu_custom_call" | custom-call | bytes 1024 | tf_op jit(solution)/shard_map/last/pallas_call | solution.py:277
  (1 shorter events, 0.0 us)
Async XLA Ops:
  1.0 9.5 %collective-permute-start.1 = (bf16[80,512]{1,0:T(8,128)(2,1)S(1)}, bf16[80,512]{1,0:T(8,128)(2,1)S(1)}, u32[]{:S(2)}, u32[]{:S(2)}) collective-permute-start(bf16[80,512]{1,0:T(8,128)(2,1)S(1)} %get-tuple-element.18), channel_id=1, source_target_pairs={{0,12},{1,9},{2,14},{3,11},{4,8},{5,13},{6,10},{7,15},{8,4},{9,1},... | collective-permute-start | bytes 245768 | tf_op jit(solution)/shard_map/ppermute | solution.py:186
  6.1 8.0 %collective-permute-start = (bf16[128,512]{1,0:T(8,128)(2,1)S(1)}, bf16[128,512]{1,0:T(8,128)(2,1)S(1)}, u32[]{:S(2)}, u32[]{:S(2)}) collective-permute-start(bf16[128,512]{1,0:T(8,128)(2,1)S(1)} %get-tuple-element.15.own), channel_id=1, source_target_pairs={{0,4},{4,0},{8,12},{12,8},{1,5},{5,1},{9,13},{13,9},{2,6},{6,2},{1... | collective-permute-start | bytes 393224 | tf_op jit(solution)/shard_map/ppermute | solution.py:181
  6.1 6.4 %collective-permute-start.2 = (bf16[48,512]{1,0:T(8,128)(2,1)S(1)}, bf16[48,512]{1,0:T(8,128)(2,1)S(1)}, u32[]{:S(2)}, u32[]{:S(2)}) collective-permute-start(bf16[48,512]{1,0:T(8,128)(2,1)S(1)} %get-tuple-element.19), channel_id=1, source_target_pairs={{0,8},{1,13},{2,10},{3,15},{4,12},{5,9},{6,14},{7,11},{8,0},{9,5},... | collective-permute-start | bytes 147464 | tf_op jit(solution)/shard_map/ppermute | solution.py:186
  6.8 7.0 %collective-permute-start.3 = (bf16[48,512]{1,0:T(8,128)(2,1)S(1)}, bf16[48,512]{1,0:T(8,128)(2,1)S(1)}, u32[]{:S(2)}, u32[]{:S(2)}) collective-permute-start(bf16[48,512]{1,0:T(8,128)(2,1)S(1)} %get-tuple-element.19), channel_id=1, source_target_pairs={{0,12},{1,9},{2,14},{3,11},{4,8},{5,13},{6,10},{7,15},{8,4},{9,1},... | collective-permute-start | bytes 147464 | tf_op jit(solution)/shard_map/ppermute | solution.py:186
  10.5 4.4 %collective-permute-start.4 = (bf16[80,512]{1,0:T(8,128)(2,1)S(1)}, bf16[80,512]{1,0:T(8,128)(2,1)S(1)}, u32[]{:S(2)}, u32[]{:S(2)}) collective-permute-start(bf16[80,512]{1,0:T(8,128)(2,1)S(1)} %collective-permute-done.1.near_second), channel_id=1, source_target_pairs={{0,4},{4,0},{8,12},{12,8},{1,5},{5,1},{9,13},{13,9},{2,6},{6,2},{1... | collective-permute-start | bytes 245768 | tf_op jit(solution)/shard_map/ppermute | solution.py:181
  14.4 4.5 %collective-permute-start.5 = (s16[272,128]{1,0:T(8,128)(2,1)S(1)}, s16[272,128]{1,0:T(8,128)(2,1)S(1)}, u32[]{:S(2)}, u32[]{:S(2)}) collective-permute-start(s16[272,128]{1,0:T(8,128)(2,1)S(1)} %get-tuple-element.22), channel_id=1, source_target_pairs={{0,3},{1,2},{2,1},{3,0},{4,6},{5,7},{6,4},{7,5},{8,11},{9,10},{10,... | collective-permute-start | bytes 208904 | tf_op jit(solution)/shard_map/ppermute | solution.py:186
  15.1 3.8 %copy-start = (f32[128,256]{1,0:T(8,128)S(1)}, f32[128,256]{1,0:T(8,128)}, u32[]{:S(2)}) copy-start(f32[128,256]{1,0:T(8,128)} %residual.1) | copy-start | bytes 393220
  15.3 5.0 %collective-permute-start.6 = (s16[272,128]{1,0:T(8,128)(2,1)S(1)}, s16[272,128]{1,0:T(8,128)(2,1)S(1)}, u32[]{:S(2)}, u32[]{:S(2)}) collective-permute-start(s16[272,128]{1,0:T(8,128)(2,1)S(1)} %get-tuple-element.23), channel_id=1, source_target_pairs={{0,2},{1,3},{2,0},{3,1},{4,7},{5,6},{6,5},{7,4},{8,10},{9,11},{10,... | collective-permute-start | bytes 208904 | tf_op jit(solution)/shard_map/ppermute | solution.py:186
  16.9 3.4 %collective-permute-start.7 = (s16[272,128]{1,0:T(8,128)(2,1)S(1)}, s16[272,128]{1,0:T(8,128)(2,1)S(1)}, u32[]{:S(2)}, u32[]{:S(2)}) collective-permute-start(s16[272,128]{1,0:T(8,128)(2,1)S(1)} %get-tuple-element.24), channel_id=1, source_target_pairs={{0,1},{1,0},{2,3},{3,2},{4,5},{5,4},{6,7},{7,6},{8,9},{9,8},{10,11... | collective-permute-start | bytes 208904 | tf_op jit(solution)/shard_map/ppermute | solution.py:181

commit v31 on v29

--- a/solution.py
+++ b/solution.py
@@ -16,7 +16,7 @@
 VMEM = pl.BlockSpec(memory_space=pltpu.VMEM)
 HBM = pl.BlockSpec(memory_space=pltpu.HBM)
 PARAMS = pltpu.CompilerParams(vmem_limit_bytes=8 * 1024 * 1024)
-DIRECT = 48
+DIRECT = 32
 PIECES = 4
 ROWS = 4
 

time: 20.6 us -> 20.6 us (level)
  starting transfers between devices: 11.3 us -> 12.5 us
  waiting for transfers between devices: 4.88 us -> 3.77 us
    ppermute x5, waiting for transfers between devices: 4.07 us -> 2.79 us  [permute(): lax.ppermute(x, ('rows', 'cols'), [(i, r * ROWS + c) for i, (r, c) in pai...]
    ppermute x3, starting transfers between devices: 0.12 us -> 0.96 us  [swap(): return lax.ppermute(x, axis, [(i, i ^ step) for i in range(ROWS)])]
    ppermute x5, starting transfers between devices: 11.1 us -> 11.6 us  [permute(): lax.ppermute(x, ('rows', 'cols'), [(i, r * ROWS + c) for i, (r, c) in pai...]
  transfers between devices with their start and end apart: 8 -> 8, of which waited for: 6 -> 4; matrix products, arithmetic and copies ran while one was open for 0% -> 0% of each run, Pallas kernels for 11% -> 11%
where the time goes in v31:
time: 20.6 us; the launch traced here: 20.4 us
  starting transfers between devices  12.5 us (61%)
  Pallas kernels  4.03 us (20%)
  waiting for transfers between devices  3.77 us (18%)
    ppermute x5, starting transfers between devices, permute(): lax.ppermute(x, ('rows', 'cols'), [(i, r * ROWS + c) for i, (r, c) in pai...  11.6 us
    ppermute x5, waiting for transfers between devices, permute(): lax.ppermute(x, ('rows', 'cols'), [(i, r * ROWS + c) for i, (r, c) in pai...  2.79 us
    pallas_call x1, Pallas kernels, local_few(): pl.pallas_call(functools.partial(prepare_kernel, tiles, slots), out_shape...  1.63 us
    pallas_call x1, Pallas kernels, local_few(): pl.pallas_call(functools.partial(pack_kernel, tiles, slots), out_shape=[j...  1.01 us
    ppermute x3, waiting for transfers between devices, swap(): return lax.ppermute(x, axis, [(i, i ^ step) for i in range(ROWS)])  0.98 us
    ppermute x3, starting transfers between devices, swap(): return lax.ppermute(x, axis, [(i, i ^ step) for i in range(ROWS)])  0.96 us
    pallas_call x1, Pallas kernels, local_few(): pl.pallas_call(last_kernel, out_shape=sums_shape, in_specs=[VMEM] * 3, ou...  0.7 us
    pallas_call x4, Pallas kernels, on_vmem(): pl.pallas_call(kernel, out_shape=out_shape, in_specs=[VMEM] * len(args),...  0.68 us
  transfers between devices with their start and end apart: 8, of which 4 were waited for; matrix products, arithmetic and copies ran while one was open for 0% of the time, Pallas kernels for 11%

profile of v31, /device:TPU:0, one launch (start us, length us, event | category | flops | bytes accessed | tf_op | source)
XLA Modules:
  0.0 20.4 jit_solution(7314867824064175897)
XLA Ops:
  0.0 1.0 %pack.1 = (bf16[128,512]{1,0:T(8,128)(2,1)S(1)}, bf16[32,512]{1,0:T(8,128)(2,1)S(1)}, bf16[96,512]{1,0:T(8,128)(2,1)S(1)}) custom-call(s32[4,8]{1,0:T(4,128)} %kept.3, bf16[128,1024]{1,0:T(8,128)(2,1)} %doubles.1), custom_call_target="tpu_custom_call" | custom-call | tf_op jit(solution)/shard_map/pack/pallas_call | solution.py:207
  1.0 5.1 %collective-permute-start.1 = (bf16[96,512]{1,0:T(8,128)(2,1)S(1)}, bf16[96,512]{1,0:T(8,128)(2,1)S(1)}, u32[]{:S(2)}, u32[]{:S(2)}) collective-permute-start(bf16[96,512]{1,0:T(8,128)(2,1)S(1)} %get-tuple-element.18), channel_id=1, source_target_pairs={{0,12},{1,9},{2,14},{3,11},{4,8},{5,13},{6,10},{7,15},{8,4},{9,1},... | collective-permute-start | bytes 294920 | tf_op jit(solution)/shard_map/ppermute | solution.py:187
  6.1 0.0 collective-permute-start
  6.1 0.6 %collective-permute-start.2 = (bf16[32,512]{1,0:T(8,128)(2,1)S(1)}, bf16[32,512]{1,0:T(8,128)(2,1)S(1)}, u32[]{:S(2)}, u32[]{:S(2)}) collective-permute-start(bf16[32,512]{1,0:T(8,128)(2,1)S(1)} %get-tuple-element.19), channel_id=1, source_target_pairs={{0,8},{1,13},{2,10},{3,15},{4,12},{5,9},{6,14},{7,11},{8,0},{9,5},... | collective-permute-start | bytes 98312 | tf_op jit(solution)/shard_map/ppermute | solution.py:187
  6.8 3.7 %collective-permute-start.3 = (bf16[32,512]{1,0:T(8,128)(2,1)S(1)}, bf16[32,512]{1,0:T(8,128)(2,1)S(1)}, u32[]{:S(2)}, u32[]{:S(2)}) collective-permute-start(bf16[32,512]{1,0:T(8,128)(2,1)S(1)} %get-tuple-element.19), channel_id=1, source_target_pairs={{0,12},{1,9},{2,14},{3,11},{4,8},{5,13},{6,10},{7,15},{8,4},{9,1},... | collective-permute-start | bytes 98312 | tf_op jit(solution)/shard_map/ppermute | solution.py:187
  10.5 0.0 collective-permute-done.1.near_second
  10.5 1.0 %collective-permute-start.4 = (bf16[96,512]{1,0:T(8,128)(2,1)S(1)}, bf16[96,512]{1,0:T(8,128)(2,1)S(1)}, u32[]{:S(2)}, u32[]{:S(2)}) collective-permute-start(bf16[96,512]{1,0:T(8,128)(2,1)S(1)} %collective-permute-done.1.near_second), channel_id=1, source_target_pairs={{0,4},{4,0},{8,12},{12,8},{1,5},{5,1},{9,13},{13,9},{2,6},{6,2},{1... | collective-permute-start | bytes 294920 | tf_op jit(solution)/shard_map/ppermute | solution.py:182
  11.5 1.6 %prepare.1 = (bf16[4,512,256]{2,1,0:T(8,128)(2,1)S(1)}, f32[128,256]{1,0:T(8,128)S(1)}) custom-call(s32[4,8]{1,0:T(4,128)} %kept.3, s32[2,8]{1,0:T(2,128)} %bitcast.1, bf16[1024,256]{1,0:T(8,128)(2,1)} %integrals.1, bf16[128,512]{1,0:T(8,128)(2,1)S(1)} %get-tuple-element.15.own), custom_call_target="tpu_custom_call" | custom-call | flops 1150000000 | bytes 1024 | tf_op jit(solution)/shard_map/prepare/pallas_call | solution.py:226
  13.1 0.0 collective-permute-done.2.far_first
  13.1 0.2 collective-permute-done.3.near_first
  13.3 0.0 collective-permute-done.pair
  13.3 0.3 %early.1 = (f32[4,128,256]{2,1,0:T(8,128)S(1)}, s16[272,128]{1,0:T(8,128)(2,1)S(1)}) custom-call(f32[128,256]{1,0:T(8,128)S(1)} %get-tuple-element.16.product, bf16[4,512,256]{2,1,0:T(8,128)(2,1)S(1)} %get-tuple-element.17.gathered, bf16[128,512]{1,0:T(8,128)(2,1)S(1)} %collective-permute-done.pair, bf16[96,512]{1,0:T(8,128)(2,1)S(1)} %collective-permute-done.1.near_second, ...), custom_call_target="tpu_custom_call" | custom-call | bytes 1024 | tf_op jit(solution)/shard_map/early/pallas_call | solution.py:244
  13.6 0.5 %collective-permute-start.5 = (s16[272,128]{1,0:T(8,128)(2,1)S(1)}, s16[272,128]{1,0:T(8,128)(2,1)S(1)}, u32[]{:S(2)}, u32[]{:S(2)}) collective-permute-start(s16[272,128]{1,0:T(8,128)(2,1)S(1)} %get-tuple-element.22), channel_id=1, source_target_pairs={{0,3},{1,2},{2,0},{3,1},{4,6},{5,7},{6,5},{7,4},{8,10},{9,11},{10,... | collective-permute-start | bytes 208904 | tf_op jit(solution)/shard_map/ppermute | solution.py:187
  14.2 1.0 %collective-permute-done.4.far_second = bf16[96,512]{1,0:T(8,128)(2,1)S(1)} collective-permute-done((bf16[96,512]{1,0:T(8,128)(2,1)S(1)}, bf16[96,512]{1,0:T(8,128)(2,1)S(1)}, u32[]{:S(2)}, u32[]{:S(2)}) %collective-permute-start.4) | collective-permute-done | bytes 98336 | tf_op jit(solution)/shard_map/ppermute | solution.py:182
  15.1 0.2 late.1.far_sums
  15.3 0.0 copy-start
  15.3 0.1 rest.1
  15.5 1.5 %collective-permute-start.6 = (s16[272,128]{1,0:T(8,128)(2,1)S(1)}, s16[272,128]{1,0:T(8,128)(2,1)S(1)}, u32[]{:S(2)}, u32[]{:S(2)}) collective-permute-start(s16[272,128]{1,0:T(8,128)(2,1)S(1)} %get-tuple-element.23), channel_id=1, source_target_pairs={{0,2},{1,3},{2,1},{3,0},{4,7},{5,6},{6,4},{7,5},{8,11},{9,10},{10,... | collective-permute-start | bytes 208904 | tf_op jit(solution)/shard_map/ppermute | solution.py:187
  17.0 0.0 collective-permute-start.7
  17.0 1.0 %collective-permute-done.5.one_far = s16[272,128]{1,0:T(8,128)(2,1)S(1)} collective-permute-done((s16[272,128]{1,0:T(8,128)(2,1)S(1)}, s16[272,128]{1,0:T(8,128)(2,1)S(1)}, u32[]{:S(2)}, u32[]{:S(2)}) %collective-permute-start.5) | collective-permute-done | bytes 69664 | tf_op jit(solution)/shard_map/ppermute | solution.py:187
  18.0 0.0 copy-done
  18.0 1.7 %collective-permute-done.6.other_far = s16[272,128]{1,0:T(8,128)(2,1)S(1)} collective-permute-done((s16[272,128]{1,0:T(8,128)(2,1)S(1)}, s16[272,128]{1,0:T(8,128)(2,1)S(1)}, u32[]{:S(2)}, u32[]{:S(2)}) %collective-permute-start.6) | collective-permute-done | bytes 69664 | tf_op jit(solution)/shard_map/ppermute | solution.py:187
  19.7 0.0 collective-permute-done.7.one
  19.7 0.7 %last.1 = f32[128,256]{1,0:T(8,128)} custom-call(f32[128,256]{1,0:T(8,128)S(1)} %first.1.base, s16[272,128]{1,0:T(8,128)(2,1)S(1)} %collective-permute-done.6.other_far, s16[272,128]{1,0:T(8,128)(2,1)S(1)} %collective-permute-done.7.one), custom_call_target="tpu_custom_call" | custom-call | bytes 1024 | tf_op jit(solution)/shard_map/last/pallas_call | solution.py:278
  (1 shorter events, 0.0 us)
Async XLA Ops:
  1.0 9.5 %collective-permute-start.1 = (bf16[96,512]{1,0:T(8,128)(2,1)S(1)}, bf16[96,512]{1,0:T(8,128)(2,1)S(1)}, u32[]{:S(2)}, u32[]{:S(2)}) collective-permute-start(bf16[96,512]{1,0:T(8,128)(2,1)S(1)} %get-tuple-element.18), channel_id=1, source_target_pairs={{0,12},{1,9},{2,14},{3,11},{4,8},{5,13},{6,10},{7,15},{8,4},{9,1},... | collective-permute-start | bytes 294920 | tf_op jit(solution)/shard_map/ppermute | solution.py:187
  6.1 7.2 %collective-permute-start = (bf16[128,512]{1,0:T(8,128)(2,1)S(1)}, bf16[128,512]{1,0:T(8,128)(2,1)S(1)}, u32[]{:S(2)}, u32[]{:S(2)}) collective-permute-start(bf16[128,512]{1,0:T(8,128)(2,1)S(1)} %get-tuple-element.15.own), channel_id=1, source_target_pairs={{0,4},{4,0},{8,12},{12,8},{1,5},{5,1},{9,13},{13,9},{2,6},{6,2},{1... | collective-permute-start | bytes 393224 | tf_op jit(solution)/shard_map/ppermute | solution.py:182
  6.1 7.0 %collective-permute-start.2 = (bf16[32,512]{1,0:T(8,128)(2,1)S(1)}, bf16[32,512]{1,0:T(8,128)(2,1)S(1)}, u32[]{:S(2)}, u32[]{:S(2)}) collective-permute-start(bf16[32,512]{1,0:T(8,128)(2,1)S(1)} %get-tuple-element.19), channel_id=1, source_target_pairs={{0,8},{1,13},{2,10},{3,15},{4,12},{5,9},{6,14},{7,11},{8,0},{9,5},... | collective-permute-start | bytes 98312 | tf_op jit(solution)/shard_map/ppermute | solution.py:187
  6.8 6.5 %collective-permute-start.3 = (bf16[32,512]{1,0:T(8,128)(2,1)S(1)}, bf16[32,512]{1,0:T(8,128)(2,1)S(1)}, u32[]{:S(2)}, u32[]{:S(2)}) collective-permute-start(bf16[32,512]{1,0:T(8,128)(2,1)S(1)} %get-tuple-element.19), channel_id=1, source_target_pairs={{0,12},{1,9},{2,14},{3,11},{4,8},{5,13},{6,10},{7,15},{8,4},{9,1},... | collective-permute-start | bytes 98312 | tf_op jit(solution)/shard_map/ppermute | solution.py:187
  10.5 4.6 %collective-permute-start.4 = (bf16[96,512]{1,0:T(8,128)(2,1)S(1)}, bf16[96,512]{1,0:T(8,128)(2,1)S(1)}, u32[]{:S(2)}, u32[]{:S(2)}) collective-permute-start(bf16[96,512]{1,0:T(8,128)(2,1)S(1)} %collective-permute-done.1.near_second), channel_id=1, source_target_pairs={{0,4},{4,0},{8,12},{12,8},{1,5},{5,1},{9,13},{13,9},{2,6},{6,2},{1... | collective-permute-start | bytes 294920 | tf_op jit(solution)/shard_map/ppermute | solution.py:182
  13.6 4.4 %collective-permute-start.5 = (s16[272,128]{1,0:T(8,128)(2,1)S(1)}, s16[272,128]{1,0:T(8,128)(2,1)S(1)}, u32[]{:S(2)}, u32[]{:S(2)}) collective-permute-start(s16[272,128]{1,0:T(8,128)(2,1)S(1)} %get-tuple-element.22), channel_id=1, source_target_pairs={{0,3},{1,2},{2,0},{3,1},{4,6},{5,7},{6,5},{7,4},{8,10},{9,11},{10,... | collective-permute-start | bytes 208904 | tf_op jit(solution)/shard_map/ppermute | solution.py:187
  15.3 2.7 %copy-start = (f32[128,256]{1,0:T(8,128)S(1)}, f32[128,256]{1,0:T(8,128)}, u32[]{:S(2)}) copy-start(f32[128,256]{1,0:T(8,128)} %residual.1) | copy-start | bytes 393220
  15.5 4.2 %collective-permute-start.6 = (s16[272,128]{1,0:T(8,128)(2,1)S(1)}, s16[272,128]{1,0:T(8,128)(2,1)S(1)}, u32[]{:S(2)}, u32[]{:S(2)}) collective-permute-start(s16[272,128]{1,0:T(8,128)(2,1)S(1)} %get-tuple-element.23), channel_id=1, source_target_pairs={{0,2},{1,3},{2,1},{3,0},{4,7},{5,6},{6,4},{7,5},{8,11},{9,10},{10,... | collective-permute-start | bytes 208904 | tf_op jit(solution)/shard_map/ppermute | solution.py:187
  17.0 2.7 %collective-permute-start.7 = (s16[272,128]{1,0:T(8,128)(2,1)S(1)}, s16[272,128]{1,0:T(8,128)(2,1)S(1)}, u32[]{:S(2)}, u32[]{:S(2)}) collective-permute-start(s16[272,128]{1,0:T(8,128)(2,1)S(1)} %get-tuple-element.24), channel_id=1, source_target_pairs={{0,1},{1,0},{2,3},{3,2},{4,5},{5,4},{6,7},{7,6},{8,9},{9,8},{10,11... | collective-permute-start | bytes 208904 | tf_op jit(solution)/shard_map/ppermute | solution.py:182
